TPU v7x, 32 devices: a whole 2x2x4 slice. The times are simulated.
32 devices in a mesh: ctx: 16 (over z, y, x), tp: 2 (over core).
Axes of the slice: x: 2, y: 2, z: 4, core: 2. Of those that a mesh axis runs over, the one named last changes fastest.
Arguments:
- tokens: bfloat16 [2048, 4096], P('ctx', 'tp'), may hold values from -216 to 216
- norm_gain: float32 [4096], P('tp'), may hold values from 0.5 to 1.5
- norm_bias: float32 [4096], P('tp'), may hold values from -3 to 3
- ema_decay: float32 [16, 4096], P(None, 'tp'), may hold values from 0.96 to 1
- ema_phase: float32 [16, 4096], P(None, 'tp'), may hold values from -1 to 1
- ema_in: float32 [16, 4096], P(None, 'tp'), may hold values from -0.6 to 0.6
- ema_out: float32 [2, 16, 4096], P(None, None, 'tp'), may hold values from -1.5 to 1.5
- ema_skip: float32 [4096], P('tp'), may hold values from -4 to 4
- rms_gain: float32 [4096], replicated, may hold values from 0.5 to 1.5
- z_weight: bfloat16 [4096, 256], P('ctx', 'tp'), may hold values from -0.09375 to 0.09375
- v_weight: bfloat16 [4096, 2048], P('ctx', 'tp'), may hold values from -0.09375 to 0.09375
- qk_affine: float32 [4, 256], P(None, 'tp'), may hold values from -1.5 to 4, as said below
Outputs:
- attended: bfloat16 [2048, 2048], P('ctx', 'tp')
Inputs may be any that keep to these rules, and one draw needn't show every extreme that they name: `qk_affine`: rows 0 and 2 are positive.
All inputs are finite; a program needn't handle non-finite values.
Results may differ from a plain program's by a relative error of at most 0.015.
The roundings to bfloat16 on the way count: a program that leaves them out, or rounds other values in their place, can miss the bound.
Values may be sent and summed in bfloat16 or wider, within the bound.
No kernel may reach another device: no remote copies, remote signals or barrier semaphores. Data moves between devices by JAX's collectives and lax.ppermute only.
A program may use at most 128 MiB of HBM per device.

v0:
```python
import math

import jax
import jax.numpy as jnp
from jax import lax
from jax.sharding import PartitionSpec as P

NDIM = 16
ZH = 128
GROUP = 64
STRETCH = 128
EBLK = 32


highest = lax.Precision.HIGHEST
epsilon = 1e-05


def carried_in(part, axis, combine, identity):
    place = lax.axis_index(axis)
    gathered = jax.tree.map(lambda a: lax.all_gather(a, axis), part)
    state = jax.tree.map(lambda a, e: jnp.zeros_like(a) + jnp.asarray(e, a.dtype), part, identity)

    def one(step, state):
        return combine(
            state, jax.tree.map(lambda a: lax.dynamic_index_in_dim(a, step, 0, False), gathered)
        )

    return lax.fori_loop(0, place, one, state)


def ema_tables(decays, phases, ema_in, ema_out, blocklen):
    log_rate = jnp.log(decays)
    powers = jnp.arange(blocklen + 1, dtype=jnp.float32)[:, None, None]
    magnitude = jnp.exp(powers * log_rate)
    power_re = magnitude * jnp.cos(powers * phases)
    power_im = magnitude * jnp.sin(powers * phases)
    coef_re = ema_out[0] * power_re - ema_out[1] * power_im
    coef_im = ema_out[0] * power_im + ema_out[1] * power_re
    kernel = jnp.sum(ema_in * coef_re[:blocklen], axis=1)
    offsets = jnp.arange(blocklen)[:, None] - jnp.arange(blocklen)[None, :]
    toeplitz = jnp.where(
        (offsets >= 0)[:, :, None], kernel[jnp.clip(offsets, 0, blocklen - 1)], 0.0
    )
    feed_re = ema_in * power_re[::-1][1:]
    feed_im = ema_in * power_im[::-1][1:]
    return (
        toeplitz,
        coef_re[1:],
        coef_im[1:],
        feed_re,
        feed_im,
        power_re[blocklen],
        power_im[blocklen],
    )


def ema_feed(tables, inputs):
    fresh_re = jnp.einsum("sc,sjc->jc", inputs, tables[3], precision=highest)
    fresh_im = jnp.einsum("sc,sjc->jc", inputs, tables[4], precision=highest)
    return (fresh_re, fresh_im)


def rotate(tables, hidden_state, inputs):
    state_re, state_im = hidden_state
    fresh_re, fresh_im = ema_feed(tables, inputs)
    new_re = tables[5] * state_re - tables[6] * state_im + fresh_re
    new_im = tables[5] * state_im + tables[6] * state_re + fresh_im
    return (new_re, new_im)


def ema_block(tables, hidden_state, inputs):
    state_re, state_im = hidden_state
    within = jnp.einsum("tsc,sc->tc", tables[0], inputs, precision=highest)
    carried = jnp.einsum("tjc,jc->tc", tables[1], state_re, precision=highest) - jnp.einsum(
        "tjc,jc->tc", tables[2], state_im, precision=highest
    )
    return (rotate(tables, hidden_state, inputs), within + carried)


def add_pair(earlier, latter):
    return (earlier[0] + latter[0], earlier[1] + latter[1])


def attention(z_total, v_total, affine):
    queries = (z_total * affine[0] + affine[1]).astype(jnp.bfloat16)
    key_rows = (z_total * affine[2] + affine[3]).astype(jnp.bfloat16)
    values = jax.nn.silu(v_total).astype(jnp.bfloat16)
    row_count = z_total.shape[0]
    stretches = row_count // STRETCH
    queries = queries.reshape(stretches, STRETCH, -1)
    key_rows = key_rows.reshape(stretches, STRETCH, -1)
    values = values.reshape(stretches, STRETCH, -1)
    scores = jnp.einsum("nqd,nkd->nqk", queries, key_rows, preferred_element_type=jnp.float32) * (
        1.0 / ZH**0.5
    )
    causal = jnp.arange(STRETCH)[:, None] >= jnp.arange(STRETCH)[None, :]
    scores = jnp.where(causal[None], scores, -1e30)
    row_max = jnp.max(scores, axis=-1, keepdims=True)
    weights = jnp.exp(scores - row_max)
    probabilities = (weights / jnp.sum(weights, axis=-1, keepdims=True)).astype(jnp.bfloat16)
    result = jnp.einsum("nqk,nkd->nqd", probabilities, values, preferred_element_type=jnp.float32)
    return result.reshape(row_count, -1).astype(jnp.bfloat16)


def body(
    tokens,
    norm_gain,
    norm_bias,
    ema_decay,
    ema_phase,
    ema_in,
    ema_out,
    ema_skip,
    rms_gain,
    z_weight,
    v_weight,
    qk_affine,
):
    length, channels = tokens.shape
    groups = channels // GROUP
    position = lax.axis_index("ctx")
    ctx_count = lax.axis_size("ctx")
    x_float = tokens.astype(jnp.float32).reshape(length, groups, GROUP)
    row_sums = jnp.sum(x_float, axis=-1)
    row_squares = jnp.sum(x_float * x_float, axis=-1)
    local_sums = jnp.sum(row_sums, axis=0)
    local_squares = jnp.sum(row_squares, axis=0)
    nothing = jnp.zeros((groups,), jnp.float32)
    before_sums, before_squares = carried_in(
        (local_sums, local_squares), "ctx", add_pair, (nothing, nothing)
    )
    prefix_sums = before_sums + jnp.cumsum(row_sums, axis=0)
    prefix_squares = before_squares + jnp.cumsum(row_squares, axis=0)
    first_token = (position * length).astype(jnp.float32)
    counts = (first_token + jnp.arange(length, dtype=jnp.float32)[:, None] + 1.0) * GROUP
    average = prefix_sums / counts
    spread = jnp.maximum(prefix_squares / counts - average * average, 0.0)
    scaled = (x_float - average[..., None]) * lax.rsqrt(spread + epsilon)[..., None]
    normed = (scaled.reshape(length, channels) * norm_gain + norm_bias).astype(jnp.bfloat16)
    inputs = normed.astype(jnp.float32)
    tables = ema_tables(ema_decay, ema_phase, ema_in, ema_out, EBLK)
    blocks = inputs.reshape(length // EBLK, EBLK, channels)

    def end_only(hidden_state, block_rows):
        return (rotate(tables, hidden_state, block_rows), None)

    zero_state = jnp.zeros((NDIM, channels), jnp.float32)
    (end_re, end_im), _ = lax.scan(end_only, (zero_state, zero_state), blocks)
    log_rate = jnp.log(ema_decay)
    ends_re, ends_im = (
        lax.all_gather(end_re[None], "ctx", axis=0, tiled=True),
        lax.all_gather(end_im[None], "ctx", axis=0, tiled=True),
    )
    distance = position - 1 - jnp.arange(ctx_count)
    reached = (distance >= 0)[:, None, None]
    lag_float = jnp.maximum(distance, 0).astype(jnp.float32)[:, None, None]
    magnitude = jnp.where(reached, jnp.exp(lag_float * length * log_rate), 0.0)
    winding = jnp.mod(length * ema_phase, 2.0 * math.pi)
    angles = lag_float * winding
    power_re = magnitude * jnp.cos(angles)
    power_im = magnitude * jnp.sin(angles)
    incoming_state = (
        jnp.sum(power_re * ends_re - power_im * ends_im, axis=0),
        jnp.sum(power_re * ends_im + power_im * ends_re, axis=0),
    )

    def advance(hidden_state, block_rows):
        return ema_block(tables, hidden_state, block_rows)

    _, outputs = lax.scan(advance, incoming_state, blocks)
    mixed_rows = jax.nn.silu(outputs.reshape(length, channels) + ema_skip * inputs).astype(
        jnp.bfloat16
    )
    full_normed, full_mixed = (
        lax.all_gather(normed, "tp", axis=1, tiled=True),
        lax.all_gather(mixed_rows, "tp", axis=1, tiled=True),
    )
    mixed_float = full_mixed.astype(jnp.float32)
    rms_normed = (
        mixed_float
        * lax.rsqrt(jnp.mean(mixed_float * mixed_float, axis=-1, keepdims=True) + 1e-06)
        * rms_gain
    ).astype(jnp.bfloat16)
    all_z, all_v = (
        lax.all_gather(z_weight, "ctx", axis=0, tiled=True),
        lax.all_gather(v_weight, "ctx", axis=0, tiled=True),
    )
    z_total = jnp.dot(rms_normed, all_z, preferred_element_type=jnp.float32)
    v_total = jnp.dot(full_normed, all_v, preferred_element_type=jnp.float32)
    return attention(z_total, v_total, qk_affine)


def solution(mesh):
    in_specs = (
        P("ctx", "tp"),
        P("tp"),
        P("tp"),
        P(None, "tp"),
        P(None, "tp"),
        P(None, "tp"),
        P(None, None, "tp"),
        P("tp"),
        P(),
        P("ctx", "tp"),
        P("ctx", "tp"),
        P(None, "tp"),
    )
    out_specs = P("ctx", "tp")
    return jax.shard_map(body, mesh=mesh, in_specs=in_specs, out_specs=out_specs, check_vma=False)
```

profile of v0, /device:TPU:0, one launch (start us, length us, event | category | flops | bytes accessed | tf_op | source)
XLA Modules:
  0.0 495.7 jit_solution(16901650628288557793)
XLA Ops:
  6.5 1.3 copy.31
  8.6 1.0 slice_bitcast_fusion.3
  9.6 0.9 log.4
  10.5 18.2 %multiply_subtract_fusion = (f32[33,16,2048]{2,1,0:T(8,128)}, f32[33,16,2048]{2,1,0:T(8,128)S(1)}, f32[33,16,2048]{2,1,0:T(8,128)S(1)}) fusion(f32[16,2048]{1,0:T(8,128)S(1)} %get-tuple-element.279, f32[16,2048]{1,0:T(8,128)S(1)} %get-tuple-element.278, f32[16,2048]{1,0:T(8,128)} %param.22, f32[16,2048]{1,0:T(8,128)S(1)} %log.4), kind=kLoop, calls=%fused_computation.17 | loop fusion | flops 7569408 | bytes 13500416 | tf_op jit(solution)/shard_map/sub | solution.py:38
  28.8 5.1 %fusion = (f32[32,16,2048]{2,1,0:T(8,128)}, f32[32,16,2048]{2,1,0:T(8,128)}, f32[32,16,2048]{2,1,0:T(8,128)}) fusion(f32[33,16,2048]{2,1,0:T(8,128)S(1)} %get-tuple-element.277, f32[33,16,2048]{2,1,0:T(8,128)S(1)} %get-tuple-element.276, f32[16,2048]{1,0:T(8,128)S(1)} %get-tuple-element.279, f32[16,2048]{1,0:T(8,128)S(1)} %get-tuple-element.278), kind=kLoop, calls=%fused_computation.23 | loop fusion | flops 3145728 | bytes 29622272 | tf_op jit(solution)/shard_map/add | solution.py:39
  36.0 43.5 %all-reduce.2 = (f32[512]{0:T(512)S(1)}, f32[512]{0:T(512)S(1)}) all-reduce(f32[512]{0:T(512)S(1)} %dynamic-update-slice, f32[512]{0:T(512)S(1)} %dynamic-update-slice.1), channel_id=2, replica_groups=mesh['ctx'=16,'tp'=2] {'ctx'}, use_global_device_ids=true, to_apply=%add | all-reduce | flops 1024 | bytes 8192
  80.4 0.7 fusion.12
  81.3 11.5 %fusion.26 = (f32[32,16,2048]{2,1,0:T(8,128)}, f32[32,2048]{1,0:T(8,128)S(1)}, f32[32,16,2048]{2,1,0:T(8,128)}, f32[32,16,2048]{2,1,0:T(8,128)}) fusion(f32[33,16,2048]{2,1,0:T(8,128)} %get-tuple-element.275, f32[16,2048]{1,0:T(8,128)S(1)} %copy-done.7, f32[32,16,2048]{2,1,0:T(8,128)} %get-tuple-element.271, f32[32,16,2048]{2,1,0:T(8,128)} %get-tuple-element.272), kind=kLoop, calls=%fused_computation.95 | loop fusion | flops 4128768 | bytes 29753344 | tf_op jit(solution)/shard_map/slice | solution.py:49
  92.9 18.7 %while.41 = (s32[]{:T(128)}, f32[16,2048]{1,0:T(8,128)S(1)}, f32[16,2048]{1,0:T(8,128)S(1)}, f32[16,2048]{1,0:T(8,128)S(1)}, f32[16,2048]{1,0:T(8,128)S(1)}, /*i...) while((s32[]{:T(128)}, f32[16,2048]{1,0:T(8,128)S(1)}, ...), condition=%wide.region_11.12_spmd.clone, body=%wide.region_10.11_spmd.clone.sunk | while | flops 4456451 | bytes 10485883 | solution.py:149
  92.9 4.5 multiply_reduce_fusion.14
  97.6 4.5 multiply_reduce_fusion.14
  102.2 4.5 multiply_reduce_fusion.14
  106.9 4.5 multiply_reduce_fusion.14
  113.3 6.9 %gather_fusion = f32[1024,2048]{1,0:T(8,128)} fusion(f32[32,2048]{1,0:T(8,128)S(1)} %get-tuple-element.274, s32[1024]{0:T(1024)S(1)} %broadcast_clamp_fusion), kind=kCustom, calls=%fused_computation | custom fusion | bytes 16781312 | tf_op jit(solution)/shard_map/gather | solution.py:43
  120.3 7.3 %broadcast_select_fusion = f32[32,32,2048]{2,1,0:T(8,128)} fusion(f32[32,32,2048]{2,1,0:T(8,128)} %bitcast.114, pred[32,32]{1,0:T(8,128)(4,1)S(1)} %subtract_compare_fusion), kind=kLoop, calls=%fused_computation.27 | loop fusion | flops 2097152 | bytes 16778240 | tf_op jit(solution)/shard_map/jit(_where)/select_n | solution.py:42
  127.6 41.6 %all-gather.19.cloned.1.call-done = f32[256,2048]{1,0:T(8,128)} async-done(((f32[16,2048]{1,0:T(8,128)}), f32[256,2048]{1,0:T(8,128)}) %all-gather.19.cloned.1.call-update) | async-done | bytes 2097168 | tf_op jit(solution)/shard_map/all_gather | solution.py:152
  169.2 62.2 %all-gather.21.cloned.1.call-done = f32[256,2048]{1,0:T(8,128)} async-done(((f32[16,2048]{1,0:T(8,128)}), f32[256,2048]{1,0:T(8,128)}) %all-gather.21.cloned.1.call-update) | async-done | bytes 2097168 | tf_op jit(solution)/shard_map/all_gather | solution.py:153
  231.4 10.0 %add_reduce_fusion = (f32[16,2048]{1,0:T(8,128)S(1)}, f32[16,2048]{1,0:T(8,128)S(1)}) fusion(f32[16,16,2048]{2,1,0:T(8,128)} %bitcast.118, f32[16,16,2048]{2,1,0:T(8,128)} %bitcast.119, f32[16,2048]{1,0:T(8,128)S(1)} %add_select_fusion, f32[16]{0:T(128)S(1)} %maximum_convert_fusion, f32[16,2048]{1,0:T(8,128)S(1)} %log.4, f32[16]{0:T(128)S(1)} %broadcast_multiply_fusion, ...), kind=kLoop, calls=%fused_computation.39 | loop fusion | flops 6750208 | bytes 4718736 | tf_op jit(solution)/shard_map/reduce_sum | solution.py:165
  241.4 45.9 %while.40 = (s32[]{:T(128)}, f32[16,2048]{1,0:T(8,128)S(1)}, f32[16,2048]{1,0:T(8,128)S(1)}, f32[4,32,2048]{2,1,0:T(8,128)}, f32[16,2048]{1,0:T(8,128)S(1)}, /*i...) while((s32[]{:T(128)}, f32[16,2048]{1,0:T(8,128)S(1)}, ...), condition=%wide.region_16.17_spmd, body=%wide.region_15.16_spmd.sunk | while | flops 12713986 | bytes 96731360 | solution.py:171
  241.4 5.4 %multiply_reduce_fusion.13 = (f32[2048,32]{0,1:T(8,128)S(1)}, f32[2048,32]{0,1:T(8,128)S(1)}) fusion(f32[32,16,2048]{2,1,0:T(8,128)} %get-tuple-element.568, f32[2048,16]{0,1:T(8,128)S(1)} %bitcast.115, f32[32,16,2048]{2,1,0:T(8,128)} %get-tuple-element.567, f32[2048,16]{0,1:T(8,128)S(1)} %bitcast.116), kind=kLoop, calls=%fused_computation.4.clone.1 | loop fusion | flops 4063232 | bytes 9175040 | tf_op jit(solution)/shard_map/while/body/eval_jaxpr/tjc,jc->tc/dot_general | solution.py:75
  247.3 1.0 multiply_reduce_fusion.11
  248.5 2.2 copy-done.2
  250.7 1.4 multiply_reduce_fusion.12
  252.1 0.8 bitcast_dynamic-update-slice_fusion.2
  252.9 5.4 %multiply_reduce_fusion.13 = (f32[2048,32]{0,1:T(8,128)S(1)}, f32[2048,32]{0,1:T(8,128)S(1)}) fusion(f32[32,16,2048]{2,1,0:T(8,128)} %get-tuple-element.568, f32[2048,16]{0,1:T(8,128)S(1)} %bitcast.115, f32[32,16,2048]{2,1,0:T(8,128)} %get-tuple-element.567, f32[2048,16]{0,1:T(8,128)S(1)} %bitcast.116), kind=kLoop, calls=%fused_computation.4.clone.1 | loop fusion | flops 4063232 | bytes 9175040 | tf_op jit(solution)/shard_map/while/body/eval_jaxpr/tjc,jc->tc/dot_general | solution.py:75
  258.8 1.0 multiply_reduce_fusion.11
  259.9 2.2 copy-done.2
  262.2 1.4 multiply_reduce_fusion.12
  263.6 0.7 bitcast_dynamic-update-slice_fusion.2
  264.3 5.4 %multiply_reduce_fusion.13 = (f32[2048,32]{0,1:T(8,128)S(1)}, f32[2048,32]{0,1:T(8,128)S(1)}) fusion(f32[32,16,2048]{2,1,0:T(8,128)} %get-tuple-element.568, f32[2048,16]{0,1:T(8,128)S(1)} %bitcast.115, f32[32,16,2048]{2,1,0:T(8,128)} %get-tuple-element.567, f32[2048,16]{0,1:T(8,128)S(1)} %bitcast.116), kind=kLoop, calls=%fused_computation.4.clone.1 | loop fusion | flops 4063232 | bytes 9175040 | tf_op jit(solution)/shard_map/while/body/eval_jaxpr/tjc,jc->tc/dot_general | solution.py:75
  270.2 1.0 multiply_reduce_fusion.11
  271.4 2.2 copy-done.2
  273.6 1.4 multiply_reduce_fusion.12
  275.0 0.7 bitcast_dynamic-update-slice_fusion.2
  275.8 5.4 %multiply_reduce_fusion.13 = (f32[2048,32]{0,1:T(8,128)S(1)}, f32[2048,32]{0,1:T(8,128)S(1)}) fusion(f32[32,16,2048]{2,1,0:T(8,128)} %get-tuple-element.568, f32[2048,16]{0,1:T(8,128)S(1)} %bitcast.115, f32[32,16,2048]{2,1,0:T(8,128)} %get-tuple-element.567, f32[2048,16]{0,1:T(8,128)S(1)} %bitcast.116), kind=kLoop, calls=%fused_computation.4.clone.1 | loop fusion | flops 4063232 | bytes 9175040 | tf_op jit(solution)/shard_map/while/body/eval_jaxpr/tjc,jc->tc/dot_general | solution.py:75
  281.7 1.0 multiply_reduce_fusion.11
  282.8 2.2 copy-done.2
  285.1 1.4 multiply_reduce_fusion.12
  286.5 0.8 bitcast_dynamic-update-slice_fusion.2
  287.2 1.6 copy.37
  288.8 1.2 multiply_convert_fusion
  291.8 6.1 %all-gather.11.cloned.1.call-done = bf16[128,4096]{0,1:T(8,128)(2,1)} async-done(((bf16[128,2048]{0,1:T(8,128)(2,1)}), bf16[128,4096]{0,1:T(8,128)(2,1)}) %all-gather.11.cloned.1.call-update) | async-done | bytes 1048592 | tf_op jit(solution)/shard_map/all_gather | solution.py:177
  297.9 1.8 fusion.2
  299.7 57.3 %all-gather.13.cloned.1.call-done = bf16[4096,128]{1,0:T(8,128)(2,1)} async-done(((bf16[256,128]{1,0:T(8,128)(2,1)}), bf16[4096,128]{1,0:T(8,128)(2,1)}) %all-gather.13.cloned.1.call-update) | async-done | bytes 1048592 | tf_op jit(solution)/shard_map/all_gather | solution.py:186
  357.0 2.6 fusion.8
  359.8 6.4 %all-gather.15.cloned.1.call-done = bf16[128,4096]{0,1:T(8,128)(2,1)} async-done(((bf16[128,2048]{0,1:T(8,128)(2,1)}), bf16[128,4096]{0,1:T(8,128)(2,1)}) %all-gather.15.cloned.1.call-update) | async-done | bytes 1048592 | tf_op jit(solution)/shard_map/all_gather | solution.py:176
  366.2 116.7 %all-gather.17.cloned.1.call-done = bf16[4096,1024]{1,0:T(8,128)(2,1)} async-done(((bf16[256,1024]{1,0:T(8,128)(2,1)}), bf16[4096,1024]{1,0:T(8,128)(2,1)}) %all-gather.17.cloned.1.call-update) | async-done | bytes 8388624 | tf_op jit(solution)/shard_map/all_gather | solution.py:187
  482.9 6.0 %convolution_convert_fusion = bf16[128,1024]{1,0:T(8,128)(2,1)} fusion(f32[128,128]{0,1:T(8,128)S(1)} %get-tuple-element.287, f32[128]{0:T(128)S(1)} %fusion.17, f32[128]{0:T(128)S(1)} %get-tuple-element.286, bf16[128,4096]{0,1:T(8,128)(2,1)} %all-gather.15.cloned.1.call-done, bf16[4096,1024]{1,0:T(8,128)(2,1)} %all-gather.17.cloned.1.call-done), kind=kOutput, calls=%fused_computation.42 | convolution fusion | flops 1108131840 | bytes 9765888 | tf_op jit(solution)/shard_map/nqk,nkd->nqd/dot_general | solution.py:102
  (111 shorter events, 10.1 us)
Async XLA Ops:
  6.5 162.7 %all-gather.19.cloned.1.call-start = ((), (), s32[]{:S(2)}) async-start(), calls=%async_computation.4 | async-start | bytes 2228224 | tf_op jit(solution)/shard_map/all_gather | solution.py:152
  28.7 5.5 %copy-start.13 = (u32[32]{0:T(128)S(1)}, u32[32]{0:T(128)}, u32[]{:S(2)}) copy-start(u32[32]{0:T(128)} %constant.87) | copy-start | bytes 388
  28.7 51.6 %copy-start.8 = (f32[2048]{0:T(1024)S(1)}, f32[2048]{0:T(1024)}, u32[]{:S(2)}) copy-start(f32[2048]{0:T(1024)} %param.20) | copy-start | bytes 24580
  28.7 51.6 %copy-start.9 = (f32[2048]{0:T(1024)S(1)}, f32[2048]{0:T(1024)}, u32[]{:S(2)}) copy-start(f32[2048]{0:T(1024)} %param.19) | copy-start | bytes 24580
  28.8 52.5 %copy-start.7 = (f32[16,2048]{1,0:T(8,128)S(1)}, f32[16,2048]{1,0:T(8,128)}, u32[]{:S(2)}) copy-start(f32[16,2048]{1,0:T(8,128)} %param.23) | copy-start | bytes 393220
  81.1 207.7 %copy-start.3 = (bf16[128,2048]{0,1:T(8,128)(2,1)}, bf16[128,2048]{0,1:T(8,128)(2,1)S(1)}, u32[]{:S(2)}) copy-start(bf16[128,2048]{0,1:T(8,128)(2,1)S(1)} %fusion.12) | copy-start | bytes 1572868
  111.5 0.7 copy-start.4
  111.6 0.7 copy-start.5
  112.2 119.1 %all-gather.21.cloned.1.call-start = ((), (), s32[]{:S(2)}) async-start(), calls=%async_computation.5 | async-start | bytes 2228224 | tf_op jit(solution)/shard_map/all_gather | solution.py:153
  113.0 184.9 %all-gather.11.cloned.1.call-start = ((), (), s32[]{:S(2)}) async-start(), calls=%async_computation | async-start | bytes 1572864 | tf_op jit(solution)/shard_map/all_gather | solution.py:177
  113.3 6.9 %copy-start.6 = (f32[16,2048]{1,0:T(8,128)S(1)}, f32[16,2048]{1,0:T(8,128)}, u32[]{:S(2)}) copy-start(f32[16,2048]{1,0:T(8,128)} %param.22) | copy-start | bytes 393220
  241.4 47.5 %copy-start.10 = (f32[2048]{0:T(1024)S(1)}, f32[2048]{0:T(1024)}, u32[]{:S(2)}) copy-start(f32[2048]{0:T(1024)} %param.25) | copy-start | bytes 24580
  241.4 5.5 %copy-start = (f32[32,16,2048]{2,1,0:T(8,128)S(1)}, f32[32,16,2048]{2,1,0:T(8,128)}, u32[]{:S(2)}) copy-start(f32[32,16,2048]{2,1,0:T(8,128)} %get-tuple-element.565) | copy-start | bytes 12582916 | tf_op jit(solution)/shard_map/while
  241.4 5.9 %copy-start.1 = (f32[32,16,2048]{2,1,0:T(8,128)S(1)}, f32[32,16,2048]{2,1,0:T(8,128)}, u32[]{:S(2)}) copy-start(f32[32,16,2048]{2,1,0:T(8,128)} %get-tuple-element.564) | copy-start | bytes 12582916 | tf_op jit(solution)/shard_map/while
  247.3 3.4 copy-start.2
  252.9 5.5 %copy-start = (f32[32,16,2048]{2,1,0:T(8,128)S(1)}, f32[32,16,2048]{2,1,0:T(8,128)}, u32[]{:S(2)}) copy-start(f32[32,16,2048]{2,1,0:T(8,128)} %get-tuple-element.565) | copy-start | bytes 12582916 | tf_op jit(solution)/shard_map/while
  252.9 5.9 %copy-start.1 = (f32[32,16,2048]{2,1,0:T(8,128)S(1)}, f32[32,16,2048]{2,1,0:T(8,128)}, u32[]{:S(2)}) copy-start(f32[32,16,2048]{2,1,0:T(8,128)} %get-tuple-element.564) | copy-start | bytes 12582916 | tf_op jit(solution)/shard_map/while
  258.8 3.4 copy-start.2
  264.3 5.5 %copy-start = (f32[32,16,2048]{2,1,0:T(8,128)S(1)}, f32[32,16,2048]{2,1,0:T(8,128)}, u32[]{:S(2)}) copy-start(f32[32,16,2048]{2,1,0:T(8,128)} %get-tuple-element.565) | copy-start | bytes 12582916 | tf_op jit(solution)/shard_map/while
  264.3 5.9 %copy-start.1 = (f32[32,16,2048]{2,1,0:T(8,128)S(1)}, f32[32,16,2048]{2,1,0:T(8,128)}, u32[]{:S(2)}) copy-start(f32[32,16,2048]{2,1,0:T(8,128)} %get-tuple-element.564) | copy-start | bytes 12582916 | tf_op jit(solution)/shard_map/while
  270.2 3.4 copy-start.2
  275.8 5.5 %copy-start = (f32[32,16,2048]{2,1,0:T(8,128)S(1)}, f32[32,16,2048]{2,1,0:T(8,128)}, u32[]{:S(2)}) copy-start(f32[32,16,2048]{2,1,0:T(8,128)} %get-tuple-element.565) | copy-start | bytes 12582916 | tf_op jit(solution)/shard_map/while
  275.8 5.9 %copy-start.1 = (f32[32,16,2048]{2,1,0:T(8,128)S(1)}, f32[32,16,2048]{2,1,0:T(8,128)}, u32[]{:S(2)}) copy-start(f32[32,16,2048]{2,1,0:T(8,128)} %get-tuple-element.564) | copy-start | bytes 12582916 | tf_op jit(solution)/shard_map/while
  281.7 3.4 copy-start.2
  287.2 4.6 copy-start.11
  287.2 69.7 %copy-start.12 = (f32[4096]{0:T(1024)S(1)}, f32[4096]{0:T(1024)}, u32[]{:S(2)}) copy-start(f32[4096]{0:T(1024)} %param.26) | copy-start | bytes 49156
  290.0 66.9 %all-gather.13.cloned.1.call-start = ((), (), s32[]{:S(2)}) async-start(), calls=%async_computation.1 | async-start | bytes 1114112 | tf_op jit(solution)/shard_map/all_gather | solution.py:186
  290.6 75.6 %all-gather.15.cloned.1.call-start = ((), (), s32[]{:S(2)}) async-start(), calls=%async_computation.2 | async-start | bytes 1572864 | tf_op jit(solution)/shard_map/all_gather | solution.py:176
  291.2 191.7 %all-gather.17.cloned.1.call-start = ((), (), s32[]{:S(2)}) async-start(), calls=%async_computation.3 | async-start | bytes 8912896 | tf_op jit(solution)/shard_map/all_gather | solution.py:187
Sparse Core Ops, SparseCore 0:
  112.3 56.8 all-gather.18
  172.0 59.3 all-gather.20
  290.2 7.6 all-gather.10
  300.5 56.4 all-gather.12
  358.4 7.8 all-gather.14
  368.9 113.9 all-gather.16
where the time goes:
time: 496 us
  waiting for transfers between devices  292 us (59%)
  other arithmetic  111 us (22%)
  blocking collectives  43.5 us (9%)
  local copies, waits for them, and re-layouts  25.3 us (5%)
  between operations  14.4 us (3%)
  matrix products  8.77 us (2%)
    all_gather x1, waiting for transfers between devices, body(): lax.all_gather(v_weight, 'ctx', axis=0, tiled=True)  117 us
    all_gather x1, waiting for transfers between devices, body(): lax.all_gather(end_im[None], 'ctx', axis=0, tiled=True)  62.2 us
    all_gather x1, waiting for transfers between devices, body(): lax.all_gather(z_weight, 'ctx', axis=0, tiled=True)  57.3 us
    unnamed x1, blocking collectives  43.5 us
    all_gather x1, waiting for transfers between devices, body(): lax.all_gather(end_re[None], 'ctx', axis=0, tiled=True)  41.6 us
    dot_general x8, other arithmetic, ema_feed(): fresh_im = jnp.einsum('sc,sjc->jc', inputs, tables[4], precision=highest)  22 us
    dot_general x4, other arithmetic, ema_block(): jnp.einsum('tjc,jc->tc', tables[2], state_im, precision=highest)  21.6 us
    sub x1, other arithmetic, ema_tables(): coef_re = ema_out[0] * power_re - ema_out[1] * power_im  18.2 us
  transfers between devices with their start and end apart: 6, of which 6 were waited for; matrix products, arithmetic and copies ran while one was open for 4% of the time, Pallas kernels for 0%

commit v1 on v0

v1 whole, which is shorter than its diff:
```python
import functools

import jax
import jax.numpy as jnp
from jax import lax
from jax.experimental import pallas as pl
from jax.experimental.pallas import tpu as pltpu
from jax.sharding import PartitionSpec as P

NDIM = 16
GROUP = 64
STRETCH = 128
CHUNK = 16
LANES = 128
epsilon = 1e-05
f32 = jnp.float32
bf16 = jnp.bfloat16
VMEM_LIMIT = 48 * 1024 * 1024


def call(kernel, outs, scratch=(), smem_first=False, n_in=1):
    specs = [pl.BlockSpec(memory_space=pltpu.VMEM) for _ in range(n_in)]
    if smem_first:
        specs[0] = pl.BlockSpec(memory_space=pltpu.SMEM)
    return pl.pallas_call(
        kernel,
        out_shape=outs,
        in_specs=specs,
        out_specs=jax.tree.map(lambda _: pl.BlockSpec(memory_space=pltpu.VMEM), outs),
        scratch_shapes=list(scratch),
        compiler_params=pltpu.CompilerParams(vmem_limit_bytes=VMEM_LIMIT),
    )


def pieces(value):
    first = value.astype(bf16)
    rest = value - first.astype(f32)
    second = rest.astype(bf16)
    third = (rest - second.astype(f32)).astype(bf16)
    return first, second, third


def mm(a, b):
    return jnp.dot(a, b, preferred_element_type=f32)


def membership(channels, width, transposed):
    shape = (width, channels) if transposed else (channels, width)
    channel = lax.broadcasted_iota(jnp.int32, shape, 1 if transposed else 0)
    group = lax.broadcasted_iota(jnp.int32, shape, 0 if transposed else 1)
    return jnp.where(channel // GROUP == group, 1.0, 0.0).astype(bf16)


def sums_kernel(x_ref, csum_ref, csq_ref, total_ref):
    length, channels = x_ref.shape
    width = csum_ref.shape[1]
    member = membership(channels, width, False)
    x = x_ref[...]
    square = x.astype(f32) * x.astype(f32)
    high = square.astype(bf16)
    low = (square - high.astype(f32)).astype(bf16)
    row_sums = mm(x, member)
    row_squares = mm(high, member) + mm(low, member)
    rows = lax.broadcasted_iota(jnp.int32, (length, length), 0)
    cols = lax.broadcasted_iota(jnp.int32, (length, length), 1)
    lower = jnp.where(rows >= cols, 1.0, 0.0).astype(bf16)
    for ref, value, at in ((csum_ref, row_sums, 0), (csq_ref, row_squares, 1)):
        one, two, three = pieces(value)
        running = mm(lower, one) + mm(lower, two) + mm(lower, three)
        ref[...] = running
        total_ref[at : at + 1, :] = running[length - 1 : length, :]


def powers_into(ref, q_ref, first_re, first_im, count):
    def one(j, _):
        q_re, q_im = q_ref[j, 0], q_ref[j, 1]
        now_re, now_im = first_re(j), first_im(j)
        for k in range(count):
            ref[k, j, 0] = now_re
            ref[k, j, 1] = now_im
            if k + 1 < count:
                now_re, now_im = now_re * q_re - now_im * q_im, now_re * q_im + now_im * q_re
        return _

    lax.fori_loop(0, NDIM, one, 0)


def feed_kernel(
    me_ref, x_ref, sums_ref, csum_ref, csq_ref, gain_ref, bias_ref, q_ref,
    normed_ref, dense_ref, fresh_ref, end_ref, power_ref,
):
    length, channels = x_ref.shape
    width = csum_ref.shape[1]
    tiles = channels // LANES
    chunks = length // CHUNK
    me = me_ref[0]
    peers = sums_ref.shape[0]
    before = [jnp.zeros((1, width), f32) for _ in range(2)]
    for peer in range(peers):
        earlier = jnp.where(peer < me, 1.0, 0.0)
        for at in range(2):
            before[at] = before[at] + sums_ref[peer, at : at + 1, :] * earlier
    place = lax.broadcasted_iota(jnp.int32, (length, width), 0) + me * length + 1
    counts = place.astype(f32) * GROUP
    average = (before[0] + csum_ref[...]) / counts
    spread = jnp.maximum((before[1] + csq_ref[...]) / counts - average * average, 0.0)
    scale = lax.rsqrt(spread + epsilon)
    member = membership(channels, width, True)
    average_pieces, scale_pieces = pieces(average), pieces(scale)
    for tile in range(tiles):
        lanes = slice(tile * LANES, (tile + 1) * LANES)
        mine = member[:, lanes]
        average_wide = sum(mm(p, mine) for p in average_pieces)
        scale_wide = sum(mm(p, mine) for p in scale_pieces)
        scaled = (x_ref[:, lanes].astype(f32) - average_wide) * scale_wide
        normed = (scaled * gain_ref[:, lanes] + bias_ref[:, lanes]).astype(bf16)
        normed_ref[:, lanes] = normed
        dense_ref[pl.ds(tile, length, stride=tiles), :] = normed.astype(f32)

    sub = q_ref.shape[2]
    powers_into(
        power_ref, q_ref, lambda j: jnp.ones((sub, LANES), f32), lambda j: jnp.zeros((sub, LANES), f32), CHUNK + 1
    )
    step = min(8, tiles)

    def one(j, _):
        for low in range(0, tiles, step):
            rows = slice(low, low + step)
            re = [jnp.zeros((step, LANES), f32) for _ in range(chunks)]
            im = [jnp.zeros((step, LANES), f32) for _ in range(chunks)]
            for b in range(CHUNK):
                p_re = power_ref[CHUNK - 1 - b, j, 0, rows, :]
                p_im = power_ref[CHUNK - 1 - b, j, 1, rows, :]
                for a in range(chunks):
                    at = (a * CHUNK + b) * tiles + low
                    value = dense_ref[at : at + step, :]
                    re[a] = re[a] + p_re * value
                    im[a] = im[a] + p_im * value
            q_re = power_ref[CHUNK, j, 0, rows, :]
            q_im = power_ref[CHUNK, j, 1, rows, :]
            s_re, s_im = re[0], im[0]
            for a in range(chunks):
                fresh_ref[a, j, 0, rows, :] = re[a]
                fresh_ref[a, j, 1, rows, :] = im[a]
                if a:
                    s_re, s_im = (
                        s_re * q_re - s_im * q_im + re[a],
                        s_re * q_im + s_im * q_re + im[a],
                    )
            end_ref[j, 0, rows, :] = s_re
            end_ref[j, 1, rows, :] = s_im
        return _

    lax.fori_loop(0, NDIM, one, 0)


def times(a, b):
    return a[0] * b[0] - a[1] * b[1], a[0] * b[1] + a[1] * b[0]


def scan_kernel(length, ends_ref, q_ref, out_ref):
    peers = ends_ref.shape[0]
    result, base, left = None, (q_ref[:, 0], q_ref[:, 1]), length
    while left:
        if left & 1:
            result = base if result is None else times(result, base)
        left >>= 1
        if left:
            base = times(base, base)
    state = (jnp.zeros_like(base[0]), jnp.zeros_like(base[1]))
    for peer in range(peers):
        out_ref[peer, :, 0] = state[0]
        out_ref[peer, :, 1] = state[1]
        if peer + 1 < peers:
            moved = times(state, result)
            state = (moved[0] + ends_ref[peer, :, 0], moved[1] + ends_ref[peer, :, 1])


def mix_kernel(
    incoming_ref, fresh_ref, dense_ref, q_ref, w_ref, skip_ref,
    mixed_ref, start_ref, coef_ref, tap_ref, out_ref,
):
    length, channels = mixed_ref.shape
    tiles = channels // LANES
    chunks = length // CHUNK
    step = min(8, tiles)

    def first_re(j):
        return w_ref[j, 0] * q_ref[j, 0] - w_ref[j, 1] * q_ref[j, 1]

    def first_im(j):
        return w_ref[j, 0] * q_ref[j, 1] + w_ref[j, 1] * q_ref[j, 0]

    powers_into(coef_ref, q_ref, first_re, first_im, CHUNK)
    tap = skip_ref[...]
    for j in range(NDIM):
        tap = tap + w_ref[j, 0]
    tap_ref[0] = tap

    def one_tap(k, _):
        tap = coef_ref[k, 0, 0]
        for j in range(1, NDIM):
            tap = tap + coef_ref[k, j, 0]
        tap_ref[k + 1] = tap
        return _

    lax.fori_loop(0, CHUNK - 1, one_tap, 0)

    def one(j, _):
        for low in range(0, tiles, step):
            rows = slice(low, low + step)
            q = (q_ref[j, 0, rows, :], q_ref[j, 1, rows, :])
            left = CHUNK
            while left > 1:
                q = times(q, q)
                left //= 2
            state = (incoming_ref[j, 0, rows, :], incoming_ref[j, 1, rows, :])
            for a in range(chunks):
                start_ref[a, j, 0, rows, :] = state[0]
                start_ref[a, j, 1, rows, :] = state[1]
                if a + 1 < chunks:
                    moved = times(state, q)
                    state = (
                        moved[0] + fresh_ref[a, j, 0, rows, :],
                        moved[1] + fresh_ref[a, j, 1, rows, :],
                    )
        return _

    lax.fori_loop(0, NDIM, one, 0)

    for low in range(0, tiles, step):
        rows = slice(low, low + step)
        for b in range(0, CHUNK, 2):
            total = [[jnp.zeros((step, LANES), f32) for _ in range(chunks)] for _ in range(2)]

            def carry(j, total, b=b, rows=rows):
                total = [list(t) for t in total]
                coefs = [(coef_ref[b + i, j, 0, rows, :], coef_ref[b + i, j, 1, rows, :]) for i in range(2)]
                for a in range(chunks):
                    re, im = start_ref[a, j, 0, rows, :], start_ref[a, j, 1, rows, :]
                    for i in range(2):
                        total[i][a] = total[i][a] + coefs[i][0] * re - coefs[i][1] * im
                return total

            total = lax.fori_loop(0, NDIM, carry, total, unroll=4)
            for s in range(b + 2):
                for i in range(2):
                    if s > b + i:
                        continue
                    tap = tap_ref[b + i - s, rows, :]
                    for a in range(chunks):
                        at = (a * CHUNK + s) * tiles + low
                        total[i][a] = total[i][a] + tap * dense_ref[at : at + step, :]
            for i in range(2):
                for a in range(chunks):
                    at = (a * CHUNK + b + i) * tiles + low
                    out_ref[at : at + step, :] = total[i][a]
    for tile in range(tiles):
        lanes = slice(tile * LANES, (tile + 1) * LANES)
        value = out_ref[pl.ds(tile, length, stride=tiles), :]
        mixed_ref[:, lanes] = (value / (1.0 + jnp.exp(-value))).astype(bf16)


def both(block):
    count = lax.axis_size("tp")
    if count == 1:
        return block
    place = lax.axis_index("tp")
    width = block.shape[1]
    others = [
        lax.ppermute(block, "tp", [(i, (i + k) % count) for i in range(count)]) for k in range(1, count)
    ]
    if count == 2:
        other = others[0]
        return jnp.where(
            place == 0, jnp.concatenate([block, other], 1), jnp.concatenate([other, block], 1)
        )
    full = jnp.zeros((block.shape[0], width * count), block.dtype)
    full = lax.dynamic_update_slice_in_dim(full, block, place * width, 1)
    for k, other in enumerate(others, 1):
        full = lax.dynamic_update_slice_in_dim(full, other, ((place - k) % count) * width, 1)
    return full


def attention(z_total, v_total, affine):
    queries = (z_total * affine[0] + affine[1]).astype(bf16)
    key_rows = (z_total * affine[2] + affine[3]).astype(bf16)
    values = jax.nn.silu(v_total).astype(bf16)
    row_count, width = z_total.shape
    stretches = row_count // STRETCH
    queries = queries.reshape(stretches, STRETCH, -1)
    key_rows = key_rows.reshape(stretches, STRETCH, -1)
    values = values.reshape(stretches, STRETCH, -1)
    scores = jnp.einsum("nqd,nkd->nqk", queries, key_rows, preferred_element_type=f32) * (
        1.0 / width**0.5
    )
    causal = jnp.arange(STRETCH)[:, None] >= jnp.arange(STRETCH)[None, :]
    scores = jnp.where(causal[None], scores, -1e30)
    row_max = jnp.max(scores, axis=-1, keepdims=True)
    weights = jnp.exp(scores - row_max)
    probabilities = (weights / jnp.sum(weights, axis=-1, keepdims=True)).astype(bf16)
    result = jnp.einsum("nqk,nkd->nqd", probabilities, values, preferred_element_type=f32)
    return result.reshape(row_count, -1).astype(bf16)


def body(
    tokens, norm_gain, norm_bias, ema_decay, ema_phase, ema_in, ema_out, ema_skip, rms_gain, z_weight, v_weight, qk_affine
):
    length, channels = tokens.shape
    tiles = channels // LANES
    chunks = length // CHUNK
    width = -(-(channels // GROUP) // LANES) * LANES
    place = lax.axis_index("ctx")
    peers = lax.axis_size("ctx")
    head = z_weight.shape[1]
    shape = jax.ShapeDtypeStruct

    weights = lax.all_gather(jnp.concatenate([z_weight, v_weight], 1), "ctx", axis=0, tiled=True)

    csum, csq, totals = call(
        sums_kernel, [shape((length, width), f32), shape((length, width), f32), shape((2, width), f32)]
    )(tokens)
    sums = lax.all_to_all(jnp.broadcast_to(totals[None], (peers, 2, width)), "ctx", 0, 0)

    def dense(a):
        return a.reshape(NDIM, tiles, LANES)

    q = jnp.stack([dense(ema_decay * jnp.cos(ema_phase)), dense(ema_decay * jnp.sin(ema_phase))], 1)
    w = jnp.stack([dense(ema_in * ema_out[0]), dense(ema_in * ema_out[1])], 1)

    normed, rows, fresh, ends = call(
        feed_kernel,
        [
            shape((length, channels), bf16),
            shape((length * tiles, LANES), f32),
            shape((chunks, NDIM, 2, tiles, LANES), f32),
            shape((NDIM, 2, tiles, LANES), f32),
        ],
        [pltpu.VMEM((CHUNK + 1, NDIM, 2, tiles, LANES), f32)],
        True,
        8,
    )(place.astype(jnp.int32).reshape(1), tokens, sums, csum, csq, norm_gain[None], norm_bias[None], q)

    more = max(1, peers // NDIM)

    def split(a):
        a = a.reshape(NDIM, 2, more, tiles // more, LANES).transpose(0, 2, 1, 3, 4)
        return a.reshape(peers, NDIM * more // peers, 2, tiles // more, LANES)

    def join(a):
        a = a.reshape(NDIM, more, 2, tiles // more, LANES).transpose(0, 2, 1, 3, 4)
        return a.reshape(NDIM, 2, tiles, LANES)

    arrived = lax.all_to_all(split(ends), "ctx", 0, 0)
    my_q = lax.dynamic_index_in_dim(split(q), place, 0, False)
    starts = call(functools.partial(scan_kernel, length), shape(arrived.shape, f32), n_in=2)(arrived, my_q)
    incoming = join(lax.all_to_all(starts, "ctx", 0, 0))

    mixed_rows = call(
        mix_kernel,
        shape((length, channels), bf16),
        [
            pltpu.VMEM((chunks, NDIM, 2, tiles, LANES), f32),
            pltpu.VMEM((CHUNK, NDIM, 2, tiles, LANES), f32),
            pltpu.VMEM((CHUNK, tiles, LANES), f32),
            pltpu.VMEM((length * tiles, LANES), f32),
        ],
        n_in=6,
    )(incoming, fresh, rows, q, w, ema_skip.reshape(tiles, LANES))

    full_normed, full_mixed = both(normed), both(mixed_rows)
    mixed_float = full_mixed.astype(f32)
    rms_normed = (
        mixed_float
        * lax.rsqrt(jnp.mean(mixed_float * mixed_float, axis=-1, keepdims=True) + 1e-06)
        * rms_gain
    ).astype(bf16)
    z_total = jnp.dot(rms_normed, weights[:, :head], preferred_element_type=f32)
    v_total = jnp.dot(full_normed, weights[:, head:], preferred_element_type=f32)
    return attention(z_total, v_total, qk_affine)


def solution(mesh):
    in_specs = (
        P("ctx", "tp"),
        P("tp"),
        P("tp"),
        P(None, "tp"),
        P(None, "tp"),
        P(None, "tp"),
        P(None, None, "tp"),
        P("tp"),
        P(),
        P("ctx", "tp"),
        P("ctx", "tp"),
        P(None, "tp"),
    )
    return jax.shard_map(body, mesh=mesh, in_specs=in_specs, out_specs=P("ctx", "tp"), check_vma=False)
```

time: 496 us -> 155 us (0.31)
  waiting for transfers between devices: 292 us -> 97.7 us
  other arithmetic: 111 us -> 3 us
  blocking collectives: 43.5 us -> 0 us
  local copies, waits for them, and re-layouts: 25.3 us -> 3.82 us
  starting transfers between devices: 0.38 us -> 16 us
  Pallas kernels: 0 us -> 12.4 us
    all_gather x6 -> x1, waiting for transfers between devices: 290 us -> 66.8 us  [body(): lax.all_gather(jnp.concatenate([z_weight, v_weight], 1), 'ctx', axis=0, t...]
    dot_general x16 -> x0, other arithmetic: 49.2 us -> none  [the longest x8 22 us: ema_feed(): fresh_im = jnp.einsum('sc,sjc->jc', inputs, tables[4], precision=highest)]
    unnamed x1 -> x0, blocking collectives: 43.5 us -> none
    all_to_all x0 -> x3, waiting for transfers between devices: none -> 29.5 us  [the longest x1 13.8 us: body(): incoming = join(lax.all_to_all(starts, 'ctx', 0, 0))]
    sub x1 -> x0, other arithmetic: 18.2 us -> none  [ema_tables(): coef_re = ema_out[0] * power_re - ema_out[1] * power_im]
    all_to_all x0 -> x3, starting transfers between devices: none -> 15.4 us  [the longest x1 8.31 us: body(): lax.all_to_all(jnp.broadcast_to(totals[None], (peers, 2, width)), 'ctx',...]
    pallas_call x0 -> x4, Pallas kernels: none -> 12.4 us  [the longest x1 5.45 us: body(): call(mix_kernel, shape((length, channels), bf16), [pltpu.VMEM((chunks, ND...]
    slice x1 -> x0, other arithmetic: 11.5 us -> none  [ema_tables(): coef_re[1:]]
  transfers between devices with their start and end apart: 6 -> 6, of which waited for: 6 -> 5; matrix products, arithmetic and copies ran while one was open for 4% -> 2% of each run, Pallas kernels for 0% -> 8%
where the time goes in v1:
time: 155 us; the launch traced here: 154 us
  waiting for transfers between devices  97.7 us (63%)
  starting transfers between devices  16 us (10%)
  between operations  13.7 us (9%)
  Pallas kernels  12.4 us (8%)
  matrix products  7.56 us (5%)
  local copies, waits for them, and re-layouts  3.82 us (2%)
  other arithmetic  3 us (2%)
    all_gather x1, waiting for transfers between devices, body(): lax.all_gather(jnp.concatenate([z_weight, v_weight], 1), 'ctx', axis=0, t...  66.8 us
    all_to_all x1, waiting for transfers between devices, body(): incoming = join(lax.all_to_all(starts, 'ctx', 0, 0))  13.8 us
    all_to_all x1, waiting for transfers between devices, body(): arrived = lax.all_to_all(split(ends), 'ctx', 0, 0)  9 us
    all_to_all x1, starting transfers between devices, body(): lax.all_to_all(jnp.broadcast_to(totals[None], (peers, 2, width)), 'ctx',...  8.31 us
    all_to_all x1, waiting for transfers between devices, body(): lax.all_to_all(jnp.broadcast_to(totals[None], (peers, 2, width)), 'ctx',...  6.7 us
    dot_general x1, matrix products, attention(): jnp.einsum('nqk,nkd->nqd', probabilities, values, preferred_element_type=...  5.56 us
    pallas_call x1, Pallas kernels, body(): call(mix_kernel, shape((length, channels), bf16), [pltpu.VMEM((chunks, ND...  5.45 us
    pallas_call x1, Pallas kernels, body(): call(feed_kernel, [shape((length, channels), bf16), shape((length * tiles...  5.32 us
  transfers between devices with their start and end apart: 6, of which 5 were waited for; matrix products, arithmetic and copies ran while one was open for 2% of the time, Pallas kernels for 8%

profile of v1, /device:TPU:0, one launch (start us, length us, event | category | flops | bytes accessed | tf_op | source)
XLA Modules:
  0.0 154.1 jit_solution(17312882151703038117)
XLA Ops:
  6.5 0.0 copy-start
  6.5 0.0 copy-start.10
  6.5 0.0 copy-start.3
  6.5 0.0 copy-start.4
  6.5 0.0 all-gather.2.cloned.1.call-start
  6.6 2.0 %pad_maximum_fusion = bf16[256,1152]{1,0:T(8,128)(2,1)} fusion(bf16[256,1024]{1,0:T(8,128)(2,1)} %param.22, bf16[256,128]{1,0:T(8,128)(2,1)} %param.21), kind=kLoop, calls=%fused_computation.22 | loop fusion | flops 1179648 | bytes 1179648 | tf_op jit(solution)/shard_map/concatenate | solution.py:318
  8.6 0.0 all-gather.2.cloned.1.call-update
  8.6 0.0 copy-done
  8.6 0.8 shard_map.118
  9.5 0.6 broadcast_in_dim.9
  10.1 8.3 %all-to-all-start = ((f32[16,2,128]{2,1,0:T(2,128)}), f32[16,2,128]{2,1,0:T(2,128)S(1)}, u32[]{:S(2)}, u32[]{:S(2)}) async-start(f32[16,2,128]{2,1,0:T(2,128)} %broadcast_in_dim.9), calls=%async_computation | async-start | bytes 32768 | tf_op jit(solution)/shard_map/all_to_all | solution.py:323
  18.4 0.0 copy-done.10
  18.4 0.0 copy-done.11
  18.4 0.0 copy-start.8
  18.4 0.0 copy-start.9
  18.4 0.5 multiply_bitcast_fusion
  19.0 6.7 %all-to-all-done.sums_ref = f32[16,2,128]{2,1,0:T(2,128)S(1)} async-done(((f32[16,2,128]{2,1,0:T(2,128)}), f32[16,2,128]{2,1,0:T(2,128)S(1)}, u32[]{:S(2)}, u32[]{:S(2)}) %all-to-all-start) | async-done | bytes 16416 | tf_op jit(solution)/shard_map/all_to_all | solution.py:323
  25.7 0.0 copy-done.3
  25.7 0.0 copy-done.4
  25.7 0.0 copy-start.5
  25.7 5.3 %shard_map.119 = (bf16[128,2048]{1,0:T(8,128)(2,1)S(1)}, f32[2048,128]{1,0:T(8,128)S(1)}, f32[8,16,2,16,128]{4,3,2,1,0:T(8,128)S(1)}, f32[16,2,16,128]{3,2,1,0:T(8,128)}) custom-call(s32[1]{0:T(128)} %bitcast.me_ref, bf16[128,2048]{1,0:T(8,128)(2,1)S(1)} %copy-done, f32[16,2,128]{2,1,0:T(2,128)S(1)} %all-to-all-done.sums_ref, ...), custom_call_target="tpu_custom_call" | custom-call | tf_op jit(solution)/shard_map/pallas_call | solution.py:331
  31.1 0.0 copy-start.1
  31.1 1.0 copy-done.1
  32.1 0.0 copy-start.6
  32.1 0.8 copy-done.6
  32.9 3.5 %all-to-all-start.1 = ((f32[16,1,2,16,128]{4,3,2,1,0:T(8,128)}), f32[16,1,2,16,128]{4,3,2,1,0:T(8,128)S(1)}, u32[]{:S(2)}, u32[]{:S(2)}) async-start(f32[16,1,2,16,128]{4,3,2,1,0:T(8,128)} %bitcast.3), calls=%async_computation.1 | async-start | bytes 524288 | tf_op jit(solution)/shard_map/all_to_all | solution.py:354
  36.4 9.0 %all-to-all-done.1.ends_ref = f32[16,1,2,16,128]{4,3,2,1,0:T(8,128)S(1)} async-done(((f32[16,1,2,16,128]{4,3,2,1,0:T(8,128)}), f32[16,1,2,16,128]{4,3,2,1,0:T(8,128)S(1)}, u32[]{:S(2)}, u32[]{:S(2)}) %all-to-all-start.1) | async-done | bytes 262176 | tf_op jit(solution)/shard_map/all_to_all | solution.py:354
  45.4 0.8 shard_map.120
  46.2 3.5 %all-to-all-start.2 = ((f32[16,1,2,16,128]{4,3,2,1,0:T(8,128)}), f32[16,1,2,16,128]{4,3,2,1,0:T(8,128)S(1)}, u32[]{:S(2)}, u32[]{:S(2)}) async-start(f32[16,1,2,16,128]{4,3,2,1,0:T(8,128)} %shard_map.120), calls=%async_computation.2 | async-start | bytes 524288 | tf_op jit(solution)/shard_map/all_to_all | solution.py:357
  49.7 0.0 copy-done.8
  49.7 0.0 copy-done.9
  49.9 13.8 %all-to-all-done.2 = f32[16,1,2,16,128]{4,3,2,1,0:T(8,128)S(1)} async-done(((f32[16,1,2,16,128]{4,3,2,1,0:T(8,128)}), f32[16,1,2,16,128]{4,3,2,1,0:T(8,128)S(1)}, u32[]{:S(2)}, u32[]{:S(2)}) %all-to-all-start.2) | async-done | bytes 262176 | tf_op jit(solution)/shard_map/all_to_all | solution.py:357
  63.7 0.0 copy-done.5
  63.7 1.2 copy-done.2
  65.0 5.4 %shard_map.121 = bf16[128,2048]{1,0:T(8,128)(2,1)S(1)} custom-call(f32[16,2,16,128]{3,2,1,0:T(8,128)S(1)} %bitcast.38, f32[8,16,2,16,128]{4,3,2,1,0:T(8,128)S(1)} %get-tuple-element.16.fresh_ref, f32[2048,128]{1,0:T(8,128)S(1)} %copy-done.2, f32[16,2,16,128]{3,2,1,0:T(8,128)S(1)} %constant_dynamic-update-slice_fusion.q_ref, ...), custom_call_target="tpu_custom_call" | custom-call | tf_op jit(solution)/shard_map/pallas_call | solution.py:359
  70.4 0.1 collective-permute-start
  70.5 0.0 copy-done.12
  70.5 0.5 collective-permute-start.1
  71.0 1.4 collective-permute-done
  72.4 0.4 fusion.2
  72.8 0.0 copy-start.7
  72.8 66.8 %all-gather.2.cloned.1.call-done = bf16[4096,1152]{1,0:T(8,128)(2,1)} async-done(((bf16[256,1152]{1,0:T(8,128)(2,1)}), bf16[4096,1152]{1,0:T(8,128)(2,1)}) %all-gather.2.cloned.1.call-update) | async-done | bytes 9437200 | tf_op jit(solution)/shard_map/all_gather | solution.py:318
  139.6 0.0 copy-done.13
  139.6 1.8 %fusion.6 = f32[128,128]{1,0:T(8,128)S(1)} fusion(bf16[4096,1152]{1,0:T(8,128)(2,1)} %all-gather.2.cloned.1.call-done, f32[4096]{0:T(1024)S(1)} %copy-done.13, f32[128]{0:T(128)S(1)} %add_rsqrt_fusion, bf16[128,2048]{1,0:T(8,128)(2,1)S(1)} %collective-permute-done, bf16[128,2048]{1,0:T(8,128)(2,1)S(1)} %shard_map.121, pred[]{:T(512)S(6)} %eq.4), kind=kOutput, calls=%fused_computation.10 | convolution fusion | flops 141033472 | bytes 2179585 | tf_op jit(solution)/shard_map/dot_general | solution.py:378
  141.5 0.2 fusion.35
  141.7 0.0 collective-permute-done.1
  141.7 0.0 copy-done.7
  141.7 5.6 %convolution_convert_fusion = bf16[128,1024]{1,0:T(8,128)(2,1)} fusion(bf16[4096,1152]{1,0:T(8,128)(2,1)} %all-gather.2.cloned.1.call-done, bf16[128,2048]{1,0:T(8,128)(2,1)S(1)} %collective-permute-done.1, bf16[128,2048]{1,0:T(8,128)(2,1)S(1)} %copy-done.7, pred[]{:T(512)S(6)} %eq.4, f32[128,128]{0,1:T(8,128)S(1)} %get-tuple-element.28, ...), kind=kOutput, calls=%fused_computation.7 | convolution fusion | flops 1112850432 | bytes 9765889 | tf_op jit(solution)/shard_map/nqk,nkd->nqd/dot_general | solution.py:302
  (16 shorter events, 0.3 us)
Async XLA Ops:
  6.5 2.1 %copy-start = (bf16[128,2048]{1,0:T(8,128)(2,1)S(1)}, bf16[128,2048]{1,0:T(8,128)(2,1)}, u32[]{:S(2)}) copy-start(bf16[128,2048]{1,0:T(8,128)(2,1)} %x_ref.3) | copy-start | bytes 1572868
  6.5 11.9 %copy-start.10 = (f32[16,2048]{1,0:T(8,128)S(1)}, f32[16,2048]{1,0:T(8,128)}, u32[]{:S(2)}) copy-start(f32[16,2048]{1,0:T(8,128)} %param.15) | copy-start | bytes 393220
  6.5 11.9 %copy-start.11 = (f32[16,2048]{1,0:T(8,128)S(1)}, f32[16,2048]{1,0:T(8,128)}, u32[]{:S(2)}) copy-start(f32[16,2048]{1,0:T(8,128)} %param.16) | copy-start | bytes 393220
  6.5 19.2 %copy-start.3 = (f32[2048]{0:T(1024)S(1)}, f32[2048]{0:T(1024)}, u32[]{:S(2)}) copy-start(f32[2048]{0:T(1024)} %param.13) | copy-start | bytes 24580
  6.5 19.2 %copy-start.4 = (f32[2048]{0:T(1024)S(1)}, f32[2048]{0:T(1024)}, u32[]{:S(2)}) copy-start(f32[2048]{0:T(1024)} %param.14) | copy-start | bytes 24580
  6.5 133.1 %all-gather.2.cloned.1.call-start = ((), (), s32[]{:S(2)}) async-start(), calls=%async_computation.3 | async-start | bytes 10027008 | tf_op jit(solution)/shard_map/all_gather | solution.py:318
  10.1 15.7 %all-to-all-start = ((f32[16,2,128]{2,1,0:T(2,128)}), f32[16,2,128]{2,1,0:T(2,128)S(1)}, u32[]{:S(2)}, u32[]{:S(2)}) async-start(f32[16,2,128]{2,1,0:T(2,128)} %broadcast_in_dim.9), calls=%async_computation | async-start | bytes 32768 | tf_op jit(solution)/shard_map/all_to_all | solution.py:323
  18.4 31.3 %copy-start.8 = (f32[2,16,2048]{2,1,0:T(8,128)S(1)}, f32[2,16,2048]{2,1,0:T(8,128)}, u32[]{:S(2)}) copy-start(f32[2,16,2048]{2,1,0:T(8,128)} %param.18) | copy-start | bytes 786436
  18.4 31.3 %copy-start.9 = (f32[16,2048]{1,0:T(8,128)S(1)}, f32[16,2048]{1,0:T(8,128)}, u32[]{:S(2)}) copy-start(f32[16,2048]{1,0:T(8,128)} %param.17) | copy-start | bytes 393220
  25.7 38.0 %copy-start.5 = (f32[2048]{0:T(1024)S(1)}, f32[2048]{0:T(1024)}, u32[]{:S(2)}) copy-start(f32[2048]{0:T(1024)} %param.19) | copy-start | bytes 24580
  31.1 1.0 copy-start.1
  32.1 0.8 copy-start.6
  32.9 12.6 %all-to-all-start.1 = ((f32[16,1,2,16,128]{4,3,2,1,0:T(8,128)}), f32[16,1,2,16,128]{4,3,2,1,0:T(8,128)S(1)}, u32[]{:S(2)}, u32[]{:S(2)}) async-start(f32[16,1,2,16,128]{4,3,2,1,0:T(8,128)} %bitcast.3), calls=%async_computation.1 | async-start | bytes 524288 | tf_op jit(solution)/shard_map/all_to_all | solution.py:354
  46.2 17.5 %all-to-all-start.2 = ((f32[16,1,2,16,128]{4,3,2,1,0:T(8,128)}), f32[16,1,2,16,128]{4,3,2,1,0:T(8,128)S(1)}, u32[]{:S(2)}, u32[]{:S(2)}) async-start(f32[16,1,2,16,128]{4,3,2,1,0:T(8,128)} %shard_map.120), calls=%async_computation.2 | async-start | bytes 524288 | tf_op jit(solution)/shard_map/all_to_all | solution.py:357
  63.7 1.2 copy-start.2
  65.0 5.5 %copy-start.12 = (f32[4,128]{1,0:T(4,128)S(1)}, f32[4,128]{1,0:T(4,128)}, u32[]{:S(2)}) copy-start(f32[4,128]{1,0:T(4,128)} %param.23) | copy-start | bytes 6148
  65.0 74.7 %copy-start.13 = (f32[4096]{0:T(1024)S(1)}, f32[4096]{0:T(1024)}, u32[]{:S(2)}) copy-start(f32[4096]{0:T(1024)} %param.20) | copy-start | bytes 49156
  70.4 2.0 %collective-permute-start = (bf16[128,2048]{1,0:T(8,128)(2,1)S(1)}, bf16[128,2048]{1,0:T(8,128)(2,1)S(1)}, u32[]{:S(2)}, u32[]{:S(2)}) collective-permute-start(bf16[128,2048]{1,0:T(8,128)(2,1)S(1)} %shard_map.121), channel_id=1, source_target_pairs={{0,1},{1,0},{2,3},{3,2},{4,5},{5,4},{6,7},{7,6},{8,9},{9,8},{10,11... | collective-permute-start | bytes 1572872 | tf_op jit(solution)/shard_map/ppermute | solution.py:271
  70.5 71.2 %collective-permute-start.1 = (bf16[128,2048]{1,0:T(8,128)(2,1)}, bf16[128,2048]{1,0:T(8,128)(2,1)S(1)}, u32[]{:S(2)}, u32[]{:S(2)}) collective-permute-start(bf16[128,2048]{1,0:T(8,128)(2,1)} %copy-done.6), channel_id=1, source_target_pairs={{0,1},{1,0},{2,3},{3,2},{4,5},{5,4},{6,7},{7,6},{8,9},{9,8},{10,11... | collective-permute-start | bytes 1572872 | tf_op jit(solution)/shard_map/ppermute | solution.py:271
  72.8 68.9 %copy-start.7 = (bf16[128,2048]{1,0:T(8,128)(2,1)S(1)}, bf16[128,2048]{1,0:T(8,128)(2,1)}, u32[]{:S(2)}) copy-start(bf16[128,2048]{1,0:T(8,128)(2,1)} %copy-done.6) | copy-start | bytes 1572868
Sparse Core Ops, SparseCore 0:
  10.2 129.4 all-gather.1

commit v2 on v1

--- a/solution.py
+++ b/solution.py
@@ -89,6 +89,7 @@
     me_ref, x_ref, sums_ref, csum_ref, csq_ref, gain_ref, bias_ref, q_ref,
     normed_ref, dense_ref, fresh_ref, end_ref, power_ref,
 ):
+    members, _, _, depth = normed_ref.shape
     length, channels = x_ref.shape
     width = csum_ref.shape[1]
     tiles = channels // LANES
@@ -114,7 +115,12 @@
         scale_wide = sum(mm(p, mine) for p in scale_pieces)
         scaled = (x_ref[:, lanes].astype(f32) - average_wide) * scale_wide
         normed = (scaled * gain_ref[:, lanes] + bias_ref[:, lanes]).astype(bf16)
-        normed_ref[:, lanes] = normed
+        part = min(depth, LANES)
+        for low in range(0, LANES, part):
+            at = tile * LANES + low
+            block = at // depth
+            away = lax.rem(block % members + members - lax.rem(me, members), members)
+            normed_ref[away, block // members, :, at % depth : at % depth + part] = normed[:, low : low + part]
         dense_ref[pl.ds(tile, length, stride=tiles), :] = normed.astype(f32)
 
     sub = q_ref.shape[2]
@@ -261,46 +267,80 @@
         mixed_ref[:, lanes] = (value / (1.0 + jnp.exp(-value))).astype(bf16)
 
 
-def both(block):
-    count = lax.axis_size("tp")
-    if count == 1:
-        return block
-    place = lax.axis_index("tp")
-    width = block.shape[1]
-    others = [
-        lax.ppermute(block, "tp", [(i, (i + k) % count) for i in range(count)]) for k in range(1, count)
-    ]
-    if count == 2:
-        other = others[0]
-        return jnp.where(
-            place == 0, jnp.concatenate([block, other], 1), jnp.concatenate([other, block], 1)
-        )
-    full = jnp.zeros((block.shape[0], width * count), block.dtype)
-    full = lax.dynamic_update_slice_in_dim(full, block, place * width, 1)
-    for k, other in enumerate(others, 1):
-        full = lax.dynamic_update_slice_in_dim(full, other, ((place - k) % count) * width, 1)
-    return full
-
-
-def attention(z_total, v_total, affine):
-    queries = (z_total * affine[0] + affine[1]).astype(bf16)
-    key_rows = (z_total * affine[2] + affine[3]).astype(bf16)
-    values = jax.nn.silu(v_total).astype(bf16)
-    row_count, width = z_total.shape
-    stretches = row_count // STRETCH
-    queries = queries.reshape(stretches, STRETCH, -1)
-    key_rows = key_rows.reshape(stretches, STRETCH, -1)
-    values = values.reshape(stretches, STRETCH, -1)
-    scores = jnp.einsum("nqd,nkd->nqk", queries, key_rows, preferred_element_type=f32) * (
-        1.0 / width**0.5
-    )
-    causal = jnp.arange(STRETCH)[:, None] >= jnp.arange(STRETCH)[None, :]
-    scores = jnp.where(causal[None], scores, -1e30)
-    row_max = jnp.max(scores, axis=-1, keepdims=True)
-    weights = jnp.exp(scores - row_max)
-    probabilities = (weights / jnp.sum(weights, axis=-1, keepdims=True)).astype(bf16)
-    result = jnp.einsum("nqk,nkd->nqd", probabilities, values, preferred_element_type=f32)
-    return result.reshape(row_count, -1).astype(bf16)
+def along(block, axis, step, group):
+    count = lax.axis_size(axis)
+    pairs = [(i, i - i % group + (i + step) % group) for i in range(count)]
+    return lax.ppermute(block, axis, pairs)
+
+
+def others(block, axis):
+    count = lax.axis_size(axis)
+    return [along(block, axis, k, count) for k in range(1, count)]
+
+
+def part_kernel(members, tp, at_ref, *refs):
+    *refs, own_ref, sent_ref, row_ref = refs
+    near, far, weights = refs[:members], refs[members : members + tp - 1], refs[members + tp - 1 :]
+    subs, length, _ = near[0].shape
+    parts = len(weights)
+    half, layer = at_ref[0], at_ref[1]
+    for away in range(tp):
+        other = lax.rem(half + tp - away, tp)
+        for sub in range(subs):
+            slot = lax.rem(layer + parts - (other * subs + sub), parts)
+            for k in range(members):
+                block = far[away - 1][k, sub] if away else near[k][sub]
+                row_ref[slot, k * length : (k + 1) * length, :] = block
+    for k in range(members):
+        here = slice(k * length, (k + 1) * length)
+        total = mm(row_ref[0, here, :], weights[0][...])
+        for slot in range(1, parts):
+            total = total + mm(row_ref[slot, here, :], weights[slot][...])
+        if k == 0:
+            own_ref[...] = total
+        else:
+            sent_ref[k - 1] = total.astype(bf16)
+
+
+def probability_kernel(head, me_ref, *refs):
+    *mixed_refs, gain_ref, weight_ref, affine_ref, out_ref = refs
+    tp = len(mixed_refs)
+    length, channels = mixed_refs[0].shape
+    square = jnp.zeros((length, 1), f32)
+    for ref in mixed_refs:
+        value = ref[...].astype(f32)
+        square = square + jnp.sum(value * value, axis=1, keepdims=True)
+    scale = lax.rsqrt(square / (channels * tp) + 1e-06)
+    z_total = jnp.zeros((length, head), f32)
+    for k, ref in enumerate(mixed_refs):
+        at = lax.rem(me_ref[0] + tp - k, tp)
+        normed = (ref[...].astype(f32) * scale * gain_ref[pl.ds(at, 1), :]).astype(bf16)
+        rows = pl.ds(pl.multiple_of(at * channels, channels), channels)
+        z_total = z_total + mm(normed, weight_ref[rows, :])
+    affine = affine_ref[...]
+    queries = (z_total * affine[0:1] + affine[1:2]).astype(bf16)
+    key_rows = (z_total * affine[2:3] + affine[3:4]).astype(bf16)
+    row = lax.broadcasted_iota(jnp.int32, (STRETCH, STRETCH), 0)
+    col = lax.broadcasted_iota(jnp.int32, (STRETCH, STRETCH), 1)
+    for low in range(0, length, STRETCH):
+        here = slice(low, low + STRETCH)
+        scores = lax.dot_general(
+            queries[here], key_rows[here], (((1,), (1,)), ((), ())), preferred_element_type=f32
+        ) * (1.0 / head**0.5)
+        scores = jnp.where(row >= col, scores, -1e30)
+        weights = jnp.exp(scores - jnp.max(scores, axis=1, keepdims=True))
+        out_ref[here, :] = (weights / jnp.sum(weights, axis=1, keepdims=True)).astype(bf16)
+
+
+def attend_kernel(own_ref, *refs):
+    *parts, probability_ref, out_ref = refs
+    total = own_ref[...]
+    for part in parts:
+        total = total + part[...].astype(f32)
+    values = (total / (1.0 + jnp.exp(-total))).astype(bf16)
+    for low in range(0, total.shape[0], STRETCH):
+        here = slice(low, low + STRETCH)
+        out_ref[here, :] = mm(probability_ref[here, :], values[here]).astype(bf16)
 
 
 def body(
@@ -313,9 +353,16 @@
     place = lax.axis_index("ctx")
     peers = lax.axis_size("ctx")
     head = z_weight.shape[1]
+    tp, half = lax.axis_size("tp"), lax.axis_index("tp")
+    depth, columns = v_weight.shape
+    blocks = channels // depth
+    members = 4 if peers % 4 == 0 and blocks % 4 == 0 else 1
+    layers = peers // members
     shape = jax.ShapeDtypeStruct
 
-    weights = lax.all_gather(jnp.concatenate([z_weight, v_weight], 1), "ctx", axis=0, tiled=True)
+    all_z = lax.all_gather(z_weight, "ctx", axis=0, tiled=True)
+    layer_pairs = [[(i, (i + members * k) % peers) for i in range(peers)] for k in range(layers)]
+    all_v = [v_weight] + [lax.ppermute(v_weight, "ctx", layer_pairs[k]) for k in range(1, layers)]
 
     csum, csq, totals = call(
         sums_kernel, [shape((length, width), f32), shape((length, width), f32), shape((2, width), f32)]
@@ -331,7 +378,7 @@
     normed, rows, fresh, ends = call(
         feed_kernel,
         [
-            shape((length, channels), bf16),
+            shape((members, blocks // members, length, depth), bf16),
             shape((length * tiles, LANES), f32),
             shape((chunks, NDIM, 2, tiles, LANES), f32),
             shape((NDIM, 2, tiles, LANES), f32),
@@ -368,16 +415,21 @@
         n_in=6,
     )(incoming, fresh, rows, q, w, ema_skip.reshape(tiles, LANES))
 
-    full_normed, full_mixed = both(normed), both(mixed_rows)
-    mixed_float = full_mixed.astype(f32)
-    rms_normed = (
-        mixed_float
-        * lax.rsqrt(jnp.mean(mixed_float * mixed_float, axis=-1, keepdims=True) + 1e-06)
-        * rms_gain
-    ).astype(bf16)
-    z_total = jnp.dot(rms_normed, weights[:, :head], preferred_element_type=f32)
-    v_total = jnp.dot(full_normed, weights[:, head:], preferred_element_type=f32)
-    return attention(z_total, v_total, qk_affine)
+    near = [normed[0]] + [along(normed[k], "ctx", k, members) for k in range(1, members)]
+    far = others(jnp.stack(near), "tp")
+    own, sent = call(
+        functools.partial(part_kernel, members, tp),
+        [shape((length, columns), f32), shape((max(members - 1, 1), length, columns), bf16)],
+        [pltpu.VMEM((layers, members * length, depth), bf16)],
+        True,
+        members + tp + layers,
+    )(jnp.stack([half, place // members]).astype(jnp.int32), *near, *far, *all_v)
+    returned = [along(sent[k - 1], "ctx", -k, members) for k in range(1, members)]
+
+    probabilities = call(
+        functools.partial(probability_kernel, head), shape((length, STRETCH), bf16), (), True, tp + 4
+    )(half.astype(jnp.int32).reshape(1), mixed_rows, *others(mixed_rows, "tp"), rms_gain.reshape(tp, channels), all_z, qk_affine)
+    return call(attend_kernel, shape((length, columns), bf16), n_in=members + 1)(own, *returned, probabilities)
 
 
 def solution(mesh):

time: 155 us -> 137 us (0.88)
  the two profiles are of different devices: /device:TPU:0 before, /device:TPU:20 now
where the time goes in v2:
time: 137 us; the launch traced here: 136 us
  waiting for transfers between devices  58.2 us (42%)
  starting transfers between devices  29.9 us (22%)
  Pallas kernels  18.7 us (14%)
  between operations  13.7 us (10%)
  local copies, waits for them, and re-layouts  10.4 us (8%)
  other arithmetic  5.43 us (4%)
    all_to_all x1, waiting for transfers between devices, body(): arrived = lax.all_to_all(split(ends), 'ctx', 0, 0)  26.6 us
    all_to_all x1, waiting for transfers between devices, body(): incoming = join(lax.all_to_all(starts, 'ctx', 0, 0))  19.4 us
    ppermute x8, waiting for transfers between devices, along(): return lax.ppermute(block, axis, pairs)  9.63 us
    unnamed x41, local copies, waits for them, and re-layouts  8.04 us
    all_to_all x1, starting transfers between devices, body(): incoming = join(lax.all_to_all(starts, 'ctx', 0, 0))  7.47 us
    all_to_all x1, starting transfers between devices, body(): lax.all_to_all(jnp.broadcast_to(totals[None], (peers, 2, width)), 'ctx',...  7.06 us
    all_to_all x1, starting transfers between devices, body(): arrived = lax.all_to_all(split(ends), 'ctx', 0, 0)  6.59 us
    ppermute x8, starting transfers between devices, along(): return lax.ppermute(block, axis, pairs)  6.15 us
  transfers between devices with their start and end apart: 15, of which 5 were waited for; matrix products, arithmetic and copies ran while one was open for 6% of the time, Pallas kernels for 12%

profile of v2, /device:TPU:20, one launch (start us, length us, event | category | flops | bytes accessed | tf_op | source)
XLA Modules:
  0.0 136.3 jit_solution(17958729063057363845)
XLA Ops:
  6.5 1.0 copy-done
  7.6 0.8 shard_map.118
  8.4 0.6 broadcast_in_dim.12
  9.0 7.1 %all-to-all-start = ((f32[16,2,128]{2,1,0:T(2,128)}), f32[16,2,128]{2,1,0:T(2,128)S(1)}, u32[]{:S(2)}, u32[]{:S(2)}) async-start(f32[16,2,128]{2,1,0:T(2,128)} %broadcast_in_dim.12), calls=%async_computation | async-start | bytes 32768 | tf_op jit(solution)/shard_map/all_to_all | solution.py:370
  16.1 0.0 all-gather.2.cloned.1.call-start
  16.1 0.7 all-gather.2.cloned.1.call-update
  16.8 1.4 %multiply_bitcast_fusion = (f32[2,8,16,128]{3,1,2,0:T(8,128)S(1)}, f32[2,8,16,128]{3,1,2,0:T(8,128)S(1)}) fusion(f32[16,2048]{1,0:T(8,128)} %param.15, f32[16,2048]{1,0:T(8,128)} %param.16), kind=kLoop, calls=%fused_computation.12 | loop fusion | flops 65536 | bytes 524288
  18.4 1.9 %all-to-all-done.sums_ref = f32[16,2,128]{2,1,0:T(2,128)S(1)} async-done(((f32[16,2,128]{2,1,0:T(2,128)}), f32[16,2,128]{2,1,0:T(2,128)S(1)}, u32[]{:S(2)}, u32[]{:S(2)}) %all-to-all-start) | async-done | bytes 16416 | tf_op jit(solution)/shard_map/all_to_all | solution.py:370
  20.3 0.7 copy-done.13
  21.0 0.7 copy-done.14
  21.7 4.6 %shard_map.119 = (bf16[4,2,128,256]{3,2,1,0:T(8,128)(2,1)S(1)}, f32[2048,128]{1,0:T(8,128)S(1)}, f32[8,16,2,16,128]{4,3,2,1,0:T(8,128)S(1)}, f32[16,2,16,128]{3,2,1,0:T(8,128)S(1)}) custom-call(s32[1]{0:T(128)} %bitcast.2.me_ref, bf16[128,2048]{1,0:T(8,128)(2,1)S(1)} %copy-done.1, f32[16,2,128]{2,1,0:T(2,128)S(1)} %all-to-all-done.sums_ref, ...), custom_call_target="tpu_custom_call" | custom-call | tf_op jit(solution)/shard_map/pallas_call | solution.py:378
  26.3 1.0 copy-done.2
  27.3 0.7 copy-done.12
  28.0 6.6 %all-to-all-start.1 = ((f32[16,1,2,16,128]{4,3,2,1,0:T(8,128)}), f32[16,1,2,16,128]{4,3,2,1,0:T(8,128)S(1)}, u32[]{:S(2)}, u32[]{:S(2)}) async-start(f32[16,1,2,16,128]{4,3,2,1,0:T(8,128)} %bitcast.53), calls=%async_computation.1 | async-start | bytes 524288 | tf_op jit(solution)/shard_map/all_to_all | solution.py:401
  34.6 0.8 fusion.2
  35.4 0.5 collective-permute-start.1
  36.0 2.4 %collective-permute-start.2 = (bf16[2,128,256]{2,1,0:T(8,128)(2,1)}, bf16[2,128,256]{2,1,0:T(8,128)(2,1)S(1)}, u32[]{:S(2)}, u32[]{:S(2)}) collective-permute-start(bf16[2,128,256]{2,1,0:T(8,128)(2,1)} %get-tuple-element.28), channel_id=1, source_target_pairs={{0,6},{2,0},{4,2},{6,4},{8,14},{10,8},{12,10},{14,12},{16,22},{18,... | collective-permute-start | bytes 393224 | tf_op jit(solution)/shard_map/ppermute | solution.py:273
  38.3 0.0 collective-permute-start
  38.3 1.5 %collective-permute-start.4 = (bf16[256,1024]{1,0:T(8,128)(2,1)}, bf16[256,1024]{1,0:T(8,128)(2,1)}, u32[]{:S(2)}, u32[]{:S(2)}) collective-permute-start(bf16[256,1024]{1,0:T(8,128)(2,1)} %refs_5_.1), channel_id=1, source_target_pairs={{0,8},{2,10},{4,12},{6,14},{8,16},{10,18},{12,20},{14,22},{16,24},... | collective-permute-start | bytes 1572872 | tf_op jit(solution)/shard_map/ppermute | solution.py:365
  39.8 0.5 collective-permute-start.5
  40.3 26.6 %all-to-all-done.1.ends_ref = f32[16,1,2,16,128]{4,3,2,1,0:T(8,128)S(1)} async-done(((f32[16,1,2,16,128]{4,3,2,1,0:T(8,128)}), f32[16,1,2,16,128]{4,3,2,1,0:T(8,128)S(1)}, u32[]{:S(2)}, u32[]{:S(2)}) %all-to-all-start.1) | async-done | bytes 262176 | tf_op jit(solution)/shard_map/all_to_all | solution.py:401
  66.9 0.8 shard_map.121
  67.7 7.5 %all-to-all-start.2 = ((f32[16,1,2,16,128]{4,3,2,1,0:T(8,128)}), f32[16,1,2,16,128]{4,3,2,1,0:T(8,128)S(1)}, u32[]{:S(2)}, u32[]{:S(2)}) async-start(f32[16,1,2,16,128]{4,3,2,1,0:T(8,128)} %shard_map.121), calls=%async_computation.2 | async-start | bytes 524288 | tf_op jit(solution)/shard_map/all_to_all | solution.py:404
  75.2 0.6 collective-permute-start.6
  75.8 0.0 collective-permute-done.refs_1_
  75.8 1.9 %pad_maximum_fusion = bf16[4,2,128,256]{3,2,1,0:T(8,128)(2,1)} fusion(bf16[1,2,128,256]{3,2,1,0:T(8,128)(2,1)S(1)} %bitcast.51, bf16[1,2,128,256]{3,2,1,0:T(8,128)(2,1)S(1)} %bitcast.50, bf16[1,2,128,256]{3,2,1,0:T(8,128)(2,1)S(1)} %bitcast.52, bf16[1,2,128,256]{3,2,1,0:T(8,128)(2,1)} %get-tuple-element.26), kind=kLoop, calls=%fused_computation | loop fusion | flops 786432 | bytes 1048576 | tf_op jit(solution)/shard_map/stack | solution.py:419
  77.7 1.1 fusion.1
  78.7 0.7 copy.16
  79.4 0.7 copy.17
  80.1 1.0 pad_maximum_fusion.1.w_ref
  81.1 19.4 %all-to-all-done.2 = f32[16,1,2,16,128]{4,3,2,1,0:T(8,128)S(1)} async-done(((f32[16,1,2,16,128]{4,3,2,1,0:T(8,128)}), f32[16,1,2,16,128]{4,3,2,1,0:T(8,128)S(1)}, u32[]{:S(2)}, u32[]{:S(2)}) %all-to-all-start.2) | async-done | bytes 262176 | tf_op jit(solution)/shard_map/all_to_all | solution.py:404
  100.5 1.2 copy-done.3
  101.7 5.5 %shard_map.122.refs_0_ = bf16[128,2048]{1,0:T(8,128)(2,1)S(1)} custom-call(f32[16,2,16,128]{3,2,1,0:T(8,128)S(1)} %bitcast.49, f32[8,16,2,16,128]{4,3,2,1,0:T(8,128)S(1)} %get-tuple-element.21.fresh_ref, f32[2048,128]{1,0:T(8,128)S(1)} %copy-done.3, f32[16,2,16,128]{3,2,1,0:T(8,128)S(1)} %constant_dynamic-update-slice_fusion.q_ref, ...), custom_call_target="tpu_custom_call" | custom-call | tf_op jit(solution)/shard_map/pallas_call | solution.py:406
  107.2 0.1 collective-permute-start.10
  107.3 0.1 pad_add_fusion.at_ref
  107.4 0.0 copy-start.17
  107.4 0.0 copy-start.16
  107.4 2.9 %shard_map.120 = (f32[128,1024]{1,0:T(8,128)S(1)}, bf16[3,128,1024]{2,1,0:T(8,128)(2,1)S(1)}) custom-call(s32[2]{0:T(128)S(1)} %pad_add_fusion.at_ref, bf16[2,128,256]{2,1,0:T(8,128)(2,1)S(1)} %get-tuple-element.27.refs_0_, bf16[2,128,256]{2,1,0:T(8,128)(2,1)S(1)} %copy-done.11, bf16[2,128,256]{2,1,0:T(8,128)(2,1)S(1)} %copy-done.7, ...), custom_call_target="tpu_custom_call" | custom-call | tf_op jit(solution)/shard_map/pallas_call | solution.py:420
  110.4 0.9 slice_bitcast_fusion
  111.3 1.9 %collective-permute-start.7 = (bf16[128,1024]{1,0:T(8,128)(2,1)}, bf16[128,1024]{1,0:T(8,128)(2,1)S(1)}, u32[]{:S(2)}, u32[]{:S(2)}) collective-permute-start(bf16[128,1024]{1,0:T(8,128)(2,1)} %get-tuple-element.25), channel_id=1, source_target_pairs={{0,6},{2,0},{4,2},{6,4},{8,14},{10,8},{12,10},{14,12},{16,22},{18,... | collective-permute-start | bytes 786440 | tf_op jit(solution)/shard_map/ppermute | solution.py:273
  113.1 0.1 collective-permute-start.8
  113.3 1.1 collective-permute-start.9
  114.4 0.0 all-gather.2.cloned.1.call-done.refs_3_
  114.5 1.2 copy-done.4
  115.7 2.0 %shard_map.123.refs_3_ = bf16[128,128]{1,0:T(8,128)(2,1)S(1)} custom-call(s32[1]{0:T(128)} %bitcast.me_ref, bf16[128,2048]{1,0:T(8,128)(2,1)S(1)} %shard_map.122.refs_0_, bf16[128,2048]{1,0:T(8,128)(2,1)} %collective-permute-done.10.refs_1_, f32[2,2048]{1,0:T(2,128)S(1)} %reshape.15.refs_2_, bf16[4096,128]{1,0:T(8,128)(2,1)S(1)} %copy-done.4, ...), custom_call_target="tpu_custom_call" | custom-call | tf_op jit(solution)/shard_map/pallas_call | solution.py:429
  117.7 2.8 %collective-permute-done.7.refs_0_ = bf16[128,1024]{1,0:T(8,128)(2,1)S(1)} collective-permute-done((bf16[128,1024]{1,0:T(8,128)(2,1)}, bf16[128,1024]{1,0:T(8,128)(2,1)S(1)}, u32[]{:S(2)}, u32[]{:S(2)}) %collective-permute-start.7) | collective-permute-done | bytes 262176 | tf_op jit(solution)/shard_map/ppermute | solution.py:273
  120.6 6.8 %collective-permute-done.8.refs_1_ = bf16[128,1024]{1,0:T(8,128)(2,1)S(1)} collective-permute-done((bf16[128,1024]{1,0:T(8,128)(2,1)}, bf16[128,1024]{1,0:T(8,128)(2,1)S(1)}, u32[]{:S(2)}, u32[]{:S(2)}) %collective-permute-start.8) | collective-permute-done | bytes 262176 | tf_op jit(solution)/shard_map/ppermute | solution.py:273
  127.4 2.1 %shard_map.124 = bf16[128,1024]{1,0:T(8,128)(2,1)} custom-call(f32[128,1024]{1,0:T(8,128)S(1)} %get-tuple-element.18.own_ref, bf16[128,1024]{1,0:T(8,128)(2,1)S(1)} %collective-permute-done.7.refs_0_, bf16[128,1024]{1,0:T(8,128)(2,1)S(1)} %collective-permute-done.8.refs_1_, bf16[128,1024]{1,0:T(8,128)(2,1)} %collective-permute-done.9.refs_2_, ...), custom_call_target="tpu_custom_call" | custom-call | tf_op jit(solution)/shard_map/pallas_call | solution.py:432
  (42 shorter events, 0.2 us)
Async XLA Ops:
  6.5 1.0 copy-start
  7.6 12.7 %copy-start.1 = (bf16[128,2048]{1,0:T(8,128)(2,1)S(1)}, bf16[128,2048]{1,0:T(8,128)(2,1)}, u32[]{:S(2)}) copy-start(bf16[128,2048]{1,0:T(8,128)(2,1)} %x_ref.3) | copy-start | bytes 1572868
  9.0 11.3 %all-to-all-start = ((f32[16,2,128]{2,1,0:T(2,128)}), f32[16,2,128]{2,1,0:T(2,128)S(1)}, u32[]{:S(2)}, u32[]{:S(2)}) async-start(f32[16,2,128]{2,1,0:T(2,128)} %broadcast_in_dim.12), calls=%async_computation | async-start | bytes 32768 | tf_op jit(solution)/shard_map/all_to_all | solution.py:370
  16.1 98.4 %all-gather.2.cloned.1.call-start = ((), (), s32[]{:S(2)}) async-start(), calls=%async_computation.3 | async-start | bytes 1114112 | tf_op jit(solution)/shard_map/all_gather | solution.py:363
  20.3 0.7 copy-start.13
  21.0 0.7 copy-start.14
  26.3 1.0 copy-start.2
  27.3 0.7 copy-start.12
  28.0 38.9 %all-to-all-start.1 = ((f32[16,1,2,16,128]{4,3,2,1,0:T(8,128)}), f32[16,1,2,16,128]{4,3,2,1,0:T(8,128)S(1)}, u32[]{:S(2)}, u32[]{:S(2)}) async-start(f32[16,1,2,16,128]{4,3,2,1,0:T(8,128)} %bitcast.53), calls=%async_computation.1 | async-start | bytes 524288 | tf_op jit(solution)/shard_map/all_to_all | solution.py:401
  35.4 65.1 %copy-start.15 = (f32[2048]{0:T(1024)S(1)}, f32[2048]{0:T(1024)}, u32[]{:S(2)}) copy-start(f32[2048]{0:T(1024)} %param.19) | copy-start | bytes 24580
  35.4 39.8 %collective-permute-start.1 = (bf16[2,128,256]{2,1,0:T(8,128)(2,1)}, bf16[2,128,256]{2,1,0:T(8,128)(2,1)S(1)}, u32[]{:S(2)}, u32[]{:S(2)}) collective-permute-start(bf16[2,128,256]{2,1,0:T(8,128)(2,1)} %get-tuple-element.29), channel_id=1, source_target_pairs={{0,4},{2,6},{4,0},{6,2},{8,12},{10,14},{12,8},{14,10},{16,20},{18,... | collective-permute-start | bytes 393224 | tf_op jit(solution)/shard_map/ppermute | solution.py:273
  36.0 39.8 %collective-permute-start.2 = (bf16[2,128,256]{2,1,0:T(8,128)(2,1)}, bf16[2,128,256]{2,1,0:T(8,128)(2,1)S(1)}, u32[]{:S(2)}, u32[]{:S(2)}) collective-permute-start(bf16[2,128,256]{2,1,0:T(8,128)(2,1)} %get-tuple-element.28), channel_id=1, source_target_pairs={{0,6},{2,0},{4,2},{6,4},{8,14},{10,8},{12,10},{14,12},{16,22},{18,... | collective-permute-start | bytes 393224 | tf_op jit(solution)/shard_map/ppermute | solution.py:273
  38.3 37.5 %collective-permute-start = (bf16[2,128,256]{2,1,0:T(8,128)(2,1)}, bf16[2,128,256]{2,1,0:T(8,128)(2,1)S(1)}, u32[]{:S(2)}, u32[]{:S(2)}) collective-permute-start(bf16[2,128,256]{2,1,0:T(8,128)(2,1)} %get-tuple-element.30), channel_id=1, source_target_pairs={{0,2},{2,4},{4,6},{6,0},{8,10},{10,12},{12,14},{14,8},{16,18},{18,... | collective-permute-start | bytes 393224 | tf_op jit(solution)/shard_map/ppermute | solution.py:273
  38.3 69.0 %collective-permute-start.4 = (bf16[256,1024]{1,0:T(8,128)(2,1)}, bf16[256,1024]{1,0:T(8,128)(2,1)}, u32[]{:S(2)}, u32[]{:S(2)}) collective-permute-start(bf16[256,1024]{1,0:T(8,128)(2,1)} %refs_5_.1), channel_id=1, source_target_pairs={{0,8},{2,10},{4,12},{6,14},{8,16},{10,18},{12,20},{14,22},{16,24},... | collective-permute-start | bytes 1572872 | tf_op jit(solution)/shard_map/ppermute | solution.py:365
  39.8 67.5 %collective-permute-start.5 = (bf16[256,1024]{1,0:T(8,128)(2,1)}, bf16[256,1024]{1,0:T(8,128)(2,1)}, u32[]{:S(2)}, u32[]{:S(2)}) collective-permute-start(bf16[256,1024]{1,0:T(8,128)(2,1)} %refs_5_.1), channel_id=1, source_target_pairs={{0,16},{2,18},{4,20},{6,22},{8,24},{10,26},{12,28},{14,30},{16,0},... | collective-permute-start | bytes 1572872 | tf_op jit(solution)/shard_map/ppermute | solution.py:365
  67.7 32.8 %all-to-all-start.2 = ((f32[16,1,2,16,128]{4,3,2,1,0:T(8,128)}), f32[16,1,2,16,128]{4,3,2,1,0:T(8,128)S(1)}, u32[]{:S(2)}, u32[]{:S(2)}) async-start(f32[16,1,2,16,128]{4,3,2,1,0:T(8,128)} %shard_map.121), calls=%async_computation.2 | async-start | bytes 524288 | tf_op jit(solution)/shard_map/all_to_all | solution.py:404
  75.2 25.3 %copy-start.6 = (bf16[2,128,256]{2,1,0:T(8,128)(2,1)}, bf16[2,128,256]{2,1,0:T(8,128)(2,1)S(1)}, u32[]{:S(2)}) copy-start(bf16[2,128,256]{2,1,0:T(8,128)(2,1)S(1)} %collective-permute-done.1.refs_2_) | copy-start | bytes 393220
  75.2 32.2 %collective-permute-start.6 = (bf16[256,1024]{1,0:T(8,128)(2,1)}, bf16[256,1024]{1,0:T(8,128)(2,1)}, u32[]{:S(2)}, u32[]{:S(2)}) collective-permute-start(bf16[256,1024]{1,0:T(8,128)(2,1)} %refs_5_.1), channel_id=1, source_target_pairs={{0,24},{2,26},{4,28},{6,30},{8,0},{10,2},{12,4},{14,6},{16,8},{18,... | collective-permute-start | bytes 1572872 | tf_op jit(solution)/shard_map/ppermute | solution.py:365
  75.8 24.7 %copy-start.8 = (bf16[2,128,256]{2,1,0:T(8,128)(2,1)}, bf16[2,128,256]{2,1,0:T(8,128)(2,1)S(1)}, u32[]{:S(2)}) copy-start(bf16[2,128,256]{2,1,0:T(8,128)(2,1)S(1)} %collective-permute-done.2.refs_3_) | copy-start | bytes 393220
  75.8 24.7 %copy-start.10 = (bf16[2,128,256]{2,1,0:T(8,128)(2,1)}, bf16[2,128,256]{2,1,0:T(8,128)(2,1)S(1)}, u32[]{:S(2)}) copy-start(bf16[2,128,256]{2,1,0:T(8,128)(2,1)S(1)} %collective-permute-done.refs_1_) | copy-start | bytes 393220
  77.7 29.7 %collective-permute-start.3 = (bf16[4,2,128,256]{3,2,1,0:T(8,128)(2,1)}, bf16[4,2,128,256]{3,2,1,0:T(8,128)(2,1)}, u32[]{:S(2)}, u32[]{:S(2)}) collective-permute-start(bf16[4,2,128,256]{3,2,1,0:T(8,128)(2,1)} %pad_maximum_fusion), channel_id=1, source_target_pairs={{0,1},{1,0},{2,3},{3,2},{4,5},{5,4},{6,7},{7,6},{8,9},{9,8},{10,11... | collective-permute-start | bytes 1572872 | tf_op jit(solution)/shard_map/ppermute | solution.py:273
  100.5 1.2 copy-start.3
  101.7 5.7 %copy-start.5 = (bf16[256,1024]{1,0:T(8,128)(2,1)S(1)}, bf16[256,1024]{1,0:T(8,128)(2,1)}, u32[]{:S(2)}) copy-start(bf16[256,1024]{1,0:T(8,128)(2,1)} %refs_5_.1) | copy-start | bytes 1572868
  101.7 5.7 %copy-start.7 = (bf16[2,128,256]{2,1,0:T(8,128)(2,1)S(1)}, bf16[2,128,256]{2,1,0:T(8,128)(2,1)}, u32[]{:S(2)}) copy-start(bf16[2,128,256]{2,1,0:T(8,128)(2,1)} %copy-done.6) | copy-start | bytes 393220
  101.7 5.7 %copy-start.9 = (bf16[2,128,256]{2,1,0:T(8,128)(2,1)S(1)}, bf16[2,128,256]{2,1,0:T(8,128)(2,1)}, u32[]{:S(2)}) copy-start(bf16[2,128,256]{2,1,0:T(8,128)(2,1)} %copy-done.8) | copy-start | bytes 393220
  101.7 5.7 %copy-start.11 = (bf16[2,128,256]{2,1,0:T(8,128)(2,1)S(1)}, bf16[2,128,256]{2,1,0:T(8,128)(2,1)}, u32[]{:S(2)}) copy-start(bf16[2,128,256]{2,1,0:T(8,128)(2,1)} %copy-done.10) | copy-start | bytes 393220
  107.2 7.2 %collective-permute-start.10 = (bf16[128,2048]{1,0:T(8,128)(2,1)S(1)}, bf16[128,2048]{1,0:T(8,128)(2,1)}, u32[]{:S(2)}, u32[]{:S(2)}) collective-permute-start(bf16[128,2048]{1,0:T(8,128)(2,1)S(1)} %shard_map.122.refs_0_), channel_id=1, source_target_pairs={{0,1},{1,0},{2,3},{3,2},{4,5},{5,4},{6,7},{7,6},{8,9},{9,8},{10,11... | collective-permute-start | bytes 1572872 | tf_op jit(solution)/shard_map/ppermute | solution.py:273
  107.4 7.0 %copy-start.17 = (f32[4096]{0:T(1024)S(1)}, f32[4096]{0:T(1024)}, u32[]{:S(2)}) copy-start(f32[4096]{0:T(1024)} %param.20) | copy-start | bytes 49156
  107.4 7.1 %copy-start.16 = (f32[4,128]{1,0:T(4,128)S(1)}, f32[4,128]{1,0:T(4,128)}, u32[]{:S(2)}) copy-start(f32[4,128]{1,0:T(4,128)} %refs_4_.1) | copy-start | bytes 6148
  111.3 9.3 %collective-permute-start.7 = (bf16[128,1024]{1,0:T(8,128)(2,1)}, bf16[128,1024]{1,0:T(8,128)(2,1)S(1)}, u32[]{:S(2)}, u32[]{:S(2)}) collective-permute-start(bf16[128,1024]{1,0:T(8,128)(2,1)} %get-tuple-element.25), channel_id=1, source_target_pairs={{0,6},{2,0},{4,2},{6,4},{8,14},{10,8},{12,10},{14,12},{16,22},{18,... | collective-permute-start | bytes 786440 | tf_op jit(solution)/shard_map/ppermute | solution.py:273
  113.1 14.2 %collective-permute-start.8 = (bf16[128,1024]{1,0:T(8,128)(2,1)}, bf16[128,1024]{1,0:T(8,128)(2,1)S(1)}, u32[]{:S(2)}, u32[]{:S(2)}) collective-permute-start(bf16[128,1024]{1,0:T(8,128)(2,1)} %get-tuple-element.24), channel_id=1, source_target_pairs={{0,4},{2,6},{4,0},{6,2},{8,12},{10,14},{12,8},{14,10},{16,20},{18,... | collective-permute-start | bytes 786440 | tf_op jit(solution)/shard_map/ppermute | solution.py:273
  113.3 14.1 %collective-permute-start.9 = (bf16[128,1024]{1,0:T(8,128)(2,1)}, bf16[128,1024]{1,0:T(8,128)(2,1)}, u32[]{:S(2)}, u32[]{:S(2)}) collective-permute-start(bf16[128,1024]{1,0:T(8,128)(2,1)} %get-tuple-element.23), channel_id=1, source_target_pairs={{0,2},{2,4},{4,6},{6,0},{8,10},{10,12},{12,14},{14,8},{16,18},{18,... | collective-permute-start | bytes 786440 | tf_op jit(solution)/shard_map/ppermute | solution.py:273
  114.5 1.2 copy-start.4
Sparse Core Ops, SparseCore 0:
  19.7 75.2 all-gather.1

commit v3 on v2

--- a/solution.py
+++ b/solution.py
@@ -278,45 +278,50 @@
     return [along(block, axis, k, count) for k in range(1, count)]
 
 
-def part_kernel(members, tp, at_ref, *refs):
-    *refs, own_ref, sent_ref, row_ref = refs
-    near, far, weights = refs[:members], refs[members : members + tp - 1], refs[members + tp - 1 :]
-    subs, length, _ = near[0].shape
-    parts = len(weights)
-    half, layer = at_ref[0], at_ref[1]
+def part_kernel(members, tp, half_ref, *refs):
+    *refs, weight_ref, own_ref, sent_ref, row_ref = refs
+    near, far = refs[:members], refs[members:]
+    subs, length, depth = near[0].shape
     for away in range(tp):
-        other = lax.rem(half + tp - away, tp)
+        other = lax.rem(half_ref[0] + tp - away, tp)
         for sub in range(subs):
-            slot = lax.rem(layer + parts - (other * subs + sub), parts)
             for k in range(members):
                 block = far[away - 1][k, sub] if away else near[k][sub]
-                row_ref[slot, k * length : (k + 1) * length, :] = block
+                row_ref[other * subs + sub, k * length : (k + 1) * length, :] = block
     for k in range(members):
         here = slice(k * length, (k + 1) * length)
-        total = mm(row_ref[0, here, :], weights[0][...])
-        for slot in range(1, parts):
-            total = total + mm(row_ref[slot, here, :], weights[slot][...])
+        total = mm(row_ref[0, here, :], weight_ref[:depth, :])
+        for slot in range(1, row_ref.shape[0]):
+            total = total + mm(row_ref[slot, here, :], weight_ref[slot * depth : (slot + 1) * depth, :])
         if k == 0:
             own_ref[...] = total
         else:
             sent_ref[k - 1] = total.astype(bf16)
 
 
-def probability_kernel(head, me_ref, *refs):
-    *mixed_refs, gain_ref, weight_ref, affine_ref, out_ref = refs
+def probability_kernel(members, at_ref, *refs):
+    *refs, gain_ref, affine_ref, out_ref, row_ref = refs
+    weights, mixed_refs = refs[:members], refs[members:]
     tp = len(mixed_refs)
+    layers, depth, head = weights[0].shape
     length, channels = mixed_refs[0].shape
+    half, member, layer = at_ref[0], at_ref[1], at_ref[2]
     square = jnp.zeros((length, 1), f32)
     for ref in mixed_refs:
         value = ref[...].astype(f32)
         square = square + jnp.sum(value * value, axis=1, keepdims=True)
     scale = lax.rsqrt(square / (channels * tp) + 1e-06)
+    blocks = channels // depth
+    for k, ref in enumerate(mixed_refs):
+        at = lax.rem(half + tp - k, tp)
+        normed = (ref[...].astype(f32) * scale * gain_ref[pl.ds(at, 1), :]).astype(bf16)
+        for block in range(blocks):
+            row_ref[at * blocks + block] = normed[:, block * depth : (block + 1) * depth]
     z_total = jnp.zeros((length, head), f32)
-    for k, ref in enumerate(mixed_refs):
-        at = lax.rem(me_ref[0] + tp - k, tp)
-        normed = (ref[...].astype(f32) * scale * gain_ref[pl.ds(at, 1), :]).astype(bf16)
-        rows = pl.ds(pl.multiple_of(at * channels, channels), channels)
-        z_total = z_total + mm(normed, weight_ref[rows, :])
+    for m in range(members):
+        for k in range(layers):
+            block = lax.rem(layer + layers - k, layers) * members + lax.rem(member + members - m, members)
+            z_total = z_total + mm(row_ref[block], weights[m][k])
     affine = affine_ref[...]
     queries = (z_total * affine[0:1] + affine[1:2]).astype(bf16)
     key_rows = (z_total * affine[2:3] + affine[3:4]).astype(bf16)
@@ -352,7 +357,6 @@
     width = -(-(channels // GROUP) // LANES) * LANES
     place = lax.axis_index("ctx")
     peers = lax.axis_size("ctx")
-    head = z_weight.shape[1]
     tp, half = lax.axis_size("tp"), lax.axis_index("tp")
     depth, columns = v_weight.shape
     blocks = channels // depth
@@ -360,14 +364,22 @@
     layers = peers // members
     shape = jax.ShapeDtypeStruct
 
-    all_z = lax.all_gather(z_weight, "ctx", axis=0, tiled=True)
-    layer_pairs = [[(i, (i + members * k) % peers) for i in range(peers)] for k in range(layers)]
-    all_v = [v_weight] + [lax.ppermute(v_weight, "ctx", layer_pairs[k]) for k in range(1, layers)]
+    member, layer = place % members, place // members
+    lines = [[r + members * k for k in range(layers)] for r in range(members)]
+    all_v = lax.all_gather(v_weight, "ctx", axis=0, tiled=True, axis_index_groups=lines)
+    line_z = [z_weight] + [
+        lax.ppermute(z_weight, "ctx", [(i, (i + members * k) % peers) for i in range(peers)])
+        for k in range(1, layers)
+    ]
+    line_z = jnp.stack(line_z)
 
     csum, csq, totals = call(
         sums_kernel, [shape((length, width), f32), shape((length, width), f32), shape((2, width), f32)]
     )(tokens)
     sums = lax.all_to_all(jnp.broadcast_to(totals[None], (peers, 2, width)), "ctx", 0, 0)
+
+    sums, line_z = lax.optimization_barrier((sums, line_z))
+    all_z = [line_z] + [along(line_z, "ctx", k, members) for k in range(1, members)]
 
     def dense(a):
         return a.reshape(NDIM, tiles, LANES)
@@ -422,13 +434,24 @@
         [shape((length, columns), f32), shape((max(members - 1, 1), length, columns), bf16)],
         [pltpu.VMEM((layers, members * length, depth), bf16)],
         True,
-        members + tp + layers,
-    )(jnp.stack([half, place // members]).astype(jnp.int32), *near, *far, *all_v)
+        members + tp + 1,
+    )(half.astype(jnp.int32).reshape(1), *near, *far, all_v)
     returned = [along(sent[k - 1], "ctx", -k, members) for k in range(1, members)]
 
     probabilities = call(
-        functools.partial(probability_kernel, head), shape((length, STRETCH), bf16), (), True, tp + 4
-    )(half.astype(jnp.int32).reshape(1), mixed_rows, *others(mixed_rows, "tp"), rms_gain.reshape(tp, channels), all_z, qk_affine)
+        functools.partial(probability_kernel, members),
+        shape((length, STRETCH), bf16),
+        [pltpu.VMEM((tp * blocks, length, depth), bf16)],
+        True,
+        members + tp + 3,
+    )(
+        jnp.stack([half, member, layer]).astype(jnp.int32),
+        *all_z,
+        mixed_rows,
+        *others(mixed_rows, "tp"),
+        rms_gain.reshape(tp, channels),
+        qk_affine,
+    )
     return call(attend_kernel, shape((length, columns), bf16), n_in=members + 1)(own, *returned, probabilities)
 
 

time: 137 us -> 113 us (0.82)
  the two profiles are of different devices: /device:TPU:20 before, /device:TPU:0 now
where the time goes in v3:
time: 113 us; the launch traced here: 112 us
  starting transfers between devices  41.2 us (36%)
  waiting for transfers between devices  22.2 us (20%)
  Pallas kernels  17.6 us (16%)
  between operations  13.6 us (12%)
  local copies, waits for them, and re-layouts  12 us (11%)
  other arithmetic  5.17 us (5%)
    ppermute x11, starting transfers between devices, along(): return lax.ppermute(block, axis, pairs)  21 us
    unnamed x41, local copies, waits for them, and re-layouts  9.77 us
    ppermute x11, waiting for transfers between devices, along(): return lax.ppermute(block, axis, pairs)  7.25 us
    ppermute x3, starting transfers between devices, body(): lax.ppermute(z_weight, 'ctx', [(i, (i + members * k) % peers) for i in ra...  7.01 us
    all_to_all x1, waiting for transfers between devices, body(): incoming = join(lax.all_to_all(starts, 'ctx', 0, 0))  5.78 us
    all_to_all x1, starting transfers between devices, body(): incoming = join(lax.all_to_all(starts, 'ctx', 0, 0))  5.71 us
    pallas_call x1, Pallas kernels, body(): call(mix_kernel, shape((length, channels), bf16), [pltpu.VMEM((chunks, ND...  5.45 us
    all_to_all x1, waiting for transfers between devices, body(): lax.all_to_all(jnp.broadcast_to(totals[None], (peers, 2, width)), 'ctx',...  5.12 us
  transfers between devices with their start and end apart: 18, of which 7 were waited for; matrix products, arithmetic and copies ran while one was open for 7% of the time, Pallas kernels for 15%

profile of v3, /device:TPU:0, one launch (start us, length us, event | category | flops | bytes accessed | tf_op | source)
XLA Modules:
  0.0 111.8 jit_solution(18304329399546630296)
XLA Ops:
  6.5 0.7 all-gather.2.cloned.1.call-update
  7.3 3.1 %collective-permute-start = (bf16[256,128]{1,0:T(8,128)(2,1)}, bf16[256,128]{1,0:T(8,128)(2,1)S(1)}, u32[]{:S(2)}, u32[]{:S(2)}) collective-permute-start(bf16[256,128]{1,0:T(8,128)(2,1)} %param.21), channel_id=1, source_target_pairs={{0,8},{2,10},{4,12},{6,14},{8,16},{10,18},{12,20},{14,22},{16,24},... | collective-permute-start | bytes 196616 | tf_op jit(solution)/shard_map/ppermute | solution.py:371
  10.3 2.6 %collective-permute-start.1 = (bf16[256,128]{1,0:T(8,128)(2,1)}, bf16[256,128]{1,0:T(8,128)(2,1)S(1)}, u32[]{:S(2)}, u32[]{:S(2)}) collective-permute-start(bf16[256,128]{1,0:T(8,128)(2,1)} %param.21), channel_id=1, source_target_pairs={{0,16},{2,18},{4,20},{6,22},{8,24},{10,26},{12,28},{14,30},{16,0},... | collective-permute-start | bytes 196616 | tf_op jit(solution)/shard_map/ppermute | solution.py:371
  12.9 1.3 %collective-permute-start.2 = (bf16[256,128]{1,0:T(8,128)(2,1)}, bf16[256,128]{1,0:T(8,128)(2,1)S(1)}, u32[]{:S(2)}, u32[]{:S(2)}) collective-permute-start(bf16[256,128]{1,0:T(8,128)(2,1)} %param.21), channel_id=1, source_target_pairs={{0,24},{2,26},{4,28},{6,30},{8,0},{10,2},{12,4},{14,6},{16,8},{18,... | collective-permute-start | bytes 196616 | tf_op jit(solution)/shard_map/ppermute | solution.py:371
  14.3 1.0 copy-done
  15.3 0.8 shard_map.118
  16.1 0.6 broadcast_in_dim.12
  16.8 3.9 %all-to-all-start = ((f32[16,2,128]{2,1,0:T(2,128)}), f32[16,2,128]{2,1,0:T(2,128)S(1)}, u32[]{:S(2)}, u32[]{:S(2)}) async-start(f32[16,2,128]{2,1,0:T(2,128)} %broadcast_in_dim.12), calls=%async_computation | async-start | bytes 32768 | tf_op jit(solution)/shard_map/all_to_all | solution.py:379
  20.7 1.4 %multiply_bitcast_fusion = (f32[2,8,16,128]{3,1,2,0:T(8,128)S(1)}, f32[2,8,16,128]{3,1,2,0:T(8,128)S(1)}) fusion(f32[16,2048]{1,0:T(8,128)} %param.15, f32[16,2048]{1,0:T(8,128)} %param.16), kind=kLoop, calls=%fused_computation.13 | loop fusion | flops 65536 | bytes 524288
  22.3 0.8 pad_maximum_fusion.1.refs_0_
  23.1 5.1 %all-to-all-done.sums_ref = f32[16,2,128]{2,1,0:T(2,128)S(1)} async-done(((f32[16,2,128]{2,1,0:T(2,128)}), f32[16,2,128]{2,1,0:T(2,128)S(1)}, u32[]{:S(2)}, u32[]{:S(2)}) %all-to-all-start) | async-done | bytes 16416 | tf_op jit(solution)/shard_map/all_to_all | solution.py:379
  28.2 0.7 copy-done.12
  28.9 0.7 copy-done.13
  29.6 4.8 %shard_map.119 = (bf16[4,2,128,256]{3,2,1,0:T(8,128)(2,1)S(1)}, f32[2048,128]{1,0:T(8,128)S(1)}, f32[8,16,2,16,128]{4,3,2,1,0:T(8,128)S(1)}, f32[16,2,16,128]{3,2,1,0:T(8,128)S(1)}) custom-call(s32[1]{0:T(128)} %bitcast.1.me_ref, bf16[128,2048]{1,0:T(8,128)(2,1)S(1)} %copy-done.1, f32[16,2,128]{2,1,0:T(2,128)S(1)} %all-to-all-done.sums_ref, ...), custom_call_target="tpu_custom_call" | custom-call | tf_op jit(solution)/shard_map/pallas_call | solution.py:390
  34.4 1.0 copy-done.3
  35.4 0.7 copy-done.11
  36.1 3.5 %all-to-all-start.1 = ((f32[16,1,2,16,128]{4,3,2,1,0:T(8,128)}), f32[16,1,2,16,128]{4,3,2,1,0:T(8,128)S(1)}, u32[]{:S(2)}, u32[]{:S(2)}) async-start(f32[16,1,2,16,128]{4,3,2,1,0:T(8,128)} %bitcast.58), calls=%async_computation.1 | async-start | bytes 524288 | tf_op jit(solution)/shard_map/all_to_all | solution.py:413
  39.6 0.9 fusion.2
  40.5 1.8 %collective-permute-start.3 = (bf16[2,128,256]{2,1,0:T(8,128)(2,1)}, bf16[2,128,256]{2,1,0:T(8,128)(2,1)S(1)}, u32[]{:S(2)}, u32[]{:S(2)}) collective-permute-start(bf16[2,128,256]{2,1,0:T(8,128)(2,1)} %get-tuple-element.34), channel_id=1, source_target_pairs={{0,2},{2,4},{4,6},{6,0},{8,10},{10,12},{12,14},{14,8},{16,18},{18,... | collective-permute-start | bytes 393224 | tf_op jit(solution)/shard_map/ppermute | solution.py:273
  42.3 1.5 %collective-permute-start.4 = (bf16[2,128,256]{2,1,0:T(8,128)(2,1)}, bf16[2,128,256]{2,1,0:T(8,128)(2,1)S(1)}, u32[]{:S(2)}, u32[]{:S(2)}) collective-permute-start(bf16[2,128,256]{2,1,0:T(8,128)(2,1)} %get-tuple-element.33), channel_id=1, source_target_pairs={{0,4},{2,6},{4,0},{6,2},{8,12},{10,14},{12,8},{14,10},{16,20},{18,... | collective-permute-start | bytes 393224 | tf_op jit(solution)/shard_map/ppermute | solution.py:273
  43.7 1.5 %collective-permute-start.5 = (bf16[2,128,256]{2,1,0:T(8,128)(2,1)}, bf16[2,128,256]{2,1,0:T(8,128)(2,1)S(1)}, u32[]{:S(2)}, u32[]{:S(2)}) collective-permute-start(bf16[2,128,256]{2,1,0:T(8,128)(2,1)} %get-tuple-element.32), channel_id=1, source_target_pairs={{0,6},{2,0},{4,2},{6,4},{8,14},{10,8},{12,10},{14,12},{16,22},{18,... | collective-permute-start | bytes 393224 | tf_op jit(solution)/shard_map/ppermute | solution.py:273
  45.2 1.9 %collective-permute-done.3.refs_1_ = bf16[2,128,256]{2,1,0:T(8,128)(2,1)S(1)} collective-permute-done((bf16[2,128,256]{2,1,0:T(8,128)(2,1)}, bf16[2,128,256]{2,1,0:T(8,128)(2,1)S(1)}, u32[]{:S(2)}, u32[]{:S(2)}) %collective-permute-start.3) | collective-permute-done | bytes 131104 | tf_op jit(solution)/shard_map/ppermute | solution.py:273
  47.1 1.7 %collective-permute-done.4.refs_2_ = bf16[2,128,256]{2,1,0:T(8,128)(2,1)S(1)} collective-permute-done((bf16[2,128,256]{2,1,0:T(8,128)(2,1)}, bf16[2,128,256]{2,1,0:T(8,128)(2,1)S(1)}, u32[]{:S(2)}, u32[]{:S(2)}) %collective-permute-start.4) | collective-permute-done | bytes 131104 | tf_op jit(solution)/shard_map/ppermute | solution.py:273
  48.9 0.5 collective-permute-done.5.refs_3_
  49.3 1.8 %pad_maximum_fusion = bf16[4,2,128,256]{3,2,1,0:T(8,128)(2,1)} fusion(bf16[1,2,128,256]{3,2,1,0:T(8,128)(2,1)S(1)} %bitcast.57, bf16[1,2,128,256]{3,2,1,0:T(8,128)(2,1)S(1)} %bitcast.56, bf16[1,2,128,256]{3,2,1,0:T(8,128)(2,1)S(1)} %bitcast.55, bf16[1,2,128,256]{3,2,1,0:T(8,128)(2,1)} %get-tuple-element.30), kind=kLoop, calls=%fused_computation | loop fusion | flops 786432 | bytes 1048576 | tf_op jit(solution)/shard_map/stack | solution.py:431
  51.1 3.3 %all-to-all-done.1.ends_ref = f32[16,1,2,16,128]{4,3,2,1,0:T(8,128)S(1)} async-done(((f32[16,1,2,16,128]{4,3,2,1,0:T(8,128)}), f32[16,1,2,16,128]{4,3,2,1,0:T(8,128)S(1)}, u32[]{:S(2)}, u32[]{:S(2)}) %all-to-all-start.1) | async-done | bytes 262176 | tf_op jit(solution)/shard_map/all_to_all | solution.py:413
  54.5 0.8 shard_map.121
  55.3 5.7 %all-to-all-start.2 = ((f32[16,1,2,16,128]{4,3,2,1,0:T(8,128)}), f32[16,1,2,16,128]{4,3,2,1,0:T(8,128)S(1)}, u32[]{:S(2)}, u32[]{:S(2)}) async-start(f32[16,1,2,16,128]{4,3,2,1,0:T(8,128)} %shard_map.121), calls=%async_computation.2 | async-start | bytes 524288 | tf_op jit(solution)/shard_map/all_to_all | solution.py:416
  61.0 1.1 fusion.1
  62.1 2.0 %collective-permute-start.10 = (bf16[4,256,128]{2,1,0:T(8,128)(2,1)}, bf16[4,256,128]{2,1,0:T(8,128)(2,1)}, u32[]{:S(2)}, u32[]{:S(2)}) collective-permute-start(bf16[4,256,128]{2,1,0:T(8,128)(2,1)} %pad_maximum_fusion.1.refs_0_), channel_id=1, source_target_pairs={{0,2},{2,4},{4,6},{6,0},{8,10},{10,12},{12,14},{14,8},{16,18},{18,... | collective-permute-start | bytes 786440 | tf_op jit(solution)/shard_map/ppermute | solution.py:273
  64.1 5.8 %all-to-all-done.2 = f32[16,1,2,16,128]{4,3,2,1,0:T(8,128)S(1)} async-done(((f32[16,1,2,16,128]{4,3,2,1,0:T(8,128)}), f32[16,1,2,16,128]{4,3,2,1,0:T(8,128)S(1)}, u32[]{:S(2)}, u32[]{:S(2)}) %all-to-all-start.2) | async-done | bytes 262176 | tf_op jit(solution)/shard_map/all_to_all | solution.py:416
  69.9 1.2 %copy-done.4 = f32[2048,128]{1,0:T(8,128)S(1)} copy-done((f32[2048,128]{1,0:T(8,128)S(1)}, f32[2048,128]{1,0:T(8,128)}, u32[]{:S(2)}) %copy-start.4) | copy-done | bytes 1048600
  71.1 5.4 %shard_map.122.refs_4_ = bf16[128,2048]{1,0:T(8,128)(2,1)S(1)} custom-call(f32[16,2,16,128]{3,2,1,0:T(8,128)S(1)} %bitcast.54, f32[8,16,2,16,128]{4,3,2,1,0:T(8,128)S(1)} %get-tuple-element.25.fresh_ref, f32[2048,128]{1,0:T(8,128)S(1)} %copy-done.4, f32[16,2,16,128]{3,2,1,0:T(8,128)S(1)} %constant_dynamic-update-slice_fusion.q_ref, ...), custom_call_target="tpu_custom_call" | custom-call | tf_op jit(solution)/shard_map/pallas_call | solution.py:418
  76.7 1.0 collective-permute-start.11
  77.6 1.6 %collective-permute-start.12 = (bf16[4,256,128]{2,1,0:T(8,128)(2,1)}, bf16[4,256,128]{2,1,0:T(8,128)(2,1)S(1)}, u32[]{:S(2)}, u32[]{:S(2)}) collective-permute-start(bf16[4,256,128]{2,1,0:T(8,128)(2,1)} %pad_maximum_fusion.1.refs_0_), channel_id=1, source_target_pairs={{0,6},{2,0},{4,2},{6,4},{8,14},{10,8},{12,10},{14,12},{16,22},{18,... | collective-permute-start | bytes 786440 | tf_op jit(solution)/shard_map/ppermute | solution.py:273
  79.2 1.6 %copy-done.2 = bf16[1024,1024]{1,0:T(8,128)(2,1)S(1)} copy-done((bf16[1024,1024]{1,0:T(8,128)(2,1)S(1)}, bf16[1024,1024]{1,0:T(8,128)(2,1)}, u32[]{:S(2)}) %copy-start.2) | copy-done | bytes 2097176
  80.8 0.9 copy-done.6
  81.7 0.9 copy-done.8
  82.6 0.9 copy-done.10
  83.5 2.4 %shard_map.120 = (f32[128,1024]{1,0:T(8,128)S(1)}, bf16[3,128,1024]{2,1,0:T(8,128)(2,1)S(1)}) custom-call(s32[1]{0:T(128)} %bitcast.half_ref, bf16[2,128,256]{2,1,0:T(8,128)(2,1)S(1)} %get-tuple-element.31.refs_0_, bf16[2,128,256]{2,1,0:T(8,128)(2,1)S(1)} %copy-done.6, bf16[2,128,256]{2,1,0:T(8,128)(2,1)S(1)} %copy-done.8, ...), custom_call_target="tpu_custom_call" | custom-call | tf_op jit(solution)/shard_map/pallas_call | solution.py:432
  85.9 0.8 slice_bitcast_fusion
  86.7 1.0 collective-permute-start.7
  87.7 0.9 collective-permute-start.8
  88.6 9.7 %collective-permute-start.9 = (bf16[128,1024]{1,0:T(8,128)(2,1)S(1)}, bf16[128,1024]{1,0:T(8,128)(2,1)S(1)}, u32[]{:S(2)}, u32[]{:S(2)}) collective-permute-start(bf16[128,1024]{1,0:T(8,128)(2,1)S(1)} %get-tuple-element.27), channel_id=1, source_target_pairs={{0,2},{2,4},{4,6},{6,0},{8,10},{10,12},{12,14},{14,8},{16,18},{18,... | collective-permute-start | bytes 786440 | tf_op jit(solution)/shard_map/ppermute | solution.py:273
  98.3 0.1 pad_add_fusion.at_ref
  98.4 2.3 %shard_map.123.refs_3_ = bf16[128,128]{1,0:T(8,128)(2,1)S(1)} custom-call(s32[3]{0:T(128)S(1)} %pad_add_fusion.at_ref, bf16[4,256,128]{2,1,0:T(8,128)(2,1)} %pad_maximum_fusion.1.refs_0_, bf16[4,256,128]{2,1,0:T(8,128)(2,1)} %collective-permute-done.10.refs_1_, bf16[4,256,128]{2,1,0:T(8,128)(2,1)S(1)} %collective-permute-done.11.refs_2_, ...), custom_call_target="tpu_custom_call" | custom-call | tf_op jit(solution)/shard_map/pallas_call | solution.py:441
  100.7 3.1 %collective-permute-done.9.refs_2_ = bf16[128,1024]{1,0:T(8,128)(2,1)S(1)} collective-permute-done((bf16[128,1024]{1,0:T(8,128)(2,1)S(1)}, bf16[128,1024]{1,0:T(8,128)(2,1)S(1)}, u32[]{:S(2)}, u32[]{:S(2)}) %collective-permute-start.9) | collective-permute-done | bytes 262176 | tf_op jit(solution)/shard_map/ppermute | solution.py:273
  103.9 1.1 shard_map.124
  (49 shorter events, 0.3 us)
Async XLA Ops:
  6.5 21.7 %copy-start.1 = (bf16[128,2048]{1,0:T(8,128)(2,1)S(1)}, bf16[128,2048]{1,0:T(8,128)(2,1)}, u32[]{:S(2)}) copy-start(bf16[128,2048]{1,0:T(8,128)(2,1)} %x_ref.3) | copy-start | bytes 1572868
  6.5 72.7 %all-gather.2.cloned.1.call-start = ((), (), s32[]{:S(2)}) async-start(), calls=%async_computation.3 | async-start | bytes 2621440 | tf_op jit(solution)/shard_map/all_gather | solution.py:369
  7.3 15.0 %collective-permute-start = (bf16[256,128]{1,0:T(8,128)(2,1)}, bf16[256,128]{1,0:T(8,128)(2,1)S(1)}, u32[]{:S(2)}, u32[]{:S(2)}) collective-permute-start(bf16[256,128]{1,0:T(8,128)(2,1)} %param.21), channel_id=1, source_target_pairs={{0,8},{2,10},{4,12},{6,14},{8,16},{10,18},{12,20},{14,22},{16,24},... | collective-permute-start | bytes 196616 | tf_op jit(solution)/shard_map/ppermute | solution.py:371
  10.3 12.0 %collective-permute-start.1 = (bf16[256,128]{1,0:T(8,128)(2,1)}, bf16[256,128]{1,0:T(8,128)(2,1)S(1)}, u32[]{:S(2)}, u32[]{:S(2)}) collective-permute-start(bf16[256,128]{1,0:T(8,128)(2,1)} %param.21), channel_id=1, source_target_pairs={{0,16},{2,18},{4,20},{6,22},{8,24},{10,26},{12,28},{14,30},{16,0},... | collective-permute-start | bytes 196616 | tf_op jit(solution)/shard_map/ppermute | solution.py:371
  12.9 9.4 %collective-permute-start.2 = (bf16[256,128]{1,0:T(8,128)(2,1)}, bf16[256,128]{1,0:T(8,128)(2,1)S(1)}, u32[]{:S(2)}, u32[]{:S(2)}) collective-permute-start(bf16[256,128]{1,0:T(8,128)(2,1)} %param.21), channel_id=1, source_target_pairs={{0,24},{2,26},{4,28},{6,30},{8,0},{10,2},{12,4},{14,6},{16,8},{18,... | collective-permute-start | bytes 196616 | tf_op jit(solution)/shard_map/ppermute | solution.py:371
  14.3 1.0 copy-start
  15.3 7.0 %copy-start.16 = (bf16[256,128]{1,0:T(8,128)(2,1)S(1)}, bf16[256,128]{1,0:T(8,128)(2,1)}, u32[]{:S(2)}) copy-start(bf16[256,128]{1,0:T(8,128)(2,1)} %param.21) | copy-start | bytes 196612
  16.8 11.4 %all-to-all-start = ((f32[16,2,128]{2,1,0:T(2,128)}), f32[16,2,128]{2,1,0:T(2,128)S(1)}, u32[]{:S(2)}, u32[]{:S(2)}) async-start(f32[16,2,128]{2,1,0:T(2,128)} %broadcast_in_dim.12), calls=%async_computation | async-start | bytes 32768 | tf_op jit(solution)/shard_map/all_to_all | solution.py:379
  28.2 0.7 copy-start.12
  28.9 0.7 copy-start.13
  34.4 1.0 copy-start.3
  35.4 0.7 copy-start.11
  36.1 18.4 %all-to-all-start.1 = ((f32[16,1,2,16,128]{4,3,2,1,0:T(8,128)}), f32[16,1,2,16,128]{4,3,2,1,0:T(8,128)S(1)}, u32[]{:S(2)}, u32[]{:S(2)}) async-start(f32[16,1,2,16,128]{4,3,2,1,0:T(8,128)} %bitcast.58), calls=%async_computation.1 | async-start | bytes 524288 | tf_op jit(solution)/shard_map/all_to_all | solution.py:413
  40.5 29.4 %copy-start.14 = (f32[2048]{0:T(1024)S(1)}, f32[2048]{0:T(1024)}, u32[]{:S(2)}) copy-start(f32[2048]{0:T(1024)} %param.19) | copy-start | bytes 24580
  40.5 6.6 %collective-permute-start.3 = (bf16[2,128,256]{2,1,0:T(8,128)(2,1)}, bf16[2,128,256]{2,1,0:T(8,128)(2,1)S(1)}, u32[]{:S(2)}, u32[]{:S(2)}) collective-permute-start(bf16[2,128,256]{2,1,0:T(8,128)(2,1)} %get-tuple-element.34), channel_id=1, source_target_pairs={{0,2},{2,4},{4,6},{6,0},{8,10},{10,12},{12,14},{14,8},{16,18},{18,... | collective-permute-start | bytes 393224 | tf_op jit(solution)/shard_map/ppermute | solution.py:273
  42.3 6.6 %collective-permute-start.4 = (bf16[2,128,256]{2,1,0:T(8,128)(2,1)}, bf16[2,128,256]{2,1,0:T(8,128)(2,1)S(1)}, u32[]{:S(2)}, u32[]{:S(2)}) collective-permute-start(bf16[2,128,256]{2,1,0:T(8,128)(2,1)} %get-tuple-element.33), channel_id=1, source_target_pairs={{0,4},{2,6},{4,0},{6,2},{8,12},{10,14},{12,8},{14,10},{16,20},{18,... | collective-permute-start | bytes 393224 | tf_op jit(solution)/shard_map/ppermute | solution.py:273
  43.7 5.6 %collective-permute-start.5 = (bf16[2,128,256]{2,1,0:T(8,128)(2,1)}, bf16[2,128,256]{2,1,0:T(8,128)(2,1)S(1)}, u32[]{:S(2)}, u32[]{:S(2)}) collective-permute-start(bf16[2,128,256]{2,1,0:T(8,128)(2,1)} %get-tuple-element.32), channel_id=1, source_target_pairs={{0,6},{2,0},{4,2},{6,4},{8,14},{10,8},{12,10},{14,12},{16,22},{18,... | collective-permute-start | bytes 393224 | tf_op jit(solution)/shard_map/ppermute | solution.py:273
  47.1 22.8 %copy-start.5 = (bf16[2,128,256]{2,1,0:T(8,128)(2,1)}, bf16[2,128,256]{2,1,0:T(8,128)(2,1)S(1)}, u32[]{:S(2)}) copy-start(bf16[2,128,256]{2,1,0:T(8,128)(2,1)S(1)} %collective-permute-done.3.refs_1_) | copy-start | bytes 393220
  48.9 21.0 %copy-start.7 = (bf16[2,128,256]{2,1,0:T(8,128)(2,1)}, bf16[2,128,256]{2,1,0:T(8,128)(2,1)S(1)}, u32[]{:S(2)}) copy-start(bf16[2,128,256]{2,1,0:T(8,128)(2,1)S(1)} %collective-permute-done.4.refs_2_) | copy-start | bytes 393220
  49.3 5.9 %copy-start.9 = (bf16[2,128,256]{2,1,0:T(8,128)(2,1)}, bf16[2,128,256]{2,1,0:T(8,128)(2,1)S(1)}, u32[]{:S(2)}) copy-start(bf16[2,128,256]{2,1,0:T(8,128)(2,1)S(1)} %collective-permute-done.5.refs_3_) | copy-start | bytes 393220
  51.1 28.1 %collective-permute-start.6 = (bf16[4,2,128,256]{3,2,1,0:T(8,128)(2,1)}, bf16[4,2,128,256]{3,2,1,0:T(8,128)(2,1)}, u32[]{:S(2)}, u32[]{:S(2)}) collective-permute-start(bf16[4,2,128,256]{3,2,1,0:T(8,128)(2,1)} %pad_maximum_fusion), channel_id=1, source_target_pairs={{0,1},{1,0},{2,3},{3,2},{4,5},{5,4},{6,7},{7,6},{8,9},{9,8},{10,11... | collective-permute-start | bytes 1572872 | tf_op jit(solution)/shard_map/ppermute | solution.py:273
  55.3 14.6 %all-to-all-start.2 = ((f32[16,1,2,16,128]{4,3,2,1,0:T(8,128)}), f32[16,1,2,16,128]{4,3,2,1,0:T(8,128)S(1)}, u32[]{:S(2)}, u32[]{:S(2)}) async-start(f32[16,1,2,16,128]{4,3,2,1,0:T(8,128)} %shard_map.121), calls=%async_computation.2 | async-start | bytes 524288 | tf_op jit(solution)/shard_map/all_to_all | solution.py:416
  62.1 25.6 %collective-permute-start.10 = (bf16[4,256,128]{2,1,0:T(8,128)(2,1)}, bf16[4,256,128]{2,1,0:T(8,128)(2,1)}, u32[]{:S(2)}, u32[]{:S(2)}) collective-permute-start(bf16[4,256,128]{2,1,0:T(8,128)(2,1)} %pad_maximum_fusion.1.refs_0_), channel_id=1, source_target_pairs={{0,2},{2,4},{4,6},{6,0},{8,10},{10,12},{12,14},{14,8},{16,18},{18,... | collective-permute-start | bytes 786440 | tf_op jit(solution)/shard_map/ppermute | solution.py:273
  69.9 1.2 %copy-start.4 = (f32[2048,128]{1,0:T(8,128)S(1)}, f32[2048,128]{1,0:T(8,128)}, u32[]{:S(2)}) copy-start(f32[2048,128]{1,0:T(8,128)} %copy-done.3) | copy-start | bytes 3145732
  76.6 21.8 %collective-permute-start.13 = (bf16[128,2048]{1,0:T(8,128)(2,1)S(1)}, bf16[128,2048]{1,0:T(8,128)(2,1)S(1)}, u32[]{:S(2)}, u32[]{:S(2)}) collective-permute-start(bf16[128,2048]{1,0:T(8,128)(2,1)S(1)} %shard_map.122.refs_4_), channel_id=1, source_target_pairs={{0,1},{1,0},{2,3},{3,2},{4,5},{5,4},{6,7},{7,6},{8,9},{9,8},{10,11... | collective-permute-start | bytes 1572872 | tf_op jit(solution)/shard_map/ppermute | solution.py:273
  76.7 11.9 %collective-permute-start.11 = (bf16[4,256,128]{2,1,0:T(8,128)(2,1)}, bf16[4,256,128]{2,1,0:T(8,128)(2,1)S(1)}, u32[]{:S(2)}, u32[]{:S(2)}) collective-permute-start(bf16[4,256,128]{2,1,0:T(8,128)(2,1)} %pad_maximum_fusion.1.refs_0_), channel_id=1, source_target_pairs={{0,4},{2,6},{4,0},{6,2},{8,12},{10,14},{12,8},{14,10},{16,20},{18,... | collective-permute-start | bytes 786440 | tf_op jit(solution)/shard_map/ppermute | solution.py:273
  77.6 20.8 %collective-permute-start.12 = (bf16[4,256,128]{2,1,0:T(8,128)(2,1)}, bf16[4,256,128]{2,1,0:T(8,128)(2,1)S(1)}, u32[]{:S(2)}, u32[]{:S(2)}) collective-permute-start(bf16[4,256,128]{2,1,0:T(8,128)(2,1)} %pad_maximum_fusion.1.refs_0_), channel_id=1, source_target_pairs={{0,6},{2,0},{4,2},{6,4},{8,14},{10,8},{12,10},{14,12},{16,22},{18,... | collective-permute-start | bytes 786440 | tf_op jit(solution)/shard_map/ppermute | solution.py:273
  79.2 1.6 %copy-start.2 = (bf16[1024,1024]{1,0:T(8,128)(2,1)S(1)}, bf16[1024,1024]{1,0:T(8,128)(2,1)}, u32[]{:S(2)}) copy-start(bf16[1024,1024]{1,0:T(8,128)(2,1)} %all-gather.2.cloned.1.call-done.refs_5_) | copy-start | bytes 6291460
  80.8 0.9 copy-start.6
  81.7 0.9 copy-start.8
  82.6 0.9 copy-start.10
  83.5 14.8 %copy-start.17 = (f32[4096]{0:T(1024)S(1)}, f32[4096]{0:T(1024)}, u32[]{:S(2)}) copy-start(f32[4096]{0:T(1024)} %param.20) | copy-start | bytes 49156
  83.5 14.9 %copy-start.15 = (f32[4,128]{1,0:T(4,128)S(1)}, f32[4,128]{1,0:T(4,128)}, u32[]{:S(2)}) copy-start(f32[4,128]{1,0:T(4,128)} %refs_7_.1) | copy-start | bytes 6148
  86.7 14.0 %collective-permute-start.7 = (bf16[128,1024]{1,0:T(8,128)(2,1)}, bf16[128,1024]{1,0:T(8,128)(2,1)S(1)}, u32[]{:S(2)}, u32[]{:S(2)}) collective-permute-start(bf16[128,1024]{1,0:T(8,128)(2,1)} %get-tuple-element.29), channel_id=1, source_target_pairs={{0,6},{2,0},{4,2},{6,4},{8,14},{10,8},{12,10},{14,12},{16,22},{18,... | collective-permute-start | bytes 786440 | tf_op jit(solution)/shard_map/ppermute | solution.py:273
  87.7 13.0 %collective-permute-start.8 = (bf16[128,1024]{1,0:T(8,128)(2,1)S(1)}, bf16[128,1024]{1,0:T(8,128)(2,1)S(1)}, u32[]{:S(2)}, u32[]{:S(2)}) collective-permute-start(bf16[128,1024]{1,0:T(8,128)(2,1)S(1)} %get-tuple-element.28), channel_id=1, source_target_pairs={{0,4},{2,6},{4,0},{6,2},{8,12},{10,14},{12,8},{14,10},{16,20},{18,... | collective-permute-start | bytes 786440 | tf_op jit(solution)/shard_map/ppermute | solution.py:273
  88.6 15.3 %collective-permute-start.9 = (bf16[128,1024]{1,0:T(8,128)(2,1)S(1)}, bf16[128,1024]{1,0:T(8,128)(2,1)S(1)}, u32[]{:S(2)}, u32[]{:S(2)}) collective-permute-start(bf16[128,1024]{1,0:T(8,128)(2,1)S(1)} %get-tuple-element.27), channel_id=1, source_target_pairs={{0,2},{2,4},{4,6},{6,0},{8,10},{10,12},{12,14},{14,8},{16,18},{18,... | collective-permute-start | bytes 786440 | tf_op jit(solution)/shard_map/ppermute | solution.py:273
Sparse Core Ops, SparseCore 0:
  8.9 56.4 all-gather.1

commit v4 on v3

v4 whole, which is shorter than its diff:
```python
import functools

import jax
import jax.numpy as jnp
from jax import lax
from jax.experimental import pallas as pl
from jax.experimental.pallas import tpu as pltpu
from jax.sharding import PartitionSpec as P

NDIM = 16
GROUP = 64
STRETCH = 128
CHUNK = 16
LANES = 128
epsilon = 1e-05
f32 = jnp.float32
bf16 = jnp.bfloat16
VMEM_LIMIT = 64 * 1024 * 1024
CHEAP = pl.CostEstimate(flops=1, bytes_accessed=1, transcendentals=0)


def call(kernel, outs, inputs, scratch=(), copies=0, plain=0):
    hbm, vmem = pl.BlockSpec(memory_space=pltpu.HBM), pl.BlockSpec(memory_space=pltpu.VMEM)
    here = vmem if plain else hbm
    extra = [pltpu.SemaphoreType.DMA((copies,))] if copies else []
    return pl.pallas_call(
        kernel,
        out_shape=outs,
        in_specs=[pl.BlockSpec(memory_space=pltpu.SMEM)] + [here] * (len(inputs) - 1),
        out_specs=[here] * len(outs),
        scratch_shapes=list(scratch) + extra,
        compiler_params=pltpu.CompilerParams(vmem_limit_bytes=VMEM_LIMIT),
        cost_estimate=CHEAP,
    )(*inputs)


class Copies:
    def __init__(self, sems):
        self.sems, self.used = sems, 0

    def start(self, source, target):
        copy = pltpu.make_async_copy(source, target, self.sems.at[self.used])
        self.used += 1
        copy.start()
        return copy


def pieces(value):
    first = value.astype(bf16)
    rest = value - first.astype(f32)
    second = rest.astype(bf16)
    third = (rest - second.astype(f32)).astype(bf16)
    return first, second, third


def mm(a, b):
    return jnp.dot(a, b, preferred_element_type=f32)


def membership(channels, width, transposed, first):
    shape = (width, channels) if transposed else (channels, width)
    channel = lax.broadcasted_iota(jnp.int32, shape, 1 if transposed else 0) + first
    group = lax.broadcasted_iota(jnp.int32, shape, 0 if transposed else 1)
    return jnp.where(channel // GROUP == group, 1.0, 0.0).astype(bf16)


def group_sums(x, first, width):
    member = membership(x.shape[1], width, False, first)
    square = x.astype(f32) * x.astype(f32)
    high = square.astype(bf16)
    low = (square - high.astype(f32)).astype(bf16)
    return mm(x, member), mm(high, member) + mm(low, member)


def sums_kernel(at_ref, x_hbm, running_hbm, total_hbm, x_ref, running_ref, total_ref, sems):
    length, channels = x_ref.shape
    width = running_ref.shape[2]
    copies = Copies(sems)
    cut = channels // min(4, channels // LANES)
    loads = [copies.start(x_hbm.at[:, low : low + cut], x_ref.at[:, low : low + cut]) for low in range(0, channels, cut)]
    rows = lax.broadcasted_iota(jnp.int32, (length, length), 0)
    cols = lax.broadcasted_iota(jnp.int32, (length, length), 1)
    lower = jnp.where(rows >= cols, 1.0, 0.0).astype(bf16)
    sums = [jnp.zeros((length, width), f32)] * 2
    for at, load in enumerate(loads):
        load.wait()
        new = group_sums(x_ref[:, at * cut : (at + 1) * cut], at * cut, width)
        sums = [old + more for old, more in zip(sums, new)]
    for at in range(2):
        one, two, three = pieces(sums[at])
        running = mm(lower, one) + mm(lower, two) + mm(lower, three)
        running_ref[at] = running
        for peer in range(total_ref.shape[0]):
            total_ref[peer, at : at + 1, :] = running[length - 1 : length, :]
    stores = [copies.start(total_ref, total_hbm), copies.start(running_ref, running_hbm)]
    for store in stores:
        store.wait()


def times(a, b):
    return a[0] * b[0] - a[1] * b[1], a[0] * b[1] + a[1] * b[0]


def row_pair(ref, j, tiles):
    start = pl.multiple_of(j * (2 * tiles), 2 * tiles)
    return ref[pl.ds(start, tiles), :], ref[pl.ds(start + tiles, tiles), :]


def powers_into(ref, first, factor, count):
    def one(j, _):
        q, now = factor(j), first(j)
        for k in range(count):
            ref[k, j, 0], ref[k, j, 1] = now
            if k + 1 < count:
                now = times(now, q)
        return _

    lax.fori_loop(0, NDIM, one, 0)


def feed_kernel(members, at_ref, *refs):
    x_hbm, sums_hbm, running_hbm, gain_hbm, bias_hbm, decay_hbm, phase_hbm, in_hbm, out_hbm = refs[:9]
    near_hbm, (dense_hbm, fresh_hbm, end_hbm, q_hbm, w_hbm) = refs[9 : 9 + members], refs[9 + members : 14 + members]
    (
        x_ref, sums_ref, running_ref, gain_ref, bias_ref, decay_ref, phase_ref, in_ref, out_ref,
        normed_ref, dense_ref, fresh_ref, end_ref, q_ref, w_ref, power_ref, sems,
    ) = refs[14 + members :]
    copies = Copies(sems)
    loads = [
        copies.start(a, b)
        for a, b in (
            (decay_hbm, decay_ref), (phase_hbm, phase_ref), (running_hbm, running_ref), (sums_hbm, sums_ref), (x_hbm, x_ref),
            (gain_hbm, gain_ref), (bias_hbm, bias_ref), (in_hbm, in_ref), (out_hbm, out_ref),
        )
    ]
    length, channels = x_ref.shape
    width = running_ref.shape[2]
    tiles = channels // LANES
    chunks = length // CHUNK
    subs, _, depth = near_hbm[0].shape
    me = at_ref[0]
    peers = sums_ref.shape[0]

    loads[0].wait()
    loads[1].wait()
    for tile in range(tiles):
        lanes = slice(tile * LANES, (tile + 1) * LANES)
        phase, decay = phase_ref[:, lanes], decay_ref[:, lanes]
        parts = (decay * jnp.cos(phase), decay * jnp.sin(phase))
        for part in range(2):
            q_ref[pl.ds(part * tiles + tile, NDIM, stride=2 * tiles), :] = parts[part]
    stores = [copies.start(q_ref, q_hbm)]
    one, zero = jnp.ones((tiles, LANES), f32), jnp.zeros((tiles, LANES), f32)
    powers_into(power_ref, lambda j: (one, zero), lambda j: row_pair(q_ref, j, tiles), CHUNK + 1)

    for load in loads[2:7]:
        load.wait()
    before = [jnp.zeros((1, width), f32) for _ in range(2)]
    for peer in range(peers):
        earlier = jnp.where(peer < me, 1.0, 0.0)
        for at in range(2):
            before[at] = before[at] + sums_ref[peer, at : at + 1, :] * earlier
    place = lax.broadcasted_iota(jnp.int32, (length, width), 0) + me * length + 1
    counts = place.astype(f32) * GROUP
    average = (before[0] + running_ref[0]) / counts
    spread = jnp.maximum((before[1] + running_ref[1]) / counts - average * average, 0.0)
    scale = lax.rsqrt(spread + epsilon)
    member = membership(channels, width, True, 0)
    average_pieces, scale_pieces = pieces(average), pieces(scale)
    for tile in range(tiles):
        lanes = slice(tile * LANES, (tile + 1) * LANES)
        mine = member[:, lanes]
        average_wide = sum(mm(p, mine) for p in average_pieces)
        scale_wide = sum(mm(p, mine) for p in scale_pieces)
        scaled = (x_ref[:, lanes].astype(f32) - average_wide) * scale_wide
        normed = (scaled * gain_ref[:, lanes] + bias_ref[:, lanes]).astype(bf16)
        part = min(depth, LANES)
        for low in range(0, LANES, part):
            at = tile * LANES + low
            normed_ref[at // depth, :, at % depth : at % depth + part] = normed[:, low : low + part]
        dense_ref[pl.ds(tile, length, stride=tiles), :] = normed.astype(f32)
    for away, ref in enumerate(near_hbm):
        to = lax.rem(me + away, members)
        for sub in range(subs):
            stores.append(copies.start(normed_ref.at[sub * members + to], ref.at[sub]))
    stores.append(copies.start(dense_ref, dense_hbm))

    loads[7].wait()
    loads[8].wait()
    for tile in range(tiles):
        lanes = slice(tile * LANES, (tile + 1) * LANES)
        for part in range(2):
            w_ref[pl.ds(part * tiles + tile, NDIM, stride=2 * tiles), :] = in_ref[:, lanes] * out_ref[part, :, lanes]
    stores.append(copies.start(w_ref, w_hbm))
    step = min(8, tiles)
    first_sem = copies.used

    def send(j):
        return pltpu.make_async_copy(fresh_ref.at[j], fresh_hbm.at[j], sems.at[first_sem + j])

    def one(j, _):
        for low in range(0, tiles, step):
            rows = slice(low, low + step)
            re = [jnp.zeros((step, LANES), f32) for _ in range(chunks)]
            im = [jnp.zeros((step, LANES), f32) for _ in range(chunks)]
            for b in range(CHUNK):
                p_re = power_ref[CHUNK - 1 - b, j, 0, rows, :]
                p_im = power_ref[CHUNK - 1 - b, j, 1, rows, :]
                for a in range(chunks):
                    at = (a * CHUNK + b) * tiles + low
                    value = dense_ref[at : at + step, :]
                    re[a] = re[a] + p_re * value
                    im[a] = im[a] + p_im * value
            q = (power_ref[CHUNK, j, 0, rows, :], power_ref[CHUNK, j, 1, rows, :])
            state = (re[0], im[0])
            for a in range(chunks):
                fresh_ref[j, a, 0, rows, :] = re[a]
                fresh_ref[j, a, 1, rows, :] = im[a]
                if a:
                    moved = times(state, q)
                    state = (moved[0] + re[a], moved[1] + im[a])
            end_ref[j, 0, rows, :], end_ref[j, 1, rows, :] = state
        send(j).start()
        return _

    lax.fori_loop(0, NDIM, one, 0)
    ends = pltpu.make_async_copy(end_ref, end_hbm, sems.at[first_sem + NDIM])
    ends.start()
    for store in stores:
        store.wait()
    lax.fori_loop(0, NDIM, lambda j, c: (send(j).wait(), c)[1], 0)
    ends.wait()


def scan_kernel(length, at_ref, ends_ref, q_ref, out_ref):
    peers = ends_ref.shape[0]
    result, base, left = None, (q_ref[:, 0], q_ref[:, 1]), length
    while left:
        if left & 1:
            result = base if result is None else times(result, base)
        left >>= 1
        if left:
            base = times(base, base)
    state = (jnp.zeros_like(base[0]), jnp.zeros_like(base[1]))
    for peer in range(peers):
        out_ref[peer, :, 0], out_ref[peer, :, 1] = state
        if peer + 1 < peers:
            moved = times(state, result)
            state = (moved[0] + ends_ref[peer, :, 0], moved[1] + ends_ref[peer, :, 1])


def mix_kernel(
    at_ref, incoming_hbm, fresh_hbm, dense_hbm, q_hbm, w_hbm, skip_hbm, mixed_hbm,
    incoming_ref, fresh_ref, dense_ref, q_ref, w_ref, skip_ref, mixed_ref, start_ref, coef_ref, tap_ref, out_ref, sems,
):
    copies = Copies(sems)
    loads = [
        copies.start(a, b)
        for a, b in (
            (q_hbm, q_ref), (w_hbm, w_ref), (skip_hbm, skip_ref), (incoming_hbm, incoming_ref), (fresh_hbm, fresh_ref), (dense_hbm, dense_ref),
        )
    ]
    length, channels = mixed_ref.shape
    tiles = channels // LANES
    chunks = length // CHUNK
    step = min(8, tiles)
    for load in loads[:3]:
        load.wait()
    powers_into(
        coef_ref,
        lambda j: times(row_pair(w_ref, j, tiles), row_pair(q_ref, j, tiles)),
        lambda j: row_pair(q_ref, j, tiles),
        CHUNK,
    )
    tap = skip_ref[...]
    for j in range(NDIM):
        tap = tap + row_pair(w_ref, j, tiles)[0]
    tap_ref[0] = tap

    def one_tap(k, _):
        tap = coef_ref[k, 0, 0]
        for j in range(1, NDIM):
            tap = tap + coef_ref[k, j, 0]
        tap_ref[k + 1] = tap
        return _

    lax.fori_loop(0, CHUNK - 1, one_tap, 0)
    for load in loads[3:]:
        load.wait()

    def one(j, _):
        q = row_pair(q_ref, j, tiles)
        left = CHUNK
        while left > 1:
            q = times(q, q)
            left //= 2
        state = (incoming_ref[j, 0], incoming_ref[j, 1])
        for a in range(chunks):
            start_ref[a, j, 0], start_ref[a, j, 1] = state
            if a + 1 < chunks:
                moved = times(state, q)
                state = (moved[0] + fresh_ref[j, a, 0], moved[1] + fresh_ref[j, a, 1])
        return _

    lax.fori_loop(0, NDIM, one, 0)

    for low in range(0, tiles, step):
        rows = slice(low, low + step)
        for b in range(0, CHUNK, 2):
            total = [[jnp.zeros((step, LANES), f32) for _ in range(chunks)] for _ in range(2)]

            def carry(j, total, b=b, rows=rows):
                total = [list(t) for t in total]
                coefs = [(coef_ref[b + i, j, 0, rows, :], coef_ref[b + i, j, 1, rows, :]) for i in range(2)]
                for a in range(chunks):
                    re, im = start_ref[a, j, 0, rows, :], start_ref[a, j, 1, rows, :]
                    for i in range(2):
                        total[i][a] = total[i][a] + coefs[i][0] * re - coefs[i][1] * im
                return total

            total = lax.fori_loop(0, NDIM, carry, total, unroll=4)
            for s in range(b + 2):
                for i in range(2):
                    if s > b + i:
                        continue
                    tap = tap_ref[b + i - s, rows, :]
                    for a in range(chunks):
                        at = (a * CHUNK + s) * tiles + low
                        total[i][a] = total[i][a] + tap * dense_ref[at : at + step, :]
            for i in range(2):
                for a in range(chunks):
                    at = (a * CHUNK + b + i) * tiles + low
                    out_ref[at : at + step, :] = total[i][a]
        for tile in range(low, low + step):
            lanes = slice(tile * LANES, (tile + 1) * LANES)
            value = out_ref[pl.ds(tile, length, stride=tiles), :]
            mixed_ref[:, lanes] = (value / (1.0 + jnp.exp(-value))).astype(bf16)
        lanes = slice(low * LANES, (low + step) * LANES)
        loads.append(copies.start(mixed_ref.at[:, lanes], mixed_hbm.at[:, lanes]))
    for store in loads[6:]:
        store.wait()


def along(block, axis, step, group):
    count = lax.axis_size(axis)
    pairs = [(i, i - i % group + (i + step) % group) for i in range(count)]
    return lax.ppermute(block, axis, pairs)


def ring_of(layers):
    return [0, *range(1, layers, 2), *reversed(range(2, layers, 2))]


def ring_on(block, members, layers, step):
    ring = ring_of(layers)
    pairs = [
        (ring[k] * members + r, ring[(k + step) % layers] * members + r) for k in range(layers) for r in range(members)
    ]
    return lax.ppermute(block, "ctx", pairs)


def ring_steps(layers):
    return [0, *[(-1) ** (k + 1) * -((k + 1) // 2) for k in range(1, layers)]]


def others(block, axis):
    count = lax.axis_size(axis)
    return [along(block, axis, k, count) for k in range(1, count)]


def part_kernel(members, tp, layers, at_ref, *refs):
    blocks_hbm, refs = refs[: members * tp], refs[members * tp :]
    weights_hbm, refs = refs[:layers], refs[layers:]
    own_hbm, sent_hbm, refs = refs[0], refs[1:members], refs[members:]
    row_ref, weight_ref, own_ref, sent_ref, sems = refs
    copies = Copies(sems)
    subs, length, depth = blocks_hbm[0].shape
    half, ring_at = at_ref[1], at_ref[2]
    loads = [copies.start(weight, weight_ref.at[at]) for at, weight in enumerate(weights_hbm)]
    for away in range(tp):
        other = lax.rem(half + tp - away, tp)
        for k in range(members):
            for sub in range(subs):
                to = row_ref.at[other * subs + sub, k * length : (k + 1) * length, :]
                loads.append(copies.start(blocks_hbm[away * members + k].at[sub], to))
    ring = ring_of(layers)
    blocks = []
    for step in ring_steps(layers):
        at = lax.rem(ring_at + layers + step, layers)
        block = jnp.int32(0)
        for place, layer in enumerate(ring):
            block = jnp.where(at == place, layer, block)
        blocks.append(block)
    for load in loads:
        load.wait()
    stores = []
    for k in [*range(1, members), 0]:
        here = slice(k * length, (k + 1) * length)
        total = mm(row_ref[blocks[0], here, :], weight_ref[0])
        for back in range(1, layers):
            total = total + mm(row_ref[blocks[back], here, :], weight_ref[back])
        if k == 0:
            own_ref[...] = total
            stores.append(copies.start(own_ref, own_hbm))
        else:
            sent_ref[k - 1] = total.astype(bf16)
            stores.append(copies.start(sent_ref.at[k - 1], sent_hbm[k - 1]))
    for store in stores:
        store.wait()


def attend_kernel(members, tp, at_ref, *refs):
    weights_hbm, refs = refs[:members], refs[members:]
    mixed_hbm, refs = refs[:tp], refs[tp:]
    parts_hbm, refs = refs[: members - 1], refs[members - 1 :]
    own_hbm, gain_hbm, affine_hbm, result_hbm = refs[:4]
    weight_ref, mixed_ref, part_ref, own_ref, gain_ref, affine_ref, row_ref, value_ref, result_ref, sems = refs[4:]
    copies = Copies(sems)
    loads = [copies.start(a, mixed_ref.at[k]) for k, a in enumerate(mixed_hbm)]
    loads += [copies.start(gain_hbm, gain_ref), copies.start(affine_hbm, affine_ref)]
    first = len(loads)
    loads += [copies.start(a, weight_ref.at[k]) for k, a in enumerate(weights_hbm)]
    second = len(loads)
    loads += [copies.start(own_hbm, own_ref)] + [copies.start(a, part_ref.at[k]) for k, a in enumerate(parts_hbm)]
    _, layers, depth, head = weight_ref.shape
    _, length, channels = mixed_ref.shape
    place, half = at_ref[0], at_ref[1]
    member, layer = lax.rem(place, members), lax.div(place, members)
    blocks = channels // depth

    for load in loads[:first]:
        load.wait()
    square = jnp.zeros((length, 1), f32)
    for k in range(tp):
        value = mixed_ref[k].astype(f32)
        square = square + jnp.sum(value * value, axis=1, keepdims=True)
    scale = lax.rsqrt(square / (channels * tp) + 1e-06)
    for k in range(tp):
        at = lax.rem(half + tp - k, tp)
        gain = gain_ref[:, pl.ds(pl.multiple_of(at * channels, LANES), channels)]
        normed = (mixed_ref[k].astype(f32) * scale * gain).astype(bf16)
        for block in range(blocks):
            row_ref[at * blocks + block] = normed[:, block * depth : (block + 1) * depth]
    for load in loads[first:second]:
        load.wait()
    z_total = jnp.zeros((length, head), f32)
    for m in range(members):
        for k in range(layers):
            block = lax.rem(layer + layers - k, layers) * members + lax.rem(member + members - m, members)
            z_total = z_total + mm(row_ref[block], weight_ref[m, k])
    queries = (z_total * affine_ref[0:1, :] + affine_ref[1:2, :]).astype(bf16)
    key_rows = (z_total * affine_ref[2:3, :] + affine_ref[3:4, :]).astype(bf16)

    for load in loads[second:]:
        load.wait()
    total = own_ref[...]
    for k in range(members - 1):
        total = total + part_ref[k].astype(f32)
    value_ref[...] = (total / (1.0 + jnp.exp(-total))).astype(bf16)
    row = lax.broadcasted_iota(jnp.int32, (STRETCH, STRETCH), 0)
    col = lax.broadcasted_iota(jnp.int32, (STRETCH, STRETCH), 1)
    for low in range(0, length, STRETCH):
        here = slice(low, low + STRETCH)
        scores = lax.dot_general(
            queries[here], key_rows[here], (((1,), (1,)), ((), ())), preferred_element_type=f32
        ) * (1.0 / head**0.5)
        scores = jnp.where(row >= col, scores, -1e30)
        weights = jnp.exp(scores - jnp.max(scores, axis=1, keepdims=True))
        probabilities = (weights / jnp.sum(weights, axis=1, keepdims=True)).astype(bf16)
        result_ref[here, :] = mm(probabilities, value_ref[here, :]).astype(bf16)
    copies.start(result_ref, result_hbm).wait()


def body(
    tokens, norm_gain, norm_bias, ema_decay, ema_phase, ema_in, ema_out, ema_skip, rms_gain, z_weight, v_weight, qk_affine
):
    length, channels = tokens.shape
    tiles = channels // LANES
    chunks = length // CHUNK
    width = -(-(channels // GROUP) // LANES) * LANES
    place, peers = lax.axis_index("ctx"), lax.axis_size("ctx")
    half, tp = lax.axis_index("tp"), lax.axis_size("tp")
    depth, columns = v_weight.shape
    head = z_weight.shape[1]
    blocks = channels // depth
    members = 4 if peers % 4 == 0 and blocks % 4 == 0 else 1
    layers = peers // members
    subs = blocks // members
    shape, vmem = jax.ShapeDtypeStruct, pltpu.VMEM
    ring_at = sum(jnp.where(place // members == at, k, 0) for k, at in enumerate(ring_of(layers)))
    here = jnp.stack([place, half, ring_at]).astype(jnp.int32)

    running, totals = call(
        sums_kernel,
        [shape((2, length, width), f32), shape((peers, 2, width), f32)],
        [here, tokens],
        [vmem((length, channels), bf16), vmem((2, length, width), f32), vmem((peers, 2, width), f32)],
        8,
    )
    line_z = [z_weight] + [
        lax.ppermute(z_weight, "ctx", [(i, (i + members * k) % peers) for i in range(peers)])
        for k in range(1, layers)
    ]
    totals, line_z, v_weight = lax.optimization_barrier((totals, line_z, v_weight))
    sums = lax.all_to_all(totals, "ctx", 0, 0)
    line_z = jnp.stack(line_z)
    all_z = [line_z] + [along(line_z, "ctx", k, members) for k in range(1, members)]
    all_v = [v_weight]
    if layers > 1:
        all_v.append(ring_on(v_weight, members, layers, 1))
    sums, all_z, all_v = lax.optimization_barrier((sums, all_z, all_v))
    for k in range(2, layers):
        all_v.append(ring_on(all_v[max(k - 2, 0)], members, layers, (-1) ** (k + 1)))

    rows = NDIM * 2 * tiles
    *near, dense, fresh, ends, q, w = call(
        functools.partial(feed_kernel, members),
        [shape((subs, length, depth), bf16)] * members
        + [
            shape((length * tiles, LANES), f32),
            shape((NDIM, chunks, 2, tiles, LANES), f32),
            shape((NDIM, 2, tiles, LANES), f32),
            shape((rows, LANES), f32),
            shape((rows, LANES), f32),
        ],
        [here, tokens, sums, running, norm_gain[None], norm_bias[None], ema_decay, ema_phase, ema_in, ema_out],
        [
            vmem((length, channels), bf16),
            vmem((peers, 2, width), f32),
            vmem((2, length, width), f32),
            vmem((1, channels), f32),
            vmem((1, channels), f32),
            vmem((NDIM, channels), f32),
            vmem((NDIM, channels), f32),
            vmem((NDIM, channels), f32),
            vmem((2, NDIM, channels), f32),
            vmem((blocks, length, depth), bf16),
            vmem((length * tiles, LANES), f32),
            vmem((NDIM, chunks, 2, tiles, LANES), f32),
            vmem((NDIM, 2, tiles, LANES), f32),
            vmem((rows, LANES), f32),
            vmem((rows, LANES), f32),
            vmem((CHUNK + 1, NDIM, 2, tiles, LANES), f32),
        ],
        9 + 3 + blocks + NDIM + 1,
    )
    more = max(1, peers // NDIM)

    def split(a):
        a = a.reshape(NDIM, 2, more, tiles // more, LANES).transpose(0, 2, 1, 3, 4)
        return a.reshape(peers, NDIM * more // peers, 2, tiles // more, LANES)

    def join(a):
        a = a.reshape(NDIM, more, 2, tiles // more, LANES).transpose(0, 2, 1, 3, 4)
        return a.reshape(NDIM, 2, tiles, LANES)

    arrived = lax.all_to_all(split(ends), "ctx", 0, 0)
    near = near[:1] + [along(near[k], "ctx", k, members) for k in range(1, members)]
    far = [along(block, "tp", k, tp) for k in range(1, tp) for block in near]
    my_q = lax.dynamic_index_in_dim(split(q.reshape(NDIM, 2, tiles, LANES)), place, 0, False)
    arrived, all_v, far, my_q = lax.optimization_barrier((arrived, all_v, far, my_q))
    (starts,) = call(functools.partial(scan_kernel, length), [shape(arrived.shape, f32)], [here, arrived, my_q], plain=1)
    incoming = lax.all_to_all(starts, "ctx", 0, 0)

    own, *sent = call(
        functools.partial(part_kernel, members, tp, layers),
        [shape((length, columns), f32)] + [shape((length, columns), bf16)] * (members - 1),
        [here, *near, *far, *all_v],
        [
            vmem((layers, members * length, depth), bf16),
            vmem((layers, depth, columns), bf16),
            vmem((length, columns), f32),
            vmem((max(members - 1, 1), length, columns), bf16),
        ],
        layers + tp * members * subs + members,
    )
    returned = [along(block, "ctx", -k, members) for k, block in enumerate(sent, 1)]
    incoming, own = lax.optimization_barrier((incoming, own))

    (mixed_rows,) = call(
        mix_kernel,
        [shape((length, channels), bf16)],
        [here, join(incoming), fresh, dense, q, w, ema_skip.reshape(tiles, LANES)],
        [
            vmem((NDIM, 2, tiles, LANES), f32),
            vmem((NDIM, chunks, 2, tiles, LANES), f32),
            vmem((length * tiles, LANES), f32),
            vmem((rows, LANES), f32),
            vmem((rows, LANES), f32),
            vmem((tiles, LANES), f32),
            vmem((length, channels), bf16),
            vmem((chunks, NDIM, 2, tiles, LANES), f32),
            vmem((CHUNK, NDIM, 2, tiles, LANES), f32),
            vmem((CHUNK, tiles, LANES), f32),
            vmem((length * tiles, LANES), f32),
        ],
        6 + max(1, tiles // 8),
    )
    mixed_rows, returned = lax.optimization_barrier((mixed_rows, returned))
    (result,) = call(
        functools.partial(attend_kernel, members, tp),
        [shape((length, columns), bf16)],
        [here, *all_z, mixed_rows, *others(mixed_rows, "tp"), *returned, own, rms_gain[None], qk_affine],
        [
            vmem((members, layers, depth, head), bf16),
            vmem((tp, length, channels), bf16),
            vmem((max(members - 1, 1), length, columns), bf16),
            vmem((length, columns), f32),
            vmem((1, tp * channels), f32),
            vmem((4, head), f32),
            vmem((tp * blocks, length, depth), bf16),
            vmem((length, columns), bf16),
            vmem((length, columns), bf16),
        ],
        tp + 2 + 2 * members + 1,
    )
    return result


def solution(mesh):
    in_specs = (
        P("ctx", "tp"),
        P("tp"),
        P("tp"),
        P(None, "tp"),
        P(None, "tp"),
        P(None, "tp"),
        P(None, None, "tp"),
        P("tp"),
        P(),
        P("ctx", "tp"),
        P("ctx", "tp"),
        P(None, "tp"),
    )
    return jax.shard_map(body, mesh=mesh, in_specs=in_specs, out_specs=P("ctx", "tp"), check_vma=False)
```

time: 113 us -> 95.2 us (0.84)
  blocking collectives: 0 us -> 13.6 us
  between operations: 13.6 us -> 0.2 us
  Pallas kernels: 17.6 us -> 30.3 us
  starting transfers between devices: 41.2 us -> 31.6 us
  local copies, waits for them, and re-layouts: 12 us -> 2.75 us
  waiting for transfers between devices: 22.2 us -> 14.6 us
  other arithmetic: 5.17 us -> 1.57 us
    all_to_all x0 -> x1, blocking collectives: none -> 13.6 us  [body(): sums = lax.all_to_all(totals, 'ctx', 0, 0)]
    pallas_call x7 -> x6, Pallas kernels: 17.6 us -> 30.3 us  [call(): pl.pallas_call(kernel, out_shape=outs, in_specs=[pl.BlockSpec(memory_spac...]
    all_to_all x2 -> x1, waiting for transfers between devices: 10.9 us -> 1.53 us  [body(): incoming = lax.all_to_all(starts, 'ctx', 0, 0)]
    unnamed x41 -> x20, local copies, waits for them, and re-layouts: 9.77 us -> 1.44 us
    ppermute x11 -> x14, starting transfers between devices: 21 us -> 12.7 us  [along(): return lax.ppermute(block, axis, pairs)]
    all_to_all x2 -> x1, starting transfers between devices: 9.65 us -> 4.71 us  [body(): incoming = lax.all_to_all(starts, 'ctx', 0, 0)]
    unnamed x2 -> x0, other arithmetic: 2.5 us -> none
    ppermute x0 -> x3, starting transfers between devices: none -> 2.09 us  [ring_on(): return lax.ppermute(block, 'ctx', pairs)]
  transfers between devices with their start and end apart: 18 -> 22, of which waited for: 7 -> 7; matrix products, arithmetic and copies ran while one was open for 7% -> 3% of each run, Pallas kernels for 15% -> 26%
where the time goes in v4:
time: 95.2 us; the launch traced here: 94.6 us
  starting transfers between devices  31.6 us (33%)
  Pallas kernels  30.3 us (32%)
  waiting for transfers between devices  14.6 us (15%)
  blocking collectives  13.6 us (14%)
  local copies, waits for them, and re-layouts  2.75 us (3%)
  other arithmetic  1.57 us (2%)
    pallas_call x6, Pallas kernels, call(): pl.pallas_call(kernel, out_shape=outs, in_specs=[pl.BlockSpec(memory_spac...  30.3 us
    all_to_all x1, blocking collectives, body(): sums = lax.all_to_all(totals, 'ctx', 0, 0)  13.6 us
    ppermute x14, starting transfers between devices, along(): return lax.ppermute(block, axis, pairs)  12.7 us
    ppermute x14, waiting for transfers between devices, along(): return lax.ppermute(block, axis, pairs)  9.28 us
    ppermute x3, starting transfers between devices, body(): lax.ppermute(z_weight, 'ctx', [(i, (i + members * k) % peers) for i in ra...  7.86 us
    all_to_all x1, starting transfers between devices, body(): incoming = lax.all_to_all(starts, 'ctx', 0, 0)  4.71 us
    all_to_all x1, starting transfers between devices, body(): arrived = lax.all_to_all(split(ends), 'ctx', 0, 0)  4.2 us
    all_to_all x1, waiting for transfers between devices, body(): arrived = lax.all_to_all(split(ends), 'ctx', 0, 0)  3.8 us
  transfers between devices with their start and end apart: 22, of which 7 were waited for; matrix products, arithmetic and copies ran while one was open for 3% of the time, Pallas kernels for 26%

profile of v4, /device:TPU:0, one launch (start us, length us, event | category | flops | bytes accessed | tf_op | source)
XLA Modules:
  0.0 94.6 jit_solution(2234889194307019855)
XLA Ops:
  0.0 4.0 %collective-permute-start.1 = (bf16[256,128]{1,0:T(8,128)(2,1)}, bf16[256,128]{1,0:T(8,128)(2,1)}, u32[]{:S(2)}, u32[]{:S(2)}) collective-permute-start(bf16[256,128]{1,0:T(8,128)(2,1)} %param.21), channel_id=1, source_target_pairs={{0,16},{2,18},{4,20},{6,22},{8,24},{10,26},{12,28},{14,30},{16,0},... | collective-permute-start | bytes 196616 | tf_op jit(solution)/shard_map/ppermute | solution.py:501
  4.0 1.6 %collective-permute-start = (bf16[256,128]{1,0:T(8,128)(2,1)}, bf16[256,128]{1,0:T(8,128)(2,1)}, u32[]{:S(2)}, u32[]{:S(2)}) collective-permute-start(bf16[256,128]{1,0:T(8,128)(2,1)} %param.21), channel_id=1, source_target_pairs={{0,8},{2,10},{4,12},{6,14},{8,16},{10,18},{12,20},{14,22},{16,24},... | collective-permute-start | bytes 196616 | tf_op jit(solution)/shard_map/ppermute | solution.py:501
  5.6 2.2 %collective-permute-start.2 = (bf16[256,128]{1,0:T(8,128)(2,1)}, bf16[256,128]{1,0:T(8,128)(2,1)}, u32[]{:S(2)}, u32[]{:S(2)}) collective-permute-start(bf16[256,128]{1,0:T(8,128)(2,1)} %param.21), channel_id=1, source_target_pairs={{0,24},{2,26},{4,28},{6,30},{8,0},{10,2},{12,4},{14,6},{16,8},{18,... | collective-permute-start | bytes 196616 | tf_op jit(solution)/shard_map/ppermute | solution.py:501
  7.9 0.6 pad_add_fusion.at_ref
  8.5 3.6 %shard_map.118 = (f32[2,128,128]{2,1,0:T(8,128)}, f32[16,2,128]{2,1,0:T(2,128)}) custom-call(s32[3]{0:T(128)} %pad_add_fusion.at_ref, bf16[128,2048]{1,0:T(8,128)(2,1)} %refs_0_.1), custom_call_target="tpu_custom_call" | custom-call | flops 1 | bytes 1 | tf_op jit(solution)/shard_map/pallas_call | solution.py:26
  12.1 0.0 collective-permute-done
  12.1 0.0 collective-permute-done.2
  12.1 0.1 collective-permute-start.6
  12.2 1.0 %pad_maximum_fusion.refs_0_ = bf16[4,256,128]{2,1,0:T(8,128)(2,1)S(1)} fusion(bf16[1,256,128]{2,1,0:T(8,128)(2,1)} %bitcast.6, bf16[1,256,128]{2,1,0:T(8,128)(2,1)} %bitcast.5, bf16[1,256,128]{2,1,0:T(8,128)(2,1)} %bitcast.4, bf16[1,256,128]{2,1,0:T(8,128)(2,1)} %bitcast.20), kind=kLoop, calls=%fused_computation | loop fusion | flops 393216 | bytes 524288 | tf_op jit(solution)/shard_map/stack | solution.py:506
  13.2 2.5 %collective-permute-start.5 = (bf16[4,256,128]{2,1,0:T(8,128)(2,1)S(1)}, bf16[4,256,128]{2,1,0:T(8,128)(2,1)S(1)}, u32[]{:S(2)}, u32[]{:S(2)}) collective-permute-start(bf16[4,256,128]{2,1,0:T(8,128)(2,1)S(1)} %pad_maximum_fusion.refs_0_), channel_id=1, source_target_pairs={{0,6},{2,0},{4,2},{6,4},{8,14},{10,8},{12,10},{14,12},{16,22},{18,... | collective-permute-start | bytes 786440 | tf_op jit(solution)/shard_map/ppermute | solution.py:347
  15.7 0.5 collective-permute-start.4
  16.2 0.6 collective-permute-start.3
  16.8 13.6 %all_to_all.15.refs_1_ = f32[16,2,128]{2,1,0:T(2,128)} all-to-all(f32[16,2,128]{2,1,0:T(2,128)} %get-tuple-element.50), channel_id=1, replica_groups=mesh['ctx'=16,'tp'=2] {'ctx'}, dimensions={0} | all-to-all | bytes 32768 | tf_op jit(solution)/shard_map/all_to_all | solution.py:505
  30.3 0.0 collective-permute-done.5.refs_3_
  30.3 0.0 collective-permute-done.4.refs_2_
  30.3 0.7 copy-done.1
  31.0 0.1 copy-done.2
  31.1 0.8 collective-permute-start.7
  31.9 1.2 %collective-permute-start.8 = (bf16[256,1024]{1,0:T(8,128)(2,1)}, bf16[256,1024]{1,0:T(8,128)(2,1)}, u32[]{:S(2)}, u32[]{:S(2)}) collective-permute-start(bf16[256,1024]{1,0:T(8,128)(2,1)} %collective-permute-done.6.refs_9_), channel_id=1, source_target_pairs={{0,8},{2,10},{4,12},{6,14},{8,24},{10,26},{12,28},{14,30},{24,16},... | collective-permute-start | bytes 1572872 | tf_op jit(solution)/shard_map/ppermute | solution.py:359
  33.2 8.1 %shard_map.119 = (bf16[2,128,256]{2,1,0:T(8,128)(2,1)}, bf16[2,128,256]{2,1,0:T(8,128)(2,1)}, bf16[2,128,256]{2,1,0:T(8,128)(2,1)}, bf16[2,128,256]{2,1,0:T(8,12...) custom-call(s32[3]{0:T(128)} %pad_add_fusion.at_ref, ...), custom_call_target="tpu_custom_call" | custom-call | flops 1 | bytes 1 | tf_op jit(solution)/shard_map/pallas_call | solution.py:26
  41.3 4.2 %all-to-all-start.1 = ((f32[16,1,2,16,128]{4,3,2,1,0:T(8,128)}), f32[16,1,2,16,128]{4,3,2,1,0:T(8,128)}, u32[]{:S(2)}, u32[]{:S(2)}) async-start(f32[16,1,2,16,128]{4,3,2,1,0:T(8,128)} %bitcast.19), calls=%async_computation.1 | async-start | bytes 524288 | tf_op jit(solution)/shard_map/all_to_all | solution.py:557
  45.5 1.7 %collective-permute-start.10 = (bf16[2,128,256]{2,1,0:T(8,128)(2,1)}, bf16[2,128,256]{2,1,0:T(8,128)(2,1)S(1)}, u32[]{:S(2)}, u32[]{:S(2)}) collective-permute-start(bf16[2,128,256]{2,1,0:T(8,128)(2,1)} %get-tuple-element.66), channel_id=1, source_target_pairs={{0,2},{2,4},{4,6},{6,0},{8,10},{10,12},{12,14},{14,8},{16,18},{18,... | collective-permute-start | bytes 393224 | tf_op jit(solution)/shard_map/ppermute | solution.py:347
  47.2 1.5 %collective-permute-start.12 = (bf16[2,128,256]{2,1,0:T(8,128)(2,1)}, bf16[2,128,256]{2,1,0:T(8,128)(2,1)S(1)}, u32[]{:S(2)}, u32[]{:S(2)}) collective-permute-start(bf16[2,128,256]{2,1,0:T(8,128)(2,1)} %get-tuple-element.67), channel_id=1, source_target_pairs={{0,4},{2,6},{4,0},{6,2},{8,12},{10,14},{12,8},{14,10},{16,20},{18,... | collective-permute-start | bytes 393224 | tf_op jit(solution)/shard_map/ppermute | solution.py:347
  48.7 1.5 %collective-permute-start.14 = (bf16[2,128,256]{2,1,0:T(8,128)(2,1)}, bf16[2,128,256]{2,1,0:T(8,128)(2,1)S(1)}, u32[]{:S(2)}, u32[]{:S(2)}) collective-permute-start(bf16[2,128,256]{2,1,0:T(8,128)(2,1)} %get-tuple-element.68), channel_id=1, source_target_pairs={{0,6},{2,0},{4,2},{6,4},{8,14},{10,8},{12,10},{14,12},{16,22},{18,... | collective-permute-start | bytes 393224 | tf_op jit(solution)/shard_map/ppermute | solution.py:347
  50.1 1.7 %collective-permute-done.10.refs_1_ = bf16[2,128,256]{2,1,0:T(8,128)(2,1)S(1)} collective-permute-done((bf16[2,128,256]{2,1,0:T(8,128)(2,1)}, bf16[2,128,256]{2,1,0:T(8,128)(2,1)S(1)}, u32[]{:S(2)}, u32[]{:S(2)}) %collective-permute-start.10) | collective-permute-done | bytes 131104 | tf_op jit(solution)/shard_map/ppermute | solution.py:347
  51.8 0.0 collective-permute-start.9
  51.8 1.4 %collective-permute-done.12.refs_2_ = bf16[2,128,256]{2,1,0:T(8,128)(2,1)S(1)} collective-permute-done((bf16[2,128,256]{2,1,0:T(8,128)(2,1)}, bf16[2,128,256]{2,1,0:T(8,128)(2,1)S(1)}, u32[]{:S(2)}, u32[]{:S(2)}) %collective-permute-start.12) | collective-permute-done | bytes 131104 | tf_op jit(solution)/shard_map/ppermute | solution.py:347
  53.2 1.1 %collective-permute-done.14.refs_3_ = bf16[2,128,256]{2,1,0:T(8,128)(2,1)S(1)} collective-permute-done((bf16[2,128,256]{2,1,0:T(8,128)(2,1)}, bf16[2,128,256]{2,1,0:T(8,128)(2,1)S(1)}, u32[]{:S(2)}, u32[]{:S(2)}) %collective-permute-start.14) | collective-permute-done | bytes 131104 | tf_op jit(solution)/shard_map/ppermute | solution.py:347
  54.3 0.0 collective-permute-start.13
  54.3 0.0 collective-permute-done.9.refs_4_
  54.3 0.5 collective-permute-start.15
  54.9 1.3 %dynamic-slice_bitcast_fusion.q_ref = f32[1,2,16,128]{3,2,1,0:T(8,128)} fusion(f32[16,1,2,16,128]{4,3,2,1,0:T(8,128)} %bitcast.18, s32[]{:T(128)S(6)} %select_n.27), kind=kLoop, calls=%fused_computation.1 | loop fusion | bytes 32772 | tf_op jit(solution)/shard_map/jit(dynamic_index_in_dim)/squeeze | solution.py:560
  56.2 0.0 collective-permute-done.11.refs_5_
  56.2 0.0 collective-permute-done.13.refs_6_
  56.2 0.6 copy-done.7
  56.8 3.8 %all-to-all-done.1.ends_ref = f32[16,1,2,16,128]{4,3,2,1,0:T(8,128)} async-done(((f32[16,1,2,16,128]{4,3,2,1,0:T(8,128)}), f32[16,1,2,16,128]{4,3,2,1,0:T(8,128)}, u32[]{:S(2)}, u32[]{:S(2)}) %all-to-all-start.1) | async-done | bytes 262176 | tf_op jit(solution)/shard_map/all_to_all | solution.py:557
  60.6 0.0 collective-permute-done.8.refs_11_
  60.7 1.7 %shard_map.120 = f32[16,1,2,16,128]{4,3,2,1,0:T(8,128)} custom-call(s32[3]{0:T(128)} %pad_add_fusion.at_ref, f32[16,1,2,16,128]{4,3,2,1,0:T(8,128)} %all-to-all-done.1.ends_ref, f32[1,2,16,128]{3,2,1,0:T(8,128)} %dynamic-slice_bitcast_fusion.q_ref), custom_call_target="tpu_custom_call" | custom-call | flops 1 | bytes 1 | tf_op jit(solution)/shard_map/pallas_call | solution.py:26
  62.4 4.7 %all-to-all-start.2 = ((f32[16,1,2,16,128]{4,3,2,1,0:T(8,128)}), f32[16,1,2,16,128]{4,3,2,1,0:T(8,128)}, u32[]{:S(2)}, u32[]{:S(2)}) async-start(f32[16,1,2,16,128]{4,3,2,1,0:T(8,128)} %shard_map.120), calls=%async_computation.2 | async-start | bytes 524288 | tf_op jit(solution)/shard_map/all_to_all | solution.py:563
  67.1 4.7 %shard_map.121 = (f32[128,1024]{1,0:T(8,128)}, bf16[128,1024]{1,0:T(8,128)(2,1)}, bf16[128,1024]{1,0:T(8,128)(2,1)}, bf16[128,1024]{1,0:T(8,128)(2,1)}) custom-call(s32[3]{0:T(128)} %pad_add_fusion.at_ref, bf16[2,128,256]{2,1,0:T(8,128)(2,1)} %get-tuple-element.65.refs_0_, bf16[2,128,256]{2,1,0:T(8,128)(2,1)} %copy-done.4, bf16[2,128,256]{2,1,0:T(8,128)(2,1)} %copy-done.5, ...), custom_call_target="tpu_custom_call" | custom-call | flops 1 | bytes 1 | tf_op jit(solution)/shard_map/pallas_call | solution.py:26
  71.8 2.8 %collective-permute-start.16 = (bf16[128,1024]{1,0:T(8,128)(2,1)}, bf16[128,1024]{1,0:T(8,128)(2,1)}, u32[]{:S(2)}, u32[]{:S(2)}) collective-permute-start(bf16[128,1024]{1,0:T(8,128)(2,1)} %get-tuple-element.85), channel_id=1, source_target_pairs={{0,6},{2,0},{4,2},{6,4},{8,14},{10,8},{12,10},{14,12},{16,22},{18,... | collective-permute-start | bytes 786440 | tf_op jit(solution)/shard_map/ppermute | solution.py:347
  74.7 0.6 collective-permute-start.17
  75.2 0.6 collective-permute-start.18
  75.8 1.5 %all-to-all-done.2 = f32[16,1,2,16,128]{4,3,2,1,0:T(8,128)} async-done(((f32[16,1,2,16,128]{4,3,2,1,0:T(8,128)}), f32[16,1,2,16,128]{4,3,2,1,0:T(8,128)}, u32[]{:S(2)}, u32[]{:S(2)}) %all-to-all-start.2) | async-done | bytes 262176 | tf_op jit(solution)/shard_map/all_to_all | solution.py:563
  77.3 8.0 %shard_map.122.refs_4_ = bf16[128,2048]{1,0:T(8,128)(2,1)} custom-call(s32[3]{0:T(128)} %pad_add_fusion.at_ref, f32[16,2,16,128]{3,2,1,0:T(8,128)} %bitcast.13.incoming_hbm, f32[16,8,2,16,128]{4,3,2,1,0:T(8,128)} %get-tuple-element.82.fresh_hbm, f32[2048,128]{1,0:T(8,128)} %get-tuple-element.83.dense_hbm, f32[512,128]{1,0:T(8,128)} %get-tuple-element.69.q_hbm, ...), custom_call_target="tpu_custom_call" | custom-call | flops 1 | bytes 1 | tf_op jit(solution)/shard_map/pallas_call | solution.py:26
  85.3 2.8 %collective-permute-done.17.refs_7_ = bf16[128,1024]{1,0:T(8,128)(2,1)} collective-permute-done((bf16[128,1024]{1,0:T(8,128)(2,1)}, bf16[128,1024]{1,0:T(8,128)(2,1)}, u32[]{:S(2)}, u32[]{:S(2)}) %collective-permute-start.17) | collective-permute-done | bytes 262176 | tf_op jit(solution)/shard_map/ppermute | solution.py:347
  88.2 2.3 %collective-permute-done.19.refs_5_ = bf16[128,2048]{1,0:T(8,128)(2,1)} collective-permute-done((bf16[128,2048]{1,0:T(8,128)(2,1)}, bf16[128,2048]{1,0:T(8,128)(2,1)}, u32[]{:S(2)}, u32[]{:S(2)}) %collective-permute-start.19) | collective-permute-done | bytes 524320 | tf_op jit(solution)/shard_map/ppermute | solution.py:347
  90.4 4.2 %shard_map.123 = bf16[128,1024]{1,0:T(8,128)(2,1)} custom-call(s32[3]{0:T(128)} %pad_add_fusion.at_ref, bf16[4,256,128]{2,1,0:T(8,128)(2,1)} %copy-done, bf16[4,256,128]{2,1,0:T(8,128)(2,1)} %copy-done.3, bf16[4,256,128]{2,1,0:T(8,128)(2,1)} %copy-done.2, bf16[4,256,128]{2,1,0:T(8,128)(2,1)} %copy-done.1, bf16[128,2048]{1,0:T(8,128)(2,1)} %shard_map.122.refs_4_, ...), custom_call_target="tpu_custom_call" | custom-call | flops 1 | bytes 1 | tf_op jit(solution)/shard_map/pallas_call | solution.py:26
  (26 shorter events, 0.1 us)
Async XLA Ops:
  0.0 12.1 %collective-permute-start.1 = (bf16[256,128]{1,0:T(8,128)(2,1)}, bf16[256,128]{1,0:T(8,128)(2,1)}, u32[]{:S(2)}, u32[]{:S(2)}) collective-permute-start(bf16[256,128]{1,0:T(8,128)(2,1)} %param.21), channel_id=1, source_target_pairs={{0,16},{2,18},{4,20},{6,22},{8,24},{10,26},{12,28},{14,30},{16,0},... | collective-permute-start | bytes 196616 | tf_op jit(solution)/shard_map/ppermute | solution.py:501
  4.0 8.0 %collective-permute-start = (bf16[256,128]{1,0:T(8,128)(2,1)}, bf16[256,128]{1,0:T(8,128)(2,1)}, u32[]{:S(2)}, u32[]{:S(2)}) collective-permute-start(bf16[256,128]{1,0:T(8,128)(2,1)} %param.21), channel_id=1, source_target_pairs={{0,8},{2,10},{4,12},{6,14},{8,16},{10,18},{12,20},{14,22},{16,24},... | collective-permute-start | bytes 196616 | tf_op jit(solution)/shard_map/ppermute | solution.py:501
  5.6 6.5 %collective-permute-start.2 = (bf16[256,128]{1,0:T(8,128)(2,1)}, bf16[256,128]{1,0:T(8,128)(2,1)}, u32[]{:S(2)}, u32[]{:S(2)}) collective-permute-start(bf16[256,128]{1,0:T(8,128)(2,1)} %param.21), channel_id=1, source_target_pairs={{0,24},{2,26},{4,28},{6,30},{8,0},{10,2},{12,4},{14,6},{16,8},{18,... | collective-permute-start | bytes 196616 | tf_op jit(solution)/shard_map/ppermute | solution.py:501
  12.1 18.9 %collective-permute-start.6 = (bf16[256,1024]{1,0:T(8,128)(2,1)}, bf16[256,1024]{1,0:T(8,128)(2,1)}, u32[]{:S(2)}, u32[]{:S(2)}) collective-permute-start(bf16[256,1024]{1,0:T(8,128)(2,1)} %refs_8_.2), channel_id=1, source_target_pairs={{0,8},{2,10},{4,12},{6,14},{8,24},{10,26},{12,28},{14,30},{24,16},... | collective-permute-start | bytes 1572872 | tf_op jit(solution)/shard_map/ppermute | solution.py:359
  13.1 3.0 %copy-start = (bf16[4,256,128]{2,1,0:T(8,128)(2,1)}, bf16[4,256,128]{2,1,0:T(8,128)(2,1)S(1)}, u32[]{:S(2)}) copy-start(bf16[4,256,128]{2,1,0:T(8,128)(2,1)S(1)} %pad_maximum_fusion.refs_0_) | copy-start | bytes 786436
  13.2 17.2 %collective-permute-start.5 = (bf16[4,256,128]{2,1,0:T(8,128)(2,1)S(1)}, bf16[4,256,128]{2,1,0:T(8,128)(2,1)S(1)}, u32[]{:S(2)}, u32[]{:S(2)}) collective-permute-start(bf16[4,256,128]{2,1,0:T(8,128)(2,1)S(1)} %pad_maximum_fusion.refs_0_), channel_id=1, source_target_pairs={{0,6},{2,0},{4,2},{6,4},{8,14},{10,8},{12,10},{14,12},{16,22},{18,... | collective-permute-start | bytes 786440 | tf_op jit(solution)/shard_map/ppermute | solution.py:347
  15.7 14.7 %collective-permute-start.4 = (bf16[4,256,128]{2,1,0:T(8,128)(2,1)S(1)}, bf16[4,256,128]{2,1,0:T(8,128)(2,1)S(1)}, u32[]{:S(2)}, u32[]{:S(2)}) collective-permute-start(bf16[4,256,128]{2,1,0:T(8,128)(2,1)S(1)} %pad_maximum_fusion.refs_0_), channel_id=1, source_target_pairs={{0,4},{2,6},{4,0},{6,2},{8,12},{10,14},{12,8},{14,10},{16,20},{18,... | collective-permute-start | bytes 786440 | tf_op jit(solution)/shard_map/ppermute | solution.py:347
  16.2 14.2 %collective-permute-start.3 = (bf16[4,256,128]{2,1,0:T(8,128)(2,1)S(1)}, bf16[4,256,128]{2,1,0:T(8,128)(2,1)S(1)}, u32[]{:S(2)}, u32[]{:S(2)}) collective-permute-start(bf16[4,256,128]{2,1,0:T(8,128)(2,1)S(1)} %pad_maximum_fusion.refs_0_), channel_id=1, source_target_pairs={{0,2},{2,4},{4,6},{6,0},{8,10},{10,12},{12,14},{14,8},{16,18},{18,... | collective-permute-start | bytes 786440 | tf_op jit(solution)/shard_map/ppermute | solution.py:347
  30.3 0.7 copy-start.1
  30.3 0.8 copy-start.2
  31.0 0.9 copy-start.3
  31.1 29.5 %collective-permute-start.7 = (bf16[256,1024]{1,0:T(8,128)(2,1)}, bf16[256,1024]{1,0:T(8,128)(2,1)}, u32[]{:S(2)}, u32[]{:S(2)}) collective-permute-start(bf16[256,1024]{1,0:T(8,128)(2,1)} %refs_8_.2), channel_id=1, source_target_pairs={{0,16},{2,18},{4,20},{6,22},{8,0},{10,2},{12,4},{14,6},{24,8},{26,... | collective-permute-start | bytes 1572872 | tf_op jit(solution)/shard_map/ppermute | solution.py:359
  31.9 28.7 %collective-permute-start.8 = (bf16[256,1024]{1,0:T(8,128)(2,1)}, bf16[256,1024]{1,0:T(8,128)(2,1)}, u32[]{:S(2)}, u32[]{:S(2)}) collective-permute-start(bf16[256,1024]{1,0:T(8,128)(2,1)} %collective-permute-done.6.refs_9_), channel_id=1, source_target_pairs={{0,8},{2,10},{4,12},{6,14},{8,24},{10,26},{12,28},{14,30},{24,16},... | collective-permute-start | bytes 1572872 | tf_op jit(solution)/shard_map/ppermute | solution.py:359
  41.3 19.4 %all-to-all-start.1 = ((f32[16,1,2,16,128]{4,3,2,1,0:T(8,128)}), f32[16,1,2,16,128]{4,3,2,1,0:T(8,128)}, u32[]{:S(2)}, u32[]{:S(2)}) async-start(f32[16,1,2,16,128]{4,3,2,1,0:T(8,128)} %bitcast.19), calls=%async_computation.1 | async-start | bytes 524288 | tf_op jit(solution)/shard_map/all_to_all | solution.py:557
  45.5 6.4 %collective-permute-start.10 = (bf16[2,128,256]{2,1,0:T(8,128)(2,1)}, bf16[2,128,256]{2,1,0:T(8,128)(2,1)S(1)}, u32[]{:S(2)}, u32[]{:S(2)}) collective-permute-start(bf16[2,128,256]{2,1,0:T(8,128)(2,1)} %get-tuple-element.66), channel_id=1, source_target_pairs={{0,2},{2,4},{4,6},{6,0},{8,10},{10,12},{12,14},{14,8},{16,18},{18,... | collective-permute-start | bytes 393224 | tf_op jit(solution)/shard_map/ppermute | solution.py:347
  47.2 6.0 %collective-permute-start.12 = (bf16[2,128,256]{2,1,0:T(8,128)(2,1)}, bf16[2,128,256]{2,1,0:T(8,128)(2,1)S(1)}, u32[]{:S(2)}, u32[]{:S(2)}) collective-permute-start(bf16[2,128,256]{2,1,0:T(8,128)(2,1)} %get-tuple-element.67), channel_id=1, source_target_pairs={{0,4},{2,6},{4,0},{6,2},{8,12},{10,14},{12,8},{14,10},{16,20},{18,... | collective-permute-start | bytes 393224 | tf_op jit(solution)/shard_map/ppermute | solution.py:347
  48.7 5.6 %collective-permute-start.14 = (bf16[2,128,256]{2,1,0:T(8,128)(2,1)}, bf16[2,128,256]{2,1,0:T(8,128)(2,1)S(1)}, u32[]{:S(2)}, u32[]{:S(2)}) collective-permute-start(bf16[2,128,256]{2,1,0:T(8,128)(2,1)} %get-tuple-element.68), channel_id=1, source_target_pairs={{0,6},{2,0},{4,2},{6,4},{8,14},{10,8},{12,10},{14,12},{16,22},{18,... | collective-permute-start | bytes 393224 | tf_op jit(solution)/shard_map/ppermute | solution.py:347
  51.8 1.4 %copy-start.4 = (bf16[2,128,256]{2,1,0:T(8,128)(2,1)}, bf16[2,128,256]{2,1,0:T(8,128)(2,1)S(1)}, u32[]{:S(2)}) copy-start(bf16[2,128,256]{2,1,0:T(8,128)(2,1)S(1)} %collective-permute-done.10.refs_1_) | copy-start | bytes 393220
  51.8 2.5 %collective-permute-start.9 = (bf16[2,128,256]{2,1,0:T(8,128)(2,1)}, bf16[2,128,256]{2,1,0:T(8,128)(2,1)}, u32[]{:S(2)}, u32[]{:S(2)}) collective-permute-start(bf16[2,128,256]{2,1,0:T(8,128)(2,1)} %get-tuple-element.65.refs_0_), channel_id=1, source_target_pairs={{0,1},{1,0},{2,3},{3,2},{4,5},{5,4},{6,7},{7,6},{8,9},{9,8},{10,11... | collective-permute-start | bytes 393224 | tf_op jit(solution)/shard_map/ppermute | solution.py:347
  53.2 3.0 %copy-start.5 = (bf16[2,128,256]{2,1,0:T(8,128)(2,1)}, bf16[2,128,256]{2,1,0:T(8,128)(2,1)S(1)}, u32[]{:S(2)}) copy-start(bf16[2,128,256]{2,1,0:T(8,128)(2,1)S(1)} %collective-permute-done.12.refs_2_) | copy-start | bytes 393220
  53.2 3.0 %collective-permute-start.11 = (bf16[2,128,256]{2,1,0:T(8,128)(2,1)S(1)}, bf16[2,128,256]{2,1,0:T(8,128)(2,1)S(1)}, u32[]{:S(2)}, u32[]{:S(2)}) collective-permute-start(bf16[2,128,256]{2,1,0:T(8,128)(2,1)S(1)} %collective-permute-done.10.refs_1_), channel_id=1, source_target_pairs={{0,1},{1,0},{2,3},{3,2},{4,5},{5,4},{6,7},{7,6},{8,9},{9,8},{10,11... | collective-permute-start | bytes 393224 | tf_op jit(solution)/shard_map/ppermute | solution.py:347
  54.3 1.9 %copy-start.6 = (bf16[2,128,256]{2,1,0:T(8,128)(2,1)}, bf16[2,128,256]{2,1,0:T(8,128)(2,1)S(1)}, u32[]{:S(2)}) copy-start(bf16[2,128,256]{2,1,0:T(8,128)(2,1)S(1)} %collective-permute-done.14.refs_3_) | copy-start | bytes 393220
  54.3 1.8 %collective-permute-start.13 = (bf16[2,128,256]{2,1,0:T(8,128)(2,1)S(1)}, bf16[2,128,256]{2,1,0:T(8,128)(2,1)S(1)}, u32[]{:S(2)}, u32[]{:S(2)}) collective-permute-start(bf16[2,128,256]{2,1,0:T(8,128)(2,1)S(1)} %collective-permute-done.12.refs_2_), channel_id=1, source_target_pairs={{0,1},{1,0},{2,3},{3,2},{4,5},{5,4},{6,7},{7,6},{8,9},{9,8},{10,11... | collective-permute-start | bytes 393224 | tf_op jit(solution)/shard_map/ppermute | solution.py:347
  54.3 1.9 %collective-permute-start.15 = (bf16[2,128,256]{2,1,0:T(8,128)(2,1)S(1)}, bf16[2,128,256]{2,1,0:T(8,128)(2,1)S(1)}, u32[]{:S(2)}, u32[]{:S(2)}) collective-permute-start(bf16[2,128,256]{2,1,0:T(8,128)(2,1)S(1)} %collective-permute-done.14.refs_3_), channel_id=1, source_target_pairs={{0,1},{1,0},{2,3},{3,2},{4,5},{5,4},{6,7},{7,6},{8,9},{9,8},{10,11... | collective-permute-start | bytes 393224 | tf_op jit(solution)/shard_map/ppermute | solution.py:347
  56.2 0.7 copy-start.7
  56.2 4.4 %copy-start.8 = (bf16[2,128,256]{2,1,0:T(8,128)(2,1)}, bf16[2,128,256]{2,1,0:T(8,128)(2,1)S(1)}, u32[]{:S(2)}) copy-start(bf16[2,128,256]{2,1,0:T(8,128)(2,1)S(1)} %collective-permute-done.13.refs_6_) | copy-start | bytes 393220
  56.8 3.8 %copy-start.9 = (bf16[2,128,256]{2,1,0:T(8,128)(2,1)}, bf16[2,128,256]{2,1,0:T(8,128)(2,1)S(1)}, u32[]{:S(2)}) copy-start(bf16[2,128,256]{2,1,0:T(8,128)(2,1)S(1)} %collective-permute-done.15.refs_7_) | copy-start | bytes 393220
  62.4 14.9 %all-to-all-start.2 = ((f32[16,1,2,16,128]{4,3,2,1,0:T(8,128)}), f32[16,1,2,16,128]{4,3,2,1,0:T(8,128)}, u32[]{:S(2)}, u32[]{:S(2)}) async-start(f32[16,1,2,16,128]{4,3,2,1,0:T(8,128)} %shard_map.120), calls=%async_computation.2 | async-start | bytes 524288 | tf_op jit(solution)/shard_map/all_to_all | solution.py:563
  71.8 13.5 %collective-permute-start.16 = (bf16[128,1024]{1,0:T(8,128)(2,1)}, bf16[128,1024]{1,0:T(8,128)(2,1)}, u32[]{:S(2)}, u32[]{:S(2)}) collective-permute-start(bf16[128,1024]{1,0:T(8,128)(2,1)} %get-tuple-element.85), channel_id=1, source_target_pairs={{0,6},{2,0},{4,2},{6,4},{8,14},{10,8},{12,10},{14,12},{16,22},{18,... | collective-permute-start | bytes 786440 | tf_op jit(solution)/shard_map/ppermute | solution.py:347
  74.7 13.5 %collective-permute-start.17 = (bf16[128,1024]{1,0:T(8,128)(2,1)}, bf16[128,1024]{1,0:T(8,128)(2,1)}, u32[]{:S(2)}, u32[]{:S(2)}) collective-permute-start(bf16[128,1024]{1,0:T(8,128)(2,1)} %get-tuple-element.86), channel_id=1, source_target_pairs={{0,4},{2,6},{4,0},{6,2},{8,12},{10,14},{12,8},{14,10},{16,20},{18,... | collective-permute-start | bytes 786440 | tf_op jit(solution)/shard_map/ppermute | solution.py:347
  75.2 12.9 %collective-permute-start.18 = (bf16[128,1024]{1,0:T(8,128)(2,1)}, bf16[128,1024]{1,0:T(8,128)(2,1)}, u32[]{:S(2)}, u32[]{:S(2)}) collective-permute-start(bf16[128,1024]{1,0:T(8,128)(2,1)} %get-tuple-element.87), channel_id=1, source_target_pairs={{0,2},{2,4},{4,6},{6,0},{8,10},{10,12},{12,14},{14,8},{16,18},{18,... | collective-permute-start | bytes 786440 | tf_op jit(solution)/shard_map/ppermute | solution.py:347
  88.2 2.3 %collective-permute-start.19 = (bf16[128,2048]{1,0:T(8,128)(2,1)}, bf16[128,2048]{1,0:T(8,128)(2,1)}, u32[]{:S(2)}, u32[]{:S(2)}) collective-permute-start(bf16[128,2048]{1,0:T(8,128)(2,1)} %shard_map.122.refs_4_), channel_id=1, source_target_pairs={{0,1},{1,0},{2,3},{3,2},{4,5},{5,4},{6,7},{7,6},{8,9},{9,8},{10,11... | collective-permute-start | bytes 1572872 | tf_op jit(solution)/shard_map/ppermute | solution.py:347

commit v5 on v4

--- a/solution.py
+++ b/solution.py
@@ -15,21 +15,22 @@
 epsilon = 1e-05
 f32 = jnp.float32
 bf16 = jnp.bfloat16
-VMEM_LIMIT = 64 * 1024 * 1024
+MIB = 1024 * 1024
+VMEM_LIMIT = 64 * MIB
 CHEAP = pl.CostEstimate(flops=1, bytes_accessed=1, transcendentals=0)
 
 
-def call(kernel, outs, inputs, scratch=(), copies=0, plain=0):
+def call(kernel, outs, inputs, scratch=(), copies=0, plain=0, grant=VMEM_LIMIT):
     hbm, vmem = pl.BlockSpec(memory_space=pltpu.HBM), pl.BlockSpec(memory_space=pltpu.VMEM)
     here = vmem if plain else hbm
     extra = [pltpu.SemaphoreType.DMA((copies,))] if copies else []
     return pl.pallas_call(
         kernel,
         out_shape=outs,
-        in_specs=[pl.BlockSpec(memory_space=pltpu.SMEM)] + [here] * (len(inputs) - 1),
+        in_specs=[here] * len(inputs),
         out_specs=[here] * len(outs),
         scratch_shapes=list(scratch) + extra,
-        compiler_params=pltpu.CompilerParams(vmem_limit_bytes=VMEM_LIMIT),
+        compiler_params=pltpu.CompilerParams(vmem_limit_bytes=grant),
         cost_estimate=CHEAP,
     )(*inputs)
 
@@ -72,29 +73,18 @@
     return mm(x, member), mm(high, member) + mm(low, member)
 
 
-def sums_kernel(at_ref, x_hbm, running_hbm, total_hbm, x_ref, running_ref, total_ref, sems):
+def sums_kernel(x_ref, running_ref, total_ref):
     length, channels = x_ref.shape
     width = running_ref.shape[2]
-    copies = Copies(sems)
-    cut = channels // min(4, channels // LANES)
-    loads = [copies.start(x_hbm.at[:, low : low + cut], x_ref.at[:, low : low + cut]) for low in range(0, channels, cut)]
     rows = lax.broadcasted_iota(jnp.int32, (length, length), 0)
     cols = lax.broadcasted_iota(jnp.int32, (length, length), 1)
     lower = jnp.where(rows >= cols, 1.0, 0.0).astype(bf16)
-    sums = [jnp.zeros((length, width), f32)] * 2
-    for at, load in enumerate(loads):
-        load.wait()
-        new = group_sums(x_ref[:, at * cut : (at + 1) * cut], at * cut, width)
-        sums = [old + more for old, more in zip(sums, new)]
-    for at in range(2):
-        one, two, three = pieces(sums[at])
+    for at, value in enumerate(group_sums(x_ref[...], 0, width)):
+        one, two, three = pieces(value)
         running = mm(lower, one) + mm(lower, two) + mm(lower, three)
         running_ref[at] = running
         for peer in range(total_ref.shape[0]):
             total_ref[peer, at : at + 1, :] = running[length - 1 : length, :]
-    stores = [copies.start(total_ref, total_hbm), copies.start(running_ref, running_hbm)]
-    for store in stores:
-        store.wait()
 
 
 def times(a, b):
@@ -118,7 +108,7 @@
     lax.fori_loop(0, NDIM, one, 0)
 
 
-def feed_kernel(members, at_ref, *refs):
+def feed_kernel(members, *refs):
     x_hbm, sums_hbm, running_hbm, gain_hbm, bias_hbm, decay_hbm, phase_hbm, in_hbm, out_hbm = refs[:9]
     near_hbm, (dense_hbm, fresh_hbm, end_hbm, q_hbm, w_hbm) = refs[9 : 9 + members], refs[9 + members : 14 + members]
     (
@@ -138,7 +128,7 @@
     tiles = channels // LANES
     chunks = length // CHUNK
     subs, _, depth = near_hbm[0].shape
-    me = at_ref[0]
+    me = lax.axis_index("ctx")
     peers = sums_ref.shape[0]
 
     loads[0].wait()
@@ -232,7 +222,7 @@
     ends.wait()
 
 
-def scan_kernel(length, at_ref, ends_ref, q_ref, out_ref):
+def scan_kernel(length, ends_ref, q_ref, out_ref):
     peers = ends_ref.shape[0]
     result, base, left = None, (q_ref[:, 0], q_ref[:, 1]), length
     while left:
@@ -250,7 +240,7 @@
 
 
 def mix_kernel(
-    at_ref, incoming_hbm, fresh_hbm, dense_hbm, q_hbm, w_hbm, skip_hbm, mixed_hbm,
+    incoming_hbm, fresh_hbm, dense_hbm, q_hbm, w_hbm, skip_hbm, mixed_hbm,
     incoming_ref, fresh_ref, dense_ref, q_ref, w_ref, skip_ref, mixed_ref, start_ref, coef_ref, tap_ref, out_ref, sems,
 ):
     copies = Copies(sems)
@@ -368,14 +358,15 @@
     return [along(block, axis, k, count) for k in range(1, count)]
 
 
-def part_kernel(members, tp, layers, at_ref, *refs):
+def part_kernel(members, tp, layers, *refs):
     blocks_hbm, refs = refs[: members * tp], refs[members * tp :]
     weights_hbm, refs = refs[:layers], refs[layers:]
     own_hbm, sent_hbm, refs = refs[0], refs[1:members], refs[members:]
     row_ref, weight_ref, own_ref, sent_ref, sems = refs
     copies = Copies(sems)
     subs, length, depth = blocks_hbm[0].shape
-    half, ring_at = at_ref[1], at_ref[2]
+    half, place = lax.axis_index("tp"), lax.axis_index("ctx")
+    ring_at = sum(jnp.where(place // members == at, k, 0) for k, at in enumerate(ring_of(layers)))
     loads = [copies.start(weight, weight_ref.at[at]) for at, weight in enumerate(weights_hbm)]
     for away in range(tp):
         other = lax.rem(half + tp - away, tp)
@@ -409,7 +400,7 @@
         store.wait()
 
 
-def attend_kernel(members, tp, at_ref, *refs):
+def attend_kernel(members, tp, *refs):
     weights_hbm, refs = refs[:members], refs[members:]
     mixed_hbm, refs = refs[:tp], refs[tp:]
     parts_hbm, refs = refs[: members - 1], refs[members - 1 :]
@@ -424,7 +415,7 @@
     loads += [copies.start(own_hbm, own_ref)] + [copies.start(a, part_ref.at[k]) for k, a in enumerate(parts_hbm)]
     _, layers, depth, head = weight_ref.shape
     _, length, channels = mixed_ref.shape
-    place, half = at_ref[0], at_ref[1]
+    place, half = lax.axis_index("ctx"), lax.axis_index("tp")
     member, layer = lax.rem(place, members), lax.div(place, members)
     blocks = channels // depth
 
@@ -467,7 +458,7 @@
         scores = jnp.where(row >= col, scores, -1e30)
         weights = jnp.exp(scores - jnp.max(scores, axis=1, keepdims=True))
         probabilities = (weights / jnp.sum(weights, axis=1, keepdims=True)).astype(bf16)
-        result_ref[here, :] = mm(probabilities, value_ref[here, :]).astype(bf16)
+        result_ref[:] = mm(probabilities, value_ref[:]).astype(bf16)
     copies.start(result_ref, result_hbm).wait()
 
 
@@ -487,30 +478,27 @@
     layers = peers // members
     subs = blocks // members
     shape, vmem = jax.ShapeDtypeStruct, pltpu.VMEM
-    ring_at = sum(jnp.where(place // members == at, k, 0) for k, at in enumerate(ring_of(layers)))
-    here = jnp.stack([place, half, ring_at]).astype(jnp.int32)
 
     running, totals = call(
         sums_kernel,
         [shape((2, length, width), f32), shape((peers, 2, width), f32)],
-        [here, tokens],
-        [vmem((length, channels), bf16), vmem((2, length, width), f32), vmem((peers, 2, width), f32)],
-        8,
+        [tokens],
+        plain=1,
+        grant=16 * MIB,
     )
+    all_v = [v_weight]
+    if layers > 1:
+        all_v.append(ring_on(v_weight, members, layers, 1))
+    sums = lax.all_to_all(totals, "ctx", 0, 0)
     line_z = [z_weight] + [
         lax.ppermute(z_weight, "ctx", [(i, (i + members * k) % peers) for i in range(peers)])
         for k in range(1, layers)
     ]
-    totals, line_z, v_weight = lax.optimization_barrier((totals, line_z, v_weight))
-    sums = lax.all_to_all(totals, "ctx", 0, 0)
     line_z = jnp.stack(line_z)
+    sums, all_v, line_z = lax.optimization_barrier((sums, all_v, line_z))
+    if layers > 2:
+        all_v.append(ring_on(v_weight, members, layers, -1))
     all_z = [line_z] + [along(line_z, "ctx", k, members) for k in range(1, members)]
-    all_v = [v_weight]
-    if layers > 1:
-        all_v.append(ring_on(v_weight, members, layers, 1))
-    sums, all_z, all_v = lax.optimization_barrier((sums, all_z, all_v))
-    for k in range(2, layers):
-        all_v.append(ring_on(all_v[max(k - 2, 0)], members, layers, (-1) ** (k + 1)))
 
     rows = NDIM * 2 * tiles
     *near, dense, fresh, ends, q, w = call(
@@ -523,7 +511,7 @@
             shape((rows, LANES), f32),
             shape((rows, LANES), f32),
         ],
-        [here, tokens, sums, running, norm_gain[None], norm_bias[None], ema_decay, ema_phase, ema_in, ema_out],
+        [tokens, sums, running, norm_gain[None], norm_bias[None], ema_decay, ema_phase, ema_in, ema_out],
         [
             vmem((length, channels), bf16),
             vmem((peers, 2, width), f32),
@@ -555,17 +543,21 @@
         return a.reshape(NDIM, 2, tiles, LANES)
 
     arrived = lax.all_to_all(split(ends), "ctx", 0, 0)
+    near, all_z = lax.optimization_barrier((near, all_z))
     near = near[:1] + [along(near[k], "ctx", k, members) for k in range(1, members)]
+    near, all_v[1] = lax.optimization_barrier((near, all_v[1]))
+    for k in range(3, layers):
+        all_v.append(ring_on(all_v[k - 2], members, layers, (-1) ** (k + 1)))
     far = [along(block, "tp", k, tp) for k in range(1, tp) for block in near]
     my_q = lax.dynamic_index_in_dim(split(q.reshape(NDIM, 2, tiles, LANES)), place, 0, False)
-    arrived, all_v, far, my_q = lax.optimization_barrier((arrived, all_v, far, my_q))
-    (starts,) = call(functools.partial(scan_kernel, length), [shape(arrived.shape, f32)], [here, arrived, my_q], plain=1)
+    arrived, far, my_q, all_v[2] = lax.optimization_barrier((arrived, far, my_q, all_v[2]))
+    (starts,) = call(functools.partial(scan_kernel, length), [shape(arrived.shape, f32)], [arrived, my_q], plain=1, grant=16 * MIB)
     incoming = lax.all_to_all(starts, "ctx", 0, 0)
 
     own, *sent = call(
         functools.partial(part_kernel, members, tp, layers),
         [shape((length, columns), f32)] + [shape((length, columns), bf16)] * (members - 1),
-        [here, *near, *far, *all_v],
+        [*near, *far, *all_v],
         [
             vmem((layers, members * length, depth), bf16),
             vmem((layers, depth, columns), bf16),
@@ -580,7 +572,7 @@
     (mixed_rows,) = call(
         mix_kernel,
         [shape((length, channels), bf16)],
-        [here, join(incoming), fresh, dense, q, w, ema_skip.reshape(tiles, LANES)],
+        [join(incoming), fresh, dense, q, w, ema_skip.reshape(tiles, LANES)],
         [
             vmem((NDIM, 2, tiles, LANES), f32),
             vmem((NDIM, chunks, 2, tiles, LANES), f32),
@@ -597,10 +589,11 @@
         6 + max(1, tiles // 8),
     )
     mixed_rows, returned = lax.optimization_barrier((mixed_rows, returned))
+    apart = others(mixed_rows, "tp")
     (result,) = call(
         functools.partial(attend_kernel, members, tp),
         [shape((length, columns), bf16)],
-        [here, *all_z, mixed_rows, *others(mixed_rows, "tp"), *returned, own, rms_gain[None], qk_affine],
+        [*all_z, mixed_rows, *apart, *returned, own, rms_gain[None], qk_affine],
         [
             vmem((members, layers, depth, head), bf16),
             vmem((tp, length, channels), bf16),

time: 95.2 us -> 87.9 us (0.923)
  blocking collectives: 13.6 us -> 0 us
  starting transfers between devices: 31.6 us -> 38.8 us
  Pallas kernels: 30.3 us -> 24.5 us
  waiting for transfers between devices: 14.6 us -> 19.9 us
    all_to_all x1 -> x0, blocking collectives: 13.6 us -> none  [body(): sums = lax.all_to_all(totals, 'ctx', 0, 0)]
    all_to_all x0 -> x1, starting transfers between devices: none -> 6.23 us  [body(): sums = lax.all_to_all(totals, 'ctx', 0, 0)]
    pallas_call x6, Pallas kernels: 30.3 us -> 24.5 us  [call(): pl.pallas_call(kernel, out_shape=outs, in_specs=[here] * len(inputs), out...]
    ppermute x3, waiting for transfers between devices: 0.01 us -> 5.65 us  [body(): lax.ppermute(z_weight, 'ctx', [(i, (i + members * k) % peers) for i in ra...]
    ppermute x3, starting transfers between devices: 2.09 us -> 6.75 us  [ring_on(): return lax.ppermute(block, 'ctx', pairs)]
    ppermute x3, waiting for transfers between devices: 0.01 us -> 4.54 us  [ring_on(): return lax.ppermute(block, 'ctx', pairs)]
    ppermute x3, starting transfers between devices: 7.86 us -> 4.05 us  [body(): lax.ppermute(z_weight, 'ctx', [(i, (i + members * k) % peers) for i in ra...]
    all_to_all x1, waiting for transfers between devices: 3.8 us -> 0.01 us  [body(): arrived = lax.all_to_all(split(ends), 'ctx', 0, 0)]
  transfers between devices with their start and end apart: 22 -> 23, of which waited for: 7 -> 11; matrix products, arithmetic and copies ran while one was open for 3% -> 3% of each run, Pallas kernels for 26% -> 24%
where the time goes in v5:
time: 87.9 us; the launch traced here: 87.4 us
  starting transfers between devices  38.8 us (44%)
  Pallas kernels  24.5 us (28%)
  waiting for transfers between devices  19.9 us (23%)
  local copies, waits for them, and re-layouts  2.42 us (3%)
  other arithmetic  1.57 us (2%)
    pallas_call x6, Pallas kernels, call(): pl.pallas_call(kernel, out_shape=outs, in_specs=[here] * len(inputs), out...  24.5 us
    ppermute x14, starting transfers between devices, along(): return lax.ppermute(block, axis, pairs)  11.6 us
    ppermute x14, waiting for transfers between devices, along(): return lax.ppermute(block, axis, pairs)  9.18 us
    ppermute x3, starting transfers between devices, ring_on(): return lax.ppermute(block, 'ctx', pairs)  6.75 us
    all_to_all x1, starting transfers between devices, body(): sums = lax.all_to_all(totals, 'ctx', 0, 0)  6.23 us
    ppermute x3, waiting for transfers between devices, body(): lax.ppermute(z_weight, 'ctx', [(i, (i + members * k) % peers) for i in ra...  5.65 us
    all_to_all x1, starting transfers between devices, body(): arrived = lax.all_to_all(split(ends), 'ctx', 0, 0)  5.17 us
    all_to_all x1, starting transfers between devices, body(): incoming = lax.all_to_all(starts, 'ctx', 0, 0)  4.98 us
  transfers between devices with their start and end apart: 23, of which 11 were waited for; matrix products, arithmetic and copies ran while one was open for 3% of the time, Pallas kernels for 24%

profile of v5, /device:TPU:0, one launch (start us, length us, event | category | flops | bytes accessed | tf_op | source)
XLA Modules:
  0.0 87.4 jit_solution(16884905725189046371)
XLA Ops:
  0.0 3.0 %collective-permute-start = (bf16[256,1024]{1,0:T(8,128)(2,1)}, bf16[256,1024]{1,0:T(8,128)(2,1)}, u32[]{:S(2)}, u32[]{:S(2)}) collective-permute-start(bf16[256,1024]{1,0:T(8,128)(2,1)} %refs_8_.2), channel_id=1, source_target_pairs={{0,8},{2,10},{4,12},{6,14},{8,24},{10,26},{12,28},{14,30},{24,16},... | collective-permute-start | bytes 1572872 | tf_op jit(solution)/shard_map/ppermute | solution.py:349
  3.0 2.6 %collective-permute-start.1 = (bf16[256,128]{1,0:T(8,128)(2,1)}, bf16[256,128]{1,0:T(8,128)(2,1)S(1)}, u32[]{:S(2)}, u32[]{:S(2)}) collective-permute-start(bf16[256,128]{1,0:T(8,128)(2,1)} %param.21), channel_id=1, source_target_pairs={{0,8},{2,10},{4,12},{6,14},{8,16},{10,18},{12,20},{14,22},{16,24},... | collective-permute-start | bytes 196616 | tf_op jit(solution)/shard_map/ppermute | solution.py:494
  5.6 1.2 %collective-permute-start.3 = (bf16[256,128]{1,0:T(8,128)(2,1)}, bf16[256,128]{1,0:T(8,128)(2,1)S(1)}, u32[]{:S(2)}, u32[]{:S(2)}) collective-permute-start(bf16[256,128]{1,0:T(8,128)(2,1)} %param.21), channel_id=1, source_target_pairs={{0,24},{2,26},{4,28},{6,30},{8,0},{10,2},{12,4},{14,6},{16,8},{18,... | collective-permute-start | bytes 196616 | tf_op jit(solution)/shard_map/ppermute | solution.py:494
  6.8 0.2 collective-permute-start.2
  7.1 1.0 %copy-done = bf16[128,2048]{1,0:T(8,128)(2,1)S(1)} copy-done((bf16[128,2048]{1,0:T(8,128)(2,1)S(1)}, bf16[128,2048]{1,0:T(8,128)(2,1)}, u32[]{:S(2)}) %copy-start) | copy-done | bytes 524312
  8.1 1.4 %shard_map.118 = (f32[2,128,128]{2,1,0:T(8,128)S(1)}, f32[16,2,128]{2,1,0:T(2,128)}) custom-call(bf16[128,2048]{1,0:T(8,128)(2,1)S(1)} %copy-done), custom_call_target="tpu_custom_call" | custom-call | flops 1 | bytes 1 | tf_op jit(solution)/shard_map/pallas_call | solution.py:27
  9.6 0.6 copy-done.1
  10.2 6.2 %all-to-all-start = ((f32[16,2,128]{2,1,0:T(2,128)}), f32[16,2,128]{2,1,0:T(2,128)}, u32[]{:S(2)}, u32[]{:S(2)}) async-start(f32[16,2,128]{2,1,0:T(2,128)} %get-tuple-element.50), calls=%async_computation | async-start | bytes 32768 | tf_op jit(solution)/shard_map/all_to_all | solution.py:492
  16.4 3.6 %collective-permute-done.1 = bf16[256,128]{1,0:T(8,128)(2,1)S(1)} collective-permute-done((bf16[256,128]{1,0:T(8,128)(2,1)}, bf16[256,128]{1,0:T(8,128)(2,1)S(1)}, u32[]{:S(2)}, u32[]{:S(2)}) %collective-permute-start.1) | collective-permute-done | bytes 65568 | tf_op jit(solution)/shard_map/ppermute | solution.py:494
  20.0 0.0 collective-permute-done.3
  20.0 2.1 %collective-permute-done.2 = bf16[256,128]{1,0:T(8,128)(2,1)S(1)} collective-permute-done((bf16[256,128]{1,0:T(8,128)(2,1)}, bf16[256,128]{1,0:T(8,128)(2,1)S(1)}, u32[]{:S(2)}, u32[]{:S(2)}) %collective-permute-start.2) | collective-permute-done | bytes 65568 | tf_op jit(solution)/shard_map/ppermute | solution.py:494
  22.1 1.6 %pad_maximum_fusion.refs_0_ = bf16[4,256,128]{2,1,0:T(8,128)(2,1)} fusion(bf16[1,256,128]{2,1,0:T(8,128)(2,1)S(1)} %bitcast.19, bf16[1,256,128]{2,1,0:T(8,128)(2,1)S(1)} %bitcast.20, bf16[1,256,128]{2,1,0:T(8,128)(2,1)S(1)} %bitcast.18, bf16[1,256,128]{2,1,0:T(8,128)(2,1)} %bitcast.17), kind=kLoop, calls=%fused_computation | loop fusion | flops 393216 | bytes 524288 | tf_op jit(solution)/shard_map/stack | solution.py:497
  23.7 0.5 all-to-all-done.refs_1_
  24.2 0.0 collective-permute-done.refs_9_
  24.2 2.0 %collective-permute-start.6 = (bf16[4,256,128]{2,1,0:T(8,128)(2,1)}, bf16[4,256,128]{2,1,0:T(8,128)(2,1)}, u32[]{:S(2)}, u32[]{:S(2)}) collective-permute-start(bf16[4,256,128]{2,1,0:T(8,128)(2,1)} %pad_maximum_fusion.refs_0_), channel_id=1, source_target_pairs={{0,6},{2,0},{4,2},{6,4},{8,14},{10,8},{12,10},{14,12},{16,22},{18,... | collective-permute-start | bytes 786440 | tf_op jit(solution)/shard_map/ppermute | solution.py:337
  26.2 0.5 collective-permute-start.5
  26.7 0.6 collective-permute-start.4
  27.3 2.2 %collective-permute-start.14 = (bf16[256,1024]{1,0:T(8,128)(2,1)}, bf16[256,1024]{1,0:T(8,128)(2,1)}, u32[]{:S(2)}, u32[]{:S(2)}) collective-permute-start(bf16[256,1024]{1,0:T(8,128)(2,1)} %refs_8_.2), channel_id=1, source_target_pairs={{0,16},{2,18},{4,20},{6,22},{8,0},{10,2},{12,4},{14,6},{24,8},{26,... | collective-permute-start | bytes 1572872 | tf_op jit(solution)/shard_map/ppermute | solution.py:349
  29.5 7.4 %shard_map.119 = (bf16[2,128,256]{2,1,0:T(8,128)(2,1)}, bf16[2,128,256]{2,1,0:T(8,128)(2,1)}, bf16[2,128,256]{2,1,0:T(8,128)(2,1)}, bf16[2,128,256]{2,1,0:T(8,12...) custom-call(bf16[128,2048]{1,0:T(8,128)(2,1)} %refs_0_.1, ...), custom_call_target="tpu_custom_call" | custom-call | flops 1 | bytes 1 | tf_op jit(solution)/shard_map/pallas_call | solution.py:27
  36.9 5.2 %all-to-all-start.1 = ((f32[16,1,2,16,128]{4,3,2,1,0:T(8,128)}), f32[16,1,2,16,128]{4,3,2,1,0:T(8,128)S(1)}, u32[]{:S(2)}, u32[]{:S(2)}) async-start(f32[16,1,2,16,128]{4,3,2,1,0:T(8,128)} %bitcast.16), calls=%async_computation.1 | async-start | bytes 524288 | tf_op jit(solution)/shard_map/all_to_all | solution.py:545
  42.1 0.0 collective-permute-done.5.refs_2_
  42.1 0.0 collective-permute-done.4.refs_1_
  42.1 2.0 %collective-permute-start.7 = (bf16[2,128,256]{2,1,0:T(8,128)(2,1)}, bf16[2,128,256]{2,1,0:T(8,128)(2,1)S(1)}, u32[]{:S(2)}, u32[]{:S(2)}) collective-permute-start(bf16[2,128,256]{2,1,0:T(8,128)(2,1)} %get-tuple-element.64), channel_id=1, source_target_pairs={{0,2},{2,4},{4,6},{6,0},{8,10},{10,12},{12,14},{14,8},{16,18},{18,... | collective-permute-start | bytes 393224 | tf_op jit(solution)/shard_map/ppermute | solution.py:337
  44.1 1.5 %collective-permute-start.8 = (bf16[2,128,256]{2,1,0:T(8,128)(2,1)}, bf16[2,128,256]{2,1,0:T(8,128)(2,1)S(1)}, u32[]{:S(2)}, u32[]{:S(2)}) collective-permute-start(bf16[2,128,256]{2,1,0:T(8,128)(2,1)} %get-tuple-element.65), channel_id=1, source_target_pairs={{0,4},{2,6},{4,0},{6,2},{8,12},{10,14},{12,8},{14,10},{16,20},{18,... | collective-permute-start | bytes 393224 | tf_op jit(solution)/shard_map/ppermute | solution.py:337
  45.5 1.5 %collective-permute-start.9 = (bf16[2,128,256]{2,1,0:T(8,128)(2,1)}, bf16[2,128,256]{2,1,0:T(8,128)(2,1)S(1)}, u32[]{:S(2)}, u32[]{:S(2)}) collective-permute-start(bf16[2,128,256]{2,1,0:T(8,128)(2,1)} %get-tuple-element.66), channel_id=1, source_target_pairs={{0,6},{2,0},{4,2},{6,4},{8,14},{10,8},{12,10},{14,12},{16,22},{18,... | collective-permute-start | bytes 393224 | tf_op jit(solution)/shard_map/ppermute | solution.py:337
  47.0 2.2 %collective-permute-done.7.refs_1_ = bf16[2,128,256]{2,1,0:T(8,128)(2,1)S(1)} collective-permute-done((bf16[2,128,256]{2,1,0:T(8,128)(2,1)}, bf16[2,128,256]{2,1,0:T(8,128)(2,1)S(1)}, u32[]{:S(2)}, u32[]{:S(2)}) %collective-permute-start.7) | collective-permute-done | bytes 131104 | tf_op jit(solution)/shard_map/ppermute | solution.py:337
  49.3 1.9 %collective-permute-done.8.refs_2_ = bf16[2,128,256]{2,1,0:T(8,128)(2,1)S(1)} collective-permute-done((bf16[2,128,256]{2,1,0:T(8,128)(2,1)}, bf16[2,128,256]{2,1,0:T(8,128)(2,1)S(1)}, u32[]{:S(2)}, u32[]{:S(2)}) %collective-permute-start.8) | collective-permute-done | bytes 131104 | tf_op jit(solution)/shard_map/ppermute | solution.py:337
  51.1 0.2 collective-permute-done.9.refs_3_
  51.3 1.5 %collective-permute-start.15 = (bf16[256,1024]{1,0:T(8,128)(2,1)}, bf16[256,1024]{1,0:T(8,128)(2,1)}, u32[]{:S(2)}, u32[]{:S(2)}) collective-permute-start(bf16[256,1024]{1,0:T(8,128)(2,1)} %collective-permute-done.refs_9_), channel_id=1, source_target_pairs={{0,8},{2,10},{4,12},{6,14},{8,24},{10,26},{12,28},{14,30},{24,16},... | collective-permute-start | bytes 1572872 | tf_op jit(solution)/shard_map/ppermute | solution.py:349
  52.8 0.5 collective-permute-start.11
  53.3 0.0 collective-permute-start.12
  53.3 0.0 collective-permute-done.14.refs_10_
  53.3 0.5 collective-permute-start.13
  53.8 0.7 dynamic-slice_bitcast_fusion.q_ref
  54.6 0.0 all-to-all-done.1.ends_ref
  54.6 0.1 collective-permute-done.12.refs_6_
  54.7 0.2 collective-permute-done.13.refs_7_
  54.9 0.8 shard_map.120
  55.6 5.0 %all-to-all-start.2 = ((f32[16,1,2,16,128]{4,3,2,1,0:T(8,128)}), f32[16,1,2,16,128]{4,3,2,1,0:T(8,128)}, u32[]{:S(2)}, u32[]{:S(2)}) async-start(f32[16,1,2,16,128]{4,3,2,1,0:T(8,128)} %shard_map.120), calls=%async_computation.2 | async-start | bytes 524288 | tf_op jit(solution)/shard_map/all_to_all | solution.py:555
  60.7 4.5 %collective-permute-done.15.refs_11_ = bf16[256,1024]{1,0:T(8,128)(2,1)} collective-permute-done((bf16[256,1024]{1,0:T(8,128)(2,1)}, bf16[256,1024]{1,0:T(8,128)(2,1)}, u32[]{:S(2)}, u32[]{:S(2)}) %collective-permute-start.15) | collective-permute-done | bytes 524320 | tf_op jit(solution)/shard_map/ppermute | solution.py:349
  65.2 4.1 %shard_map.121 = (f32[128,1024]{1,0:T(8,128)}, bf16[128,1024]{1,0:T(8,128)(2,1)}, bf16[128,1024]{1,0:T(8,128)(2,1)}, bf16[128,1024]{1,0:T(8,128)(2,1)}) custom-call(bf16[2,128,256]{2,1,0:T(8,128)(2,1)} %get-tuple-element.68.refs_0_, bf16[2,128,256]{2,1,0:T(8,128)(2,1)} %copy-done.2, bf16[2,128,256]{2,1,0:T(8,128)(2,1)} %copy-done.3, ...), custom_call_target="tpu_custom_call" | custom-call | flops 1 | bytes 1 | tf_op jit(solution)/shard_map/pallas_call | solution.py:27
  69.3 0.1 collective-permute-start.16
  69.4 1.1 %collective-permute-start.17 = (bf16[128,1024]{1,0:T(8,128)(2,1)}, bf16[128,1024]{1,0:T(8,128)(2,1)}, u32[]{:S(2)}, u32[]{:S(2)}) collective-permute-start(bf16[128,1024]{1,0:T(8,128)(2,1)} %get-tuple-element.88), channel_id=1, source_target_pairs={{0,4},{2,6},{4,0},{6,2},{8,12},{10,14},{12,8},{14,10},{16,20},{18,... | collective-permute-start | bytes 786440 | tf_op jit(solution)/shard_map/ppermute | solution.py:337
  70.5 1.4 %collective-permute-start.18 = (bf16[128,1024]{1,0:T(8,128)(2,1)}, bf16[128,1024]{1,0:T(8,128)(2,1)}, u32[]{:S(2)}, u32[]{:S(2)}) collective-permute-start(bf16[128,1024]{1,0:T(8,128)(2,1)} %get-tuple-element.89), channel_id=1, source_target_pairs={{0,2},{2,4},{4,6},{6,0},{8,10},{10,12},{12,14},{14,8},{16,18},{18,... | collective-permute-start | bytes 786440 | tf_op jit(solution)/shard_map/ppermute | solution.py:337
  71.9 7.3 %shard_map.122.refs_4_ = bf16[128,2048]{1,0:T(8,128)(2,1)} custom-call(f32[16,2,16,128]{3,2,1,0:T(8,128)} %bitcast.10.incoming_hbm, f32[16,8,2,16,128]{4,3,2,1,0:T(8,128)} %get-tuple-element.84.fresh_hbm, f32[2048,128]{1,0:T(8,128)} %get-tuple-element.85.dense_hbm, f32[512,128]{1,0:T(8,128)} %get-tuple-element.72.q_hbm, f32[512,128]{1,0:T(8,128)} %get-tuple-element.86.w_hbm, ...), custom_call_target="tpu_custom_call" | custom-call | flops 1 | bytes 1 | tf_op jit(solution)/shard_map/pallas_call | solution.py:27
  79.2 2.4 %collective-permute-done.17.refs_7_ = bf16[128,1024]{1,0:T(8,128)(2,1)} collective-permute-done((bf16[128,1024]{1,0:T(8,128)(2,1)}, bf16[128,1024]{1,0:T(8,128)(2,1)}, u32[]{:S(2)}, u32[]{:S(2)}) %collective-permute-start.17) | collective-permute-done | bytes 262176 | tf_op jit(solution)/shard_map/ppermute | solution.py:337
  81.6 2.3 %collective-permute-done.19.refs_5_ = bf16[128,2048]{1,0:T(8,128)(2,1)} collective-permute-done((bf16[128,2048]{1,0:T(8,128)(2,1)}, bf16[128,2048]{1,0:T(8,128)(2,1)}, u32[]{:S(2)}, u32[]{:S(2)}) %collective-permute-start.19) | collective-permute-done | bytes 524320 | tf_op jit(solution)/shard_map/ppermute | solution.py:337
  83.9 3.5 %shard_map.123 = bf16[128,1024]{1,0:T(8,128)(2,1)} custom-call(bf16[4,256,128]{2,1,0:T(8,128)(2,1)} %pad_maximum_fusion.refs_0_, bf16[4,256,128]{2,1,0:T(8,128)(2,1)} %collective-permute-done.4.refs_1_, bf16[4,256,128]{2,1,0:T(8,128)(2,1)} %collective-permute-done.5.refs_2_, bf16[4,256,128]{2,1,0:T(8,128)(2,1)} %collective-permute-done.6.refs_3_, ...), custom_call_target="tpu_custom_call" | custom-call | flops 1 | bytes 1 | tf_op jit(solution)/shard_map/pallas_call | solution.py:27
  (24 shorter events, 0.1 us)
Async XLA Ops:
  0.0 24.2 %collective-permute-start = (bf16[256,1024]{1,0:T(8,128)(2,1)}, bf16[256,1024]{1,0:T(8,128)(2,1)}, u32[]{:S(2)}, u32[]{:S(2)}) collective-permute-start(bf16[256,1024]{1,0:T(8,128)(2,1)} %refs_8_.2), channel_id=1, source_target_pairs={{0,8},{2,10},{4,12},{6,14},{8,24},{10,26},{12,28},{14,30},{24,16},... | collective-permute-start | bytes 1572872 | tf_op jit(solution)/shard_map/ppermute | solution.py:349
  3.0 17.0 %collective-permute-start.1 = (bf16[256,128]{1,0:T(8,128)(2,1)}, bf16[256,128]{1,0:T(8,128)(2,1)S(1)}, u32[]{:S(2)}, u32[]{:S(2)}) collective-permute-start(bf16[256,128]{1,0:T(8,128)(2,1)} %param.21), channel_id=1, source_target_pairs={{0,8},{2,10},{4,12},{6,14},{8,16},{10,18},{12,20},{14,22},{16,24},... | collective-permute-start | bytes 196616 | tf_op jit(solution)/shard_map/ppermute | solution.py:494
  5.6 14.4 %collective-permute-start.3 = (bf16[256,128]{1,0:T(8,128)(2,1)}, bf16[256,128]{1,0:T(8,128)(2,1)S(1)}, u32[]{:S(2)}, u32[]{:S(2)}) collective-permute-start(bf16[256,128]{1,0:T(8,128)(2,1)} %param.21), channel_id=1, source_target_pairs={{0,24},{2,26},{4,28},{6,30},{8,0},{10,2},{12,4},{14,6},{16,8},{18,... | collective-permute-start | bytes 196616 | tf_op jit(solution)/shard_map/ppermute | solution.py:494
  6.8 15.2 %collective-permute-start.2 = (bf16[256,128]{1,0:T(8,128)(2,1)}, bf16[256,128]{1,0:T(8,128)(2,1)S(1)}, u32[]{:S(2)}, u32[]{:S(2)}) collective-permute-start(bf16[256,128]{1,0:T(8,128)(2,1)} %param.21), channel_id=1, source_target_pairs={{0,16},{2,18},{4,20},{6,22},{8,24},{10,26},{12,28},{14,30},{16,0},... | collective-permute-start | bytes 196616 | tf_op jit(solution)/shard_map/ppermute | solution.py:494
  7.1 1.0 %copy-start = (bf16[128,2048]{1,0:T(8,128)(2,1)S(1)}, bf16[128,2048]{1,0:T(8,128)(2,1)}, u32[]{:S(2)}) copy-start(bf16[128,2048]{1,0:T(8,128)(2,1)} %refs_0_.1) | copy-start | bytes 1572868
  9.6 0.6 copy-start.1
  10.2 14.0 %all-to-all-start = ((f32[16,2,128]{2,1,0:T(2,128)}), f32[16,2,128]{2,1,0:T(2,128)}, u32[]{:S(2)}, u32[]{:S(2)}) async-start(f32[16,2,128]{2,1,0:T(2,128)} %get-tuple-element.50), calls=%async_computation | async-start | bytes 32768 | tf_op jit(solution)/shard_map/all_to_all | solution.py:492
  24.2 17.9 %collective-permute-start.6 = (bf16[4,256,128]{2,1,0:T(8,128)(2,1)}, bf16[4,256,128]{2,1,0:T(8,128)(2,1)}, u32[]{:S(2)}, u32[]{:S(2)}) collective-permute-start(bf16[4,256,128]{2,1,0:T(8,128)(2,1)} %pad_maximum_fusion.refs_0_), channel_id=1, source_target_pairs={{0,6},{2,0},{4,2},{6,4},{8,14},{10,8},{12,10},{14,12},{16,22},{18,... | collective-permute-start | bytes 786440 | tf_op jit(solution)/shard_map/ppermute | solution.py:337
  26.2 15.9 %collective-permute-start.5 = (bf16[4,256,128]{2,1,0:T(8,128)(2,1)}, bf16[4,256,128]{2,1,0:T(8,128)(2,1)}, u32[]{:S(2)}, u32[]{:S(2)}) collective-permute-start(bf16[4,256,128]{2,1,0:T(8,128)(2,1)} %pad_maximum_fusion.refs_0_), channel_id=1, source_target_pairs={{0,4},{2,6},{4,0},{6,2},{8,12},{10,14},{12,8},{14,10},{16,20},{18,... | collective-permute-start | bytes 786440 | tf_op jit(solution)/shard_map/ppermute | solution.py:337
  26.7 15.4 %collective-permute-start.4 = (bf16[4,256,128]{2,1,0:T(8,128)(2,1)}, bf16[4,256,128]{2,1,0:T(8,128)(2,1)}, u32[]{:S(2)}, u32[]{:S(2)}) collective-permute-start(bf16[4,256,128]{2,1,0:T(8,128)(2,1)} %pad_maximum_fusion.refs_0_), channel_id=1, source_target_pairs={{0,2},{2,4},{4,6},{6,0},{8,10},{10,12},{12,14},{14,8},{16,18},{18,... | collective-permute-start | bytes 786440 | tf_op jit(solution)/shard_map/ppermute | solution.py:337
  27.3 26.1 %collective-permute-start.14 = (bf16[256,1024]{1,0:T(8,128)(2,1)}, bf16[256,1024]{1,0:T(8,128)(2,1)}, u32[]{:S(2)}, u32[]{:S(2)}) collective-permute-start(bf16[256,1024]{1,0:T(8,128)(2,1)} %refs_8_.2), channel_id=1, source_target_pairs={{0,16},{2,18},{4,20},{6,22},{8,0},{10,2},{12,4},{14,6},{24,8},{26,... | collective-permute-start | bytes 1572872 | tf_op jit(solution)/shard_map/ppermute | solution.py:349
  36.9 17.7 %all-to-all-start.1 = ((f32[16,1,2,16,128]{4,3,2,1,0:T(8,128)}), f32[16,1,2,16,128]{4,3,2,1,0:T(8,128)S(1)}, u32[]{:S(2)}, u32[]{:S(2)}) async-start(f32[16,1,2,16,128]{4,3,2,1,0:T(8,128)} %bitcast.16), calls=%async_computation.1 | async-start | bytes 524288 | tf_op jit(solution)/shard_map/all_to_all | solution.py:545
  42.1 7.1 %collective-permute-start.7 = (bf16[2,128,256]{2,1,0:T(8,128)(2,1)}, bf16[2,128,256]{2,1,0:T(8,128)(2,1)S(1)}, u32[]{:S(2)}, u32[]{:S(2)}) collective-permute-start(bf16[2,128,256]{2,1,0:T(8,128)(2,1)} %get-tuple-element.64), channel_id=1, source_target_pairs={{0,2},{2,4},{4,6},{6,0},{8,10},{10,12},{12,14},{14,8},{16,18},{18,... | collective-permute-start | bytes 393224 | tf_op jit(solution)/shard_map/ppermute | solution.py:337
  44.1 7.0 %collective-permute-start.8 = (bf16[2,128,256]{2,1,0:T(8,128)(2,1)}, bf16[2,128,256]{2,1,0:T(8,128)(2,1)S(1)}, u32[]{:S(2)}, u32[]{:S(2)}) collective-permute-start(bf16[2,128,256]{2,1,0:T(8,128)(2,1)} %get-tuple-element.65), channel_id=1, source_target_pairs={{0,4},{2,6},{4,0},{6,2},{8,12},{10,14},{12,8},{14,10},{16,20},{18,... | collective-permute-start | bytes 393224 | tf_op jit(solution)/shard_map/ppermute | solution.py:337
  45.5 5.7 %collective-permute-start.9 = (bf16[2,128,256]{2,1,0:T(8,128)(2,1)}, bf16[2,128,256]{2,1,0:T(8,128)(2,1)S(1)}, u32[]{:S(2)}, u32[]{:S(2)}) collective-permute-start(bf16[2,128,256]{2,1,0:T(8,128)(2,1)} %get-tuple-element.66), channel_id=1, source_target_pairs={{0,6},{2,0},{4,2},{6,4},{8,14},{10,8},{12,10},{14,12},{16,22},{18,... | collective-permute-start | bytes 393224 | tf_op jit(solution)/shard_map/ppermute | solution.py:337
  49.3 6.4 %copy-start.2 = (bf16[2,128,256]{2,1,0:T(8,128)(2,1)}, bf16[2,128,256]{2,1,0:T(8,128)(2,1)S(1)}, u32[]{:S(2)}) copy-start(bf16[2,128,256]{2,1,0:T(8,128)(2,1)S(1)} %collective-permute-done.7.refs_1_) | copy-start | bytes 393220
  51.1 4.5 %copy-start.3 = (bf16[2,128,256]{2,1,0:T(8,128)(2,1)}, bf16[2,128,256]{2,1,0:T(8,128)(2,1)S(1)}, u32[]{:S(2)}) copy-start(bf16[2,128,256]{2,1,0:T(8,128)(2,1)S(1)} %collective-permute-done.8.refs_2_) | copy-start | bytes 393220
  51.3 4.3 %copy-start.4 = (bf16[2,128,256]{2,1,0:T(8,128)(2,1)}, bf16[2,128,256]{2,1,0:T(8,128)(2,1)S(1)}, u32[]{:S(2)}) copy-start(bf16[2,128,256]{2,1,0:T(8,128)(2,1)S(1)} %collective-permute-done.9.refs_3_) | copy-start | bytes 393220
  51.3 13.9 %collective-permute-start.15 = (bf16[256,1024]{1,0:T(8,128)(2,1)}, bf16[256,1024]{1,0:T(8,128)(2,1)}, u32[]{:S(2)}, u32[]{:S(2)}) collective-permute-start(bf16[256,1024]{1,0:T(8,128)(2,1)} %collective-permute-done.refs_9_), channel_id=1, source_target_pairs={{0,8},{2,10},{4,12},{6,14},{8,24},{10,26},{12,28},{14,30},{24,16},... | collective-permute-start | bytes 1572872 | tf_op jit(solution)/shard_map/ppermute | solution.py:349
  52.8 1.8 %collective-permute-start.10 = (bf16[2,128,256]{2,1,0:T(8,128)(2,1)}, bf16[2,128,256]{2,1,0:T(8,128)(2,1)S(1)}, u32[]{:S(2)}, u32[]{:S(2)}) collective-permute-start(bf16[2,128,256]{2,1,0:T(8,128)(2,1)} %get-tuple-element.68.refs_0_), channel_id=1, source_target_pairs={{0,1},{1,0},{2,3},{3,2},{4,5},{5,4},{6,7},{7,6},{8,9},{9,8},{10,11... | collective-permute-start | bytes 393224 | tf_op jit(solution)/shard_map/ppermute | solution.py:337
  52.8 1.8 %collective-permute-start.11 = (bf16[2,128,256]{2,1,0:T(8,128)(2,1)S(1)}, bf16[2,128,256]{2,1,0:T(8,128)(2,1)S(1)}, u32[]{:S(2)}, u32[]{:S(2)}) collective-permute-start(bf16[2,128,256]{2,1,0:T(8,128)(2,1)S(1)} %collective-permute-done.7.refs_1_), channel_id=1, source_target_pairs={{0,1},{1,0},{2,3},{3,2},{4,5},{5,4},{6,7},{7,6},{8,9},{9,8},{10,11... | collective-permute-start | bytes 393224 | tf_op jit(solution)/shard_map/ppermute | solution.py:337
  53.3 1.3 %collective-permute-start.12 = (bf16[2,128,256]{2,1,0:T(8,128)(2,1)S(1)}, bf16[2,128,256]{2,1,0:T(8,128)(2,1)S(1)}, u32[]{:S(2)}, u32[]{:S(2)}) collective-permute-start(bf16[2,128,256]{2,1,0:T(8,128)(2,1)S(1)} %collective-permute-done.8.refs_2_), channel_id=1, source_target_pairs={{0,1},{1,0},{2,3},{3,2},{4,5},{5,4},{6,7},{7,6},{8,9},{9,8},{10,11... | collective-permute-start | bytes 393224 | tf_op jit(solution)/shard_map/ppermute | solution.py:337
  53.3 1.5 %collective-permute-start.13 = (bf16[2,128,256]{2,1,0:T(8,128)(2,1)S(1)}, bf16[2,128,256]{2,1,0:T(8,128)(2,1)S(1)}, u32[]{:S(2)}, u32[]{:S(2)}) collective-permute-start(bf16[2,128,256]{2,1,0:T(8,128)(2,1)S(1)} %collective-permute-done.9.refs_3_), channel_id=1, source_target_pairs={{0,1},{1,0},{2,3},{3,2},{4,5},{5,4},{6,7},{7,6},{8,9},{9,8},{10,11... | collective-permute-start | bytes 393224 | tf_op jit(solution)/shard_map/ppermute | solution.py:337
  54.6 6.1 %copy-start.5 = (bf16[2,128,256]{2,1,0:T(8,128)(2,1)}, bf16[2,128,256]{2,1,0:T(8,128)(2,1)S(1)}, u32[]{:S(2)}) copy-start(bf16[2,128,256]{2,1,0:T(8,128)(2,1)S(1)} %collective-permute-done.10.refs_4_) | copy-start | bytes 393220
  54.6 6.1 %copy-start.6 = (bf16[2,128,256]{2,1,0:T(8,128)(2,1)}, bf16[2,128,256]{2,1,0:T(8,128)(2,1)S(1)}, u32[]{:S(2)}) copy-start(bf16[2,128,256]{2,1,0:T(8,128)(2,1)S(1)} %collective-permute-done.11.refs_5_) | copy-start | bytes 393220
  54.7 6.0 %copy-start.7 = (bf16[2,128,256]{2,1,0:T(8,128)(2,1)}, bf16[2,128,256]{2,1,0:T(8,128)(2,1)S(1)}, u32[]{:S(2)}) copy-start(bf16[2,128,256]{2,1,0:T(8,128)(2,1)S(1)} %collective-permute-done.12.refs_6_) | copy-start | bytes 393220
  54.9 5.8 %copy-start.8 = (bf16[2,128,256]{2,1,0:T(8,128)(2,1)}, bf16[2,128,256]{2,1,0:T(8,128)(2,1)S(1)}, u32[]{:S(2)}) copy-start(bf16[2,128,256]{2,1,0:T(8,128)(2,1)S(1)} %collective-permute-done.13.refs_7_) | copy-start | bytes 393220
  55.6 16.2 %all-to-all-start.2 = ((f32[16,1,2,16,128]{4,3,2,1,0:T(8,128)}), f32[16,1,2,16,128]{4,3,2,1,0:T(8,128)}, u32[]{:S(2)}, u32[]{:S(2)}) async-start(f32[16,1,2,16,128]{4,3,2,1,0:T(8,128)} %shard_map.120), calls=%async_computation.2 | async-start | bytes 524288 | tf_op jit(solution)/shard_map/all_to_all | solution.py:555
  69.3 9.9 %collective-permute-start.16 = (bf16[128,1024]{1,0:T(8,128)(2,1)}, bf16[128,1024]{1,0:T(8,128)(2,1)}, u32[]{:S(2)}, u32[]{:S(2)}) collective-permute-start(bf16[128,1024]{1,0:T(8,128)(2,1)} %get-tuple-element.87), channel_id=1, source_target_pairs={{0,6},{2,0},{4,2},{6,4},{8,14},{10,8},{12,10},{14,12},{16,22},{18,... | collective-permute-start | bytes 786440 | tf_op jit(solution)/shard_map/ppermute | solution.py:337
  69.4 12.2 %collective-permute-start.17 = (bf16[128,1024]{1,0:T(8,128)(2,1)}, bf16[128,1024]{1,0:T(8,128)(2,1)}, u32[]{:S(2)}, u32[]{:S(2)}) collective-permute-start(bf16[128,1024]{1,0:T(8,128)(2,1)} %get-tuple-element.88), channel_id=1, source_target_pairs={{0,4},{2,6},{4,0},{6,2},{8,12},{10,14},{12,8},{14,10},{16,20},{18,... | collective-permute-start | bytes 786440 | tf_op jit(solution)/shard_map/ppermute | solution.py:337
  70.5 11.1 %collective-permute-start.18 = (bf16[128,1024]{1,0:T(8,128)(2,1)}, bf16[128,1024]{1,0:T(8,128)(2,1)}, u32[]{:S(2)}, u32[]{:S(2)}) collective-permute-start(bf16[128,1024]{1,0:T(8,128)(2,1)} %get-tuple-element.89), channel_id=1, source_target_pairs={{0,2},{2,4},{4,6},{6,0},{8,10},{10,12},{12,14},{14,8},{16,18},{18,... | collective-permute-start | bytes 786440 | tf_op jit(solution)/shard_map/ppermute | solution.py:337
  81.6 2.3 %collective-permute-start.19 = (bf16[128,2048]{1,0:T(8,128)(2,1)}, bf16[128,2048]{1,0:T(8,128)(2,1)}, u32[]{:S(2)}, u32[]{:S(2)}) collective-permute-start(bf16[128,2048]{1,0:T(8,128)(2,1)} %shard_map.122.refs_4_), channel_id=1, source_target_pairs={{0,1},{1,0},{2,3},{3,2},{4,5},{5,4},{6,7},{7,6},{8,9},{9,8},{10,11... | collective-permute-start | bytes 1572872 | tf_op jit(solution)/shard_map/ppermute | solution.py:337

commit v6 on v5

--- a/solution.py
+++ b/solution.py
@@ -486,18 +486,14 @@
         plain=1,
         grant=16 * MIB,
     )
-    all_v = [v_weight]
-    if layers > 1:
-        all_v.append(ring_on(v_weight, members, layers, 1))
     sums = lax.all_to_all(totals, "ctx", 0, 0)
     line_z = [z_weight] + [
         lax.ppermute(z_weight, "ctx", [(i, (i + members * k) % peers) for i in range(peers)])
         for k in range(1, layers)
     ]
     line_z = jnp.stack(line_z)
-    sums, all_v, line_z = lax.optimization_barrier((sums, all_v, line_z))
-    if layers > 2:
-        all_v.append(ring_on(v_weight, members, layers, -1))
+    sums, v_weight, line_z = lax.optimization_barrier((sums, v_weight, line_z))
+    all_v = [v_weight] + [ring_on(v_weight, members, layers, (-1) ** (k + 1)) for k in range(1, min(layers, 3))]
     all_z = [line_z] + [along(line_z, "ctx", k, members) for k in range(1, members)]
 
     rows = NDIM * 2 * tiles

time: 87.9 us -> 87.4 us (level)
  starting transfers between devices: 38.8 us -> 36 us
  waiting for transfers between devices: 19.9 us -> 22 us
    ppermute x3, waiting for transfers between devices: 5.65 us -> 0.01 us  [body(): lax.ppermute(z_weight, 'ctx', [(i, (i + members * k) % peers) for i in ra...]
    all_to_all x1, waiting for transfers between devices: 0.52 us -> 5.78 us  [body(): sums = lax.all_to_all(totals, 'ctx', 0, 0)]
    ppermute x3, waiting for transfers between devices: 4.54 us -> 9.03 us  [ring_on(): return lax.ppermute(block, 'ctx', pairs)]
    ppermute x3, starting transfers between devices: 6.75 us -> 3.21 us  [ring_on(): return lax.ppermute(block, 'ctx', pairs)]
    ppermute x14, waiting for transfers between devices: 9.18 us -> 6.85 us  [along(): return lax.ppermute(block, axis, pairs)]
    ppermute x3, starting transfers between devices: 4.05 us -> 6.06 us  [body(): lax.ppermute(z_weight, 'ctx', [(i, (i + members * k) % peers) for i in ra...]
    all_to_all x1, starting transfers between devices: 4.98 us -> 6.88 us  [body(): incoming = lax.all_to_all(starts, 'ctx', 0, 0)]
    all_to_all x1, starting transfers between devices: 5.17 us -> 3.83 us  [body(): arrived = lax.all_to_all(split(ends), 'ctx', 0, 0)]
  transfers between devices with their start and end apart: 23 -> 23, of which waited for: 11 -> 9; matrix products, arithmetic and copies ran while one was open for 3% -> 3% of each run, Pallas kernels for 24% -> 24%
where the time goes in v6:
time: 87.4 us; the launch traced here: 86.8 us
  starting transfers between devices  36 us (41%)
  Pallas kernels  24.6 us (28%)
  waiting for transfers between devices  22 us (25%)
  local copies, waits for them, and re-layouts  2.42 us (3%)
  other arithmetic  1.57 us (2%)
    pallas_call x6, Pallas kernels, call(): pl.pallas_call(kernel, out_shape=outs, in_specs=[here] * len(inputs), out...  24.6 us
    ppermute x14, starting transfers between devices, along(): return lax.ppermute(block, axis, pairs)  10.6 us
    ppermute x3, waiting for transfers between devices, ring_on(): return lax.ppermute(block, 'ctx', pairs)  9.03 us
    all_to_all x1, starting transfers between devices, body(): incoming = lax.all_to_all(starts, 'ctx', 0, 0)  6.88 us
    ppermute x14, waiting for transfers between devices, along(): return lax.ppermute(block, axis, pairs)  6.85 us
    ppermute x3, starting transfers between devices, body(): lax.ppermute(z_weight, 'ctx', [(i, (i + members * k) % peers) for i in ra...  6.06 us
    all_to_all x1, waiting for transfers between devices, body(): sums = lax.all_to_all(totals, 'ctx', 0, 0)  5.78 us
    all_to_all x1, starting transfers between devices, body(): sums = lax.all_to_all(totals, 'ctx', 0, 0)  5.45 us
  transfers between devices with their start and end apart: 23, of which 9 were waited for; matrix products, arithmetic and copies ran while one was open for 3% of the time, Pallas kernels for 24%

profile of v6, /device:TPU:0, one launch (start us, length us, event | category | flops | bytes accessed | tf_op | source)
XLA Modules:
  0.0 86.8 jit_solution(15233333857292942749)
XLA Ops:
  0.0 3.0 %collective-permute-start = (bf16[256,128]{1,0:T(8,128)(2,1)}, bf16[256,128]{1,0:T(8,128)(2,1)S(1)}, u32[]{:S(2)}, u32[]{:S(2)}) collective-permute-start(bf16[256,128]{1,0:T(8,128)(2,1)} %param.21), channel_id=1, source_target_pairs={{0,8},{2,10},{4,12},{6,14},{8,16},{10,18},{12,20},{14,22},{16,24},... | collective-permute-start | bytes 196616 | tf_op jit(solution)/shard_map/ppermute | solution.py:491
  3.0 2.0 %collective-permute-start.2 = (bf16[256,128]{1,0:T(8,128)(2,1)}, bf16[256,128]{1,0:T(8,128)(2,1)S(1)}, u32[]{:S(2)}, u32[]{:S(2)}) collective-permute-start(bf16[256,128]{1,0:T(8,128)(2,1)} %param.21), channel_id=1, source_target_pairs={{0,24},{2,26},{4,28},{6,30},{8,0},{10,2},{12,4},{14,6},{16,8},{18,... | collective-permute-start | bytes 196616 | tf_op jit(solution)/shard_map/ppermute | solution.py:491
  5.1 1.0 %collective-permute-start.1 = (bf16[256,128]{1,0:T(8,128)(2,1)}, bf16[256,128]{1,0:T(8,128)(2,1)S(1)}, u32[]{:S(2)}, u32[]{:S(2)}) collective-permute-start(bf16[256,128]{1,0:T(8,128)(2,1)} %param.21), channel_id=1, source_target_pairs={{0,16},{2,18},{4,20},{6,22},{8,24},{10,26},{12,28},{14,30},{16,0},... | collective-permute-start | bytes 196616 | tf_op jit(solution)/shard_map/ppermute | solution.py:491
  6.1 1.0 %copy-done = bf16[128,2048]{1,0:T(8,128)(2,1)S(1)} copy-done((bf16[128,2048]{1,0:T(8,128)(2,1)S(1)}, bf16[128,2048]{1,0:T(8,128)(2,1)}, u32[]{:S(2)}) %copy-start) | copy-done | bytes 524312
  7.1 1.4 %shard_map.118 = (f32[2,128,128]{2,1,0:T(8,128)S(1)}, f32[16,2,128]{2,1,0:T(2,128)}) custom-call(bf16[128,2048]{1,0:T(8,128)(2,1)S(1)} %copy-done), custom_call_target="tpu_custom_call" | custom-call | flops 1 | bytes 1 | tf_op jit(solution)/shard_map/pallas_call | solution.py:27
  8.6 0.6 copy-done.1
  9.2 5.4 %all-to-all-start = ((f32[16,2,128]{2,1,0:T(2,128)}), f32[16,2,128]{2,1,0:T(2,128)}, u32[]{:S(2)}, u32[]{:S(2)}) async-start(f32[16,2,128]{2,1,0:T(2,128)} %get-tuple-element.49), calls=%async_computation | async-start | bytes 32768 | tf_op jit(solution)/shard_map/all_to_all | solution.py:489
  14.6 0.0 collective-permute-done
  14.7 0.0 collective-permute-done.2
  14.7 1.6 %pad_maximum_fusion.refs_0_ = bf16[4,256,128]{2,1,0:T(8,128)(2,1)} fusion(bf16[1,256,128]{2,1,0:T(8,128)(2,1)S(1)} %bitcast.19, bf16[1,256,128]{2,1,0:T(8,128)(2,1)S(1)} %bitcast.20, bf16[1,256,128]{2,1,0:T(8,128)(2,1)S(1)} %bitcast.18, bf16[1,256,128]{2,1,0:T(8,128)(2,1)} %bitcast.17), kind=kLoop, calls=%fused_computation | loop fusion | flops 393216 | bytes 524288 | tf_op jit(solution)/shard_map/stack | solution.py:494
  16.2 5.8 %all-to-all-done.refs_1_ = f32[16,2,128]{2,1,0:T(2,128)} async-done(((f32[16,2,128]{2,1,0:T(2,128)}), f32[16,2,128]{2,1,0:T(2,128)}, u32[]{:S(2)}, u32[]{:S(2)}) %all-to-all-start) | async-done | bytes 16416 | tf_op jit(solution)/shard_map/all_to_all | solution.py:489
  22.0 0.6 collective-permute-start.9
  22.6 0.6 collective-permute-start.5
  23.2 1.4 %collective-permute-start.4 = (bf16[4,256,128]{2,1,0:T(8,128)(2,1)}, bf16[4,256,128]{2,1,0:T(8,128)(2,1)}, u32[]{:S(2)}, u32[]{:S(2)}) collective-permute-start(bf16[4,256,128]{2,1,0:T(8,128)(2,1)} %pad_maximum_fusion.refs_0_), channel_id=1, source_target_pairs={{0,4},{2,6},{4,0},{6,2},{8,12},{10,14},{12,8},{14,10},{16,20},{18,... | collective-permute-start | bytes 786440 | tf_op jit(solution)/shard_map/ppermute | solution.py:337
  24.6 0.6 collective-permute-start.3
  25.2 2.3 %collective-permute-start.14 = (bf16[256,1024]{1,0:T(8,128)(2,1)}, bf16[256,1024]{1,0:T(8,128)(2,1)}, u32[]{:S(2)}, u32[]{:S(2)}) collective-permute-start(bf16[256,1024]{1,0:T(8,128)(2,1)} %refs_8_.2), channel_id=1, source_target_pairs={{0,16},{2,18},{4,20},{6,22},{8,0},{10,2},{12,4},{14,6},{24,8},{26,... | collective-permute-start | bytes 1572872 | tf_op jit(solution)/shard_map/ppermute | solution.py:349
  27.6 7.4 %shard_map.119 = (bf16[2,128,256]{2,1,0:T(8,128)(2,1)}, bf16[2,128,256]{2,1,0:T(8,128)(2,1)}, bf16[2,128,256]{2,1,0:T(8,128)(2,1)}, bf16[2,128,256]{2,1,0:T(8,12...) custom-call(bf16[128,2048]{1,0:T(8,128)(2,1)} %refs_0_.1, ...), custom_call_target="tpu_custom_call" | custom-call | flops 1 | bytes 1 | tf_op jit(solution)/shard_map/pallas_call | solution.py:27
  35.0 3.8 %all-to-all-start.1 = ((f32[16,1,2,16,128]{4,3,2,1,0:T(8,128)}), f32[16,1,2,16,128]{4,3,2,1,0:T(8,128)S(1)}, u32[]{:S(2)}, u32[]{:S(2)}) async-start(f32[16,1,2,16,128]{4,3,2,1,0:T(8,128)} %bitcast.16), calls=%async_computation.1 | async-start | bytes 524288 | tf_op jit(solution)/shard_map/all_to_all | solution.py:541
  38.8 0.0 collective-permute-done.3.refs_1_
  38.8 2.0 %collective-permute-start.6 = (bf16[2,128,256]{2,1,0:T(8,128)(2,1)}, bf16[2,128,256]{2,1,0:T(8,128)(2,1)S(1)}, u32[]{:S(2)}, u32[]{:S(2)}) collective-permute-start(bf16[2,128,256]{2,1,0:T(8,128)(2,1)} %get-tuple-element.63), channel_id=1, source_target_pairs={{0,2},{2,4},{4,6},{6,0},{8,10},{10,12},{12,14},{14,8},{16,18},{18,... | collective-permute-start | bytes 393224 | tf_op jit(solution)/shard_map/ppermute | solution.py:337
  40.8 1.5 %collective-permute-start.7 = (bf16[2,128,256]{2,1,0:T(8,128)(2,1)}, bf16[2,128,256]{2,1,0:T(8,128)(2,1)S(1)}, u32[]{:S(2)}, u32[]{:S(2)}) collective-permute-start(bf16[2,128,256]{2,1,0:T(8,128)(2,1)} %get-tuple-element.64), channel_id=1, source_target_pairs={{0,4},{2,6},{4,0},{6,2},{8,12},{10,14},{12,8},{14,10},{16,20},{18,... | collective-permute-start | bytes 393224 | tf_op jit(solution)/shard_map/ppermute | solution.py:337
  42.3 1.5 %collective-permute-start.8 = (bf16[2,128,256]{2,1,0:T(8,128)(2,1)}, bf16[2,128,256]{2,1,0:T(8,128)(2,1)S(1)}, u32[]{:S(2)}, u32[]{:S(2)}) collective-permute-start(bf16[2,128,256]{2,1,0:T(8,128)(2,1)} %get-tuple-element.65), channel_id=1, source_target_pairs={{0,6},{2,0},{4,2},{6,4},{8,14},{10,8},{12,10},{14,12},{16,22},{18,... | collective-permute-start | bytes 393224 | tf_op jit(solution)/shard_map/ppermute | solution.py:337
  43.7 1.9 %collective-permute-done.6.refs_1_ = bf16[2,128,256]{2,1,0:T(8,128)(2,1)S(1)} collective-permute-done((bf16[2,128,256]{2,1,0:T(8,128)(2,1)}, bf16[2,128,256]{2,1,0:T(8,128)(2,1)S(1)}, u32[]{:S(2)}, u32[]{:S(2)}) %collective-permute-start.6) | collective-permute-done | bytes 131104 | tf_op jit(solution)/shard_map/ppermute | solution.py:337
  45.6 1.9 %collective-permute-done.7.refs_2_ = bf16[2,128,256]{2,1,0:T(8,128)(2,1)S(1)} collective-permute-done((bf16[2,128,256]{2,1,0:T(8,128)(2,1)}, bf16[2,128,256]{2,1,0:T(8,128)(2,1)S(1)}, u32[]{:S(2)}, u32[]{:S(2)}) %collective-permute-start.7) | collective-permute-done | bytes 131104 | tf_op jit(solution)/shard_map/ppermute | solution.py:337
  47.5 0.1 collective-permute-done.8.refs_3_
  47.6 1.2 %collective-permute-done.9.refs_9_ = bf16[256,1024]{1,0:T(8,128)(2,1)} collective-permute-done((bf16[256,1024]{1,0:T(8,128)(2,1)}, bf16[256,1024]{1,0:T(8,128)(2,1)}, u32[]{:S(2)}, u32[]{:S(2)}) %collective-permute-start.9) | collective-permute-done | bytes 524320 | tf_op jit(solution)/shard_map/ppermute | solution.py:349
  48.8 0.3 collective-permute-start.15
  49.1 0.5 collective-permute-start.11
  49.6 0.0 collective-permute-start.12
  49.6 0.0 collective-permute-done.14.refs_10_
  49.6 0.5 collective-permute-start.13
  50.1 0.7 dynamic-slice_bitcast_fusion.q_ref
  50.8 0.3 all-to-all-done.1.ends_ref
  51.2 0.0 collective-permute-done.10.refs_4_
  51.2 0.0 collective-permute-done.12.refs_6_
  51.2 0.0 collective-permute-done.13.refs_7_
  51.2 0.8 shard_map.120
  52.1 6.9 %all-to-all-start.2 = ((f32[16,1,2,16,128]{4,3,2,1,0:T(8,128)}), f32[16,1,2,16,128]{4,3,2,1,0:T(8,128)}, u32[]{:S(2)}, u32[]{:S(2)}) async-start(f32[16,1,2,16,128]{4,3,2,1,0:T(8,128)} %shard_map.120), calls=%async_computation.2 | async-start | bytes 524288 | tf_op jit(solution)/shard_map/all_to_all | solution.py:551
  59.0 7.8 %collective-permute-done.15.refs_11_ = bf16[256,1024]{1,0:T(8,128)(2,1)} collective-permute-done((bf16[256,1024]{1,0:T(8,128)(2,1)}, bf16[256,1024]{1,0:T(8,128)(2,1)}, u32[]{:S(2)}, u32[]{:S(2)}) %collective-permute-start.15) | collective-permute-done | bytes 524320 | tf_op jit(solution)/shard_map/ppermute | solution.py:349
  66.8 4.1 %shard_map.121 = (f32[128,1024]{1,0:T(8,128)}, bf16[128,1024]{1,0:T(8,128)(2,1)}, bf16[128,1024]{1,0:T(8,128)(2,1)}, bf16[128,1024]{1,0:T(8,128)(2,1)}) custom-call(bf16[2,128,256]{2,1,0:T(8,128)(2,1)} %get-tuple-element.67.refs_0_, bf16[2,128,256]{2,1,0:T(8,128)(2,1)} %copy-done.2, bf16[2,128,256]{2,1,0:T(8,128)(2,1)} %copy-done.3, ...), custom_call_target="tpu_custom_call" | custom-call | flops 1 | bytes 1 | tf_op jit(solution)/shard_map/pallas_call | solution.py:27
  70.9 0.1 collective-permute-start.16
  71.0 0.1 collective-permute-start.17
  71.0 1.9 %collective-permute-start.18 = (bf16[128,1024]{1,0:T(8,128)(2,1)}, bf16[128,1024]{1,0:T(8,128)(2,1)}, u32[]{:S(2)}, u32[]{:S(2)}) collective-permute-start(bf16[128,1024]{1,0:T(8,128)(2,1)} %get-tuple-element.87), channel_id=1, source_target_pairs={{0,2},{2,4},{4,6},{6,0},{8,10},{10,12},{12,14},{14,8},{16,18},{18,... | collective-permute-start | bytes 786440 | tf_op jit(solution)/shard_map/ppermute | solution.py:337
  73.0 7.3 %shard_map.122.refs_4_ = bf16[128,2048]{1,0:T(8,128)(2,1)} custom-call(f32[16,2,16,128]{3,2,1,0:T(8,128)} %bitcast.10.incoming_hbm, f32[16,8,2,16,128]{4,3,2,1,0:T(8,128)} %get-tuple-element.82.fresh_hbm, f32[2048,128]{1,0:T(8,128)} %get-tuple-element.83.dense_hbm, f32[512,128]{1,0:T(8,128)} %get-tuple-element.71.q_hbm, f32[512,128]{1,0:T(8,128)} %get-tuple-element.84.w_hbm, ...), custom_call_target="tpu_custom_call" | custom-call | flops 1 | bytes 1 | tf_op jit(solution)/shard_map/pallas_call | solution.py:27
  80.3 0.7 collective-permute-done.17.refs_7_
  81.1 0.0 collective-permute-done.18.refs_8_
  81.1 2.3 %collective-permute-done.19.refs_5_ = bf16[128,2048]{1,0:T(8,128)(2,1)} collective-permute-done((bf16[128,2048]{1,0:T(8,128)(2,1)}, bf16[128,2048]{1,0:T(8,128)(2,1)}, u32[]{:S(2)}, u32[]{:S(2)}) %collective-permute-start.19) | collective-permute-done | bytes 524320 | tf_op jit(solution)/shard_map/ppermute | solution.py:337
  83.3 3.5 %shard_map.123 = bf16[128,1024]{1,0:T(8,128)(2,1)} custom-call(bf16[4,256,128]{2,1,0:T(8,128)(2,1)} %pad_maximum_fusion.refs_0_, bf16[4,256,128]{2,1,0:T(8,128)(2,1)} %collective-permute-done.3.refs_1_, bf16[4,256,128]{2,1,0:T(8,128)(2,1)} %collective-permute-done.4.refs_2_, bf16[4,256,128]{2,1,0:T(8,128)(2,1)} %collective-permute-done.5.refs_3_, ...), custom_call_target="tpu_custom_call" | custom-call | flops 1 | bytes 1 | tf_op jit(solution)/shard_map/pallas_call | solution.py:27
  (24 shorter events, 0.1 us)
Async XLA Ops:
  0.0 14.6 %collective-permute-start = (bf16[256,128]{1,0:T(8,128)(2,1)}, bf16[256,128]{1,0:T(8,128)(2,1)S(1)}, u32[]{:S(2)}, u32[]{:S(2)}) collective-permute-start(bf16[256,128]{1,0:T(8,128)(2,1)} %param.21), channel_id=1, source_target_pairs={{0,8},{2,10},{4,12},{6,14},{8,16},{10,18},{12,20},{14,22},{16,24},... | collective-permute-start | bytes 196616 | tf_op jit(solution)/shard_map/ppermute | solution.py:491
  3.0 11.6 %collective-permute-start.2 = (bf16[256,128]{1,0:T(8,128)(2,1)}, bf16[256,128]{1,0:T(8,128)(2,1)S(1)}, u32[]{:S(2)}, u32[]{:S(2)}) collective-permute-start(bf16[256,128]{1,0:T(8,128)(2,1)} %param.21), channel_id=1, source_target_pairs={{0,24},{2,26},{4,28},{6,30},{8,0},{10,2},{12,4},{14,6},{16,8},{18,... | collective-permute-start | bytes 196616 | tf_op jit(solution)/shard_map/ppermute | solution.py:491
  5.1 9.6 %collective-permute-start.1 = (bf16[256,128]{1,0:T(8,128)(2,1)}, bf16[256,128]{1,0:T(8,128)(2,1)S(1)}, u32[]{:S(2)}, u32[]{:S(2)}) collective-permute-start(bf16[256,128]{1,0:T(8,128)(2,1)} %param.21), channel_id=1, source_target_pairs={{0,16},{2,18},{4,20},{6,22},{8,24},{10,26},{12,28},{14,30},{16,0},... | collective-permute-start | bytes 196616 | tf_op jit(solution)/shard_map/ppermute | solution.py:491
  6.1 1.0 %copy-start = (bf16[128,2048]{1,0:T(8,128)(2,1)S(1)}, bf16[128,2048]{1,0:T(8,128)(2,1)}, u32[]{:S(2)}) copy-start(bf16[128,2048]{1,0:T(8,128)(2,1)} %refs_0_.1) | copy-start | bytes 1572868
  8.5 0.6 copy-start.1
  9.2 12.8 %all-to-all-start = ((f32[16,2,128]{2,1,0:T(2,128)}), f32[16,2,128]{2,1,0:T(2,128)}, u32[]{:S(2)}, u32[]{:S(2)}) async-start(f32[16,2,128]{2,1,0:T(2,128)} %get-tuple-element.49), calls=%async_computation | async-start | bytes 32768 | tf_op jit(solution)/shard_map/all_to_all | solution.py:489
  22.0 26.8 %collective-permute-start.9 = (bf16[256,1024]{1,0:T(8,128)(2,1)}, bf16[256,1024]{1,0:T(8,128)(2,1)}, u32[]{:S(2)}, u32[]{:S(2)}) collective-permute-start(bf16[256,1024]{1,0:T(8,128)(2,1)} %refs_8_.2), channel_id=1, source_target_pairs={{0,8},{2,10},{4,12},{6,14},{8,24},{10,26},{12,28},{14,30},{24,16},... | collective-permute-start | bytes 1572872 | tf_op jit(solution)/shard_map/ppermute | solution.py:349
  22.6 16.2 %collective-permute-start.5 = (bf16[4,256,128]{2,1,0:T(8,128)(2,1)}, bf16[4,256,128]{2,1,0:T(8,128)(2,1)}, u32[]{:S(2)}, u32[]{:S(2)}) collective-permute-start(bf16[4,256,128]{2,1,0:T(8,128)(2,1)} %pad_maximum_fusion.refs_0_), channel_id=1, source_target_pairs={{0,6},{2,0},{4,2},{6,4},{8,14},{10,8},{12,10},{14,12},{16,22},{18,... | collective-permute-start | bytes 786440 | tf_op jit(solution)/shard_map/ppermute | solution.py:337
  23.2 15.6 %collective-permute-start.4 = (bf16[4,256,128]{2,1,0:T(8,128)(2,1)}, bf16[4,256,128]{2,1,0:T(8,128)(2,1)}, u32[]{:S(2)}, u32[]{:S(2)}) collective-permute-start(bf16[4,256,128]{2,1,0:T(8,128)(2,1)} %pad_maximum_fusion.refs_0_), channel_id=1, source_target_pairs={{0,4},{2,6},{4,0},{6,2},{8,12},{10,14},{12,8},{14,10},{16,20},{18,... | collective-permute-start | bytes 786440 | tf_op jit(solution)/shard_map/ppermute | solution.py:337
  24.6 14.2 %collective-permute-start.3 = (bf16[4,256,128]{2,1,0:T(8,128)(2,1)}, bf16[4,256,128]{2,1,0:T(8,128)(2,1)}, u32[]{:S(2)}, u32[]{:S(2)}) collective-permute-start(bf16[4,256,128]{2,1,0:T(8,128)(2,1)} %pad_maximum_fusion.refs_0_), channel_id=1, source_target_pairs={{0,2},{2,4},{4,6},{6,0},{8,10},{10,12},{12,14},{14,8},{16,18},{18,... | collective-permute-start | bytes 786440 | tf_op jit(solution)/shard_map/ppermute | solution.py:337
  25.2 24.4 %collective-permute-start.14 = (bf16[256,1024]{1,0:T(8,128)(2,1)}, bf16[256,1024]{1,0:T(8,128)(2,1)}, u32[]{:S(2)}, u32[]{:S(2)}) collective-permute-start(bf16[256,1024]{1,0:T(8,128)(2,1)} %refs_8_.2), channel_id=1, source_target_pairs={{0,16},{2,18},{4,20},{6,22},{8,0},{10,2},{12,4},{14,6},{24,8},{26,... | collective-permute-start | bytes 1572872 | tf_op jit(solution)/shard_map/ppermute | solution.py:349
  35.0 16.2 %all-to-all-start.1 = ((f32[16,1,2,16,128]{4,3,2,1,0:T(8,128)}), f32[16,1,2,16,128]{4,3,2,1,0:T(8,128)S(1)}, u32[]{:S(2)}, u32[]{:S(2)}) async-start(f32[16,1,2,16,128]{4,3,2,1,0:T(8,128)} %bitcast.16), calls=%async_computation.1 | async-start | bytes 524288 | tf_op jit(solution)/shard_map/all_to_all | solution.py:541
  38.8 6.8 %collective-permute-start.6 = (bf16[2,128,256]{2,1,0:T(8,128)(2,1)}, bf16[2,128,256]{2,1,0:T(8,128)(2,1)S(1)}, u32[]{:S(2)}, u32[]{:S(2)}) collective-permute-start(bf16[2,128,256]{2,1,0:T(8,128)(2,1)} %get-tuple-element.63), channel_id=1, source_target_pairs={{0,2},{2,4},{4,6},{6,0},{8,10},{10,12},{12,14},{14,8},{16,18},{18,... | collective-permute-start | bytes 393224 | tf_op jit(solution)/shard_map/ppermute | solution.py:337
  40.8 6.7 %collective-permute-start.7 = (bf16[2,128,256]{2,1,0:T(8,128)(2,1)}, bf16[2,128,256]{2,1,0:T(8,128)(2,1)S(1)}, u32[]{:S(2)}, u32[]{:S(2)}) collective-permute-start(bf16[2,128,256]{2,1,0:T(8,128)(2,1)} %get-tuple-element.64), channel_id=1, source_target_pairs={{0,4},{2,6},{4,0},{6,2},{8,12},{10,14},{12,8},{14,10},{16,20},{18,... | collective-permute-start | bytes 393224 | tf_op jit(solution)/shard_map/ppermute | solution.py:337
  42.3 5.3 %collective-permute-start.8 = (bf16[2,128,256]{2,1,0:T(8,128)(2,1)}, bf16[2,128,256]{2,1,0:T(8,128)(2,1)S(1)}, u32[]{:S(2)}, u32[]{:S(2)}) collective-permute-start(bf16[2,128,256]{2,1,0:T(8,128)(2,1)} %get-tuple-element.65), channel_id=1, source_target_pairs={{0,6},{2,0},{4,2},{6,4},{8,14},{10,8},{12,10},{14,12},{16,22},{18,... | collective-permute-start | bytes 393224 | tf_op jit(solution)/shard_map/ppermute | solution.py:337
  45.6 6.4 %copy-start.2 = (bf16[2,128,256]{2,1,0:T(8,128)(2,1)}, bf16[2,128,256]{2,1,0:T(8,128)(2,1)S(1)}, u32[]{:S(2)}) copy-start(bf16[2,128,256]{2,1,0:T(8,128)(2,1)S(1)} %collective-permute-done.6.refs_1_) | copy-start | bytes 393220
  47.5 4.5 %copy-start.3 = (bf16[2,128,256]{2,1,0:T(8,128)(2,1)}, bf16[2,128,256]{2,1,0:T(8,128)(2,1)S(1)}, u32[]{:S(2)}) copy-start(bf16[2,128,256]{2,1,0:T(8,128)(2,1)S(1)} %collective-permute-done.7.refs_2_) | copy-start | bytes 393220
  47.6 4.5 %copy-start.4 = (bf16[2,128,256]{2,1,0:T(8,128)(2,1)}, bf16[2,128,256]{2,1,0:T(8,128)(2,1)S(1)}, u32[]{:S(2)}) copy-start(bf16[2,128,256]{2,1,0:T(8,128)(2,1)S(1)} %collective-permute-done.8.refs_3_) | copy-start | bytes 393220
  48.8 18.0 %collective-permute-start.15 = (bf16[256,1024]{1,0:T(8,128)(2,1)}, bf16[256,1024]{1,0:T(8,128)(2,1)}, u32[]{:S(2)}, u32[]{:S(2)}) collective-permute-start(bf16[256,1024]{1,0:T(8,128)(2,1)} %collective-permute-done.9.refs_9_), channel_id=1, source_target_pairs={{0,8},{2,10},{4,12},{6,14},{8,24},{10,26},{12,28},{14,30},{24,16},... | collective-permute-start | bytes 1572872 | tf_op jit(solution)/shard_map/ppermute | solution.py:349
  49.1 2.1 %collective-permute-start.10 = (bf16[2,128,256]{2,1,0:T(8,128)(2,1)}, bf16[2,128,256]{2,1,0:T(8,128)(2,1)S(1)}, u32[]{:S(2)}, u32[]{:S(2)}) collective-permute-start(bf16[2,128,256]{2,1,0:T(8,128)(2,1)} %get-tuple-element.67.refs_0_), channel_id=1, source_target_pairs={{0,1},{1,0},{2,3},{3,2},{4,5},{5,4},{6,7},{7,6},{8,9},{9,8},{10,11... | collective-permute-start | bytes 393224 | tf_op jit(solution)/shard_map/ppermute | solution.py:337
  49.1 2.1 %collective-permute-start.11 = (bf16[2,128,256]{2,1,0:T(8,128)(2,1)S(1)}, bf16[2,128,256]{2,1,0:T(8,128)(2,1)S(1)}, u32[]{:S(2)}, u32[]{:S(2)}) collective-permute-start(bf16[2,128,256]{2,1,0:T(8,128)(2,1)S(1)} %collective-permute-done.6.refs_1_), channel_id=1, source_target_pairs={{0,1},{1,0},{2,3},{3,2},{4,5},{5,4},{6,7},{7,6},{8,9},{9,8},{10,11... | collective-permute-start | bytes 393224 | tf_op jit(solution)/shard_map/ppermute | solution.py:337
  49.6 1.6 %collective-permute-start.12 = (bf16[2,128,256]{2,1,0:T(8,128)(2,1)S(1)}, bf16[2,128,256]{2,1,0:T(8,128)(2,1)S(1)}, u32[]{:S(2)}, u32[]{:S(2)}) collective-permute-start(bf16[2,128,256]{2,1,0:T(8,128)(2,1)S(1)} %collective-permute-done.7.refs_2_), channel_id=1, source_target_pairs={{0,1},{1,0},{2,3},{3,2},{4,5},{5,4},{6,7},{7,6},{8,9},{9,8},{10,11... | collective-permute-start | bytes 393224 | tf_op jit(solution)/shard_map/ppermute | solution.py:337
  49.6 1.6 %collective-permute-start.13 = (bf16[2,128,256]{2,1,0:T(8,128)(2,1)S(1)}, bf16[2,128,256]{2,1,0:T(8,128)(2,1)S(1)}, u32[]{:S(2)}, u32[]{:S(2)}) collective-permute-start(bf16[2,128,256]{2,1,0:T(8,128)(2,1)S(1)} %collective-permute-done.8.refs_3_), channel_id=1, source_target_pairs={{0,1},{1,0},{2,3},{3,2},{4,5},{5,4},{6,7},{7,6},{8,9},{9,8},{10,11... | collective-permute-start | bytes 393224 | tf_op jit(solution)/shard_map/ppermute | solution.py:337
  51.2 7.8 %copy-start.5 = (bf16[2,128,256]{2,1,0:T(8,128)(2,1)}, bf16[2,128,256]{2,1,0:T(8,128)(2,1)S(1)}, u32[]{:S(2)}) copy-start(bf16[2,128,256]{2,1,0:T(8,128)(2,1)S(1)} %collective-permute-done.10.refs_4_) | copy-start | bytes 393220
  51.2 7.8 %copy-start.6 = (bf16[2,128,256]{2,1,0:T(8,128)(2,1)}, bf16[2,128,256]{2,1,0:T(8,128)(2,1)S(1)}, u32[]{:S(2)}) copy-start(bf16[2,128,256]{2,1,0:T(8,128)(2,1)S(1)} %collective-permute-done.11.refs_5_) | copy-start | bytes 393220
  51.2 7.8 %copy-start.7 = (bf16[2,128,256]{2,1,0:T(8,128)(2,1)}, bf16[2,128,256]{2,1,0:T(8,128)(2,1)S(1)}, u32[]{:S(2)}) copy-start(bf16[2,128,256]{2,1,0:T(8,128)(2,1)S(1)} %collective-permute-done.12.refs_6_) | copy-start | bytes 393220
  51.2 7.8 %copy-start.8 = (bf16[2,128,256]{2,1,0:T(8,128)(2,1)}, bf16[2,128,256]{2,1,0:T(8,128)(2,1)S(1)}, u32[]{:S(2)}) copy-start(bf16[2,128,256]{2,1,0:T(8,128)(2,1)S(1)} %collective-permute-done.13.refs_7_) | copy-start | bytes 393220
  52.1 20.9 %all-to-all-start.2 = ((f32[16,1,2,16,128]{4,3,2,1,0:T(8,128)}), f32[16,1,2,16,128]{4,3,2,1,0:T(8,128)}, u32[]{:S(2)}, u32[]{:S(2)}) async-start(f32[16,1,2,16,128]{4,3,2,1,0:T(8,128)} %shard_map.120), calls=%async_computation.2 | async-start | bytes 524288 | tf_op jit(solution)/shard_map/all_to_all | solution.py:551
  70.9 9.4 %collective-permute-start.16 = (bf16[128,1024]{1,0:T(8,128)(2,1)}, bf16[128,1024]{1,0:T(8,128)(2,1)}, u32[]{:S(2)}, u32[]{:S(2)}) collective-permute-start(bf16[128,1024]{1,0:T(8,128)(2,1)} %get-tuple-element.85), channel_id=1, source_target_pairs={{0,6},{2,0},{4,2},{6,4},{8,14},{10,8},{12,10},{14,12},{16,22},{18,... | collective-permute-start | bytes 786440 | tf_op jit(solution)/shard_map/ppermute | solution.py:337
  71.0 10.1 %collective-permute-start.17 = (bf16[128,1024]{1,0:T(8,128)(2,1)}, bf16[128,1024]{1,0:T(8,128)(2,1)}, u32[]{:S(2)}, u32[]{:S(2)}) collective-permute-start(bf16[128,1024]{1,0:T(8,128)(2,1)} %get-tuple-element.86), channel_id=1, source_target_pairs={{0,4},{2,6},{4,0},{6,2},{8,12},{10,14},{12,8},{14,10},{16,20},{18,... | collective-permute-start | bytes 786440 | tf_op jit(solution)/shard_map/ppermute | solution.py:337
  71.0 10.0 %collective-permute-start.18 = (bf16[128,1024]{1,0:T(8,128)(2,1)}, bf16[128,1024]{1,0:T(8,128)(2,1)}, u32[]{:S(2)}, u32[]{:S(2)}) collective-permute-start(bf16[128,1024]{1,0:T(8,128)(2,1)} %get-tuple-element.87), channel_id=1, source_target_pairs={{0,2},{2,4},{4,6},{6,0},{8,10},{10,12},{12,14},{14,8},{16,18},{18,... | collective-permute-start | bytes 786440 | tf_op jit(solution)/shard_map/ppermute | solution.py:337
  81.1 2.3 %collective-permute-start.19 = (bf16[128,2048]{1,0:T(8,128)(2,1)}, bf16[128,2048]{1,0:T(8,128)(2,1)}, u32[]{:S(2)}, u32[]{:S(2)}) collective-permute-start(bf16[128,2048]{1,0:T(8,128)(2,1)} %shard_map.122.refs_4_), channel_id=1, source_target_pairs={{0,1},{1,0},{2,3},{3,2},{4,5},{5,4},{6,7},{7,6},{8,9},{9,8},{10,11... | collective-permute-start | bytes 1572872 | tf_op jit(solution)/shard_map/ppermute | solution.py:337

commit v7 on v6

--- a/solution.py
+++ b/solution.py
@@ -275,7 +275,7 @@
         return _
 
     lax.fori_loop(0, CHUNK - 1, one_tap, 0)
-    for load in loads[3:]:
+    for load in loads[3:5]:
         load.wait()
 
     def one(j, _):
@@ -294,6 +294,7 @@
 
     lax.fori_loop(0, NDIM, one, 0)
 
+    loads[5].wait()
     for low in range(0, tiles, step):
         rows = slice(low, low + step)
         for b in range(0, CHUNK, 2):
@@ -367,13 +368,14 @@
     subs, length, depth = blocks_hbm[0].shape
     half, place = lax.axis_index("tp"), lax.axis_index("ctx")
     ring_at = sum(jnp.where(place // members == at, k, 0) for k, at in enumerate(ring_of(layers)))
-    loads = [copies.start(weight, weight_ref.at[at]) for at, weight in enumerate(weights_hbm)]
+    loads = []
     for away in range(tp):
         other = lax.rem(half + tp - away, tp)
         for k in range(members):
             for sub in range(subs):
                 to = row_ref.at[other * subs + sub, k * length : (k + 1) * length, :]
                 loads.append(copies.start(blocks_hbm[away * members + k].at[sub], to))
+    later = [copies.start(weight, weight_ref.at[at]) for at, weight in enumerate(weights_hbm)]
     ring = ring_of(layers)
     blocks = []
     for step in ring_steps(layers):
@@ -385,11 +387,14 @@
     for load in loads:
         load.wait()
     stores = []
-    for k in [*range(1, members), 0]:
+    for k in range(members):
         here = slice(k * length, (k + 1) * length)
-        total = mm(row_ref[blocks[0], here, :], weight_ref[0])
-        for back in range(1, layers):
-            total = total + mm(row_ref[blocks[back], here, :], weight_ref[back])
+        total = None
+        for back in range(layers):
+            if k == 0:
+                later[back].wait()
+            product = mm(row_ref[blocks[back], here, :], weight_ref[back])
+            total = product if total is None else total + product
         if k == 0:
             own_ref[...] = total
             stores.append(copies.start(own_ref, own_hbm))
@@ -492,7 +497,7 @@
         for k in range(1, layers)
     ]
     line_z = jnp.stack(line_z)
-    sums, v_weight, line_z = lax.optimization_barrier((sums, v_weight, line_z))
+    sums, v_weight = lax.optimization_barrier((sums, v_weight))
     all_v = [v_weight] + [ring_on(v_weight, members, layers, (-1) ** (k + 1)) for k in range(1, min(layers, 3))]
     all_z = [line_z] + [along(line_z, "ctx", k, members) for k in range(1, members)]
 
@@ -541,11 +546,11 @@
     arrived = lax.all_to_all(split(ends), "ctx", 0, 0)
     near, all_z = lax.optimization_barrier((near, all_z))
     near = near[:1] + [along(near[k], "ctx", k, members) for k in range(1, members)]
-    near, all_v[1] = lax.optimization_barrier((near, all_v[1]))
+    my_q = lax.dynamic_index_in_dim(split(q.reshape(NDIM, 2, tiles, LANES)), place, 0, False)
+    near, all_v[1], my_q = lax.optimization_barrier((near, all_v[1], my_q))
     for k in range(3, layers):
         all_v.append(ring_on(all_v[k - 2], members, layers, (-1) ** (k + 1)))
     far = [along(block, "tp", k, tp) for k in range(1, tp) for block in near]
-    my_q = lax.dynamic_index_in_dim(split(q.reshape(NDIM, 2, tiles, LANES)), place, 0, False)
     arrived, far, my_q, all_v[2] = lax.optimization_barrier((arrived, far, my_q, all_v[2]))
     (starts,) = call(functools.partial(scan_kernel, length), [shape(arrived.shape, f32)], [arrived, my_q], plain=1, grant=16 * MIB)
     incoming = lax.all_to_all(starts, "ctx", 0, 0)

time: 87.4 us -> 86.2 us (0.986)
  blocking collectives: 0 us -> 12.6 us
  waiting for transfers between devices: 22 us -> 14.4 us
  starting transfers between devices: 36 us -> 30.9 us
  Pallas kernels: 24.6 us -> 23.6 us
    all_to_all x0 -> x1, blocking collectives: none -> 12.6 us  [body(): sums = lax.all_to_all(totals, 'ctx', 0, 0)]
    ppermute x3, waiting for transfers between devices: 9.03 us -> 3.01 us  [ring_on(): return lax.ppermute(block, 'ctx', pairs)]
    all_to_all x1 -> x0, waiting for transfers between devices: 5.78 us -> none  [body(): sums = lax.all_to_all(totals, 'ctx', 0, 0)]
    all_to_all x1 -> x0, starting transfers between devices: 5.45 us -> none  [body(): sums = lax.all_to_all(totals, 'ctx', 0, 0)]
    ppermute x14, waiting for transfers between devices: 6.85 us -> 10.6 us  [along(): return lax.ppermute(block, axis, pairs)]
    pallas_call x6, Pallas kernels: 24.6 us -> 23.6 us  [call(): pl.pallas_call(kernel, out_shape=outs, in_specs=[here] * len(inputs), out...]
    all_to_all x1, starting transfers between devices: 6.88 us -> 5.97 us  [body(): incoming = lax.all_to_all(starts, 'ctx', 0, 0)]
  transfers between devices with their start and end apart: 23 -> 22, of which waited for: 9 -> 10; matrix products, arithmetic and copies ran while one was open for 3% -> 3% of each run, Pallas kernels for 24% -> 23%
where the time goes in v7:
time: 86.2 us; the launch traced here: 85.7 us
  starting transfers between devices  30.9 us (36%)
  Pallas kernels  23.6 us (27%)
  waiting for transfers between devices  14.4 us (17%)
  blocking collectives  12.6 us (15%)
  local copies, waits for them, and re-layouts  2.43 us (3%)
  other arithmetic  1.58 us (2%)
    pallas_call x6, Pallas kernels, call(): pl.pallas_call(kernel, out_shape=outs, in_specs=[here] * len(inputs), out...  23.6 us
    all_to_all x1, blocking collectives, body(): sums = lax.all_to_all(totals, 'ctx', 0, 0)  12.6 us
    ppermute x14, starting transfers between devices, along(): return lax.ppermute(block, axis, pairs)  11.2 us
    ppermute x14, waiting for transfers between devices, along(): return lax.ppermute(block, axis, pairs)  10.6 us
    ppermute x3, starting transfers between devices, body(): lax.ppermute(z_weight, 'ctx', [(i, (i + members * k) % peers) for i in ra...  6.06 us
    all_to_all x1, starting transfers between devices, body(): incoming = lax.all_to_all(starts, 'ctx', 0, 0)  5.97 us
    ppermute x3, starting transfers between devices, ring_on(): return lax.ppermute(block, 'ctx', pairs)  3.89 us
    all_to_all x1, starting transfers between devices, body(): arrived = lax.all_to_all(split(ends), 'ctx', 0, 0)  3.83 us
  transfers between devices with their start and end apart: 22, of which 10 were waited for; matrix products, arithmetic and copies ran while one was open for 3% of the time, Pallas kernels for 23%

profile of v7, /device:TPU:0, one launch (start us, length us, event | category | flops | bytes accessed | tf_op | source)
XLA Modules:
  0.0 85.7 jit_solution(2999243803832968849)
XLA Ops:
  0.0 3.0 %collective-permute-start = (bf16[256,128]{1,0:T(8,128)(2,1)}, bf16[256,128]{1,0:T(8,128)(2,1)S(1)}, u32[]{:S(2)}, u32[]{:S(2)}) collective-permute-start(bf16[256,128]{1,0:T(8,128)(2,1)} %param.21), channel_id=1, source_target_pairs={{0,8},{2,10},{4,12},{6,14},{8,16},{10,18},{12,20},{14,22},{16,24},... | collective-permute-start | bytes 196616 | tf_op jit(solution)/shard_map/ppermute | solution.py:496
  3.0 2.0 %collective-permute-start.2 = (bf16[256,128]{1,0:T(8,128)(2,1)}, bf16[256,128]{1,0:T(8,128)(2,1)S(1)}, u32[]{:S(2)}, u32[]{:S(2)}) collective-permute-start(bf16[256,128]{1,0:T(8,128)(2,1)} %param.21), channel_id=1, source_target_pairs={{0,24},{2,26},{4,28},{6,30},{8,0},{10,2},{12,4},{14,6},{16,8},{18,... | collective-permute-start | bytes 196616 | tf_op jit(solution)/shard_map/ppermute | solution.py:496
  5.1 1.0 %collective-permute-start.1 = (bf16[256,128]{1,0:T(8,128)(2,1)}, bf16[256,128]{1,0:T(8,128)(2,1)S(1)}, u32[]{:S(2)}, u32[]{:S(2)}) collective-permute-start(bf16[256,128]{1,0:T(8,128)(2,1)} %param.21), channel_id=1, source_target_pairs={{0,16},{2,18},{4,20},{6,22},{8,24},{10,26},{12,28},{14,30},{16,0},... | collective-permute-start | bytes 196616 | tf_op jit(solution)/shard_map/ppermute | solution.py:496
  6.1 1.0 %copy-done = bf16[128,2048]{1,0:T(8,128)(2,1)S(1)} copy-done((bf16[128,2048]{1,0:T(8,128)(2,1)S(1)}, bf16[128,2048]{1,0:T(8,128)(2,1)}, u32[]{:S(2)}) %copy-start) | copy-done | bytes 524312
  7.1 0.8 shard_map.118
  8.0 0.6 copy-done.1
  8.6 12.6 %all_to_all.15.refs_1_ = f32[16,2,128]{2,1,0:T(2,128)} all-to-all(f32[16,2,128]{2,1,0:T(2,128)S(1)} %get-tuple-element.49), channel_id=1, replica_groups=mesh['ctx'=16,'tp'=2] {'ctx'}, dimensions={0} | all-to-all | bytes 32768 | tf_op jit(solution)/shard_map/all_to_all | solution.py:494
  21.2 0.6 collective-permute-start.9
  21.8 0.0 collective-permute-done
  21.8 0.0 collective-permute-done.2
  21.8 0.0 collective-permute-done.1
  21.8 1.6 %pad_maximum_fusion.refs_0_ = bf16[4,256,128]{2,1,0:T(8,128)(2,1)} fusion(bf16[1,256,128]{2,1,0:T(8,128)(2,1)S(1)} %bitcast.19, bf16[1,256,128]{2,1,0:T(8,128)(2,1)S(1)} %bitcast.20, bf16[1,256,128]{2,1,0:T(8,128)(2,1)S(1)} %bitcast.18, bf16[1,256,128]{2,1,0:T(8,128)(2,1)} %bitcast.17), kind=kLoop, calls=%fused_computation | loop fusion | flops 393216 | bytes 524288 | tf_op jit(solution)/shard_map/stack | solution.py:499
  23.4 0.6 collective-permute-start.5
  24.0 1.4 %collective-permute-start.4 = (bf16[4,256,128]{2,1,0:T(8,128)(2,1)}, bf16[4,256,128]{2,1,0:T(8,128)(2,1)}, u32[]{:S(2)}, u32[]{:S(2)}) collective-permute-start(bf16[4,256,128]{2,1,0:T(8,128)(2,1)} %pad_maximum_fusion.refs_0_), channel_id=1, source_target_pairs={{0,4},{2,6},{4,0},{6,2},{8,12},{10,14},{12,8},{14,10},{16,20},{18,... | collective-permute-start | bytes 786440 | tf_op jit(solution)/shard_map/ppermute | solution.py:338
  25.4 0.6 collective-permute-start.3
  26.0 2.3 %collective-permute-start.14 = (bf16[256,1024]{1,0:T(8,128)(2,1)}, bf16[256,1024]{1,0:T(8,128)(2,1)}, u32[]{:S(2)}, u32[]{:S(2)}) collective-permute-start(bf16[256,1024]{1,0:T(8,128)(2,1)} %refs_8_.2), channel_id=1, source_target_pairs={{0,16},{2,18},{4,20},{6,22},{8,0},{10,2},{12,4},{14,6},{24,8},{26,... | collective-permute-start | bytes 1572872 | tf_op jit(solution)/shard_map/ppermute | solution.py:350
  28.3 7.4 %shard_map.119 = (bf16[2,128,256]{2,1,0:T(8,128)(2,1)}, bf16[2,128,256]{2,1,0:T(8,128)(2,1)}, bf16[2,128,256]{2,1,0:T(8,128)(2,1)}, bf16[2,128,256]{2,1,0:T(8,12...) custom-call(bf16[128,2048]{1,0:T(8,128)(2,1)} %refs_0_.1, ...), custom_call_target="tpu_custom_call" | custom-call | flops 1 | bytes 1 | tf_op jit(solution)/shard_map/pallas_call | solution.py:27
  35.8 3.8 %all-to-all-start.1 = ((f32[16,1,2,16,128]{4,3,2,1,0:T(8,128)}), f32[16,1,2,16,128]{4,3,2,1,0:T(8,128)S(1)}, u32[]{:S(2)}, u32[]{:S(2)}) async-start(f32[16,1,2,16,128]{4,3,2,1,0:T(8,128)} %bitcast.16), calls=%async_computation.1 | async-start | bytes 524288 | tf_op jit(solution)/shard_map/all_to_all | solution.py:546
  39.6 0.0 collective-permute-done.5.refs_3_
  39.6 0.0 collective-permute-done.4.refs_2_
  39.6 0.0 collective-permute-done.3.refs_1_
  39.6 2.0 %collective-permute-start.6 = (bf16[2,128,256]{2,1,0:T(8,128)(2,1)}, bf16[2,128,256]{2,1,0:T(8,128)(2,1)S(1)}, u32[]{:S(2)}, u32[]{:S(2)}) collective-permute-start(bf16[2,128,256]{2,1,0:T(8,128)(2,1)} %get-tuple-element.62), channel_id=1, source_target_pairs={{0,2},{2,4},{4,6},{6,0},{8,10},{10,12},{12,14},{14,8},{16,18},{18,... | collective-permute-start | bytes 393224 | tf_op jit(solution)/shard_map/ppermute | solution.py:338
  41.6 1.5 %collective-permute-start.7 = (bf16[2,128,256]{2,1,0:T(8,128)(2,1)}, bf16[2,128,256]{2,1,0:T(8,128)(2,1)S(1)}, u32[]{:S(2)}, u32[]{:S(2)}) collective-permute-start(bf16[2,128,256]{2,1,0:T(8,128)(2,1)} %get-tuple-element.63), channel_id=1, source_target_pairs={{0,4},{2,6},{4,0},{6,2},{8,12},{10,14},{12,8},{14,10},{16,20},{18,... | collective-permute-start | bytes 393224 | tf_op jit(solution)/shard_map/ppermute | solution.py:338
  43.1 1.5 %collective-permute-start.8 = (bf16[2,128,256]{2,1,0:T(8,128)(2,1)}, bf16[2,128,256]{2,1,0:T(8,128)(2,1)S(1)}, u32[]{:S(2)}, u32[]{:S(2)}) collective-permute-start(bf16[2,128,256]{2,1,0:T(8,128)(2,1)} %get-tuple-element.64), channel_id=1, source_target_pairs={{0,6},{2,0},{4,2},{6,4},{8,14},{10,8},{12,10},{14,12},{16,22},{18,... | collective-permute-start | bytes 393224 | tf_op jit(solution)/shard_map/ppermute | solution.py:338
  44.5 0.7 dynamic-slice_bitcast_fusion.q_ref
  45.2 1.6 %collective-permute-done.6.refs_1_ = bf16[2,128,256]{2,1,0:T(8,128)(2,1)S(1)} collective-permute-done((bf16[2,128,256]{2,1,0:T(8,128)(2,1)}, bf16[2,128,256]{2,1,0:T(8,128)(2,1)S(1)}, u32[]{:S(2)}, u32[]{:S(2)}) %collective-permute-start.6) | collective-permute-done | bytes 131104 | tf_op jit(solution)/shard_map/ppermute | solution.py:338
  46.9 2.1 %collective-permute-done.7.refs_2_ = bf16[2,128,256]{2,1,0:T(8,128)(2,1)S(1)} collective-permute-done((bf16[2,128,256]{2,1,0:T(8,128)(2,1)}, bf16[2,128,256]{2,1,0:T(8,128)(2,1)S(1)}, u32[]{:S(2)}, u32[]{:S(2)}) %collective-permute-start.7) | collective-permute-done | bytes 131104 | tf_op jit(solution)/shard_map/ppermute | solution.py:338
  49.0 0.3 collective-permute-done.8.refs_3_
  49.2 1.0 %collective-permute-start.15 = (bf16[256,1024]{1,0:T(8,128)(2,1)}, bf16[256,1024]{1,0:T(8,128)(2,1)}, u32[]{:S(2)}, u32[]{:S(2)}) collective-permute-start(bf16[256,1024]{1,0:T(8,128)(2,1)} %collective-permute-done.9.refs_9_), channel_id=1, source_target_pairs={{0,8},{2,10},{4,12},{6,14},{8,24},{10,26},{12,28},{14,30},{24,16},... | collective-permute-start | bytes 1572872 | tf_op jit(solution)/shard_map/ppermute | solution.py:350
  50.2 0.0 collective-permute-start.10
  50.2 0.5 collective-permute-start.11
  50.7 0.5 collective-permute-start.13
  51.2 0.7 collective-permute-done.10.refs_4_
  51.9 0.0 collective-permute-done.11.refs_5_
  51.9 0.1 collective-permute-done.12.refs_6_
  52.1 0.2 collective-permute-done.13.refs_7_
  52.2 0.8 shard_map.120
  53.0 6.0 %all-to-all-start.2 = ((f32[16,1,2,16,128]{4,3,2,1,0:T(8,128)}), f32[16,1,2,16,128]{4,3,2,1,0:T(8,128)}, u32[]{:S(2)}, u32[]{:S(2)}) async-start(f32[16,1,2,16,128]{4,3,2,1,0:T(8,128)} %shard_map.120), calls=%async_computation.2 | async-start | bytes 524288 | tf_op jit(solution)/shard_map/all_to_all | solution.py:556
  59.0 3.0 %collective-permute-done.15.refs_11_ = bf16[256,1024]{1,0:T(8,128)(2,1)} collective-permute-done((bf16[256,1024]{1,0:T(8,128)(2,1)}, bf16[256,1024]{1,0:T(8,128)(2,1)}, u32[]{:S(2)}, u32[]{:S(2)}) %collective-permute-start.15) | collective-permute-done | bytes 524320 | tf_op jit(solution)/shard_map/ppermute | solution.py:350
  62.0 4.0 %shard_map.121 = (f32[128,1024]{1,0:T(8,128)}, bf16[128,1024]{1,0:T(8,128)(2,1)}, bf16[128,1024]{1,0:T(8,128)(2,1)}, bf16[128,1024]{1,0:T(8,128)(2,1)}) custom-call(bf16[2,128,256]{2,1,0:T(8,128)(2,1)} %get-tuple-element.67.refs_0_, bf16[2,128,256]{2,1,0:T(8,128)(2,1)} %copy-done.2, bf16[2,128,256]{2,1,0:T(8,128)(2,1)} %copy-done.3, ...), custom_call_target="tpu_custom_call" | custom-call | flops 1 | bytes 1 | tf_op jit(solution)/shard_map/pallas_call | solution.py:27
  66.0 0.6 collective-permute-start.16
  66.6 1.5 %collective-permute-start.17 = (bf16[128,1024]{1,0:T(8,128)(2,1)}, bf16[128,1024]{1,0:T(8,128)(2,1)}, u32[]{:S(2)}, u32[]{:S(2)}) collective-permute-start(bf16[128,1024]{1,0:T(8,128)(2,1)} %get-tuple-element.86), channel_id=1, source_target_pairs={{0,4},{2,6},{4,0},{6,2},{8,12},{10,14},{12,8},{14,10},{16,20},{18,... | collective-permute-start | bytes 786440 | tf_op jit(solution)/shard_map/ppermute | solution.py:338
  68.1 0.5 collective-permute-start.18
  68.7 0.8 all-to-all-done.2
  69.4 7.2 %shard_map.122.refs_4_ = bf16[128,2048]{1,0:T(8,128)(2,1)} custom-call(f32[16,2,16,128]{3,2,1,0:T(8,128)} %bitcast.10.incoming_hbm, f32[16,8,2,16,128]{4,3,2,1,0:T(8,128)} %get-tuple-element.82.fresh_hbm, f32[2048,128]{1,0:T(8,128)} %get-tuple-element.83.dense_hbm, f32[512,128]{1,0:T(8,128)} %get-tuple-element.66.q_hbm, f32[512,128]{1,0:T(8,128)} %get-tuple-element.84.w_hbm, ...), custom_call_target="tpu_custom_call" | custom-call | flops 1 | bytes 1 | tf_op jit(solution)/shard_map/pallas_call | solution.py:27
  76.6 3.3 %collective-permute-done.17.refs_7_ = bf16[128,1024]{1,0:T(8,128)(2,1)} collective-permute-done((bf16[128,1024]{1,0:T(8,128)(2,1)}, bf16[128,1024]{1,0:T(8,128)(2,1)}, u32[]{:S(2)}, u32[]{:S(2)}) %collective-permute-start.17) | collective-permute-done | bytes 262176 | tf_op jit(solution)/shard_map/ppermute | solution.py:338
  79.9 2.3 %collective-permute-done.19.refs_5_ = bf16[128,2048]{1,0:T(8,128)(2,1)} collective-permute-done((bf16[128,2048]{1,0:T(8,128)(2,1)}, bf16[128,2048]{1,0:T(8,128)(2,1)}, u32[]{:S(2)}, u32[]{:S(2)}) %collective-permute-start.19) | collective-permute-done | bytes 524320 | tf_op jit(solution)/shard_map/ppermute | solution.py:338
  82.2 3.5 %shard_map.123 = bf16[128,1024]{1,0:T(8,128)(2,1)} custom-call(bf16[4,256,128]{2,1,0:T(8,128)(2,1)} %pad_maximum_fusion.refs_0_, bf16[4,256,128]{2,1,0:T(8,128)(2,1)} %collective-permute-done.3.refs_1_, bf16[4,256,128]{2,1,0:T(8,128)(2,1)} %collective-permute-done.4.refs_2_, bf16[4,256,128]{2,1,0:T(8,128)(2,1)} %collective-permute-done.5.refs_3_, ...), custom_call_target="tpu_custom_call" | custom-call | flops 1 | bytes 1 | tf_op jit(solution)/shard_map/pallas_call | solution.py:27
  (23 shorter events, 0.0 us)
Async XLA Ops:
  0.0 21.8 %collective-permute-start = (bf16[256,128]{1,0:T(8,128)(2,1)}, bf16[256,128]{1,0:T(8,128)(2,1)S(1)}, u32[]{:S(2)}, u32[]{:S(2)}) collective-permute-start(bf16[256,128]{1,0:T(8,128)(2,1)} %param.21), channel_id=1, source_target_pairs={{0,8},{2,10},{4,12},{6,14},{8,16},{10,18},{12,20},{14,22},{16,24},... | collective-permute-start | bytes 196616 | tf_op jit(solution)/shard_map/ppermute | solution.py:496
  3.0 18.8 %collective-permute-start.2 = (bf16[256,128]{1,0:T(8,128)(2,1)}, bf16[256,128]{1,0:T(8,128)(2,1)S(1)}, u32[]{:S(2)}, u32[]{:S(2)}) collective-permute-start(bf16[256,128]{1,0:T(8,128)(2,1)} %param.21), channel_id=1, source_target_pairs={{0,24},{2,26},{4,28},{6,30},{8,0},{10,2},{12,4},{14,6},{16,8},{18,... | collective-permute-start | bytes 196616 | tf_op jit(solution)/shard_map/ppermute | solution.py:496
  5.1 16.8 %collective-permute-start.1 = (bf16[256,128]{1,0:T(8,128)(2,1)}, bf16[256,128]{1,0:T(8,128)(2,1)S(1)}, u32[]{:S(2)}, u32[]{:S(2)}) collective-permute-start(bf16[256,128]{1,0:T(8,128)(2,1)} %param.21), channel_id=1, source_target_pairs={{0,16},{2,18},{4,20},{6,22},{8,24},{10,26},{12,28},{14,30},{16,0},... | collective-permute-start | bytes 196616 | tf_op jit(solution)/shard_map/ppermute | solution.py:496
  6.1 1.0 %copy-start = (bf16[128,2048]{1,0:T(8,128)(2,1)S(1)}, bf16[128,2048]{1,0:T(8,128)(2,1)}, u32[]{:S(2)}) copy-start(bf16[128,2048]{1,0:T(8,128)(2,1)} %refs_0_.1) | copy-start | bytes 1572868
  7.9 0.6 copy-start.1
  21.2 28.0 %collective-permute-start.9 = (bf16[256,1024]{1,0:T(8,128)(2,1)}, bf16[256,1024]{1,0:T(8,128)(2,1)}, u32[]{:S(2)}, u32[]{:S(2)}) collective-permute-start(bf16[256,1024]{1,0:T(8,128)(2,1)} %refs_8_.2), channel_id=1, source_target_pairs={{0,8},{2,10},{4,12},{6,14},{8,24},{10,26},{12,28},{14,30},{24,16},... | collective-permute-start | bytes 1572872 | tf_op jit(solution)/shard_map/ppermute | solution.py:350
  23.4 16.2 %collective-permute-start.5 = (bf16[4,256,128]{2,1,0:T(8,128)(2,1)}, bf16[4,256,128]{2,1,0:T(8,128)(2,1)}, u32[]{:S(2)}, u32[]{:S(2)}) collective-permute-start(bf16[4,256,128]{2,1,0:T(8,128)(2,1)} %pad_maximum_fusion.refs_0_), channel_id=1, source_target_pairs={{0,6},{2,0},{4,2},{6,4},{8,14},{10,8},{12,10},{14,12},{16,22},{18,... | collective-permute-start | bytes 786440 | tf_op jit(solution)/shard_map/ppermute | solution.py:338
  24.0 15.6 %collective-permute-start.4 = (bf16[4,256,128]{2,1,0:T(8,128)(2,1)}, bf16[4,256,128]{2,1,0:T(8,128)(2,1)}, u32[]{:S(2)}, u32[]{:S(2)}) collective-permute-start(bf16[4,256,128]{2,1,0:T(8,128)(2,1)} %pad_maximum_fusion.refs_0_), channel_id=1, source_target_pairs={{0,4},{2,6},{4,0},{6,2},{8,12},{10,14},{12,8},{14,10},{16,20},{18,... | collective-permute-start | bytes 786440 | tf_op jit(solution)/shard_map/ppermute | solution.py:338
  25.4 14.2 %collective-permute-start.3 = (bf16[4,256,128]{2,1,0:T(8,128)(2,1)}, bf16[4,256,128]{2,1,0:T(8,128)(2,1)}, u32[]{:S(2)}, u32[]{:S(2)}) collective-permute-start(bf16[4,256,128]{2,1,0:T(8,128)(2,1)} %pad_maximum_fusion.refs_0_), channel_id=1, source_target_pairs={{0,2},{2,4},{4,6},{6,0},{8,10},{10,12},{12,14},{14,8},{16,18},{18,... | collective-permute-start | bytes 786440 | tf_op jit(solution)/shard_map/ppermute | solution.py:338
  26.0 24.7 %collective-permute-start.14 = (bf16[256,1024]{1,0:T(8,128)(2,1)}, bf16[256,1024]{1,0:T(8,128)(2,1)}, u32[]{:S(2)}, u32[]{:S(2)}) collective-permute-start(bf16[256,1024]{1,0:T(8,128)(2,1)} %refs_8_.2), channel_id=1, source_target_pairs={{0,16},{2,18},{4,20},{6,22},{8,0},{10,2},{12,4},{14,6},{24,8},{26,... | collective-permute-start | bytes 1572872 | tf_op jit(solution)/shard_map/ppermute | solution.py:350
  35.8 15.5 %all-to-all-start.1 = ((f32[16,1,2,16,128]{4,3,2,1,0:T(8,128)}), f32[16,1,2,16,128]{4,3,2,1,0:T(8,128)S(1)}, u32[]{:S(2)}, u32[]{:S(2)}) async-start(f32[16,1,2,16,128]{4,3,2,1,0:T(8,128)} %bitcast.16), calls=%async_computation.1 | async-start | bytes 524288 | tf_op jit(solution)/shard_map/all_to_all | solution.py:546
  39.6 7.2 %collective-permute-start.6 = (bf16[2,128,256]{2,1,0:T(8,128)(2,1)}, bf16[2,128,256]{2,1,0:T(8,128)(2,1)S(1)}, u32[]{:S(2)}, u32[]{:S(2)}) collective-permute-start(bf16[2,128,256]{2,1,0:T(8,128)(2,1)} %get-tuple-element.62), channel_id=1, source_target_pairs={{0,2},{2,4},{4,6},{6,0},{8,10},{10,12},{12,14},{14,8},{16,18},{18,... | collective-permute-start | bytes 393224 | tf_op jit(solution)/shard_map/ppermute | solution.py:338
  41.6 7.4 %collective-permute-start.7 = (bf16[2,128,256]{2,1,0:T(8,128)(2,1)}, bf16[2,128,256]{2,1,0:T(8,128)(2,1)S(1)}, u32[]{:S(2)}, u32[]{:S(2)}) collective-permute-start(bf16[2,128,256]{2,1,0:T(8,128)(2,1)} %get-tuple-element.63), channel_id=1, source_target_pairs={{0,4},{2,6},{4,0},{6,2},{8,12},{10,14},{12,8},{14,10},{16,20},{18,... | collective-permute-start | bytes 393224 | tf_op jit(solution)/shard_map/ppermute | solution.py:338
  43.1 6.2 %collective-permute-start.8 = (bf16[2,128,256]{2,1,0:T(8,128)(2,1)}, bf16[2,128,256]{2,1,0:T(8,128)(2,1)S(1)}, u32[]{:S(2)}, u32[]{:S(2)}) collective-permute-start(bf16[2,128,256]{2,1,0:T(8,128)(2,1)} %get-tuple-element.64), channel_id=1, source_target_pairs={{0,6},{2,0},{4,2},{6,4},{8,14},{10,8},{12,10},{14,12},{16,22},{18,... | collective-permute-start | bytes 393224 | tf_op jit(solution)/shard_map/ppermute | solution.py:338
  46.9 6.2 %copy-start.2 = (bf16[2,128,256]{2,1,0:T(8,128)(2,1)}, bf16[2,128,256]{2,1,0:T(8,128)(2,1)S(1)}, u32[]{:S(2)}) copy-start(bf16[2,128,256]{2,1,0:T(8,128)(2,1)S(1)} %collective-permute-done.6.refs_1_) | copy-start | bytes 393220
  49.0 4.1 %copy-start.3 = (bf16[2,128,256]{2,1,0:T(8,128)(2,1)}, bf16[2,128,256]{2,1,0:T(8,128)(2,1)S(1)}, u32[]{:S(2)}) copy-start(bf16[2,128,256]{2,1,0:T(8,128)(2,1)S(1)} %collective-permute-done.7.refs_2_) | copy-start | bytes 393220
  49.2 3.8 %copy-start.4 = (bf16[2,128,256]{2,1,0:T(8,128)(2,1)}, bf16[2,128,256]{2,1,0:T(8,128)(2,1)S(1)}, u32[]{:S(2)}) copy-start(bf16[2,128,256]{2,1,0:T(8,128)(2,1)S(1)} %collective-permute-done.8.refs_3_) | copy-start | bytes 393220
  49.2 12.8 %collective-permute-start.15 = (bf16[256,1024]{1,0:T(8,128)(2,1)}, bf16[256,1024]{1,0:T(8,128)(2,1)}, u32[]{:S(2)}, u32[]{:S(2)}) collective-permute-start(bf16[256,1024]{1,0:T(8,128)(2,1)} %collective-permute-done.9.refs_9_), channel_id=1, source_target_pairs={{0,8},{2,10},{4,12},{6,14},{8,24},{10,26},{12,28},{14,30},{24,16},... | collective-permute-start | bytes 1572872 | tf_op jit(solution)/shard_map/ppermute | solution.py:350
  50.2 1.7 %collective-permute-start.10 = (bf16[2,128,256]{2,1,0:T(8,128)(2,1)}, bf16[2,128,256]{2,1,0:T(8,128)(2,1)S(1)}, u32[]{:S(2)}, u32[]{:S(2)}) collective-permute-start(bf16[2,128,256]{2,1,0:T(8,128)(2,1)} %get-tuple-element.67.refs_0_), channel_id=1, source_target_pairs={{0,1},{1,0},{2,3},{3,2},{4,5},{5,4},{6,7},{7,6},{8,9},{9,8},{10,11... | collective-permute-start | bytes 393224 | tf_op jit(solution)/shard_map/ppermute | solution.py:338
  50.2 1.7 %collective-permute-start.11 = (bf16[2,128,256]{2,1,0:T(8,128)(2,1)S(1)}, bf16[2,128,256]{2,1,0:T(8,128)(2,1)S(1)}, u32[]{:S(2)}, u32[]{:S(2)}) collective-permute-start(bf16[2,128,256]{2,1,0:T(8,128)(2,1)S(1)} %collective-permute-done.6.refs_1_), channel_id=1, source_target_pairs={{0,1},{1,0},{2,3},{3,2},{4,5},{5,4},{6,7},{7,6},{8,9},{9,8},{10,11... | collective-permute-start | bytes 393224 | tf_op jit(solution)/shard_map/ppermute | solution.py:338
  50.7 1.3 %collective-permute-start.12 = (bf16[2,128,256]{2,1,0:T(8,128)(2,1)S(1)}, bf16[2,128,256]{2,1,0:T(8,128)(2,1)S(1)}, u32[]{:S(2)}, u32[]{:S(2)}) collective-permute-start(bf16[2,128,256]{2,1,0:T(8,128)(2,1)S(1)} %collective-permute-done.7.refs_2_), channel_id=1, source_target_pairs={{0,1},{1,0},{2,3},{3,2},{4,5},{5,4},{6,7},{7,6},{8,9},{9,8},{10,11... | collective-permute-start | bytes 393224 | tf_op jit(solution)/shard_map/ppermute | solution.py:338
  50.7 1.5 %collective-permute-start.13 = (bf16[2,128,256]{2,1,0:T(8,128)(2,1)S(1)}, bf16[2,128,256]{2,1,0:T(8,128)(2,1)S(1)}, u32[]{:S(2)}, u32[]{:S(2)}) collective-permute-start(bf16[2,128,256]{2,1,0:T(8,128)(2,1)S(1)} %collective-permute-done.8.refs_3_), channel_id=1, source_target_pairs={{0,1},{1,0},{2,3},{3,2},{4,5},{5,4},{6,7},{7,6},{8,9},{9,8},{10,11... | collective-permute-start | bytes 393224 | tf_op jit(solution)/shard_map/ppermute | solution.py:338
  51.9 7.1 %copy-start.5 = (bf16[2,128,256]{2,1,0:T(8,128)(2,1)}, bf16[2,128,256]{2,1,0:T(8,128)(2,1)S(1)}, u32[]{:S(2)}) copy-start(bf16[2,128,256]{2,1,0:T(8,128)(2,1)S(1)} %collective-permute-done.10.refs_4_) | copy-start | bytes 393220
  51.9 7.1 %copy-start.6 = (bf16[2,128,256]{2,1,0:T(8,128)(2,1)}, bf16[2,128,256]{2,1,0:T(8,128)(2,1)S(1)}, u32[]{:S(2)}) copy-start(bf16[2,128,256]{2,1,0:T(8,128)(2,1)S(1)} %collective-permute-done.11.refs_5_) | copy-start | bytes 393220
  52.0 7.0 %copy-start.7 = (bf16[2,128,256]{2,1,0:T(8,128)(2,1)}, bf16[2,128,256]{2,1,0:T(8,128)(2,1)S(1)}, u32[]{:S(2)}) copy-start(bf16[2,128,256]{2,1,0:T(8,128)(2,1)S(1)} %collective-permute-done.12.refs_6_) | copy-start | bytes 393220
  52.2 6.8 %copy-start.8 = (bf16[2,128,256]{2,1,0:T(8,128)(2,1)}, bf16[2,128,256]{2,1,0:T(8,128)(2,1)S(1)}, u32[]{:S(2)}) copy-start(bf16[2,128,256]{2,1,0:T(8,128)(2,1)S(1)} %collective-permute-done.13.refs_7_) | copy-start | bytes 393220
  53.0 16.4 %all-to-all-start.2 = ((f32[16,1,2,16,128]{4,3,2,1,0:T(8,128)}), f32[16,1,2,16,128]{4,3,2,1,0:T(8,128)}, u32[]{:S(2)}, u32[]{:S(2)}) async-start(f32[16,1,2,16,128]{4,3,2,1,0:T(8,128)} %shard_map.120), calls=%async_computation.2 | async-start | bytes 524288 | tf_op jit(solution)/shard_map/all_to_all | solution.py:556
  66.0 10.6 %collective-permute-start.16 = (bf16[128,1024]{1,0:T(8,128)(2,1)}, bf16[128,1024]{1,0:T(8,128)(2,1)}, u32[]{:S(2)}, u32[]{:S(2)}) collective-permute-start(bf16[128,1024]{1,0:T(8,128)(2,1)} %get-tuple-element.85), channel_id=1, source_target_pairs={{0,6},{2,0},{4,2},{6,4},{8,14},{10,8},{12,10},{14,12},{16,22},{18,... | collective-permute-start | bytes 786440 | tf_op jit(solution)/shard_map/ppermute | solution.py:338
  66.6 13.3 %collective-permute-start.17 = (bf16[128,1024]{1,0:T(8,128)(2,1)}, bf16[128,1024]{1,0:T(8,128)(2,1)}, u32[]{:S(2)}, u32[]{:S(2)}) collective-permute-start(bf16[128,1024]{1,0:T(8,128)(2,1)} %get-tuple-element.86), channel_id=1, source_target_pairs={{0,4},{2,6},{4,0},{6,2},{8,12},{10,14},{12,8},{14,10},{16,20},{18,... | collective-permute-start | bytes 786440 | tf_op jit(solution)/shard_map/ppermute | solution.py:338
  68.1 11.8 %collective-permute-start.18 = (bf16[128,1024]{1,0:T(8,128)(2,1)}, bf16[128,1024]{1,0:T(8,128)(2,1)}, u32[]{:S(2)}, u32[]{:S(2)}) collective-permute-start(bf16[128,1024]{1,0:T(8,128)(2,1)} %get-tuple-element.87), channel_id=1, source_target_pairs={{0,2},{2,4},{4,6},{6,0},{8,10},{10,12},{12,14},{14,8},{16,18},{18,... | collective-permute-start | bytes 786440 | tf_op jit(solution)/shard_map/ppermute | solution.py:338
  79.9 2.3 %collective-permute-start.19 = (bf16[128,2048]{1,0:T(8,128)(2,1)}, bf16[128,2048]{1,0:T(8,128)(2,1)}, u32[]{:S(2)}, u32[]{:S(2)}) collective-permute-start(bf16[128,2048]{1,0:T(8,128)(2,1)} %shard_map.122.refs_4_), channel_id=1, source_target_pairs={{0,1},{1,0},{2,3},{3,2},{4,5},{5,4},{6,7},{7,6},{8,9},{9,8},{10,11... | collective-permute-start | bytes 1572872 | tf_op jit(solution)/shard_map/ppermute | solution.py:338

commit v8 on v7

--- a/solution.py
+++ b/solution.py
@@ -106,6 +106,11 @@
         return _
 
     lax.fori_loop(0, NDIM, one, 0)
+
+
+def partner(member, step):
+    low, high = lax.rem(member, 2), lax.div(member, 2)
+    return (1 - low if step & 1 else low) + 2 * (1 - high if step & 2 else high)
 
 
 def feed_kernel(members, *refs):
@@ -170,7 +175,7 @@
             normed_ref[at // depth, :, at % depth : at % depth + part] = normed[:, low : low + part]
         dense_ref[pl.ds(tile, length, stride=tiles), :] = normed.astype(f32)
     for away, ref in enumerate(near_hbm):
-        to = lax.rem(me + away, members)
+        to = partner(lax.rem(me, members), away)
         for sub in range(subs):
             stores.append(copies.start(normed_ref.at[sub * members + to], ref.at[sub]))
     stores.append(copies.start(dense_ref, dense_hbm))
@@ -336,6 +341,10 @@
     count = lax.axis_size(axis)
     pairs = [(i, i - i % group + (i + step) % group) for i in range(count)]
     return lax.ppermute(block, axis, pairs)
+
+
+def swap(block, step, group):
+    return lax.ppermute(block, "ctx", [(i, i - i % group + (i % group ^ step)) for i in range(lax.axis_size("ctx"))])
 
 
 def ring_of(layers):
@@ -442,7 +451,7 @@
     z_total = jnp.zeros((length, head), f32)
     for m in range(members):
         for k in range(layers):
-            block = lax.rem(layer + layers - k, layers) * members + lax.rem(member + members - m, members)
+            block = lax.rem(layer + layers - k, layers) * members + partner(member, m)
             z_total = z_total + mm(row_ref[block], weight_ref[m, k])
     queries = (z_total * affine_ref[0:1, :] + affine_ref[1:2, :]).astype(bf16)
     key_rows = (z_total * affine_ref[2:3, :] + affine_ref[3:4, :]).astype(bf16)
@@ -499,7 +508,7 @@
     line_z = jnp.stack(line_z)
     sums, v_weight = lax.optimization_barrier((sums, v_weight))
     all_v = [v_weight] + [ring_on(v_weight, members, layers, (-1) ** (k + 1)) for k in range(1, min(layers, 3))]
-    all_z = [line_z] + [along(line_z, "ctx", k, members) for k in range(1, members)]
+    all_z = [line_z] + [swap(line_z, k, members) for k in range(1, members)]
 
     rows = NDIM * 2 * tiles
     *near, dense, fresh, ends, q, w = call(
@@ -545,7 +554,7 @@
 
     arrived = lax.all_to_all(split(ends), "ctx", 0, 0)
     near, all_z = lax.optimization_barrier((near, all_z))
-    near = near[:1] + [along(near[k], "ctx", k, members) for k in range(1, members)]
+    near = near[:1] + [swap(near[k], k, members) for k in range(1, members)]
     my_q = lax.dynamic_index_in_dim(split(q.reshape(NDIM, 2, tiles, LANES)), place, 0, False)
     near, all_v[1], my_q = lax.optimization_barrier((near, all_v[1], my_q))
     for k in range(3, layers):
@@ -567,7 +576,7 @@
         ],
         layers + tp * members * subs + members,
     )
-    returned = [along(block, "ctx", -k, members) for k, block in enumerate(sent, 1)]
+    returned = [swap(block, k, members) for k, block in enumerate(sent, 1)]
     incoming, own = lax.optimization_barrier((incoming, own))
 
     (mixed_rows,) = call(

time: 86.2 us -> 85.6 us (level)
  starting transfers between devices: 30.9 us -> 29.6 us
    ppermute x0 -> x9, starting transfers between devices: none -> 10.6 us  [swap(): lax.ppermute(block, 'ctx', [(i, i - i % group + (i % group ^ step)) for i...]
    ppermute x14 -> x5, starting transfers between devices: 11.2 us -> 1.02 us  [along(): return lax.ppermute(block, axis, pairs)]
    ppermute x0 -> x9, waiting for transfers between devices: none -> 8.62 us  [swap(): lax.ppermute(block, 'ctx', [(i, i - i % group + (i % group ^ step)) for i...]
    ppermute x14 -> x5, waiting for transfers between devices: 10.6 us -> 3.26 us  [along(): return lax.ppermute(block, axis, pairs)]
    all_to_all x1, starting transfers between devices: 5.97 us -> 4.2 us  [body(): incoming = lax.all_to_all(starts, 'ctx', 0, 0)]
  transfers between devices with their start and end apart: 22 -> 22, of which waited for: 10 -> 11; matrix products, arithmetic and copies ran while one was open for 3% -> 3% of each run, Pallas kernels for 23% -> 24%
where the time goes in v8:
time: 85.6 us; the launch traced here: 85.1 us
  starting transfers between devices  29.6 us (35%)
  Pallas kernels  23.6 us (28%)
  waiting for transfers between devices  15.1 us (18%)
  blocking collectives  12.6 us (15%)
  local copies, waits for them, and re-layouts  2.43 us (3%)
  other arithmetic  1.58 us (2%)
    pallas_call x6, Pallas kernels, call(): pl.pallas_call(kernel, out_shape=outs, in_specs=[here] * len(inputs), out...  23.6 us
    all_to_all x1, blocking collectives, body(): sums = lax.all_to_all(totals, 'ctx', 0, 0)  12.6 us
    ppermute x9, starting transfers between devices, swap(): lax.ppermute(block, 'ctx', [(i, i - i % group + (i % group ^ step)) for i...  10.6 us
    ppermute x9, waiting for transfers between devices, swap(): lax.ppermute(block, 'ctx', [(i, i - i % group + (i % group ^ step)) for i...  8.62 us
    ppermute x3, starting transfers between devices, body(): lax.ppermute(z_weight, 'ctx', [(i, (i + members * k) % peers) for i in ra...  6.06 us
    all_to_all x1, starting transfers between devices, body(): incoming = lax.all_to_all(starts, 'ctx', 0, 0)  4.2 us
    ppermute x3, starting transfers between devices, ring_on(): return lax.ppermute(block, 'ctx', pairs)  4.2 us
    all_to_all x1, starting transfers between devices, body(): arrived = lax.all_to_all(split(ends), 'ctx', 0, 0)  3.55 us
  transfers between devices with their start and end apart: 22, of which 11 were waited for; matrix products, arithmetic and copies ran while one was open for 3% of the time, Pallas kernels for 24%

profile of v8, /device:TPU:0, one launch (start us, length us, event | category | flops | bytes accessed | tf_op | source)
XLA Modules:
  0.0 85.1 jit_solution(10464570359412592296)
XLA Ops:
  0.0 3.0 %collective-permute-start = (bf16[256,128]{1,0:T(8,128)(2,1)}, bf16[256,128]{1,0:T(8,128)(2,1)S(1)}, u32[]{:S(2)}, u32[]{:S(2)}) collective-permute-start(bf16[256,128]{1,0:T(8,128)(2,1)} %param.21), channel_id=1, source_target_pairs={{0,8},{2,10},{4,12},{6,14},{8,16},{10,18},{12,20},{14,22},{16,24},... | collective-permute-start | bytes 196616 | tf_op jit(solution)/shard_map/ppermute | solution.py:505
  3.0 2.0 %collective-permute-start.2 = (bf16[256,128]{1,0:T(8,128)(2,1)}, bf16[256,128]{1,0:T(8,128)(2,1)S(1)}, u32[]{:S(2)}, u32[]{:S(2)}) collective-permute-start(bf16[256,128]{1,0:T(8,128)(2,1)} %param.21), channel_id=1, source_target_pairs={{0,24},{2,26},{4,28},{6,30},{8,0},{10,2},{12,4},{14,6},{16,8},{18,... | collective-permute-start | bytes 196616 | tf_op jit(solution)/shard_map/ppermute | solution.py:505
  5.1 1.0 %collective-permute-start.1 = (bf16[256,128]{1,0:T(8,128)(2,1)}, bf16[256,128]{1,0:T(8,128)(2,1)S(1)}, u32[]{:S(2)}, u32[]{:S(2)}) collective-permute-start(bf16[256,128]{1,0:T(8,128)(2,1)} %param.21), channel_id=1, source_target_pairs={{0,16},{2,18},{4,20},{6,22},{8,24},{10,26},{12,28},{14,30},{16,0},... | collective-permute-start | bytes 196616 | tf_op jit(solution)/shard_map/ppermute | solution.py:505
  6.1 1.0 %copy-done = bf16[128,2048]{1,0:T(8,128)(2,1)S(1)} copy-done((bf16[128,2048]{1,0:T(8,128)(2,1)S(1)}, bf16[128,2048]{1,0:T(8,128)(2,1)}, u32[]{:S(2)}) %copy-start) | copy-done | bytes 524312
  7.1 0.8 shard_map.118
  8.0 0.6 copy-done.1
  8.6 12.6 %all_to_all.15.refs_1_ = f32[16,2,128]{2,1,0:T(2,128)} all-to-all(f32[16,2,128]{2,1,0:T(2,128)S(1)} %get-tuple-element.49), channel_id=1, replica_groups=mesh['ctx'=16,'tp'=2] {'ctx'}, dimensions={0} | all-to-all | bytes 32768 | tf_op jit(solution)/shard_map/all_to_all | solution.py:503
  21.2 0.6 collective-permute-start.9
  21.8 0.0 collective-permute-done
  21.8 0.0 collective-permute-done.2
  21.8 0.0 collective-permute-done.1
  21.8 1.6 %pad_maximum_fusion.refs_0_ = bf16[4,256,128]{2,1,0:T(8,128)(2,1)} fusion(bf16[1,256,128]{2,1,0:T(8,128)(2,1)S(1)} %bitcast.19, bf16[1,256,128]{2,1,0:T(8,128)(2,1)S(1)} %bitcast.20, bf16[1,256,128]{2,1,0:T(8,128)(2,1)S(1)} %bitcast.18, bf16[1,256,128]{2,1,0:T(8,128)(2,1)} %bitcast.17), kind=kLoop, calls=%fused_computation | loop fusion | flops 393216 | bytes 524288 | tf_op jit(solution)/shard_map/stack | solution.py:508
  23.4 0.6 collective-permute-start.5
  24.0 1.4 %collective-permute-start.4 = (bf16[4,256,128]{2,1,0:T(8,128)(2,1)}, bf16[4,256,128]{2,1,0:T(8,128)(2,1)}, u32[]{:S(2)}, u32[]{:S(2)}) collective-permute-start(bf16[4,256,128]{2,1,0:T(8,128)(2,1)} %pad_maximum_fusion.refs_0_), channel_id=1, source_target_pairs={{0,4},{2,6},{4,0},{6,2},{8,12},{10,14},{12,8},{14,10},{16,20},{18,... | collective-permute-start | bytes 786440 | tf_op jit(solution)/shard_map/ppermute | solution.py:347
  25.4 1.5 %collective-permute-start.3 = (bf16[4,256,128]{2,1,0:T(8,128)(2,1)}, bf16[4,256,128]{2,1,0:T(8,128)(2,1)}, u32[]{:S(2)}, u32[]{:S(2)}) collective-permute-start(bf16[4,256,128]{2,1,0:T(8,128)(2,1)} %pad_maximum_fusion.refs_0_), channel_id=1, source_target_pairs={{0,2},{2,0},{4,6},{6,4},{8,10},{10,8},{12,14},{14,12},{16,18},{18,... | collective-permute-start | bytes 786440 | tf_op jit(solution)/shard_map/ppermute | solution.py:347
  26.9 2.3 %collective-permute-start.14 = (bf16[256,1024]{1,0:T(8,128)(2,1)}, bf16[256,1024]{1,0:T(8,128)(2,1)}, u32[]{:S(2)}, u32[]{:S(2)}) collective-permute-start(bf16[256,1024]{1,0:T(8,128)(2,1)} %refs_8_.2), channel_id=1, source_target_pairs={{0,16},{2,18},{4,20},{6,22},{8,0},{10,2},{12,4},{14,6},{24,8},{26,... | collective-permute-start | bytes 1572872 | tf_op jit(solution)/shard_map/ppermute | solution.py:359
  29.2 7.4 %shard_map.119 = (bf16[2,128,256]{2,1,0:T(8,128)(2,1)}, bf16[2,128,256]{2,1,0:T(8,128)(2,1)}, bf16[2,128,256]{2,1,0:T(8,128)(2,1)}, bf16[2,128,256]{2,1,0:T(8,12...) custom-call(bf16[128,2048]{1,0:T(8,128)(2,1)} %refs_0_.1, ...), custom_call_target="tpu_custom_call" | custom-call | flops 1 | bytes 1 | tf_op jit(solution)/shard_map/pallas_call | solution.py:27
  36.6 3.5 %all-to-all-start.1 = ((f32[16,1,2,16,128]{4,3,2,1,0:T(8,128)}), f32[16,1,2,16,128]{4,3,2,1,0:T(8,128)S(1)}, u32[]{:S(2)}, u32[]{:S(2)}) async-start(f32[16,1,2,16,128]{4,3,2,1,0:T(8,128)} %bitcast.16), calls=%async_computation.1 | async-start | bytes 524288 | tf_op jit(solution)/shard_map/all_to_all | solution.py:555
  40.2 0.0 collective-permute-done.5.refs_3_
  40.2 0.0 collective-permute-done.3.refs_1_
  40.2 1.9 %collective-permute-start.6 = (bf16[2,128,256]{2,1,0:T(8,128)(2,1)}, bf16[2,128,256]{2,1,0:T(8,128)(2,1)S(1)}, u32[]{:S(2)}, u32[]{:S(2)}) collective-permute-start(bf16[2,128,256]{2,1,0:T(8,128)(2,1)} %get-tuple-element.62), channel_id=1, source_target_pairs={{0,2},{2,0},{4,6},{6,4},{8,10},{10,8},{12,14},{14,12},{16,18},{18,... | collective-permute-start | bytes 393224 | tf_op jit(solution)/shard_map/ppermute | solution.py:347
  42.1 1.5 %collective-permute-start.7 = (bf16[2,128,256]{2,1,0:T(8,128)(2,1)}, bf16[2,128,256]{2,1,0:T(8,128)(2,1)S(1)}, u32[]{:S(2)}, u32[]{:S(2)}) collective-permute-start(bf16[2,128,256]{2,1,0:T(8,128)(2,1)} %get-tuple-element.63), channel_id=1, source_target_pairs={{0,4},{2,6},{4,0},{6,2},{8,12},{10,14},{12,8},{14,10},{16,20},{18,... | collective-permute-start | bytes 393224 | tf_op jit(solution)/shard_map/ppermute | solution.py:347
  43.6 0.2 collective-permute-start.8
  43.8 0.7 dynamic-slice_bitcast_fusion.q_ref
  44.5 1.4 %collective-permute-done.6.refs_1_ = bf16[2,128,256]{2,1,0:T(8,128)(2,1)S(1)} collective-permute-done((bf16[2,128,256]{2,1,0:T(8,128)(2,1)}, bf16[2,128,256]{2,1,0:T(8,128)(2,1)S(1)}, u32[]{:S(2)}, u32[]{:S(2)}) %collective-permute-start.6) | collective-permute-done | bytes 131104 | tf_op jit(solution)/shard_map/ppermute | solution.py:347
  45.9 2.2 %collective-permute-done.7.refs_2_ = bf16[2,128,256]{2,1,0:T(8,128)(2,1)S(1)} collective-permute-done((bf16[2,128,256]{2,1,0:T(8,128)(2,1)}, bf16[2,128,256]{2,1,0:T(8,128)(2,1)S(1)}, u32[]{:S(2)}, u32[]{:S(2)}) %collective-permute-start.7) | collective-permute-done | bytes 131104 | tf_op jit(solution)/shard_map/ppermute | solution.py:347
  48.1 2.4 %collective-permute-done.8.refs_3_ = bf16[2,128,256]{2,1,0:T(8,128)(2,1)S(1)} collective-permute-done((bf16[2,128,256]{2,1,0:T(8,128)(2,1)}, bf16[2,128,256]{2,1,0:T(8,128)(2,1)S(1)}, u32[]{:S(2)}, u32[]{:S(2)}) %collective-permute-start.8) | collective-permute-done | bytes 131104 | tf_op jit(solution)/shard_map/ppermute | solution.py:347
  50.6 1.3 %collective-permute-start.15 = (bf16[256,1024]{1,0:T(8,128)(2,1)}, bf16[256,1024]{1,0:T(8,128)(2,1)}, u32[]{:S(2)}, u32[]{:S(2)}) collective-permute-start(bf16[256,1024]{1,0:T(8,128)(2,1)} %collective-permute-done.9.refs_9_), channel_id=1, source_target_pairs={{0,8},{2,10},{4,12},{6,14},{8,24},{10,26},{12,28},{14,30},{24,16},... | collective-permute-start | bytes 1572872 | tf_op jit(solution)/shard_map/ppermute | solution.py:359
  51.8 0.0 collective-permute-start.10
  51.8 0.5 collective-permute-start.11
  52.4 0.5 collective-permute-start.13
  52.9 0.0 all-to-all-done.1.ends_ref
  52.9 0.7 collective-permute-done.10.refs_4_
  53.6 0.1 collective-permute-done.12.refs_6_
  53.7 0.2 collective-permute-done.13.refs_7_
  53.9 0.8 shard_map.120
  54.7 4.2 %all-to-all-start.2 = ((f32[16,1,2,16,128]{4,3,2,1,0:T(8,128)}), f32[16,1,2,16,128]{4,3,2,1,0:T(8,128)}, u32[]{:S(2)}, u32[]{:S(2)}) async-start(f32[16,1,2,16,128]{4,3,2,1,0:T(8,128)} %shard_map.120), calls=%async_computation.2 | async-start | bytes 524288 | tf_op jit(solution)/shard_map/all_to_all | solution.py:565
  58.9 3.1 %collective-permute-done.15.refs_11_ = bf16[256,1024]{1,0:T(8,128)(2,1)} collective-permute-done((bf16[256,1024]{1,0:T(8,128)(2,1)}, bf16[256,1024]{1,0:T(8,128)(2,1)}, u32[]{:S(2)}, u32[]{:S(2)}) %collective-permute-start.15) | collective-permute-done | bytes 524320 | tf_op jit(solution)/shard_map/ppermute | solution.py:359
  62.0 4.0 %shard_map.121 = (f32[128,1024]{1,0:T(8,128)}, bf16[128,1024]{1,0:T(8,128)(2,1)}, bf16[128,1024]{1,0:T(8,128)(2,1)}, bf16[128,1024]{1,0:T(8,128)(2,1)}) custom-call(bf16[2,128,256]{2,1,0:T(8,128)(2,1)} %get-tuple-element.67.refs_0_, bf16[2,128,256]{2,1,0:T(8,128)(2,1)} %copy-done.2, bf16[2,128,256]{2,1,0:T(8,128)(2,1)} %copy-done.3, ...), custom_call_target="tpu_custom_call" | custom-call | flops 1 | bytes 1 | tf_op jit(solution)/shard_map/pallas_call | solution.py:27
  66.0 0.7 collective-permute-start.16
  66.7 0.5 collective-permute-start.17
  67.2 2.3 %collective-permute-start.18 = (bf16[128,1024]{1,0:T(8,128)(2,1)}, bf16[128,1024]{1,0:T(8,128)(2,1)}, u32[]{:S(2)}, u32[]{:S(2)}) collective-permute-start(bf16[128,1024]{1,0:T(8,128)(2,1)} %get-tuple-element.87), channel_id=1, source_target_pairs={{0,6},{2,4},{4,2},{6,0},{8,14},{10,12},{12,10},{14,8},{16,22},{18,... | collective-permute-start | bytes 786440 | tf_op jit(solution)/shard_map/ppermute | solution.py:347
  69.5 0.1 all-to-all-done.2
  69.6 7.2 %shard_map.122.refs_4_ = bf16[128,2048]{1,0:T(8,128)(2,1)} custom-call(f32[16,2,16,128]{3,2,1,0:T(8,128)} %bitcast.10.incoming_hbm, f32[16,8,2,16,128]{4,3,2,1,0:T(8,128)} %get-tuple-element.82.fresh_hbm, f32[2048,128]{1,0:T(8,128)} %get-tuple-element.83.dense_hbm, f32[512,128]{1,0:T(8,128)} %get-tuple-element.66.q_hbm, f32[512,128]{1,0:T(8,128)} %get-tuple-element.84.w_hbm, ...), custom_call_target="tpu_custom_call" | custom-call | flops 1 | bytes 1 | tf_op jit(solution)/shard_map/pallas_call | solution.py:27
  76.8 1.2 %collective-permute-done.17.refs_7_ = bf16[128,1024]{1,0:T(8,128)(2,1)} collective-permute-done((bf16[128,1024]{1,0:T(8,128)(2,1)}, bf16[128,1024]{1,0:T(8,128)(2,1)}, u32[]{:S(2)}, u32[]{:S(2)}) %collective-permute-start.17) | collective-permute-done | bytes 262176 | tf_op jit(solution)/shard_map/ppermute | solution.py:347
  78.0 1.3 %collective-permute-done.18.refs_8_ = bf16[128,1024]{1,0:T(8,128)(2,1)} collective-permute-done((bf16[128,1024]{1,0:T(8,128)(2,1)}, bf16[128,1024]{1,0:T(8,128)(2,1)}, u32[]{:S(2)}, u32[]{:S(2)}) %collective-permute-start.18) | collective-permute-done | bytes 262176 | tf_op jit(solution)/shard_map/ppermute | solution.py:347
  79.4 2.2 %collective-permute-done.19.refs_5_ = bf16[128,2048]{1,0:T(8,128)(2,1)} collective-permute-done((bf16[128,2048]{1,0:T(8,128)(2,1)}, bf16[128,2048]{1,0:T(8,128)(2,1)}, u32[]{:S(2)}, u32[]{:S(2)}) %collective-permute-start.19) | collective-permute-done | bytes 524320 | tf_op jit(solution)/shard_map/ppermute | solution.py:343
  81.6 3.5 %shard_map.123 = bf16[128,1024]{1,0:T(8,128)(2,1)} custom-call(bf16[4,256,128]{2,1,0:T(8,128)(2,1)} %pad_maximum_fusion.refs_0_, bf16[4,256,128]{2,1,0:T(8,128)(2,1)} %collective-permute-done.3.refs_1_, bf16[4,256,128]{2,1,0:T(8,128)(2,1)} %collective-permute-done.4.refs_2_, bf16[4,256,128]{2,1,0:T(8,128)(2,1)} %collective-permute-done.5.refs_3_, ...), custom_call_target="tpu_custom_call" | custom-call | flops 1 | bytes 1 | tf_op jit(solution)/shard_map/pallas_call | solution.py:27
  (23 shorter events, 0.0 us)
Async XLA Ops:
  0.0 21.8 %collective-permute-start = (bf16[256,128]{1,0:T(8,128)(2,1)}, bf16[256,128]{1,0:T(8,128)(2,1)S(1)}, u32[]{:S(2)}, u32[]{:S(2)}) collective-permute-start(bf16[256,128]{1,0:T(8,128)(2,1)} %param.21), channel_id=1, source_target_pairs={{0,8},{2,10},{4,12},{6,14},{8,16},{10,18},{12,20},{14,22},{16,24},... | collective-permute-start | bytes 196616 | tf_op jit(solution)/shard_map/ppermute | solution.py:505
  3.0 18.8 %collective-permute-start.2 = (bf16[256,128]{1,0:T(8,128)(2,1)}, bf16[256,128]{1,0:T(8,128)(2,1)S(1)}, u32[]{:S(2)}, u32[]{:S(2)}) collective-permute-start(bf16[256,128]{1,0:T(8,128)(2,1)} %param.21), channel_id=1, source_target_pairs={{0,24},{2,26},{4,28},{6,30},{8,0},{10,2},{12,4},{14,6},{16,8},{18,... | collective-permute-start | bytes 196616 | tf_op jit(solution)/shard_map/ppermute | solution.py:505
  5.1 16.8 %collective-permute-start.1 = (bf16[256,128]{1,0:T(8,128)(2,1)}, bf16[256,128]{1,0:T(8,128)(2,1)S(1)}, u32[]{:S(2)}, u32[]{:S(2)}) collective-permute-start(bf16[256,128]{1,0:T(8,128)(2,1)} %param.21), channel_id=1, source_target_pairs={{0,16},{2,18},{4,20},{6,22},{8,24},{10,26},{12,28},{14,30},{16,0},... | collective-permute-start | bytes 196616 | tf_op jit(solution)/shard_map/ppermute | solution.py:505
  6.1 1.0 %copy-start = (bf16[128,2048]{1,0:T(8,128)(2,1)S(1)}, bf16[128,2048]{1,0:T(8,128)(2,1)}, u32[]{:S(2)}) copy-start(bf16[128,2048]{1,0:T(8,128)(2,1)} %refs_0_.1) | copy-start | bytes 1572868
  7.9 0.6 copy-start.1
  21.2 29.4 %collective-permute-start.9 = (bf16[256,1024]{1,0:T(8,128)(2,1)}, bf16[256,1024]{1,0:T(8,128)(2,1)}, u32[]{:S(2)}, u32[]{:S(2)}) collective-permute-start(bf16[256,1024]{1,0:T(8,128)(2,1)} %refs_8_.2), channel_id=1, source_target_pairs={{0,8},{2,10},{4,12},{6,14},{8,24},{10,26},{12,28},{14,30},{24,16},... | collective-permute-start | bytes 1572872 | tf_op jit(solution)/shard_map/ppermute | solution.py:359
  23.4 16.8 %collective-permute-start.5 = (bf16[4,256,128]{2,1,0:T(8,128)(2,1)}, bf16[4,256,128]{2,1,0:T(8,128)(2,1)}, u32[]{:S(2)}, u32[]{:S(2)}) collective-permute-start(bf16[4,256,128]{2,1,0:T(8,128)(2,1)} %pad_maximum_fusion.refs_0_), channel_id=1, source_target_pairs={{0,6},{2,4},{4,2},{6,0},{8,14},{10,12},{12,10},{14,8},{16,22},{18,... | collective-permute-start | bytes 786440 | tf_op jit(solution)/shard_map/ppermute | solution.py:347
  24.0 16.2 %collective-permute-start.4 = (bf16[4,256,128]{2,1,0:T(8,128)(2,1)}, bf16[4,256,128]{2,1,0:T(8,128)(2,1)}, u32[]{:S(2)}, u32[]{:S(2)}) collective-permute-start(bf16[4,256,128]{2,1,0:T(8,128)(2,1)} %pad_maximum_fusion.refs_0_), channel_id=1, source_target_pairs={{0,4},{2,6},{4,0},{6,2},{8,12},{10,14},{12,8},{14,10},{16,20},{18,... | collective-permute-start | bytes 786440 | tf_op jit(solution)/shard_map/ppermute | solution.py:347
  25.4 14.8 %collective-permute-start.3 = (bf16[4,256,128]{2,1,0:T(8,128)(2,1)}, bf16[4,256,128]{2,1,0:T(8,128)(2,1)}, u32[]{:S(2)}, u32[]{:S(2)}) collective-permute-start(bf16[4,256,128]{2,1,0:T(8,128)(2,1)} %pad_maximum_fusion.refs_0_), channel_id=1, source_target_pairs={{0,2},{2,0},{4,6},{6,4},{8,10},{10,8},{12,14},{14,12},{16,18},{18,... | collective-permute-start | bytes 786440 | tf_op jit(solution)/shard_map/ppermute | solution.py:347
  26.9 25.5 %collective-permute-start.14 = (bf16[256,1024]{1,0:T(8,128)(2,1)}, bf16[256,1024]{1,0:T(8,128)(2,1)}, u32[]{:S(2)}, u32[]{:S(2)}) collective-permute-start(bf16[256,1024]{1,0:T(8,128)(2,1)} %refs_8_.2), channel_id=1, source_target_pairs={{0,16},{2,18},{4,20},{6,22},{8,0},{10,2},{12,4},{14,6},{24,8},{26,... | collective-permute-start | bytes 1572872 | tf_op jit(solution)/shard_map/ppermute | solution.py:359
  36.6 16.2 %all-to-all-start.1 = ((f32[16,1,2,16,128]{4,3,2,1,0:T(8,128)}), f32[16,1,2,16,128]{4,3,2,1,0:T(8,128)S(1)}, u32[]{:S(2)}, u32[]{:S(2)}) async-start(f32[16,1,2,16,128]{4,3,2,1,0:T(8,128)} %bitcast.16), calls=%async_computation.1 | async-start | bytes 524288 | tf_op jit(solution)/shard_map/all_to_all | solution.py:555
  40.2 5.7 %collective-permute-start.6 = (bf16[2,128,256]{2,1,0:T(8,128)(2,1)}, bf16[2,128,256]{2,1,0:T(8,128)(2,1)S(1)}, u32[]{:S(2)}, u32[]{:S(2)}) collective-permute-start(bf16[2,128,256]{2,1,0:T(8,128)(2,1)} %get-tuple-element.62), channel_id=1, source_target_pairs={{0,2},{2,0},{4,6},{6,4},{8,10},{10,8},{12,14},{14,12},{16,18},{18,... | collective-permute-start | bytes 393224 | tf_op jit(solution)/shard_map/ppermute | solution.py:347
  42.1 6.1 %collective-permute-start.7 = (bf16[2,128,256]{2,1,0:T(8,128)(2,1)}, bf16[2,128,256]{2,1,0:T(8,128)(2,1)S(1)}, u32[]{:S(2)}, u32[]{:S(2)}) collective-permute-start(bf16[2,128,256]{2,1,0:T(8,128)(2,1)} %get-tuple-element.63), channel_id=1, source_target_pairs={{0,4},{2,6},{4,0},{6,2},{8,12},{10,14},{12,8},{14,10},{16,20},{18,... | collective-permute-start | bytes 393224 | tf_op jit(solution)/shard_map/ppermute | solution.py:347
  43.6 7.0 %collective-permute-start.8 = (bf16[2,128,256]{2,1,0:T(8,128)(2,1)}, bf16[2,128,256]{2,1,0:T(8,128)(2,1)S(1)}, u32[]{:S(2)}, u32[]{:S(2)}) collective-permute-start(bf16[2,128,256]{2,1,0:T(8,128)(2,1)} %get-tuple-element.64), channel_id=1, source_target_pairs={{0,6},{2,4},{4,2},{6,0},{8,14},{10,12},{12,10},{14,8},{16,22},{18,... | collective-permute-start | bytes 393224 | tf_op jit(solution)/shard_map/ppermute | solution.py:347
  45.9 8.7 %copy-start.2 = (bf16[2,128,256]{2,1,0:T(8,128)(2,1)}, bf16[2,128,256]{2,1,0:T(8,128)(2,1)S(1)}, u32[]{:S(2)}) copy-start(bf16[2,128,256]{2,1,0:T(8,128)(2,1)S(1)} %collective-permute-done.6.refs_1_) | copy-start | bytes 393220
  48.1 6.5 %copy-start.3 = (bf16[2,128,256]{2,1,0:T(8,128)(2,1)}, bf16[2,128,256]{2,1,0:T(8,128)(2,1)S(1)}, u32[]{:S(2)}) copy-start(bf16[2,128,256]{2,1,0:T(8,128)(2,1)S(1)} %collective-permute-done.7.refs_2_) | copy-start | bytes 393220
  50.6 4.1 %copy-start.4 = (bf16[2,128,256]{2,1,0:T(8,128)(2,1)}, bf16[2,128,256]{2,1,0:T(8,128)(2,1)S(1)}, u32[]{:S(2)}) copy-start(bf16[2,128,256]{2,1,0:T(8,128)(2,1)S(1)} %collective-permute-done.8.refs_3_) | copy-start | bytes 393220
  50.6 11.5 %collective-permute-start.15 = (bf16[256,1024]{1,0:T(8,128)(2,1)}, bf16[256,1024]{1,0:T(8,128)(2,1)}, u32[]{:S(2)}, u32[]{:S(2)}) collective-permute-start(bf16[256,1024]{1,0:T(8,128)(2,1)} %collective-permute-done.9.refs_9_), channel_id=1, source_target_pairs={{0,8},{2,10},{4,12},{6,14},{8,24},{10,26},{12,28},{14,30},{24,16},... | collective-permute-start | bytes 1572872 | tf_op jit(solution)/shard_map/ppermute | solution.py:359
  51.8 1.7 %collective-permute-start.10 = (bf16[2,128,256]{2,1,0:T(8,128)(2,1)}, bf16[2,128,256]{2,1,0:T(8,128)(2,1)S(1)}, u32[]{:S(2)}, u32[]{:S(2)}) collective-permute-start(bf16[2,128,256]{2,1,0:T(8,128)(2,1)} %get-tuple-element.67.refs_0_), channel_id=1, source_target_pairs={{0,1},{1,0},{2,3},{3,2},{4,5},{5,4},{6,7},{7,6},{8,9},{9,8},{10,11... | collective-permute-start | bytes 393224 | tf_op jit(solution)/shard_map/ppermute | solution.py:343
  51.8 1.7 %collective-permute-start.11 = (bf16[2,128,256]{2,1,0:T(8,128)(2,1)S(1)}, bf16[2,128,256]{2,1,0:T(8,128)(2,1)S(1)}, u32[]{:S(2)}, u32[]{:S(2)}) collective-permute-start(bf16[2,128,256]{2,1,0:T(8,128)(2,1)S(1)} %collective-permute-done.6.refs_1_), channel_id=1, source_target_pairs={{0,1},{1,0},{2,3},{3,2},{4,5},{5,4},{6,7},{7,6},{8,9},{9,8},{10,11... | collective-permute-start | bytes 393224 | tf_op jit(solution)/shard_map/ppermute | solution.py:343
  52.4 1.3 %collective-permute-start.12 = (bf16[2,128,256]{2,1,0:T(8,128)(2,1)S(1)}, bf16[2,128,256]{2,1,0:T(8,128)(2,1)S(1)}, u32[]{:S(2)}, u32[]{:S(2)}) collective-permute-start(bf16[2,128,256]{2,1,0:T(8,128)(2,1)S(1)} %collective-permute-done.7.refs_2_), channel_id=1, source_target_pairs={{0,1},{1,0},{2,3},{3,2},{4,5},{5,4},{6,7},{7,6},{8,9},{9,8},{10,11... | collective-permute-start | bytes 393224 | tf_op jit(solution)/shard_map/ppermute | solution.py:343
  52.4 1.5 %collective-permute-start.13 = (bf16[2,128,256]{2,1,0:T(8,128)(2,1)S(1)}, bf16[2,128,256]{2,1,0:T(8,128)(2,1)S(1)}, u32[]{:S(2)}, u32[]{:S(2)}) collective-permute-start(bf16[2,128,256]{2,1,0:T(8,128)(2,1)S(1)} %collective-permute-done.8.refs_3_), channel_id=1, source_target_pairs={{0,1},{1,0},{2,3},{3,2},{4,5},{5,4},{6,7},{7,6},{8,9},{9,8},{10,11... | collective-permute-start | bytes 393224 | tf_op jit(solution)/shard_map/ppermute | solution.py:343
  53.6 5.3 %copy-start.5 = (bf16[2,128,256]{2,1,0:T(8,128)(2,1)}, bf16[2,128,256]{2,1,0:T(8,128)(2,1)S(1)}, u32[]{:S(2)}) copy-start(bf16[2,128,256]{2,1,0:T(8,128)(2,1)S(1)} %collective-permute-done.10.refs_4_) | copy-start | bytes 393220
  53.6 5.3 %copy-start.6 = (bf16[2,128,256]{2,1,0:T(8,128)(2,1)}, bf16[2,128,256]{2,1,0:T(8,128)(2,1)S(1)}, u32[]{:S(2)}) copy-start(bf16[2,128,256]{2,1,0:T(8,128)(2,1)S(1)} %collective-permute-done.11.refs_5_) | copy-start | bytes 393220
  53.7 5.2 %copy-start.7 = (bf16[2,128,256]{2,1,0:T(8,128)(2,1)}, bf16[2,128,256]{2,1,0:T(8,128)(2,1)S(1)}, u32[]{:S(2)}) copy-start(bf16[2,128,256]{2,1,0:T(8,128)(2,1)S(1)} %collective-permute-done.12.refs_6_) | copy-start | bytes 393220
  53.9 5.0 %copy-start.8 = (bf16[2,128,256]{2,1,0:T(8,128)(2,1)}, bf16[2,128,256]{2,1,0:T(8,128)(2,1)S(1)}, u32[]{:S(2)}) copy-start(bf16[2,128,256]{2,1,0:T(8,128)(2,1)S(1)} %collective-permute-done.13.refs_7_) | copy-start | bytes 393220
  54.7 14.9 %all-to-all-start.2 = ((f32[16,1,2,16,128]{4,3,2,1,0:T(8,128)}), f32[16,1,2,16,128]{4,3,2,1,0:T(8,128)}, u32[]{:S(2)}, u32[]{:S(2)}) async-start(f32[16,1,2,16,128]{4,3,2,1,0:T(8,128)} %shard_map.120), calls=%async_computation.2 | async-start | bytes 524288 | tf_op jit(solution)/shard_map/all_to_all | solution.py:565
  66.0 10.8 %collective-permute-start.16 = (bf16[128,1024]{1,0:T(8,128)(2,1)}, bf16[128,1024]{1,0:T(8,128)(2,1)}, u32[]{:S(2)}, u32[]{:S(2)}) collective-permute-start(bf16[128,1024]{1,0:T(8,128)(2,1)} %get-tuple-element.85), channel_id=1, source_target_pairs={{0,2},{2,0},{4,6},{6,4},{8,10},{10,8},{12,14},{14,12},{16,18},{18,... | collective-permute-start | bytes 786440 | tf_op jit(solution)/shard_map/ppermute | solution.py:347
  66.7 11.3 %collective-permute-start.17 = (bf16[128,1024]{1,0:T(8,128)(2,1)}, bf16[128,1024]{1,0:T(8,128)(2,1)}, u32[]{:S(2)}, u32[]{:S(2)}) collective-permute-start(bf16[128,1024]{1,0:T(8,128)(2,1)} %get-tuple-element.86), channel_id=1, source_target_pairs={{0,4},{2,6},{4,0},{6,2},{8,12},{10,14},{12,8},{14,10},{16,20},{18,... | collective-permute-start | bytes 786440 | tf_op jit(solution)/shard_map/ppermute | solution.py:347
  67.2 12.1 %collective-permute-start.18 = (bf16[128,1024]{1,0:T(8,128)(2,1)}, bf16[128,1024]{1,0:T(8,128)(2,1)}, u32[]{:S(2)}, u32[]{:S(2)}) collective-permute-start(bf16[128,1024]{1,0:T(8,128)(2,1)} %get-tuple-element.87), channel_id=1, source_target_pairs={{0,6},{2,4},{4,2},{6,0},{8,14},{10,12},{12,10},{14,8},{16,22},{18,... | collective-permute-start | bytes 786440 | tf_op jit(solution)/shard_map/ppermute | solution.py:347
  79.4 2.3 %collective-permute-start.19 = (bf16[128,2048]{1,0:T(8,128)(2,1)}, bf16[128,2048]{1,0:T(8,128)(2,1)}, u32[]{:S(2)}, u32[]{:S(2)}) collective-permute-start(bf16[128,2048]{1,0:T(8,128)(2,1)} %shard_map.122.refs_4_), channel_id=1, source_target_pairs={{0,1},{1,0},{2,3},{3,2},{4,5},{5,4},{6,7},{7,6},{8,9},{9,8},{10,11... | collective-permute-start | bytes 1572872 | tf_op jit(solution)/shard_map/ppermute | solution.py:343

commit v9 on v8

--- a/solution.py
+++ b/solution.py
@@ -414,24 +414,39 @@
         store.wait()
 
 
+def values_kernel(*refs):
+    *parts_hbm, own_hbm, result_hbm, part_ref, own_ref, value_ref, sems = refs
+    copies = Copies(sems)
+    loads = [copies.start(own_hbm, own_ref)] + [copies.start(a, part_ref.at[k]) for k, a in enumerate(parts_hbm)]
+    for load in loads:
+        load.wait()
+    total = own_ref[...]
+    for k in range(len(parts_hbm)):
+        total = total + part_ref[k].astype(f32)
+    value_ref[...] = (total / (1.0 + jnp.exp(-total))).astype(bf16)
+    copies.start(value_ref, result_hbm).wait()
+
+
 def attend_kernel(members, tp, *refs):
     weights_hbm, refs = refs[:members], refs[members:]
     mixed_hbm, refs = refs[:tp], refs[tp:]
-    parts_hbm, refs = refs[: members - 1], refs[members - 1 :]
-    own_hbm, gain_hbm, affine_hbm, result_hbm = refs[:4]
-    weight_ref, mixed_ref, part_ref, own_ref, gain_ref, affine_ref, row_ref, value_ref, result_ref, sems = refs[4:]
+    values_hbm, gain_hbm, affine_hbm, result_hbm = refs[:4]
+    weight_ref, mixed_ref, gain_ref, affine_ref, value_ref, result_ref, sems = refs[4:]
     copies = Copies(sems)
     loads = [copies.start(a, mixed_ref.at[k]) for k, a in enumerate(mixed_hbm)]
     loads += [copies.start(gain_hbm, gain_ref), copies.start(affine_hbm, affine_ref)]
     first = len(loads)
-    loads += [copies.start(a, weight_ref.at[k]) for k, a in enumerate(weights_hbm)]
-    second = len(loads)
-    loads += [copies.start(own_hbm, own_ref)] + [copies.start(a, part_ref.at[k]) for k, a in enumerate(parts_hbm)]
-    _, layers, depth, head = weight_ref.shape
-    _, length, channels = mixed_ref.shape
     place, half = lax.axis_index("ctx"), lax.axis_index("tp")
     member, layer = lax.rem(place, members), lax.div(place, members)
-    blocks = channels // depth
+    layers, depth, head = weights_hbm[0].shape
+    for m in range(members):
+        for k in range(layers):
+            block = lax.rem(layer + layers - k, layers) * members + partner(member, m)
+            rows = pl.ds(pl.multiple_of(block * depth, depth), depth)
+            loads.append(copies.start(weights_hbm[m].at[k], weight_ref.at[rows, :]))
+    second = len(loads)
+    loads.append(copies.start(values_hbm, value_ref))
+    _, length, channels = mixed_ref.shape
 
     for load in loads[:first]:
         load.wait()
@@ -440,28 +455,22 @@
         value = mixed_ref[k].astype(f32)
         square = square + jnp.sum(value * value, axis=1, keepdims=True)
     scale = lax.rsqrt(square / (channels * tp) + 1e-06)
+    normed = []
     for k in range(tp):
         at = lax.rem(half + tp - k, tp)
-        gain = gain_ref[:, pl.ds(pl.multiple_of(at * channels, LANES), channels)]
-        normed = (mixed_ref[k].astype(f32) * scale * gain).astype(bf16)
-        for block in range(blocks):
-            row_ref[at * blocks + block] = normed[:, block * depth : (block + 1) * depth]
+        gain = gain_ref[:, pl.ds(pl.multiple_of(at * channels, channels), channels)]
+        normed.append((mixed_ref[k].astype(f32) * scale * gain).astype(bf16))
     for load in loads[first:second]:
         load.wait()
     z_total = jnp.zeros((length, head), f32)
-    for m in range(members):
-        for k in range(layers):
-            block = lax.rem(layer + layers - k, layers) * members + partner(member, m)
-            z_total = z_total + mm(row_ref[block], weight_ref[m, k])
+    for k in range(tp):
+        at = lax.rem(half + tp - k, tp)
+        z_total = z_total + mm(normed[k], weight_ref[pl.ds(pl.multiple_of(at * channels, channels), channels), :])
     queries = (z_total * affine_ref[0:1, :] + affine_ref[1:2, :]).astype(bf16)
     key_rows = (z_total * affine_ref[2:3, :] + affine_ref[3:4, :]).astype(bf16)
 
     for load in loads[second:]:
         load.wait()
-    total = own_ref[...]
-    for k in range(members - 1):
-        total = total + part_ref[k].astype(f32)
-    value_ref[...] = (total / (1.0 + jnp.exp(-total))).astype(bf16)
     row = lax.broadcasted_iota(jnp.int32, (STRETCH, STRETCH), 0)
     col = lax.broadcasted_iota(jnp.int32, (STRETCH, STRETCH), 1)
     for low in range(0, length, STRETCH):
@@ -472,7 +481,7 @@
         scores = jnp.where(row >= col, scores, -1e30)
         weights = jnp.exp(scores - jnp.max(scores, axis=1, keepdims=True))
         probabilities = (weights / jnp.sum(weights, axis=1, keepdims=True)).astype(bf16)
-        result_ref[:] = mm(probabilities, value_ref[:]).astype(bf16)
+        result_ref[here, :] = mm(probabilities, value_ref[here, :]).astype(bf16)
     copies.start(result_ref, result_hbm).wait()
 
 
@@ -600,22 +609,30 @@
     )
     mixed_rows, returned = lax.optimization_barrier((mixed_rows, returned))
     apart = others(mixed_rows, "tp")
+    (values,) = call(
+        values_kernel,
+        [shape((length, columns), bf16)],
+        [*returned, own],
+        [
+            vmem((max(members - 1, 1), length, columns), bf16),
+            vmem((length, columns), f32),
+            vmem((length, columns), bf16),
+        ],
+        members + 1,
+    )
     (result,) = call(
         functools.partial(attend_kernel, members, tp),
         [shape((length, columns), bf16)],
-        [*all_z, mixed_rows, *apart, *returned, own, rms_gain[None], qk_affine],
+        [*all_z, mixed_rows, *apart, values, rms_gain[None], qk_affine],
         [
-            vmem((members, layers, depth, head), bf16),
+            vmem((tp * channels, head), bf16),
             vmem((tp, length, channels), bf16),
-            vmem((max(members - 1, 1), length, columns), bf16),
-            vmem((length, columns), f32),
             vmem((1, tp * channels), f32),
             vmem((4, head), f32),
-            vmem((tp * blocks, length, depth), bf16),
             vmem((length, columns), bf16),
             vmem((length, columns), bf16),
         ],
-        tp + 2 + 2 * members + 1,
+        tp + 2 + peers + 2,
     )
     return result
 

time: 85.6 us -> 85.7 us (level)
  waiting for transfers between devices: 15.1 us -> 12.8 us
  Pallas kernels: 23.6 us -> 25.8 us
    ppermute x5, waiting for transfers between devices: 3.26 us -> 1.01 us  [along(): return lax.ppermute(block, axis, pairs)]
    pallas_call x6 -> x7, Pallas kernels: 23.6 us -> 25.8 us  [call(): pl.pallas_call(kernel, out_shape=outs, in_specs=[here] * len(inputs), out...]
  transfers between devices with their start and end apart: 22 -> 22, of which waited for: 11 -> 10; matrix products, arithmetic and copies ran while one was open for 3% -> 3% of each run, Pallas kernels for 24% -> 26%
where the time goes in v9:
time: 85.7 us; the launch traced here: 85.1 us
  starting transfers between devices  29.6 us (35%)
  Pallas kernels  25.8 us (30%)
  waiting for transfers between devices  12.8 us (15%)
  blocking collectives  12.6 us (15%)
  local copies, waits for them, and re-layouts  2.42 us (3%)
  other arithmetic  1.58 us (2%)
    pallas_call x7, Pallas kernels, call(): pl.pallas_call(kernel, out_shape=outs, in_specs=[here] * len(inputs), out...  25.8 us
    all_to_all x1, blocking collectives, body(): sums = lax.all_to_all(totals, 'ctx', 0, 0)  12.6 us
    ppermute x9, starting transfers between devices, swap(): lax.ppermute(block, 'ctx', [(i, i - i % group + (i % group ^ step)) for i...  10.6 us
    ppermute x9, waiting for transfers between devices, swap(): lax.ppermute(block, 'ctx', [(i, i - i % group + (i % group ^ step)) for i...  8.62 us
    ppermute x3, starting transfers between devices, body(): lax.ppermute(z_weight, 'ctx', [(i, (i + members * k) % peers) for i in ra...  6.06 us
    all_to_all x1, starting transfers between devices, body(): incoming = lax.all_to_all(starts, 'ctx', 0, 0)  4.2 us
    ppermute x3, starting transfers between devices, ring_on(): return lax.ppermute(block, 'ctx', pairs)  4.2 us
    all_to_all x1, starting transfers between devices, body(): arrived = lax.all_to_all(split(ends), 'ctx', 0, 0)  3.55 us
  transfers between devices with their start and end apart: 22, of which 10 were waited for; matrix products, arithmetic and copies ran while one was open for 3% of the time, Pallas kernels for 26%

profile of v9, /device:TPU:0, one launch (start us, length us, event | category | flops | bytes accessed | tf_op | source)
XLA Modules:
  0.0 85.1 jit_solution(1438978917469424475)
XLA Ops:
  0.0 3.0 %collective-permute-start = (bf16[256,128]{1,0:T(8,128)(2,1)}, bf16[256,128]{1,0:T(8,128)(2,1)S(1)}, u32[]{:S(2)}, u32[]{:S(2)}) collective-permute-start(bf16[256,128]{1,0:T(8,128)(2,1)} %param.21), channel_id=1, source_target_pairs={{0,8},{2,10},{4,12},{6,14},{8,16},{10,18},{12,20},{14,22},{16,24},... | collective-permute-start | bytes 196616 | tf_op jit(solution)/shard_map/ppermute | solution.py:514
  3.0 2.0 %collective-permute-start.2 = (bf16[256,128]{1,0:T(8,128)(2,1)}, bf16[256,128]{1,0:T(8,128)(2,1)S(1)}, u32[]{:S(2)}, u32[]{:S(2)}) collective-permute-start(bf16[256,128]{1,0:T(8,128)(2,1)} %param.21), channel_id=1, source_target_pairs={{0,24},{2,26},{4,28},{6,30},{8,0},{10,2},{12,4},{14,6},{16,8},{18,... | collective-permute-start | bytes 196616 | tf_op jit(solution)/shard_map/ppermute | solution.py:514
  5.1 1.0 %collective-permute-start.1 = (bf16[256,128]{1,0:T(8,128)(2,1)}, bf16[256,128]{1,0:T(8,128)(2,1)S(1)}, u32[]{:S(2)}, u32[]{:S(2)}) collective-permute-start(bf16[256,128]{1,0:T(8,128)(2,1)} %param.21), channel_id=1, source_target_pairs={{0,16},{2,18},{4,20},{6,22},{8,24},{10,26},{12,28},{14,30},{16,0},... | collective-permute-start | bytes 196616 | tf_op jit(solution)/shard_map/ppermute | solution.py:514
  6.1 1.0 %copy-done = bf16[128,2048]{1,0:T(8,128)(2,1)S(1)} copy-done((bf16[128,2048]{1,0:T(8,128)(2,1)S(1)}, bf16[128,2048]{1,0:T(8,128)(2,1)}, u32[]{:S(2)}) %copy-start) | copy-done | bytes 524312
  7.1 0.8 shard_map.118
  8.0 0.6 copy-done.1
  8.6 12.6 %all_to_all.15.refs_1_ = f32[16,2,128]{2,1,0:T(2,128)} all-to-all(f32[16,2,128]{2,1,0:T(2,128)S(1)} %get-tuple-element.49), channel_id=1, replica_groups=mesh['ctx'=16,'tp'=2] {'ctx'}, dimensions={0} | all-to-all | bytes 32768 | tf_op jit(solution)/shard_map/all_to_all | solution.py:512
  21.2 0.6 collective-permute-start.9
  21.8 1.6 %pad_maximum_fusion.refs_0_ = bf16[4,256,128]{2,1,0:T(8,128)(2,1)} fusion(bf16[1,256,128]{2,1,0:T(8,128)(2,1)S(1)} %bitcast.19, bf16[1,256,128]{2,1,0:T(8,128)(2,1)S(1)} %bitcast.20, bf16[1,256,128]{2,1,0:T(8,128)(2,1)S(1)} %bitcast.18, bf16[1,256,128]{2,1,0:T(8,128)(2,1)} %bitcast.17), kind=kLoop, calls=%fused_computation | loop fusion | flops 393216 | bytes 524288 | tf_op jit(solution)/shard_map/stack | solution.py:517
  23.4 0.6 collective-permute-start.5
  24.0 1.4 %collective-permute-start.4 = (bf16[4,256,128]{2,1,0:T(8,128)(2,1)}, bf16[4,256,128]{2,1,0:T(8,128)(2,1)}, u32[]{:S(2)}, u32[]{:S(2)}) collective-permute-start(bf16[4,256,128]{2,1,0:T(8,128)(2,1)} %pad_maximum_fusion.refs_0_), channel_id=1, source_target_pairs={{0,4},{2,6},{4,0},{6,2},{8,12},{10,14},{12,8},{14,10},{16,20},{18,... | collective-permute-start | bytes 786440 | tf_op jit(solution)/shard_map/ppermute | solution.py:347
  25.4 1.5 %collective-permute-start.3 = (bf16[4,256,128]{2,1,0:T(8,128)(2,1)}, bf16[4,256,128]{2,1,0:T(8,128)(2,1)}, u32[]{:S(2)}, u32[]{:S(2)}) collective-permute-start(bf16[4,256,128]{2,1,0:T(8,128)(2,1)} %pad_maximum_fusion.refs_0_), channel_id=1, source_target_pairs={{0,2},{2,0},{4,6},{6,4},{8,10},{10,8},{12,14},{14,12},{16,18},{18,... | collective-permute-start | bytes 786440 | tf_op jit(solution)/shard_map/ppermute | solution.py:347
  26.9 2.3 %collective-permute-start.14 = (bf16[256,1024]{1,0:T(8,128)(2,1)}, bf16[256,1024]{1,0:T(8,128)(2,1)}, u32[]{:S(2)}, u32[]{:S(2)}) collective-permute-start(bf16[256,1024]{1,0:T(8,128)(2,1)} %refs_8_.3), channel_id=1, source_target_pairs={{0,16},{2,18},{4,20},{6,22},{8,0},{10,2},{12,4},{14,6},{24,8},{26,... | collective-permute-start | bytes 1572872 | tf_op jit(solution)/shard_map/ppermute | solution.py:359
  29.2 7.4 %shard_map.119 = (bf16[2,128,256]{2,1,0:T(8,128)(2,1)}, bf16[2,128,256]{2,1,0:T(8,128)(2,1)}, bf16[2,128,256]{2,1,0:T(8,128)(2,1)}, bf16[2,128,256]{2,1,0:T(8,12...) custom-call(bf16[128,2048]{1,0:T(8,128)(2,1)} %refs_0_.1, ...), custom_call_target="tpu_custom_call" | custom-call | flops 1 | bytes 1 | tf_op jit(solution)/shard_map/pallas_call | solution.py:27
  36.6 3.5 %all-to-all-start.1 = ((f32[16,1,2,16,128]{4,3,2,1,0:T(8,128)}), f32[16,1,2,16,128]{4,3,2,1,0:T(8,128)S(1)}, u32[]{:S(2)}, u32[]{:S(2)}) async-start(f32[16,1,2,16,128]{4,3,2,1,0:T(8,128)} %bitcast.16), calls=%async_computation.1 | async-start | bytes 524288 | tf_op jit(solution)/shard_map/all_to_all | solution.py:564
  40.2 0.0 collective-permute-done.4.refs_2_
  40.2 1.9 %collective-permute-start.6 = (bf16[2,128,256]{2,1,0:T(8,128)(2,1)}, bf16[2,128,256]{2,1,0:T(8,128)(2,1)S(1)}, u32[]{:S(2)}, u32[]{:S(2)}) collective-permute-start(bf16[2,128,256]{2,1,0:T(8,128)(2,1)} %get-tuple-element.62), channel_id=1, source_target_pairs={{0,2},{2,0},{4,6},{6,4},{8,10},{10,8},{12,14},{14,12},{16,18},{18,... | collective-permute-start | bytes 393224 | tf_op jit(solution)/shard_map/ppermute | solution.py:347
  42.1 1.5 %collective-permute-start.7 = (bf16[2,128,256]{2,1,0:T(8,128)(2,1)}, bf16[2,128,256]{2,1,0:T(8,128)(2,1)S(1)}, u32[]{:S(2)}, u32[]{:S(2)}) collective-permute-start(bf16[2,128,256]{2,1,0:T(8,128)(2,1)} %get-tuple-element.63), channel_id=1, source_target_pairs={{0,4},{2,6},{4,0},{6,2},{8,12},{10,14},{12,8},{14,10},{16,20},{18,... | collective-permute-start | bytes 393224 | tf_op jit(solution)/shard_map/ppermute | solution.py:347
  43.6 0.2 collective-permute-start.8
  43.8 0.7 dynamic-slice_bitcast_fusion.q_ref
  44.5 1.4 %collective-permute-done.6.refs_1_ = bf16[2,128,256]{2,1,0:T(8,128)(2,1)S(1)} collective-permute-done((bf16[2,128,256]{2,1,0:T(8,128)(2,1)}, bf16[2,128,256]{2,1,0:T(8,128)(2,1)S(1)}, u32[]{:S(2)}, u32[]{:S(2)}) %collective-permute-start.6) | collective-permute-done | bytes 131104 | tf_op jit(solution)/shard_map/ppermute | solution.py:347
  45.9 2.2 %collective-permute-done.7.refs_2_ = bf16[2,128,256]{2,1,0:T(8,128)(2,1)S(1)} collective-permute-done((bf16[2,128,256]{2,1,0:T(8,128)(2,1)}, bf16[2,128,256]{2,1,0:T(8,128)(2,1)S(1)}, u32[]{:S(2)}, u32[]{:S(2)}) %collective-permute-start.7) | collective-permute-done | bytes 131104 | tf_op jit(solution)/shard_map/ppermute | solution.py:347
  48.1 2.4 %collective-permute-done.8.refs_3_ = bf16[2,128,256]{2,1,0:T(8,128)(2,1)S(1)} collective-permute-done((bf16[2,128,256]{2,1,0:T(8,128)(2,1)}, bf16[2,128,256]{2,1,0:T(8,128)(2,1)S(1)}, u32[]{:S(2)}, u32[]{:S(2)}) %collective-permute-start.8) | collective-permute-done | bytes 131104 | tf_op jit(solution)/shard_map/ppermute | solution.py:347
  50.6 0.0 collective-permute-done.9.refs_9_
  50.6 1.3 %collective-permute-start.15 = (bf16[256,1024]{1,0:T(8,128)(2,1)}, bf16[256,1024]{1,0:T(8,128)(2,1)}, u32[]{:S(2)}, u32[]{:S(2)}) collective-permute-start(bf16[256,1024]{1,0:T(8,128)(2,1)} %collective-permute-done.9.refs_9_), channel_id=1, source_target_pairs={{0,8},{2,10},{4,12},{6,14},{8,24},{10,26},{12,28},{14,30},{24,16},... | collective-permute-start | bytes 1572872 | tf_op jit(solution)/shard_map/ppermute | solution.py:359
  51.8 0.0 collective-permute-start.10
  51.8 0.5 collective-permute-start.11
  52.3 0.0 collective-permute-start.12
  52.3 0.0 collective-permute-done.14.refs_10_
  52.3 0.5 collective-permute-start.13
  52.9 0.0 all-to-all-done.1.ends_ref
  52.9 0.7 collective-permute-done.10.refs_4_
  53.6 0.1 collective-permute-done.12.refs_6_
  53.7 0.2 collective-permute-done.13.refs_7_
  53.9 0.8 shard_map.120
  54.7 4.2 %all-to-all-start.2 = ((f32[16,1,2,16,128]{4,3,2,1,0:T(8,128)}), f32[16,1,2,16,128]{4,3,2,1,0:T(8,128)}, u32[]{:S(2)}, u32[]{:S(2)}) async-start(f32[16,1,2,16,128]{4,3,2,1,0:T(8,128)} %shard_map.120), calls=%async_computation.2 | async-start | bytes 524288 | tf_op jit(solution)/shard_map/all_to_all | solution.py:574
  58.9 3.1 %collective-permute-done.15.refs_11_ = bf16[256,1024]{1,0:T(8,128)(2,1)} collective-permute-done((bf16[256,1024]{1,0:T(8,128)(2,1)}, bf16[256,1024]{1,0:T(8,128)(2,1)}, u32[]{:S(2)}, u32[]{:S(2)}) %collective-permute-start.15) | collective-permute-done | bytes 524320 | tf_op jit(solution)/shard_map/ppermute | solution.py:359
  62.0 4.0 %shard_map.121 = (f32[128,1024]{1,0:T(8,128)}, bf16[128,1024]{1,0:T(8,128)(2,1)}, bf16[128,1024]{1,0:T(8,128)(2,1)}, bf16[128,1024]{1,0:T(8,128)(2,1)}) custom-call(bf16[2,128,256]{2,1,0:T(8,128)(2,1)} %get-tuple-element.67.refs_0_, bf16[2,128,256]{2,1,0:T(8,128)(2,1)} %copy-done.2, bf16[2,128,256]{2,1,0:T(8,128)(2,1)} %copy-done.3, ...), custom_call_target="tpu_custom_call" | custom-call | flops 1 | bytes 1 | tf_op jit(solution)/shard_map/pallas_call | solution.py:27
  66.0 0.7 collective-permute-start.16
  66.7 0.5 collective-permute-start.17
  67.2 2.3 %collective-permute-start.18 = (bf16[128,1024]{1,0:T(8,128)(2,1)}, bf16[128,1024]{1,0:T(8,128)(2,1)}, u32[]{:S(2)}, u32[]{:S(2)}) collective-permute-start(bf16[128,1024]{1,0:T(8,128)(2,1)} %get-tuple-element.87), channel_id=1, source_target_pairs={{0,6},{2,4},{4,2},{6,0},{8,14},{10,12},{12,10},{14,8},{16,22},{18,... | collective-permute-start | bytes 786440 | tf_op jit(solution)/shard_map/ppermute | solution.py:347
  69.5 0.1 all-to-all-done.2
  69.6 7.2 %shard_map.122.refs_4_ = bf16[128,2048]{1,0:T(8,128)(2,1)} custom-call(f32[16,2,16,128]{3,2,1,0:T(8,128)} %bitcast.10.incoming_hbm, f32[16,8,2,16,128]{4,3,2,1,0:T(8,128)} %get-tuple-element.82.fresh_hbm, f32[2048,128]{1,0:T(8,128)} %get-tuple-element.83.dense_hbm, f32[512,128]{1,0:T(8,128)} %get-tuple-element.66.q_hbm, f32[512,128]{1,0:T(8,128)} %get-tuple-element.84.w_hbm, ...), custom_call_target="tpu_custom_call" | custom-call | flops 1 | bytes 1 | tf_op jit(solution)/shard_map/pallas_call | solution.py:27
  76.8 1.2 %collective-permute-done.17.refs_1_ = bf16[128,1024]{1,0:T(8,128)(2,1)} collective-permute-done((bf16[128,1024]{1,0:T(8,128)(2,1)}, bf16[128,1024]{1,0:T(8,128)(2,1)}, u32[]{:S(2)}, u32[]{:S(2)}) %collective-permute-start.17) | collective-permute-done | bytes 262176 | tf_op jit(solution)/shard_map/ppermute | solution.py:347
  78.0 1.3 %collective-permute-done.18.refs_2_ = bf16[128,1024]{1,0:T(8,128)(2,1)} collective-permute-done((bf16[128,1024]{1,0:T(8,128)(2,1)}, bf16[128,1024]{1,0:T(8,128)(2,1)}, u32[]{:S(2)}, u32[]{:S(2)}) %collective-permute-start.18) | collective-permute-done | bytes 262176 | tf_op jit(solution)/shard_map/ppermute | solution.py:347
  79.3 2.2 %shard_map.123.refs_6_ = bf16[128,1024]{1,0:T(8,128)(2,1)} custom-call(bf16[128,1024]{1,0:T(8,128)(2,1)} %collective-permute-done.16.refs_0_, bf16[128,1024]{1,0:T(8,128)(2,1)} %collective-permute-done.17.refs_1_, bf16[128,1024]{1,0:T(8,128)(2,1)} %collective-permute-done.18.refs_2_, f32[128,1024]{1,0:T(8,128)} %get-tuple-element.92.refs_3_), custom_call_target="tpu_custom_call" | custom-call | flops 1 | bytes 1 | tf_op jit(solution)/shard_map/pallas_call | solution.py:27
  81.6 0.0 collective-permute-done.19.refs_5_
  81.6 3.5 %shard_map.124 = bf16[128,1024]{1,0:T(8,128)(2,1)} custom-call(bf16[4,256,128]{2,1,0:T(8,128)(2,1)} %pad_maximum_fusion.refs_0_, bf16[4,256,128]{2,1,0:T(8,128)(2,1)} %collective-permute-done.3.refs_1_, bf16[4,256,128]{2,1,0:T(8,128)(2,1)} %collective-permute-done.4.refs_2_, bf16[4,256,128]{2,1,0:T(8,128)(2,1)} %collective-permute-done.5.refs_3_, ...), custom_call_target="tpu_custom_call" | custom-call | flops 1 | bytes 1 | tf_op jit(solution)/shard_map/pallas_call | solution.py:27
  (24 shorter events, 0.1 us)
Async XLA Ops:
  0.0 21.8 %collective-permute-start = (bf16[256,128]{1,0:T(8,128)(2,1)}, bf16[256,128]{1,0:T(8,128)(2,1)S(1)}, u32[]{:S(2)}, u32[]{:S(2)}) collective-permute-start(bf16[256,128]{1,0:T(8,128)(2,1)} %param.21), channel_id=1, source_target_pairs={{0,8},{2,10},{4,12},{6,14},{8,16},{10,18},{12,20},{14,22},{16,24},... | collective-permute-start | bytes 196616 | tf_op jit(solution)/shard_map/ppermute | solution.py:514
  3.0 18.8 %collective-permute-start.2 = (bf16[256,128]{1,0:T(8,128)(2,1)}, bf16[256,128]{1,0:T(8,128)(2,1)S(1)}, u32[]{:S(2)}, u32[]{:S(2)}) collective-permute-start(bf16[256,128]{1,0:T(8,128)(2,1)} %param.21), channel_id=1, source_target_pairs={{0,24},{2,26},{4,28},{6,30},{8,0},{10,2},{12,4},{14,6},{16,8},{18,... | collective-permute-start | bytes 196616 | tf_op jit(solution)/shard_map/ppermute | solution.py:514
  5.1 16.7 %collective-permute-start.1 = (bf16[256,128]{1,0:T(8,128)(2,1)}, bf16[256,128]{1,0:T(8,128)(2,1)S(1)}, u32[]{:S(2)}, u32[]{:S(2)}) collective-permute-start(bf16[256,128]{1,0:T(8,128)(2,1)} %param.21), channel_id=1, source_target_pairs={{0,16},{2,18},{4,20},{6,22},{8,24},{10,26},{12,28},{14,30},{16,0},... | collective-permute-start | bytes 196616 | tf_op jit(solution)/shard_map/ppermute | solution.py:514
  6.1 1.0 %copy-start = (bf16[128,2048]{1,0:T(8,128)(2,1)S(1)}, bf16[128,2048]{1,0:T(8,128)(2,1)}, u32[]{:S(2)}) copy-start(bf16[128,2048]{1,0:T(8,128)(2,1)} %refs_0_.1) | copy-start | bytes 1572868
  7.9 0.6 copy-start.1
  21.2 29.4 %collective-permute-start.9 = (bf16[256,1024]{1,0:T(8,128)(2,1)}, bf16[256,1024]{1,0:T(8,128)(2,1)}, u32[]{:S(2)}, u32[]{:S(2)}) collective-permute-start(bf16[256,1024]{1,0:T(8,128)(2,1)} %refs_8_.3), channel_id=1, source_target_pairs={{0,8},{2,10},{4,12},{6,14},{8,24},{10,26},{12,28},{14,30},{24,16},... | collective-permute-start | bytes 1572872 | tf_op jit(solution)/shard_map/ppermute | solution.py:359
  23.4 16.8 %collective-permute-start.5 = (bf16[4,256,128]{2,1,0:T(8,128)(2,1)}, bf16[4,256,128]{2,1,0:T(8,128)(2,1)}, u32[]{:S(2)}, u32[]{:S(2)}) collective-permute-start(bf16[4,256,128]{2,1,0:T(8,128)(2,1)} %pad_maximum_fusion.refs_0_), channel_id=1, source_target_pairs={{0,6},{2,4},{4,2},{6,0},{8,14},{10,12},{12,10},{14,8},{16,22},{18,... | collective-permute-start | bytes 786440 | tf_op jit(solution)/shard_map/ppermute | solution.py:347
  24.0 16.2 %collective-permute-start.4 = (bf16[4,256,128]{2,1,0:T(8,128)(2,1)}, bf16[4,256,128]{2,1,0:T(8,128)(2,1)}, u32[]{:S(2)}, u32[]{:S(2)}) collective-permute-start(bf16[4,256,128]{2,1,0:T(8,128)(2,1)} %pad_maximum_fusion.refs_0_), channel_id=1, source_target_pairs={{0,4},{2,6},{4,0},{6,2},{8,12},{10,14},{12,8},{14,10},{16,20},{18,... | collective-permute-start | bytes 786440 | tf_op jit(solution)/shard_map/ppermute | solution.py:347
  25.4 14.8 %collective-permute-start.3 = (bf16[4,256,128]{2,1,0:T(8,128)(2,1)}, bf16[4,256,128]{2,1,0:T(8,128)(2,1)}, u32[]{:S(2)}, u32[]{:S(2)}) collective-permute-start(bf16[4,256,128]{2,1,0:T(8,128)(2,1)} %pad_maximum_fusion.refs_0_), channel_id=1, source_target_pairs={{0,2},{2,0},{4,6},{6,4},{8,10},{10,8},{12,14},{14,12},{16,18},{18,... | collective-permute-start | bytes 786440 | tf_op jit(solution)/shard_map/ppermute | solution.py:347
  26.9 25.5 %collective-permute-start.14 = (bf16[256,1024]{1,0:T(8,128)(2,1)}, bf16[256,1024]{1,0:T(8,128)(2,1)}, u32[]{:S(2)}, u32[]{:S(2)}) collective-permute-start(bf16[256,1024]{1,0:T(8,128)(2,1)} %refs_8_.3), channel_id=1, source_target_pairs={{0,16},{2,18},{4,20},{6,22},{8,0},{10,2},{12,4},{14,6},{24,8},{26,... | collective-permute-start | bytes 1572872 | tf_op jit(solution)/shard_map/ppermute | solution.py:359
  36.6 16.2 %all-to-all-start.1 = ((f32[16,1,2,16,128]{4,3,2,1,0:T(8,128)}), f32[16,1,2,16,128]{4,3,2,1,0:T(8,128)S(1)}, u32[]{:S(2)}, u32[]{:S(2)}) async-start(f32[16,1,2,16,128]{4,3,2,1,0:T(8,128)} %bitcast.16), calls=%async_computation.1 | async-start | bytes 524288 | tf_op jit(solution)/shard_map/all_to_all | solution.py:564
  40.2 5.7 %collective-permute-start.6 = (bf16[2,128,256]{2,1,0:T(8,128)(2,1)}, bf16[2,128,256]{2,1,0:T(8,128)(2,1)S(1)}, u32[]{:S(2)}, u32[]{:S(2)}) collective-permute-start(bf16[2,128,256]{2,1,0:T(8,128)(2,1)} %get-tuple-element.62), channel_id=1, source_target_pairs={{0,2},{2,0},{4,6},{6,4},{8,10},{10,8},{12,14},{14,12},{16,18},{18,... | collective-permute-start | bytes 393224 | tf_op jit(solution)/shard_map/ppermute | solution.py:347
  42.1 6.1 %collective-permute-start.7 = (bf16[2,128,256]{2,1,0:T(8,128)(2,1)}, bf16[2,128,256]{2,1,0:T(8,128)(2,1)S(1)}, u32[]{:S(2)}, u32[]{:S(2)}) collective-permute-start(bf16[2,128,256]{2,1,0:T(8,128)(2,1)} %get-tuple-element.63), channel_id=1, source_target_pairs={{0,4},{2,6},{4,0},{6,2},{8,12},{10,14},{12,8},{14,10},{16,20},{18,... | collective-permute-start | bytes 393224 | tf_op jit(solution)/shard_map/ppermute | solution.py:347
  43.6 7.0 %collective-permute-start.8 = (bf16[2,128,256]{2,1,0:T(8,128)(2,1)}, bf16[2,128,256]{2,1,0:T(8,128)(2,1)S(1)}, u32[]{:S(2)}, u32[]{:S(2)}) collective-permute-start(bf16[2,128,256]{2,1,0:T(8,128)(2,1)} %get-tuple-element.64), channel_id=1, source_target_pairs={{0,6},{2,4},{4,2},{6,0},{8,14},{10,12},{12,10},{14,8},{16,22},{18,... | collective-permute-start | bytes 393224 | tf_op jit(solution)/shard_map/ppermute | solution.py:347
  45.9 8.7 %copy-start.2 = (bf16[2,128,256]{2,1,0:T(8,128)(2,1)}, bf16[2,128,256]{2,1,0:T(8,128)(2,1)S(1)}, u32[]{:S(2)}) copy-start(bf16[2,128,256]{2,1,0:T(8,128)(2,1)S(1)} %collective-permute-done.6.refs_1_) | copy-start | bytes 393220
  48.1 6.5 %copy-start.3 = (bf16[2,128,256]{2,1,0:T(8,128)(2,1)}, bf16[2,128,256]{2,1,0:T(8,128)(2,1)S(1)}, u32[]{:S(2)}) copy-start(bf16[2,128,256]{2,1,0:T(8,128)(2,1)S(1)} %collective-permute-done.7.refs_2_) | copy-start | bytes 393220
  50.6 4.1 %copy-start.4 = (bf16[2,128,256]{2,1,0:T(8,128)(2,1)}, bf16[2,128,256]{2,1,0:T(8,128)(2,1)S(1)}, u32[]{:S(2)}) copy-start(bf16[2,128,256]{2,1,0:T(8,128)(2,1)S(1)} %collective-permute-done.8.refs_3_) | copy-start | bytes 393220
  50.6 11.5 %collective-permute-start.15 = (bf16[256,1024]{1,0:T(8,128)(2,1)}, bf16[256,1024]{1,0:T(8,128)(2,1)}, u32[]{:S(2)}, u32[]{:S(2)}) collective-permute-start(bf16[256,1024]{1,0:T(8,128)(2,1)} %collective-permute-done.9.refs_9_), channel_id=1, source_target_pairs={{0,8},{2,10},{4,12},{6,14},{8,24},{10,26},{12,28},{14,30},{24,16},... | collective-permute-start | bytes 1572872 | tf_op jit(solution)/shard_map/ppermute | solution.py:359
  51.8 1.7 %collective-permute-start.10 = (bf16[2,128,256]{2,1,0:T(8,128)(2,1)}, bf16[2,128,256]{2,1,0:T(8,128)(2,1)S(1)}, u32[]{:S(2)}, u32[]{:S(2)}) collective-permute-start(bf16[2,128,256]{2,1,0:T(8,128)(2,1)} %get-tuple-element.67.refs_0_), channel_id=1, source_target_pairs={{0,1},{1,0},{2,3},{3,2},{4,5},{5,4},{6,7},{7,6},{8,9},{9,8},{10,11... | collective-permute-start | bytes 393224 | tf_op jit(solution)/shard_map/ppermute | solution.py:343
  51.8 1.7 %collective-permute-start.11 = (bf16[2,128,256]{2,1,0:T(8,128)(2,1)S(1)}, bf16[2,128,256]{2,1,0:T(8,128)(2,1)S(1)}, u32[]{:S(2)}, u32[]{:S(2)}) collective-permute-start(bf16[2,128,256]{2,1,0:T(8,128)(2,1)S(1)} %collective-permute-done.6.refs_1_), channel_id=1, source_target_pairs={{0,1},{1,0},{2,3},{3,2},{4,5},{5,4},{6,7},{7,6},{8,9},{9,8},{10,11... | collective-permute-start | bytes 393224 | tf_op jit(solution)/shard_map/ppermute | solution.py:343
  52.3 1.3 %collective-permute-start.12 = (bf16[2,128,256]{2,1,0:T(8,128)(2,1)S(1)}, bf16[2,128,256]{2,1,0:T(8,128)(2,1)S(1)}, u32[]{:S(2)}, u32[]{:S(2)}) collective-permute-start(bf16[2,128,256]{2,1,0:T(8,128)(2,1)S(1)} %collective-permute-done.7.refs_2_), channel_id=1, source_target_pairs={{0,1},{1,0},{2,3},{3,2},{4,5},{5,4},{6,7},{7,6},{8,9},{9,8},{10,11... | collective-permute-start | bytes 393224 | tf_op jit(solution)/shard_map/ppermute | solution.py:343
  52.3 1.5 %collective-permute-start.13 = (bf16[2,128,256]{2,1,0:T(8,128)(2,1)S(1)}, bf16[2,128,256]{2,1,0:T(8,128)(2,1)S(1)}, u32[]{:S(2)}, u32[]{:S(2)}) collective-permute-start(bf16[2,128,256]{2,1,0:T(8,128)(2,1)S(1)} %collective-permute-done.8.refs_3_), channel_id=1, source_target_pairs={{0,1},{1,0},{2,3},{3,2},{4,5},{5,4},{6,7},{7,6},{8,9},{9,8},{10,11... | collective-permute-start | bytes 393224 | tf_op jit(solution)/shard_map/ppermute | solution.py:343
  53.5 5.3 %copy-start.5 = (bf16[2,128,256]{2,1,0:T(8,128)(2,1)}, bf16[2,128,256]{2,1,0:T(8,128)(2,1)S(1)}, u32[]{:S(2)}) copy-start(bf16[2,128,256]{2,1,0:T(8,128)(2,1)S(1)} %collective-permute-done.10.refs_4_) | copy-start | bytes 393220
  53.6 5.3 %copy-start.6 = (bf16[2,128,256]{2,1,0:T(8,128)(2,1)}, bf16[2,128,256]{2,1,0:T(8,128)(2,1)S(1)}, u32[]{:S(2)}) copy-start(bf16[2,128,256]{2,1,0:T(8,128)(2,1)S(1)} %collective-permute-done.11.refs_5_) | copy-start | bytes 393220
  53.7 5.2 %copy-start.7 = (bf16[2,128,256]{2,1,0:T(8,128)(2,1)}, bf16[2,128,256]{2,1,0:T(8,128)(2,1)S(1)}, u32[]{:S(2)}) copy-start(bf16[2,128,256]{2,1,0:T(8,128)(2,1)S(1)} %collective-permute-done.12.refs_6_) | copy-start | bytes 393220
  53.9 5.0 %copy-start.8 = (bf16[2,128,256]{2,1,0:T(8,128)(2,1)}, bf16[2,128,256]{2,1,0:T(8,128)(2,1)S(1)}, u32[]{:S(2)}) copy-start(bf16[2,128,256]{2,1,0:T(8,128)(2,1)S(1)} %collective-permute-done.13.refs_7_) | copy-start | bytes 393220
  54.7 14.9 %all-to-all-start.2 = ((f32[16,1,2,16,128]{4,3,2,1,0:T(8,128)}), f32[16,1,2,16,128]{4,3,2,1,0:T(8,128)}, u32[]{:S(2)}, u32[]{:S(2)}) async-start(f32[16,1,2,16,128]{4,3,2,1,0:T(8,128)} %shard_map.120), calls=%async_computation.2 | async-start | bytes 524288 | tf_op jit(solution)/shard_map/all_to_all | solution.py:574
  66.0 10.8 %collective-permute-start.16 = (bf16[128,1024]{1,0:T(8,128)(2,1)}, bf16[128,1024]{1,0:T(8,128)(2,1)}, u32[]{:S(2)}, u32[]{:S(2)}) collective-permute-start(bf16[128,1024]{1,0:T(8,128)(2,1)} %get-tuple-element.85), channel_id=1, source_target_pairs={{0,2},{2,0},{4,6},{6,4},{8,10},{10,8},{12,14},{14,12},{16,18},{18,... | collective-permute-start | bytes 786440 | tf_op jit(solution)/shard_map/ppermute | solution.py:347
  66.7 11.3 %collective-permute-start.17 = (bf16[128,1024]{1,0:T(8,128)(2,1)}, bf16[128,1024]{1,0:T(8,128)(2,1)}, u32[]{:S(2)}, u32[]{:S(2)}) collective-permute-start(bf16[128,1024]{1,0:T(8,128)(2,1)} %get-tuple-element.86), channel_id=1, source_target_pairs={{0,4},{2,6},{4,0},{6,2},{8,12},{10,14},{12,8},{14,10},{16,20},{18,... | collective-permute-start | bytes 786440 | tf_op jit(solution)/shard_map/ppermute | solution.py:347
  67.2 12.1 %collective-permute-start.18 = (bf16[128,1024]{1,0:T(8,128)(2,1)}, bf16[128,1024]{1,0:T(8,128)(2,1)}, u32[]{:S(2)}, u32[]{:S(2)}) collective-permute-start(bf16[128,1024]{1,0:T(8,128)(2,1)} %get-tuple-element.87), channel_id=1, source_target_pairs={{0,6},{2,4},{4,2},{6,0},{8,14},{10,12},{12,10},{14,8},{16,22},{18,... | collective-permute-start | bytes 786440 | tf_op jit(solution)/shard_map/ppermute | solution.py:347
  79.3 2.3 %collective-permute-start.19 = (bf16[128,2048]{1,0:T(8,128)(2,1)}, bf16[128,2048]{1,0:T(8,128)(2,1)}, u32[]{:S(2)}, u32[]{:S(2)}) collective-permute-start(bf16[128,2048]{1,0:T(8,128)(2,1)} %shard_map.122.refs_4_), channel_id=1, source_target_pairs={{0,1},{1,0},{2,3},{3,2},{4,5},{5,4},{6,7},{7,6},{8,9},{9,8},{10,11... | collective-permute-start | bytes 1572872 | tf_op jit(solution)/shard_map/ppermute | solution.py:343

commit v10 on v9

--- a/solution.py
+++ b/solution.py
@@ -106,6 +106,12 @@
         return _
 
     lax.fori_loop(0, NDIM, one, 0)
+
+
+def differ(number, step, count):
+    bits = range(count.bit_length() - 1)
+    digits = [lax.rem(lax.div(number, 1 << bit), 2) for bit in bits]
+    return sum((1 - digit if step >> bit & 1 else digit) * (1 << bit) for bit, digit in zip(bits, digits))
 
 
 def partner(member, step):
@@ -343,6 +349,10 @@
     return lax.ppermute(block, axis, pairs)
 
 
+def line_target(layer, step, layers):
+    return (layer + step) % layers if layers & (layers - 1) else layer ^ step
+
+
 def swap(block, step, group):
     return lax.ppermute(block, "ctx", [(i, i - i % group + (i % group ^ step)) for i in range(lax.axis_size("ctx"))])
 
@@ -441,7 +451,11 @@
     layers, depth, head = weights_hbm[0].shape
     for m in range(members):
         for k in range(layers):
-            block = lax.rem(layer + layers - k, layers) * members + partner(member, m)
+            if layers & (layers - 1):
+                source = lax.rem(layer + layers - k, layers)
+            else:
+                source = differ(layer, k, layers)
+            block = source * members + partner(member, m)
             rows = pl.ds(pl.multiple_of(block * depth, depth), depth)
             loads.append(copies.start(weights_hbm[m].at[k], weight_ref.at[rows, :]))
     second = len(loads)
@@ -511,7 +525,7 @@
     )
     sums = lax.all_to_all(totals, "ctx", 0, 0)
     line_z = [z_weight] + [
-        lax.ppermute(z_weight, "ctx", [(i, (i + members * k) % peers) for i in range(peers)])
+        lax.ppermute(z_weight, "ctx", [(i, line_target(i // members, k, layers) * members + i % members) for i in range(peers)])
         for k in range(1, layers)
     ]
     line_z = jnp.stack(line_z)

time: 85.7 us -> 86 us (level)
  no operation moved by 1% of the time
where the time goes in v10:
time: 86 us; the launch traced here: 85.4 us
  starting transfers between devices  29.2 us (34%)
  Pallas kernels  25.9 us (30%)
  blocking collectives  13.4 us (16%)
  waiting for transfers between devices  12.8 us (15%)
  local copies, waits for them, and re-layouts  2.42 us (3%)
  other arithmetic  1.58 us (2%)
    pallas_call x7, Pallas kernels, call(): pl.pallas_call(kernel, out_shape=outs, in_specs=[here] * len(inputs), out...  25.9 us
    all_to_all x1, blocking collectives, body(): sums = lax.all_to_all(totals, 'ctx', 0, 0)  13.4 us
    ppermute x9, starting transfers between devices, swap(): lax.ppermute(block, 'ctx', [(i, i - i % group + (i % group ^ step)) for i...  10.6 us
    ppermute x9, waiting for transfers between devices, swap(): lax.ppermute(block, 'ctx', [(i, i - i % group + (i % group ^ step)) for i...  8.59 us
    ppermute x3, starting transfers between devices, body(): lax.ppermute(z_weight, 'ctx', [(i, line_target(i // members, k, layers) *...  5.62 us
    ppermute x3, starting transfers between devices, ring_on(): return lax.ppermute(block, 'ctx', pairs)  4.23 us
    all_to_all x1, starting transfers between devices, body(): incoming = lax.all_to_all(starts, 'ctx', 0, 0)  4.2 us
    all_to_all x1, starting transfers between devices, body(): arrived = lax.all_to_all(split(ends), 'ctx', 0, 0)  3.55 us
  transfers between devices with their start and end apart: 22, of which 10 were waited for; matrix products, arithmetic and copies ran while one was open for 3% of the time, Pallas kernels for 26%

profile of v10, /device:TPU:0, one launch (start us, length us, event | category | flops | bytes accessed | tf_op | source)
XLA Modules:
  0.0 85.4 jit_solution(6553910851282703155)
XLA Ops:
  0.0 3.0 %collective-permute-start = (bf16[256,128]{1,0:T(8,128)(2,1)}, bf16[256,128]{1,0:T(8,128)(2,1)S(1)}, u32[]{:S(2)}, u32[]{:S(2)}) collective-permute-start(bf16[256,128]{1,0:T(8,128)(2,1)} %param.21), channel_id=1, source_target_pairs={{0,8},{2,10},{4,12},{6,14},{8,0},{10,2},{12,4},{14,6},{16,24},{18,... | collective-permute-start | bytes 196616 | tf_op jit(solution)/shard_map/ppermute | solution.py:528
  3.0 2.5 %collective-permute-start.2 = (bf16[256,128]{1,0:T(8,128)(2,1)}, bf16[256,128]{1,0:T(8,128)(2,1)S(1)}, u32[]{:S(2)}, u32[]{:S(2)}) collective-permute-start(bf16[256,128]{1,0:T(8,128)(2,1)} %param.21), channel_id=1, source_target_pairs={{0,24},{2,26},{4,28},{6,30},{8,16},{10,18},{12,20},{14,22},{16,8},... | collective-permute-start | bytes 196616 | tf_op jit(solution)/shard_map/ppermute | solution.py:528
  5.5 0.1 collective-permute-start.1
  5.6 1.0 %copy-done = bf16[128,2048]{1,0:T(8,128)(2,1)S(1)} copy-done((bf16[128,2048]{1,0:T(8,128)(2,1)S(1)}, bf16[128,2048]{1,0:T(8,128)(2,1)}, u32[]{:S(2)}) %copy-start) | copy-done | bytes 524312
  6.7 0.8 shard_map.118
  7.5 0.6 copy-done.1
  8.1 13.4 %all_to_all.15.refs_1_ = f32[16,2,128]{2,1,0:T(2,128)} all-to-all(f32[16,2,128]{2,1,0:T(2,128)S(1)} %get-tuple-element.49), channel_id=1, replica_groups=mesh['ctx'=16,'tp'=2] {'ctx'}, dimensions={0} | all-to-all | bytes 32768 | tf_op jit(solution)/shard_map/all_to_all | solution.py:526
  21.6 0.6 collective-permute-start.9
  22.1 0.0 collective-permute-done
  22.1 0.0 collective-permute-done.2
  22.1 0.0 collective-permute-done.1
  22.1 1.6 %pad_maximum_fusion.refs_0_ = bf16[4,256,128]{2,1,0:T(8,128)(2,1)} fusion(bf16[1,256,128]{2,1,0:T(8,128)(2,1)S(1)} %bitcast.19, bf16[1,256,128]{2,1,0:T(8,128)(2,1)S(1)} %bitcast.20, bf16[1,256,128]{2,1,0:T(8,128)(2,1)S(1)} %bitcast.18, bf16[1,256,128]{2,1,0:T(8,128)(2,1)} %bitcast.17), kind=kLoop, calls=%fused_computation | loop fusion | flops 393216 | bytes 524288 | tf_op jit(solution)/shard_map/stack | solution.py:531
  23.7 0.6 collective-permute-start.5
  24.3 1.4 %collective-permute-start.4 = (bf16[4,256,128]{2,1,0:T(8,128)(2,1)}, bf16[4,256,128]{2,1,0:T(8,128)(2,1)}, u32[]{:S(2)}, u32[]{:S(2)}) collective-permute-start(bf16[4,256,128]{2,1,0:T(8,128)(2,1)} %pad_maximum_fusion.refs_0_), channel_id=1, source_target_pairs={{0,4},{2,6},{4,0},{6,2},{8,12},{10,14},{12,8},{14,10},{16,20},{18,... | collective-permute-start | bytes 786440 | tf_op jit(solution)/shard_map/ppermute | solution.py:357
  25.8 1.5 %collective-permute-start.3 = (bf16[4,256,128]{2,1,0:T(8,128)(2,1)}, bf16[4,256,128]{2,1,0:T(8,128)(2,1)}, u32[]{:S(2)}, u32[]{:S(2)}) collective-permute-start(bf16[4,256,128]{2,1,0:T(8,128)(2,1)} %pad_maximum_fusion.refs_0_), channel_id=1, source_target_pairs={{0,2},{2,0},{4,6},{6,4},{8,10},{10,8},{12,14},{14,12},{16,18},{18,... | collective-permute-start | bytes 786440 | tf_op jit(solution)/shard_map/ppermute | solution.py:357
  27.2 2.3 %collective-permute-start.14 = (bf16[256,1024]{1,0:T(8,128)(2,1)}, bf16[256,1024]{1,0:T(8,128)(2,1)}, u32[]{:S(2)}, u32[]{:S(2)}) collective-permute-start(bf16[256,1024]{1,0:T(8,128)(2,1)} %refs_8_.3), channel_id=1, source_target_pairs={{0,16},{2,18},{4,20},{6,22},{8,0},{10,2},{12,4},{14,6},{24,8},{26,... | collective-permute-start | bytes 1572872 | tf_op jit(solution)/shard_map/ppermute | solution.py:369
  29.6 7.4 %shard_map.119 = (bf16[2,128,256]{2,1,0:T(8,128)(2,1)}, bf16[2,128,256]{2,1,0:T(8,128)(2,1)}, bf16[2,128,256]{2,1,0:T(8,128)(2,1)}, bf16[2,128,256]{2,1,0:T(8,12...) custom-call(bf16[128,2048]{1,0:T(8,128)(2,1)} %refs_0_.1, ...), custom_call_target="tpu_custom_call" | custom-call | flops 1 | bytes 1 | tf_op jit(solution)/shard_map/pallas_call | solution.py:27
  37.0 3.5 %all-to-all-start.1 = ((f32[16,1,2,16,128]{4,3,2,1,0:T(8,128)}), f32[16,1,2,16,128]{4,3,2,1,0:T(8,128)S(1)}, u32[]{:S(2)}, u32[]{:S(2)}) async-start(f32[16,1,2,16,128]{4,3,2,1,0:T(8,128)} %bitcast.16), calls=%async_computation.1 | async-start | bytes 524288 | tf_op jit(solution)/shard_map/all_to_all | solution.py:578
  40.5 0.0 collective-permute-done.4.refs_2_
  40.6 1.9 %collective-permute-start.6 = (bf16[2,128,256]{2,1,0:T(8,128)(2,1)}, bf16[2,128,256]{2,1,0:T(8,128)(2,1)S(1)}, u32[]{:S(2)}, u32[]{:S(2)}) collective-permute-start(bf16[2,128,256]{2,1,0:T(8,128)(2,1)} %get-tuple-element.62), channel_id=1, source_target_pairs={{0,2},{2,0},{4,6},{6,4},{8,10},{10,8},{12,14},{14,12},{16,18},{18,... | collective-permute-start | bytes 393224 | tf_op jit(solution)/shard_map/ppermute | solution.py:357
  42.4 1.5 %collective-permute-start.7 = (bf16[2,128,256]{2,1,0:T(8,128)(2,1)}, bf16[2,128,256]{2,1,0:T(8,128)(2,1)S(1)}, u32[]{:S(2)}, u32[]{:S(2)}) collective-permute-start(bf16[2,128,256]{2,1,0:T(8,128)(2,1)} %get-tuple-element.63), channel_id=1, source_target_pairs={{0,4},{2,6},{4,0},{6,2},{8,12},{10,14},{12,8},{14,10},{16,20},{18,... | collective-permute-start | bytes 393224 | tf_op jit(solution)/shard_map/ppermute | solution.py:357
  43.9 0.2 collective-permute-start.8
  44.1 0.7 dynamic-slice_bitcast_fusion.q_ref
  44.8 1.4 %collective-permute-done.6.refs_1_ = bf16[2,128,256]{2,1,0:T(8,128)(2,1)S(1)} collective-permute-done((bf16[2,128,256]{2,1,0:T(8,128)(2,1)}, bf16[2,128,256]{2,1,0:T(8,128)(2,1)S(1)}, u32[]{:S(2)}, u32[]{:S(2)}) %collective-permute-start.6) | collective-permute-done | bytes 131104 | tf_op jit(solution)/shard_map/ppermute | solution.py:357
  46.2 2.2 %collective-permute-done.7.refs_2_ = bf16[2,128,256]{2,1,0:T(8,128)(2,1)S(1)} collective-permute-done((bf16[2,128,256]{2,1,0:T(8,128)(2,1)}, bf16[2,128,256]{2,1,0:T(8,128)(2,1)S(1)}, u32[]{:S(2)}, u32[]{:S(2)}) %collective-permute-start.7) | collective-permute-done | bytes 131104 | tf_op jit(solution)/shard_map/ppermute | solution.py:357
  48.5 2.4 %collective-permute-done.8.refs_3_ = bf16[2,128,256]{2,1,0:T(8,128)(2,1)S(1)} collective-permute-done((bf16[2,128,256]{2,1,0:T(8,128)(2,1)}, bf16[2,128,256]{2,1,0:T(8,128)(2,1)S(1)}, u32[]{:S(2)}, u32[]{:S(2)}) %collective-permute-start.8) | collective-permute-done | bytes 131104 | tf_op jit(solution)/shard_map/ppermute | solution.py:357
  50.9 0.0 collective-permute-done.9.refs_9_
  50.9 1.3 %collective-permute-start.15 = (bf16[256,1024]{1,0:T(8,128)(2,1)}, bf16[256,1024]{1,0:T(8,128)(2,1)}, u32[]{:S(2)}, u32[]{:S(2)}) collective-permute-start(bf16[256,1024]{1,0:T(8,128)(2,1)} %collective-permute-done.9.refs_9_), channel_id=1, source_target_pairs={{0,8},{2,10},{4,12},{6,14},{8,24},{10,26},{12,28},{14,30},{24,16},... | collective-permute-start | bytes 1572872 | tf_op jit(solution)/shard_map/ppermute | solution.py:369
  52.2 0.0 collective-permute-start.10
  52.2 0.5 collective-permute-start.11
  52.7 0.0 collective-permute-start.12
  52.7 0.5 collective-permute-start.13
  53.2 0.7 collective-permute-done.10.refs_4_
  53.9 0.1 collective-permute-done.12.refs_6_
  54.0 0.2 collective-permute-done.13.refs_7_
  54.2 0.8 shard_map.120
  55.0 4.2 %all-to-all-start.2 = ((f32[16,1,2,16,128]{4,3,2,1,0:T(8,128)}), f32[16,1,2,16,128]{4,3,2,1,0:T(8,128)}, u32[]{:S(2)}, u32[]{:S(2)}) async-start(f32[16,1,2,16,128]{4,3,2,1,0:T(8,128)} %shard_map.120), calls=%async_computation.2 | async-start | bytes 524288 | tf_op jit(solution)/shard_map/all_to_all | solution.py:588
  59.3 3.0 %collective-permute-done.15.refs_11_ = bf16[256,1024]{1,0:T(8,128)(2,1)} collective-permute-done((bf16[256,1024]{1,0:T(8,128)(2,1)}, bf16[256,1024]{1,0:T(8,128)(2,1)}, u32[]{:S(2)}, u32[]{:S(2)}) %collective-permute-start.15) | collective-permute-done | bytes 524320 | tf_op jit(solution)/shard_map/ppermute | solution.py:369
  62.3 4.0 %shard_map.121 = (f32[128,1024]{1,0:T(8,128)}, bf16[128,1024]{1,0:T(8,128)(2,1)}, bf16[128,1024]{1,0:T(8,128)(2,1)}, bf16[128,1024]{1,0:T(8,128)(2,1)}) custom-call(bf16[2,128,256]{2,1,0:T(8,128)(2,1)} %get-tuple-element.67.refs_0_, bf16[2,128,256]{2,1,0:T(8,128)(2,1)} %copy-done.2, bf16[2,128,256]{2,1,0:T(8,128)(2,1)} %copy-done.3, ...), custom_call_target="tpu_custom_call" | custom-call | flops 1 | bytes 1 | tf_op jit(solution)/shard_map/pallas_call | solution.py:27
  66.3 0.7 collective-permute-start.16
  67.0 0.5 collective-permute-start.17
  67.5 2.3 %collective-permute-start.18 = (bf16[128,1024]{1,0:T(8,128)(2,1)}, bf16[128,1024]{1,0:T(8,128)(2,1)}, u32[]{:S(2)}, u32[]{:S(2)}) collective-permute-start(bf16[128,1024]{1,0:T(8,128)(2,1)} %get-tuple-element.87), channel_id=1, source_target_pairs={{0,6},{2,4},{4,2},{6,0},{8,14},{10,12},{12,10},{14,8},{16,22},{18,... | collective-permute-start | bytes 786440 | tf_op jit(solution)/shard_map/ppermute | solution.py:357
  69.8 0.1 all-to-all-done.2
  70.0 7.2 %shard_map.122.refs_4_ = bf16[128,2048]{1,0:T(8,128)(2,1)} custom-call(f32[16,2,16,128]{3,2,1,0:T(8,128)} %bitcast.10.incoming_hbm, f32[16,8,2,16,128]{4,3,2,1,0:T(8,128)} %get-tuple-element.82.fresh_hbm, f32[2048,128]{1,0:T(8,128)} %get-tuple-element.83.dense_hbm, f32[512,128]{1,0:T(8,128)} %get-tuple-element.66.q_hbm, f32[512,128]{1,0:T(8,128)} %get-tuple-element.84.w_hbm, ...), custom_call_target="tpu_custom_call" | custom-call | flops 1 | bytes 1 | tf_op jit(solution)/shard_map/pallas_call | solution.py:27
  77.1 1.2 %collective-permute-done.17.refs_1_ = bf16[128,1024]{1,0:T(8,128)(2,1)} collective-permute-done((bf16[128,1024]{1,0:T(8,128)(2,1)}, bf16[128,1024]{1,0:T(8,128)(2,1)}, u32[]{:S(2)}, u32[]{:S(2)}) %collective-permute-start.17) | collective-permute-done | bytes 262176 | tf_op jit(solution)/shard_map/ppermute | solution.py:357
  78.4 1.3 %collective-permute-done.18.refs_2_ = bf16[128,1024]{1,0:T(8,128)(2,1)} collective-permute-done((bf16[128,1024]{1,0:T(8,128)(2,1)}, bf16[128,1024]{1,0:T(8,128)(2,1)}, u32[]{:S(2)}, u32[]{:S(2)}) %collective-permute-start.18) | collective-permute-done | bytes 262176 | tf_op jit(solution)/shard_map/ppermute | solution.py:357
  79.7 2.2 %shard_map.123.refs_6_ = bf16[128,1024]{1,0:T(8,128)(2,1)} custom-call(bf16[128,1024]{1,0:T(8,128)(2,1)} %collective-permute-done.16.refs_0_, bf16[128,1024]{1,0:T(8,128)(2,1)} %collective-permute-done.17.refs_1_, bf16[128,1024]{1,0:T(8,128)(2,1)} %collective-permute-done.18.refs_2_, f32[128,1024]{1,0:T(8,128)} %get-tuple-element.92.refs_3_), custom_call_target="tpu_custom_call" | custom-call | flops 1 | bytes 1 | tf_op jit(solution)/shard_map/pallas_call | solution.py:27
  81.9 3.5 %shard_map.124 = bf16[128,1024]{1,0:T(8,128)(2,1)} custom-call(bf16[4,256,128]{2,1,0:T(8,128)(2,1)} %pad_maximum_fusion.refs_0_, bf16[4,256,128]{2,1,0:T(8,128)(2,1)} %collective-permute-done.3.refs_1_, bf16[4,256,128]{2,1,0:T(8,128)(2,1)} %collective-permute-done.4.refs_2_, bf16[4,256,128]{2,1,0:T(8,128)(2,1)} %collective-permute-done.5.refs_3_, ...), custom_call_target="tpu_custom_call" | custom-call | flops 1 | bytes 1 | tf_op jit(solution)/shard_map/pallas_call | solution.py:27
  (24 shorter events, 0.1 us)
Async XLA Ops:
  0.0 22.1 %collective-permute-start = (bf16[256,128]{1,0:T(8,128)(2,1)}, bf16[256,128]{1,0:T(8,128)(2,1)S(1)}, u32[]{:S(2)}, u32[]{:S(2)}) collective-permute-start(bf16[256,128]{1,0:T(8,128)(2,1)} %param.21), channel_id=1, source_target_pairs={{0,8},{2,10},{4,12},{6,14},{8,0},{10,2},{12,4},{14,6},{16,24},{18,... | collective-permute-start | bytes 196616 | tf_op jit(solution)/shard_map/ppermute | solution.py:528
  3.0 19.1 %collective-permute-start.2 = (bf16[256,128]{1,0:T(8,128)(2,1)}, bf16[256,128]{1,0:T(8,128)(2,1)S(1)}, u32[]{:S(2)}, u32[]{:S(2)}) collective-permute-start(bf16[256,128]{1,0:T(8,128)(2,1)} %param.21), channel_id=1, source_target_pairs={{0,24},{2,26},{4,28},{6,30},{8,16},{10,18},{12,20},{14,22},{16,8},... | collective-permute-start | bytes 196616 | tf_op jit(solution)/shard_map/ppermute | solution.py:528
  5.5 16.6 %collective-permute-start.1 = (bf16[256,128]{1,0:T(8,128)(2,1)}, bf16[256,128]{1,0:T(8,128)(2,1)S(1)}, u32[]{:S(2)}, u32[]{:S(2)}) collective-permute-start(bf16[256,128]{1,0:T(8,128)(2,1)} %param.21), channel_id=1, source_target_pairs={{0,16},{2,18},{4,20},{6,22},{8,24},{10,26},{12,28},{14,30},{16,0},... | collective-permute-start | bytes 196616 | tf_op jit(solution)/shard_map/ppermute | solution.py:528
  5.6 1.0 %copy-start = (bf16[128,2048]{1,0:T(8,128)(2,1)S(1)}, bf16[128,2048]{1,0:T(8,128)(2,1)}, u32[]{:S(2)}) copy-start(bf16[128,2048]{1,0:T(8,128)(2,1)} %refs_0_.1) | copy-start | bytes 1572868
  7.5 0.6 copy-start.1
  21.6 29.3 %collective-permute-start.9 = (bf16[256,1024]{1,0:T(8,128)(2,1)}, bf16[256,1024]{1,0:T(8,128)(2,1)}, u32[]{:S(2)}, u32[]{:S(2)}) collective-permute-start(bf16[256,1024]{1,0:T(8,128)(2,1)} %refs_8_.3), channel_id=1, source_target_pairs={{0,8},{2,10},{4,12},{6,14},{8,24},{10,26},{12,28},{14,30},{24,16},... | collective-permute-start | bytes 1572872 | tf_op jit(solution)/shard_map/ppermute | solution.py:369
  23.7 16.8 %collective-permute-start.5 = (bf16[4,256,128]{2,1,0:T(8,128)(2,1)}, bf16[4,256,128]{2,1,0:T(8,128)(2,1)}, u32[]{:S(2)}, u32[]{:S(2)}) collective-permute-start(bf16[4,256,128]{2,1,0:T(8,128)(2,1)} %pad_maximum_fusion.refs_0_), channel_id=1, source_target_pairs={{0,6},{2,4},{4,2},{6,0},{8,14},{10,12},{12,10},{14,8},{16,22},{18,... | collective-permute-start | bytes 786440 | tf_op jit(solution)/shard_map/ppermute | solution.py:357
  24.3 16.2 %collective-permute-start.4 = (bf16[4,256,128]{2,1,0:T(8,128)(2,1)}, bf16[4,256,128]{2,1,0:T(8,128)(2,1)}, u32[]{:S(2)}, u32[]{:S(2)}) collective-permute-start(bf16[4,256,128]{2,1,0:T(8,128)(2,1)} %pad_maximum_fusion.refs_0_), channel_id=1, source_target_pairs={{0,4},{2,6},{4,0},{6,2},{8,12},{10,14},{12,8},{14,10},{16,20},{18,... | collective-permute-start | bytes 786440 | tf_op jit(solution)/shard_map/ppermute | solution.py:357
  25.8 14.8 %collective-permute-start.3 = (bf16[4,256,128]{2,1,0:T(8,128)(2,1)}, bf16[4,256,128]{2,1,0:T(8,128)(2,1)}, u32[]{:S(2)}, u32[]{:S(2)}) collective-permute-start(bf16[4,256,128]{2,1,0:T(8,128)(2,1)} %pad_maximum_fusion.refs_0_), channel_id=1, source_target_pairs={{0,2},{2,0},{4,6},{6,4},{8,10},{10,8},{12,14},{14,12},{16,18},{18,... | collective-permute-start | bytes 786440 | tf_op jit(solution)/shard_map/ppermute | solution.py:357
  27.2 25.5 %collective-permute-start.14 = (bf16[256,1024]{1,0:T(8,128)(2,1)}, bf16[256,1024]{1,0:T(8,128)(2,1)}, u32[]{:S(2)}, u32[]{:S(2)}) collective-permute-start(bf16[256,1024]{1,0:T(8,128)(2,1)} %refs_8_.3), channel_id=1, source_target_pairs={{0,16},{2,18},{4,20},{6,22},{8,0},{10,2},{12,4},{14,6},{24,8},{26,... | collective-permute-start | bytes 1572872 | tf_op jit(solution)/shard_map/ppermute | solution.py:369
  37.0 16.2 %all-to-all-start.1 = ((f32[16,1,2,16,128]{4,3,2,1,0:T(8,128)}), f32[16,1,2,16,128]{4,3,2,1,0:T(8,128)S(1)}, u32[]{:S(2)}, u32[]{:S(2)}) async-start(f32[16,1,2,16,128]{4,3,2,1,0:T(8,128)} %bitcast.16), calls=%async_computation.1 | async-start | bytes 524288 | tf_op jit(solution)/shard_map/all_to_all | solution.py:578
  40.6 5.7 %collective-permute-start.6 = (bf16[2,128,256]{2,1,0:T(8,128)(2,1)}, bf16[2,128,256]{2,1,0:T(8,128)(2,1)S(1)}, u32[]{:S(2)}, u32[]{:S(2)}) collective-permute-start(bf16[2,128,256]{2,1,0:T(8,128)(2,1)} %get-tuple-element.62), channel_id=1, source_target_pairs={{0,2},{2,0},{4,6},{6,4},{8,10},{10,8},{12,14},{14,12},{16,18},{18,... | collective-permute-start | bytes 393224 | tf_op jit(solution)/shard_map/ppermute | solution.py:357
  42.4 6.1 %collective-permute-start.7 = (bf16[2,128,256]{2,1,0:T(8,128)(2,1)}, bf16[2,128,256]{2,1,0:T(8,128)(2,1)S(1)}, u32[]{:S(2)}, u32[]{:S(2)}) collective-permute-start(bf16[2,128,256]{2,1,0:T(8,128)(2,1)} %get-tuple-element.63), channel_id=1, source_target_pairs={{0,4},{2,6},{4,0},{6,2},{8,12},{10,14},{12,8},{14,10},{16,20},{18,... | collective-permute-start | bytes 393224 | tf_op jit(solution)/shard_map/ppermute | solution.py:357
  43.9 7.0 %collective-permute-start.8 = (bf16[2,128,256]{2,1,0:T(8,128)(2,1)}, bf16[2,128,256]{2,1,0:T(8,128)(2,1)S(1)}, u32[]{:S(2)}, u32[]{:S(2)}) collective-permute-start(bf16[2,128,256]{2,1,0:T(8,128)(2,1)} %get-tuple-element.64), channel_id=1, source_target_pairs={{0,6},{2,4},{4,2},{6,0},{8,14},{10,12},{12,10},{14,8},{16,22},{18,... | collective-permute-start | bytes 393224 | tf_op jit(solution)/shard_map/ppermute | solution.py:357
  46.2 8.8 %copy-start.2 = (bf16[2,128,256]{2,1,0:T(8,128)(2,1)}, bf16[2,128,256]{2,1,0:T(8,128)(2,1)S(1)}, u32[]{:S(2)}) copy-start(bf16[2,128,256]{2,1,0:T(8,128)(2,1)S(1)} %collective-permute-done.6.refs_1_) | copy-start | bytes 393220
  48.5 6.5 %copy-start.3 = (bf16[2,128,256]{2,1,0:T(8,128)(2,1)}, bf16[2,128,256]{2,1,0:T(8,128)(2,1)S(1)}, u32[]{:S(2)}) copy-start(bf16[2,128,256]{2,1,0:T(8,128)(2,1)S(1)} %collective-permute-done.7.refs_2_) | copy-start | bytes 393220
  50.9 4.1 %copy-start.4 = (bf16[2,128,256]{2,1,0:T(8,128)(2,1)}, bf16[2,128,256]{2,1,0:T(8,128)(2,1)S(1)}, u32[]{:S(2)}) copy-start(bf16[2,128,256]{2,1,0:T(8,128)(2,1)S(1)} %collective-permute-done.8.refs_3_) | copy-start | bytes 393220
  50.9 11.4 %collective-permute-start.15 = (bf16[256,1024]{1,0:T(8,128)(2,1)}, bf16[256,1024]{1,0:T(8,128)(2,1)}, u32[]{:S(2)}, u32[]{:S(2)}) collective-permute-start(bf16[256,1024]{1,0:T(8,128)(2,1)} %collective-permute-done.9.refs_9_), channel_id=1, source_target_pairs={{0,8},{2,10},{4,12},{6,14},{8,24},{10,26},{12,28},{14,30},{24,16},... | collective-permute-start | bytes 1572872 | tf_op jit(solution)/shard_map/ppermute | solution.py:369
  52.2 1.7 %collective-permute-start.10 = (bf16[2,128,256]{2,1,0:T(8,128)(2,1)}, bf16[2,128,256]{2,1,0:T(8,128)(2,1)S(1)}, u32[]{:S(2)}, u32[]{:S(2)}) collective-permute-start(bf16[2,128,256]{2,1,0:T(8,128)(2,1)} %get-tuple-element.67.refs_0_), channel_id=1, source_target_pairs={{0,1},{1,0},{2,3},{3,2},{4,5},{5,4},{6,7},{7,6},{8,9},{9,8},{10,11... | collective-permute-start | bytes 393224 | tf_op jit(solution)/shard_map/ppermute | solution.py:349
  52.2 1.7 %collective-permute-start.11 = (bf16[2,128,256]{2,1,0:T(8,128)(2,1)S(1)}, bf16[2,128,256]{2,1,0:T(8,128)(2,1)S(1)}, u32[]{:S(2)}, u32[]{:S(2)}) collective-permute-start(bf16[2,128,256]{2,1,0:T(8,128)(2,1)S(1)} %collective-permute-done.6.refs_1_), channel_id=1, source_target_pairs={{0,1},{1,0},{2,3},{3,2},{4,5},{5,4},{6,7},{7,6},{8,9},{9,8},{10,11... | collective-permute-start | bytes 393224 | tf_op jit(solution)/shard_map/ppermute | solution.py:349
  52.7 1.3 %collective-permute-start.12 = (bf16[2,128,256]{2,1,0:T(8,128)(2,1)S(1)}, bf16[2,128,256]{2,1,0:T(8,128)(2,1)S(1)}, u32[]{:S(2)}, u32[]{:S(2)}) collective-permute-start(bf16[2,128,256]{2,1,0:T(8,128)(2,1)S(1)} %collective-permute-done.7.refs_2_), channel_id=1, source_target_pairs={{0,1},{1,0},{2,3},{3,2},{4,5},{5,4},{6,7},{7,6},{8,9},{9,8},{10,11... | collective-permute-start | bytes 393224 | tf_op jit(solution)/shard_map/ppermute | solution.py:349
  52.7 1.5 %collective-permute-start.13 = (bf16[2,128,256]{2,1,0:T(8,128)(2,1)S(1)}, bf16[2,128,256]{2,1,0:T(8,128)(2,1)S(1)}, u32[]{:S(2)}, u32[]{:S(2)}) collective-permute-start(bf16[2,128,256]{2,1,0:T(8,128)(2,1)S(1)} %collective-permute-done.8.refs_3_), channel_id=1, source_target_pairs={{0,1},{1,0},{2,3},{3,2},{4,5},{5,4},{6,7},{7,6},{8,9},{9,8},{10,11... | collective-permute-start | bytes 393224 | tf_op jit(solution)/shard_map/ppermute | solution.py:349
  53.9 5.3 %copy-start.5 = (bf16[2,128,256]{2,1,0:T(8,128)(2,1)}, bf16[2,128,256]{2,1,0:T(8,128)(2,1)S(1)}, u32[]{:S(2)}) copy-start(bf16[2,128,256]{2,1,0:T(8,128)(2,1)S(1)} %collective-permute-done.10.refs_4_) | copy-start | bytes 393220
  53.9 5.3 %copy-start.6 = (bf16[2,128,256]{2,1,0:T(8,128)(2,1)}, bf16[2,128,256]{2,1,0:T(8,128)(2,1)S(1)}, u32[]{:S(2)}) copy-start(bf16[2,128,256]{2,1,0:T(8,128)(2,1)S(1)} %collective-permute-done.11.refs_5_) | copy-start | bytes 393220
  54.0 5.2 %copy-start.7 = (bf16[2,128,256]{2,1,0:T(8,128)(2,1)}, bf16[2,128,256]{2,1,0:T(8,128)(2,1)S(1)}, u32[]{:S(2)}) copy-start(bf16[2,128,256]{2,1,0:T(8,128)(2,1)S(1)} %collective-permute-done.12.refs_6_) | copy-start | bytes 393220
  54.2 5.0 %copy-start.8 = (bf16[2,128,256]{2,1,0:T(8,128)(2,1)}, bf16[2,128,256]{2,1,0:T(8,128)(2,1)S(1)}, u32[]{:S(2)}) copy-start(bf16[2,128,256]{2,1,0:T(8,128)(2,1)S(1)} %collective-permute-done.13.refs_7_) | copy-start | bytes 393220
  55.0 14.9 %all-to-all-start.2 = ((f32[16,1,2,16,128]{4,3,2,1,0:T(8,128)}), f32[16,1,2,16,128]{4,3,2,1,0:T(8,128)}, u32[]{:S(2)}, u32[]{:S(2)}) async-start(f32[16,1,2,16,128]{4,3,2,1,0:T(8,128)} %shard_map.120), calls=%async_computation.2 | async-start | bytes 524288 | tf_op jit(solution)/shard_map/all_to_all | solution.py:588
  66.3 10.9 %collective-permute-start.16 = (bf16[128,1024]{1,0:T(8,128)(2,1)}, bf16[128,1024]{1,0:T(8,128)(2,1)}, u32[]{:S(2)}, u32[]{:S(2)}) collective-permute-start(bf16[128,1024]{1,0:T(8,128)(2,1)} %get-tuple-element.85), channel_id=1, source_target_pairs={{0,2},{2,0},{4,6},{6,4},{8,10},{10,8},{12,14},{14,12},{16,18},{18,... | collective-permute-start | bytes 786440 | tf_op jit(solution)/shard_map/ppermute | solution.py:357
  67.0 11.4 %collective-permute-start.17 = (bf16[128,1024]{1,0:T(8,128)(2,1)}, bf16[128,1024]{1,0:T(8,128)(2,1)}, u32[]{:S(2)}, u32[]{:S(2)}) collective-permute-start(bf16[128,1024]{1,0:T(8,128)(2,1)} %get-tuple-element.86), channel_id=1, source_target_pairs={{0,4},{2,6},{4,0},{6,2},{8,12},{10,14},{12,8},{14,10},{16,20},{18,... | collective-permute-start | bytes 786440 | tf_op jit(solution)/shard_map/ppermute | solution.py:357
  67.5 12.2 %collective-permute-start.18 = (bf16[128,1024]{1,0:T(8,128)(2,1)}, bf16[128,1024]{1,0:T(8,128)(2,1)}, u32[]{:S(2)}, u32[]{:S(2)}) collective-permute-start(bf16[128,1024]{1,0:T(8,128)(2,1)} %get-tuple-element.87), channel_id=1, source_target_pairs={{0,6},{2,4},{4,2},{6,0},{8,14},{10,12},{12,10},{14,8},{16,22},{18,... | collective-permute-start | bytes 786440 | tf_op jit(solution)/shard_map/ppermute | solution.py:357
  79.7 2.3 %collective-permute-start.19 = (bf16[128,2048]{1,0:T(8,128)(2,1)}, bf16[128,2048]{1,0:T(8,128)(2,1)}, u32[]{:S(2)}, u32[]{:S(2)}) collective-permute-start(bf16[128,2048]{1,0:T(8,128)(2,1)} %shard_map.122.refs_4_), channel_id=1, source_target_pairs={{0,1},{1,0},{2,3},{3,2},{4,5},{5,4},{6,7},{7,6},{8,9},{9,8},{10,11... | collective-permute-start | bytes 1572872 | tf_op jit(solution)/shard_map/ppermute | solution.py:349
